TPU v7x, 128 devices: a whole 4x4x4 slice. The times are simulated.
128 devices in a mesh: dp: 8 (over z, core), wide: 16 (over x, y).
Axes of the slice: x: 4, y: 4, z: 4, core: 2. Of those that a mesh axis runs over, the one named last changes fastest.
Arguments:
- weights_flat: float32 [344064], P(('dp', 'wide')), as said below
- moment_one: float32 [344064], P(('dp', 'wide')), as said below
- moment_two: float32 [344064], P(('dp', 'wide')), as said below
- codes: float32 [32768, 256], P(('dp', 'wide')), may hold values from -1.8 to 1.8
- code_first: float32 [32768, 256], P(('dp', 'wide'))
- code_second: float32 [32768, 256], P(('dp', 'wide')), as said below
- coords: float32 [3, 131072], P(None, ('dp', 'wide')), may hold values from -1 to 1
- distances: float32 [131072], P(('dp', 'wide')), may hold values from -0.5 to 0.5
- shape_index: int32 [131072], P(('dp', 'wide')), may hold values from 0 to 32767, as said below
Outputs:
- loss_value: float32 [], replicated
- grad_norm: float32 [], replicated
- new_weights: float32 [344064], P(('dp', 'wide'))
- new_moment_one: float32 [344064], P(('dp', 'wide'))
- new_moment_two: float32 [344064], P(('dp', 'wide'))
- weights_copy: bfloat16 [344064], P(('dp', 'wide'))
- new_codes: float32 [32768, 256], P(('dp', 'wide'))
- new_code_first: float32 [32768, 256], P(('dp', 'wide'))
- new_code_second: float32 [32768, 256], P(('dp', 'wide'))
- codes_copy: bfloat16 [32768, 256], P(('dp', 'wide'))
Inputs may be any that keep to these rules, and one draw needn't show every extreme that they name: `shape_index`: of the points of one device, at most 16 have shapes among one device's 256 rows of the table; this is reached on every device, and one device's rows are named by 16 points of every device. `weights_flat`: entries after the first 329714 are zero. `moment_one`: entries after the first 329714 are zero. `moment_two`: Positive, and zero after the first 329714 entries. `code_second`: Positive.
All inputs are finite; a program needn't handle non-finite values.
Results may differ from a plain program's by a relative error of at most 0.001.
Values sent between devices are 32-bit elements; how exact they have to be, the bound alone decides.
No kernel may reach another device: no remote copies, remote signals or barrier semaphores. Data moves between devices by JAX's collectives and lax.ppermute only.
A program may use at most 128 MiB of HBM per device.

v0:
```python
import jax
import jax.numpy as jnp
from jax import lax
from jax.sharding import PartitionSpec as P

LATENT = 256
HID = 512
STEP = 10


DELTA = 0.1
SMOOTH = 0.01
CODE_WEIGHT = 0.001
EIK_WEIGHT = 0.1
CLIP = 0.001
WEIGHT_RATE = 0.02
CODE_RATE = 0.15
BETA_ONE = 0.9
BETA_TWO = 0.999
ADAM_EPS = 1e-08
DECAY = 0.01
HIGH = lax.Precision.HIGHEST


def unpack(flat):
    middle = HID - LATENT - 3
    width_in = LATENT + 3
    first_size = middle * (width_in + 2)
    second_size = HID * (HID + 3)
    first_block = flat[:first_size].reshape(middle, width_in + 2)
    second_block = flat[first_size : first_size + second_size].reshape(HID, HID + 3)
    head_bias = flat[first_size + second_size : first_size + second_size + 1]
    return [
        first_block[:, :width_in].T,
        first_block[:, width_in],
        first_block[:, width_in + 1],
        second_block[:, :HID].T,
        second_block[:, HID],
        second_block[:, HID + 1],
        second_block[:, HID + 2],
        head_bias,
    ]


def normed(direction, gain):
    return direction * (gain * lax.rsqrt(jnp.sum(direction * direction, axis=0) + 1e-12))


def forward_points(pieces, latent, spots):
    (
        first_dir,
        first_gain,
        first_bias,
        second_dir,
        second_gain,
        second_bias,
        head_weight,
        head_bias,
    ) = pieces
    joined = jnp.concatenate([latent, spots], axis=1)
    hidden_one = jax.nn.silu(
        jnp.dot(joined, normed(first_dir, first_gain), precision=HIGH) + first_bias
    )
    widened = jnp.concatenate([hidden_one, joined], axis=1)
    hidden_two = jax.nn.silu(
        jnp.dot(widened, normed(second_dir, second_gain), precision=HIGH) + second_bias
    )
    return jnp.tanh(jnp.dot(hidden_two, head_weight, precision=HIGH) + head_bias[0])


def point_losses(pieces, latent, spots, targets):
    predicted, pullback = jax.vjp(lambda places: forward_points(pieces, latent, places), spots)
    (slope,) = pullback(jnp.ones_like(predicted))
    eikonal = (jnp.sum(slope * slope, axis=1) - 1.0) ** 2
    misfit = DELTA * jnp.tanh(predicted / DELTA) - DELTA * jnp.tanh(targets / DELTA)
    fitting = jnp.sqrt(misfit * misfit + SMOOTH * SMOOTH)
    return fitting + CODE_WEIGHT * jnp.sum(latent * latent, axis=1) + EIK_WEIGHT * eikonal


def adam_update(value, first, second, grad, rate):
    first_new = BETA_ONE * first + (1.0 - BETA_ONE) * grad
    second_new = BETA_TWO * second + (1.0 - BETA_TWO) * grad * grad
    first_hat = first_new / (1.0 - BETA_ONE**STEP)
    second_hat = second_new / (1.0 - BETA_TWO**STEP)
    value_new = value - rate * (first_hat / (jnp.sqrt(second_hat) + ADAM_EPS) + DECAY * value)
    return (value_new, first_new, second_new)


def body(
    weights_flat,
    moment_one,
    moment_two,
    codes,
    code_first,
    code_second,
    coords,
    distances,
    shape_index,
):
    count = coords.shape[1]
    devices = lax.axis_size(("dp", "wide"))
    table_rows = codes.shape[0]
    capacity = max(2, 2 * count // devices)
    every_slot = devices * capacity
    all_points = count * devices
    whole = lax.all_gather(weights_flat, ("dp", "wide"), axis=0, tiled=True)
    owners = shape_index // table_rows
    row_index = shape_index % table_rows
    order = jnp.arange(count, dtype=jnp.int32)
    before = (owners[:, None] == owners[None, :]) & (order[None, :] < order[:, None])
    placed = jnp.sum(before.astype(jnp.int32), axis=1)
    slot_index = owners * capacity + placed
    packed = jnp.concatenate(
        [coords, distances[None, :], row_index[None, :].astype(jnp.float32)], axis=0
    )
    outgoing = jnp.zeros((5, every_slot), jnp.float32).at[4].set(-1.0).at[:, slot_index].set(packed)
    arrived = lax.all_to_all(outgoing, ("dp", "wide"), split_axis=1, concat_axis=1, tiled=True)
    rows_in = arrived[4].astype(jnp.int32)
    filled = (rows_in >= 0).astype(jnp.float32)
    safe_rows = jnp.maximum(rows_in, 0)

    def local_loss(flat, table):
        latent = jnp.take(table, safe_rows, axis=0)
        losses = point_losses(unpack(flat), latent, arrived[0:3].T, arrived[3])
        return jnp.sum(filled * losses) / all_points

    loss_part, pullback = jax.vjp(local_loss, whole, codes)
    weight_full, code_grad = pullback(jnp.ones_like(loss_part))
    weight_grad = lax.psum_scatter(weight_full, ("dp", "wide"), scatter_dimension=0, tiled=True)
    squares_part = jnp.sum(weight_grad * weight_grad) + jnp.sum(code_grad * code_grad)
    loss_value, squares = lax.psum((loss_part, squares_part), ("dp", "wide"))
    grad_norm = jnp.sqrt(squares)
    factor = jnp.minimum(1.0, CLIP / (grad_norm + 1e-06))
    new_weights, first_new, second_new = adam_update(
        weights_flat, moment_one, moment_two, factor * weight_grad, WEIGHT_RATE
    )
    new_codes, code_first_new, code_second_new = adam_update(
        codes, code_first, code_second, factor * code_grad, CODE_RATE
    )
    return (
        loss_value,
        grad_norm,
        new_weights,
        first_new,
        second_new,
        new_weights.astype(jnp.bfloat16),
        new_codes,
        code_first_new,
        code_second_new,
        new_codes.astype(jnp.bfloat16),
    )


def solution(mesh):
    return jax.shard_map(
        body,
        mesh=mesh,
        in_specs=(
            P(("dp", "wide")),
            P(("dp", "wide")),
            P(("dp", "wide")),
            P(("dp", "wide"), None),
            P(("dp", "wide"), None),
            P(("dp", "wide"), None),
            P(None, ("dp", "wide")),
            P(("dp", "wide")),
            P(("dp", "wide")),
        ),
        out_specs=(
            P(),
            P(),
            P(("dp", "wide")),
            P(("dp", "wide")),
            P(("dp", "wide")),
            P(("dp", "wide")),
            P(("dp", "wide"), None),
            P(("dp", "wide"), None),
            P(("dp", "wide"), None),
            P(("dp", "wide"), None),
        ),
        check_vma=False,
    )
```

profile of v0, /device:TPU:0, one launch (start us, length us, event | category | flops | bytes accessed | tf_op | source)
XLA Modules:
  0.0 445.6 jit_solution(5020616792415749870)
XLA Ops:
  11.6 3.5 scatter_fusion
  16.7 11.1 %all-to-all-start = ((f32[5,128,16]{2,0,1:T(8,128)}), f32[5,128,16]{2,0,1:T(8,128)S(1)}, u32[]{:S(2)}, u32[]{:S(2)}) async-start(f32[5,128,16]{2,0,1:T(8,128)} %copy.76), calls=%async_computation | async-start | bytes 1048576 | tf_op jit(solution)/shard_map/all_to_all | solution.py:117
  28.6 13.0 %all-to-all-done = f32[5,128,16]{2,0,1:T(8,128)S(1)} async-done(((f32[5,128,16]{2,0,1:T(8,128)}), f32[5,128,16]{2,0,1:T(8,128)S(1)}, u32[]{:S(2)}, u32[]{:S(2)}) %all-to-all-start) | async-done | bytes 40992 | tf_op jit(solution)/shard_map/all_to_all | solution.py:117
  43.1 6.6 %gather_fusion = f32[2048,256]{1,0:T(8,128)S(1)} fusion(f32[256,256]{1,0:T(8,128)S(1)} %copy-done, s32[2048]{0:T(1024)S(1)} %broadcast_clamp_fusion), kind=kCustom, calls=%fused_computation | custom fusion | bytes 4202496 | tf_op jit(solution)/shard_map/jvp(jit(_take))/gather | solution.py:123
  49.8 2.1 copy.77
  53.9 26.2 %all-gather.3.cloned.1.call-done = f32[128,1,2688]{2,1,0:T(1,128)} async-done(((f32[1,1,2688]{2,1,0:T(1,128)}), f32[128,1,2688]{2,1,0:T(1,128)}) %all-gather.3.cloned.1.call-update) | async-done | bytes 1376272 | tf_op jit(solution)/shard_map/all_gather | solution.py:106
  88.3 2.3 slice.81
  96.5 4.9 %fusion.27 = (f32[2048,253]{0,1:T(8,128)S(1)}, f32[2048,253]{0,1:T(8,128)S(1)}) fusion(f32[253]{0:T(256)S(1)} %get-tuple-element.28, f32[253,259]{0,1:T(8,128)} %copy.93, f32[253]{0:T(256)S(1)} %rsqrt_multiply_fusion.3, f32[2048,3]{0,1:T(4,128)S(1)} %bitcast.74, f32[2048,256]{0,1:T(8,128)S(1)} %get-tuple-element.46), kind=kOutput, calls=%fused_computation.56 | convolution fusion | flops 1613578240 | bytes 6531012 | tf_op jit(solution)/shard_map/jvp(jvp())/dot_general | solution.py:62
  101.5 7.5 %convolution_add_fusion = f32[2048,512]{1,0:T(8,128)S(1)} fusion(f32[2048,3]{0,1:T(4,128)S(1)} %bitcast.75, f32[2048,256]{0,1:T(8,128)S(1)} %get-tuple-element.46, f32[2048,253]{0,1:T(8,128)S(1)} %get-tuple-element.56, f32[512]{0:T(512)S(1)} %get-tuple-element.23, f32[512,512]{0,1:T(8,128)S(1)} %copy.94, f32[512]{0:T(512)S(1)} %rsqrt_multiply_fusion.1), kind=kOutput, calls=%fused_computation.27 | convolution fusion | flops 6445858816 | bytes 9441280 | tf_op jit(solution)/shard_map/jvp(jvp())/dot_general | solution.py:66
  108.9 4.4 fusion.36
  114.1 8.8 %fusion.33 = f32[2048,512]{0,1:T(8,128)S(1)} fusion(f32[512,512]{0,1:T(8,128)S(1)} %copy.94, f32[512]{0:T(512)S(1)} %rsqrt_multiply_fusion.1, f32[2048,512]{1,0:T(8,128)S(1)} %convolution_add_fusion, f32[512]{0:T(512)S(1)} %get-tuple-element.22, f32[2048]{0:T(1024)S(1)} %subtract_multiply_fusion.4), kind=kOutput, calls=%fused_computation.68 | convolution fusion | flops 6453198848 | bytes 9449472 | tf_op jit(solution)/shard_map/jvp(transpose(jvp()))/dot_general | solution.py:66
  125.8 2.1 fusion.46
  128.0 2.6 fusion.11
  131.9 6.6 %multiply_add_fusion.1 = (f32[2048,253]{0,1:T(8,128)}, f32[2048,253]{0,1:T(8,128)}) fusion(f32[2048,253]{0,1:T(8,128)} %copy-done.5, f32[253,259]{0,1:T(8,128)} %copy.93, f32[253]{0:T(256)S(1)} %rsqrt_multiply_fusion.3, f32[2048,3]{0,1:T(4,128)S(1)} %add_multiply_fusion), kind=kOutput, calls=%fused_computation.48 | convolution fusion | flops 1615120384 | bytes 6505424 | tf_op jit(solution)/shard_map/transpose(jvp(transpose(jvp())))/dot_general | solution.py:62
  138.5 3.0 copy.83
  141.5 19.4 %fusion.8 = f32[512,512]{1,0:T(8,128)S(1)} fusion(f32[2048,3]{1,0:T(8,128)} %copy.84, f32[2048,253]{1,0:T(8,128)} %copy.83, f32[512]{0:T(512)S(1)} %copy-done.27, f32[2048,512]{1,0:T(8,128)} %copy-done.8, f32[512]{0:T(512)S(1)} %get-tuple-element.22, f32[2048]{0:T(1024)S(1)} %subtract_multiply_fusion.4), kind=kOutput, calls=%fused_computation.25 | convolution fusion | flops 6455033856 | bytes 7352320 | tf_op jit(solution)/shard_map/transpose(jvp(transpose(jvp())))/dot_general | solution.py:66
  161.0 8.4 %multiply_add_fusion = (f32[2048,512]{1,0:T(8,128)S(1)}, f32[2048,512]{1,0:T(8,128)S(1)}) fusion(f32[2048,512]{1,0:T(8,128)S(1)} %copy-done.9, f32[512,512]{0,1:T(8,128)S(1)} %copy.94, f32[512]{0:T(512)S(1)} %rsqrt_multiply_fusion.1, f32[2048,3]{1,0:T(8,128)S(1)} %copy-done.17, f32[2048,253]{1,0:T(8,128)S(1)} %copy-done.13, f32[512]{0:T(512)S(1)} %copy-done.27), kind=kOutput, calls=%fused_computation.20 | convolution fusion | flops 6454247424 | bytes 15732736 | tf_op jit(solution)/shard_map/transpose(jvp(transpose(jvp())))/dot_general | solution.py:66
  169.4 3.6 fusion.95
  173.1 2.5 fusion.96
  176.8 3.9 fusion.91
  180.8 6.9 %fusion.32 = f32[2048,512]{0,1:T(8,128)S(1)} fusion(f32[2048,512]{1,0:T(8,128)S(1)} %get-tuple-element.42, f32[512,512]{0,1:T(8,128)S(1)} %copy.94, f32[512]{0:T(512)S(1)} %rsqrt_multiply_fusion.1), kind=kOutput, calls=%fused_computation.67 | convolution fusion | flops 6442713088 | bytes 9439232 | tf_op jit(solution)/shard_map/transpose(jvp(jvp()))/dot_general | solution.py:66
  187.7 8.2 %fusion.31 = (f32[512]{0:T(512)S(1)}, f32[512,512]{1,0:T(8,128)}) fusion(f32[512,512]{0,1:T(8,128)S(1)} %copy.94, f32[512,512]{1,0:T(8,128)S(1)} %fusion.8, f32[2048,512]{1,0:T(8,128)S(1)} %get-tuple-element.42, f32[2048,3]{0,1:T(4,128)S(1)} %bitcast.76, f32[2048,256]{0,1:T(8,128)S(1)} %get-tuple-element.46, f32[2048,253]{0,1:T(8,128)S(1)} %copy-done.12), kind=kOutput, calls=%fused_computation.65 | convolution fusion | flops 6445334016 | bytes 11536384 | tf_op jit(solution)/shard_map/transpose(jvp(jvp()))/dot_general | solution.py:66
  200.6 3.4 fusion.45
  206.0 2.8 fusion.34
  211.5 2.0 reshape.179
  216.6 2.3 reshape.178
  218.8 3.0 pad_add_fusion
  221.9 4.4 fusion.22
  226.2 3.0 copy.90
  229.2 12.3 %scatter_custom_fusion.1 = f32[256,256]{1,0:T(8,128)S(1)} fusion(s32[2048]{0:T(1024)S(1)} %reshape.182, f32[2048,256]{1,0:T(8,128)} %copy.90, f32[]{:T(128)} %constant.134.clone.1), kind=kCustom, calls=%fused_computation.100 | custom fusion | flops 524288 | bytes 262656 | tf_op jit(solution)/shard_map/transpose(jvp(jit(_take)))/scatter-add | solution.py:123
  242.9 124.9 %all-reduce.15.cloned.1.call-done = f32[344064]{0:T(1024)} async-done(((f32[344064]{0:T(1024)}), f32[344064]{0:T(1024)}) %all-reduce.15.cloned.1.call-update) | async-done | bytes 1376272
  370.4 63.5 %all-reduce.12 = (f32[]{:T(128)}, f32[]{:T(128)}) all-reduce(f32[]{:T(128)S(6)} %div.85, f32[]{:T(128)S(6)} %add.202), channel_id=1, replica_groups=mesh['dp'=8,'wide'=16] {'dp','wide'}, use_global_device_ids=true, to_apply=%region_7.8 | all-reduce | flops 2 | bytes 16 | tf_op jit(solution)/shard_map/psum | solution.py:131
  (118 shorter events, 47.6 us)
Async XLA Ops:
  7.2 4.4 copy-start.7
  7.2 72.8 %all-gather.3.cloned.1.call-start = ((), (), s32[]{:S(2)}) async-start(), calls=%async_computation.1 | async-start | bytes 1387008 | tf_op jit(solution)/shard_map/all_gather | solution.py:106
  15.1 28.1 %copy-start = (f32[256,256]{1,0:T(8,128)S(1)}, f32[256,256]{1,0:T(8,128)}, u32[]{:S(2)}) copy-start(f32[256,256]{1,0:T(8,128)} %param.14) | copy-start | bytes 786436
  16.7 24.8 %all-to-all-start = ((f32[5,128,16]{2,0,1:T(8,128)}), f32[5,128,16]{2,0,1:T(8,128)S(1)}, u32[]{:S(2)}, u32[]{:S(2)}) async-start(f32[5,128,16]{2,0,1:T(8,128)} %copy.76), calls=%async_computation | async-start | bytes 1048576 | tf_op jit(solution)/shard_map/all_to_all | solution.py:117
  27.9 339.9 %all-reduce.15.cloned.1.call-start = ((), (), s32[]{:S(2)}) async-start(), calls=%async_computation.2 | async-start | bytes 2752512
  86.5 4.0 copy-start.16
  91.0 0.7 copy-start.10
  91.9 9.5 %copy-start.23 = (f32[253]{0:T(256)}, f32[253]{0:T(256)S(1)}, u32[]{:S(2)}) copy-start(f32[253]{0:T(256)S(1)} %get-tuple-element.27) | copy-start | bytes 3040
  96.5 5.0 %copy-start.25 = (f32[253]{0:T(256)}, f32[253]{0:T(256)S(1)}, u32[]{:S(2)}) copy-start(f32[253]{0:T(256)S(1)} %fusion.42) | copy-start | bytes 3040
  101.4 7.5 %copy-start.11 = (f32[2048,253]{0,1:T(8,128)}, f32[2048,253]{0,1:T(8,128)S(1)}, u32[]{:S(2)}) copy-start(f32[2048,253]{0,1:T(8,128)S(1)} %get-tuple-element.56) | copy-start | bytes 6217732
  101.5 21.6 %copy-start.5 = (f32[2048,253]{0,1:T(8,128)}, f32[2048,253]{0,1:T(8,128)S(1)}, u32[]{:S(2)}) copy-start(f32[2048,253]{0,1:T(8,128)S(1)} %get-tuple-element.57) | copy-start | bytes 6217732
  108.9 5.1 %copy-start.8 = (f32[2048,512]{1,0:T(8,128)}, f32[2048,512]{1,0:T(8,128)S(1)}, u32[]{:S(2)}) copy-start(f32[2048,512]{1,0:T(8,128)S(1)} %convolution_add_fusion) | copy-start | bytes 12582916
  122.8 1.9 copy-start.3
  124.8 1.0 copy-start.1
  138.5 3.0 copy-start.27
  141.5 19.4 %copy-start.9 = (f32[2048,512]{1,0:T(8,128)S(1)}, f32[2048,512]{1,0:T(8,128)}, u32[]{:S(2)}) copy-start(f32[2048,512]{1,0:T(8,128)} %copy-done.8) | copy-start | bytes 12582916
  141.5 19.4 %copy-start.13 = (f32[2048,253]{1,0:T(8,128)S(1)}, f32[2048,253]{1,0:T(8,128)}, u32[]{:S(2)}) copy-start(f32[2048,253]{1,0:T(8,128)} %copy.83) | copy-start | bytes 6217732
  141.5 19.4 %copy-start.17 = (f32[2048,3]{1,0:T(8,128)S(1)}, f32[2048,3]{1,0:T(8,128)}, u32[]{:S(2)}) copy-start(f32[2048,3]{1,0:T(8,128)} %copy.84) | copy-start | bytes 73732
  180.8 6.9 %copy-start.12 = (f32[2048,253]{0,1:T(8,128)S(1)}, f32[2048,253]{0,1:T(8,128)}, u32[]{:S(2)}) copy-start(f32[2048,253]{0,1:T(8,128)} %copy-done.11) | copy-start | bytes 6217732
  187.7 9.8 %copy-start.6 = (f32[2048,253]{0,1:T(8,128)S(1)}, f32[2048,253]{0,1:T(8,128)}, u32[]{:S(2)}) copy-start(f32[2048,253]{0,1:T(8,128)} %copy-done.5) | copy-start | bytes 6217732
  187.7 9.8 %copy-start.14 = (f32[2048,253]{0,1:T(8,128)S(1)}, f32[2048,253]{0,1:T(8,128)}, u32[]{:S(2)}) copy-start(f32[2048,253]{0,1:T(8,128)} %get-tuple-element.59) | copy-start | bytes 6217732
  195.9 3.0 copy-start.4
  198.8 1.8 copy-start.2
  200.6 3.4 copy-start.15
  204.1 1.9 copy-start.24
  204.1 2.0 copy-start.26
  226.2 208.5 %copy-start.18 = (f32[256,256]{1,0:T(8,128)S(1)}, f32[256,256]{1,0:T(8,128)}, u32[]{:S(2)}) copy-start(f32[256,256]{1,0:T(8,128)} %param.15) | copy-start | bytes 786436
  226.2 208.5 %copy-start.19 = (f32[256,256]{1,0:T(8,128)S(1)}, f32[256,256]{1,0:T(8,128)}, u32[]{:S(2)}) copy-start(f32[256,256]{1,0:T(8,128)} %param.16) | copy-start | bytes 786436
  229.2 206.5 %copy-start.20 = (f32[2688]{0:T(1024)S(1)}, f32[2688]{0:T(1024)}, u32[]{:S(2)}) copy-start(f32[2688]{0:T(1024)} %param.11) | copy-start | bytes 32260
  229.2 206.5 %copy-start.21 = (f32[2688]{0:T(1024)S(1)}, f32[2688]{0:T(1024)}, u32[]{:S(2)}) copy-start(f32[2688]{0:T(1024)} %param.12) | copy-start | bytes 32260
  229.2 206.5 %copy-start.22 = (f32[2688]{0:T(1024)S(1)}, f32[2688]{0:T(1024)}, u32[]{:S(2)}) copy-start(f32[2688]{0:T(1024)} %param.13) | copy-start | bytes 32260
Sparse Core Ops, SparseCore 0:
  11.4 68.5 all-gather.2
  222.0 145.7 all-reduce.14
where the time goes:
time: 452 us; the launch traced here: 446 us
  waiting for transfers between devices  164 us (36%)
  matrix products  94.1 us (21%)
  blocking collectives  63.5 us (14%)
  local copies, waits for them, and re-layouts  51.8 us (11%)
  other arithmetic  42.1 us (9%)
  between operations  18.9 us (4%)
  starting transfers between devices  11.2 us (2%)
    unnamed x3, waiting for transfers between devices  125 us
    psum x1, blocking collectives, body(): loss_value, squares = lax.psum((loss_part, squares_part), ('dp', 'wide'))  63.5 us
    dot_general x6, matrix products, forward_points(): jnp.dot(widened, normed(second_dir, second_gain), precision=HIGH)  59.1 us
    all_gather x1, waiting for transfers between devices, body(): whole = lax.all_gather(weights_flat, ('dp', 'wide'), axis=0, tiled=True)  26.2 us
    dot_general x6, matrix products, forward_points(): jnp.dot(joined, normed(first_dir, first_gain), precision=HIGH) + first_bias  21.6 us
    dot_general x4, matrix products, forward_points(): jnp.dot(hidden_two, head_weight, precision=HIGH) + head_bias[0]  13.4 us
    all_to_all x1, waiting for transfers between devices, body(): lax.all_to_all(outgoing, ('dp', 'wide'), split_axis=1, concat_axis=1, til...  13 us
    scatter-add x1, other arithmetic, local_loss(): latent = jnp.take(table, safe_rows, axis=0)  12.3 us
  transfers between devices with their start and end apart: 3, of which 3 were waited for; matrix products, arithmetic and copies ran while one was open for 9% of the time, Pallas kernels for 0%

commit v1 on v0

--- a/solution.py
+++ b/solution.py
@@ -103,7 +103,8 @@
     capacity = max(2, 2 * count // devices)
     every_slot = devices * capacity
     all_points = count * devices
-    whole = lax.all_gather(weights_flat, ("dp", "wide"), axis=0, tiled=True)
+    row = lax.all_gather(weights_flat, "wide", axis=0, tiled=True)
+    whole = lax.all_gather(row, "dp", axis=0, tiled=True)
     owners = shape_index // table_rows
     row_index = shape_index % table_rows
     order = jnp.arange(count, dtype=jnp.int32)
@@ -114,7 +115,11 @@
         [coords, distances[None, :], row_index[None, :].astype(jnp.float32)], axis=0
     )
     outgoing = jnp.zeros((5, every_slot), jnp.float32).at[4].set(-1.0).at[:, slot_index].set(packed)
-    arrived = lax.all_to_all(outgoing, ("dp", "wide"), split_axis=1, concat_axis=1, tiled=True)
+    n_dp, n_wide = lax.axis_size("dp"), lax.axis_size("wide")
+    boxes = outgoing.reshape(5, n_dp, n_wide, capacity).transpose(2, 1, 0, 3)
+    boxes = lax.all_to_all(boxes, "wide", split_axis=0, concat_axis=0)
+    boxes = lax.all_to_all(boxes.transpose(1, 0, 2, 3), "dp", split_axis=0, concat_axis=0)
+    arrived = boxes.transpose(2, 0, 1, 3).reshape(5, every_slot)
     rows_in = arrived[4].astype(jnp.int32)
     filled = (rows_in >= 0).astype(jnp.float32)
     safe_rows = jnp.maximum(rows_in, 0)
@@ -126,9 +131,13 @@
 
     loss_part, pullback = jax.vjp(local_loss, whole, codes)
     weight_full, code_grad = pullback(jnp.ones_like(loss_part))
-    weight_grad = lax.psum_scatter(weight_full, ("dp", "wide"), scatter_dimension=0, tiled=True)
+    pieces = weight_full.reshape(n_dp, n_wide, weights_flat.shape[0]).transpose(1, 0, 2)
+    pieces = jnp.sum(lax.all_to_all(pieces, "wide", split_axis=0, concat_axis=0), axis=0)
+    weight_grad = jnp.sum(lax.all_to_all(pieces, "dp", split_axis=0, concat_axis=0), axis=0)
     squares_part = jnp.sum(weight_grad * weight_grad) + jnp.sum(code_grad * code_grad)
-    loss_value, squares = lax.psum((loss_part, squares_part), ("dp", "wide"))
+    totals = lax.psum(jnp.stack([loss_part, squares_part]), "wide")
+    totals = lax.psum(totals, "dp")
+    loss_value, squares = totals[0], totals[1]
     grad_norm = jnp.sqrt(squares)
     factor = jnp.minimum(1.0, CLIP / (grad_norm + 1e-06))
     new_weights, first_new, second_new = adam_update(

time: 452 us -> 329 us (0.73)
  waiting for transfers between devices: 164 us -> 9.86 us
  blocking collectives: 63.5 us -> 91.4 us
    unnamed x3 -> x1, waiting for transfers between devices: 125 us -> 0.02 us
    all_gather x1, waiting for transfers between devices: 26.2 us -> 0.02 us  [body(): whole = lax.all_gather(row, 'dp', axis=0, tiled=True)]
    all_gather x0 -> x1, blocking collectives: none -> 26 us  [body(): row = lax.all_gather(weights_flat, 'wide', axis=0, tiled=True)]
    all_to_all x0 -> x1, blocking collectives: none -> 12.3 us  [body(): boxes = lax.all_to_all(boxes, 'wide', split_axis=0, concat_axis=0)]
    psum x1 -> x2, blocking collectives: 63.5 us -> 53.1 us  [the longest x1 40.7 us: body(): totals = lax.psum(jnp.stack([loss_part, squares_part]), 'wide')]
    all_to_all x1 -> x3, waiting for transfers between devices: 13 us -> 9.82 us  [the longest x1 4.98 us: body(): lax.all_to_all(pieces, 'dp', split_axis=0, concat_axis=0)]
    all_to_all x1 -> x3, starting transfers between devices: 11.1 us -> 13.3 us  [the longest x1 5.31 us: body(): lax.all_to_all(boxes.transpose(1, 0, 2, 3), 'dp', split_axis=0, concat_ax...]
  transfers between devices with their start and end apart: 3 -> 4, of which waited for: 3 -> 2; matrix products, arithmetic and copies ran while one was open for 9% -> 14% of each run, Pallas kernels for 0% -> 0%
where the time goes in v1:
time: 329 us; the launch traced here: 323 us
  matrix products  92.7 us (28%)
  blocking collectives  91.4 us (28%)
  local copies, waits for them, and re-layouts  56.1 us (17%)
  other arithmetic  40 us (12%)
  between operations  19.1 us (6%)
  starting transfers between devices  13.4 us (4%)
  waiting for transfers between devices  9.86 us (3%)
    dot_general x6, matrix products, forward_points(): jnp.dot(widened, normed(second_dir, second_gain), precision=HIGH)  59.1 us
    psum x1, blocking collectives, body(): totals = lax.psum(jnp.stack([loss_part, squares_part]), 'wide')  40.7 us
    all_gather x1, blocking collectives, body(): row = lax.all_gather(weights_flat, 'wide', axis=0, tiled=True)  26 us
    dot_general x6, matrix products, forward_points(): jnp.dot(joined, normed(first_dir, first_gain), precision=HIGH) + first_bias  20.2 us
    dot_general x4, matrix products, forward_points(): jnp.dot(hidden_two, head_weight, precision=HIGH) + head_bias[0]  13.4 us
    psum x1, blocking collectives, body(): totals = lax.psum(totals, 'dp')  12.4 us
    all_to_all x1, blocking collectives, body(): boxes = lax.all_to_all(boxes, 'wide', split_axis=0, concat_axis=0)  12.3 us
    scatter-add x1, other arithmetic, local_loss(): latent = jnp.take(table, safe_rows, axis=0)  12.1 us
  transfers between devices with their start and end apart: 4, of which 2 were waited for; matrix products, arithmetic and copies ran while one was open for 14% of the time, Pallas kernels for 0%

profile of v1, /device:TPU:0, one launch (start us, length us, event | category | flops | bytes accessed | tf_op | source)
XLA Modules:
  0.0 322.6 jit_solution(425206998111944864)
XLA Ops:
  8.0 26.0 %all-gather = f32[16,1,2688]{2,1,0:T(1,128)} all-gather(f32[1,1,2688]{2,1,0:T(1,128)S(1)} %reshape.215), channel_id=1, replica_groups=mesh['dp'=8,'wide'=16] {'wide'}, dimensions={0}, use_global_device_ids=true | all-gather | bytes 182784 | tf_op jit(solution)/shard_map/all_gather | solution.py:106
  37.0 3.5 %scatter_fusion = f32[5,2048]{0,1:T(8,128)S(1)} fusion(f32[5,2048]{0,1:T(8,128)S(1)} %copy-done.11, s32[1024]{0:T(1024)S(1)} %get-tuple-element.49, f32[1024,5]{1,0:T(8,128)S(1)} %copy.94), kind=kCustom, calls=%fused_computation.1 | custom fusion | bytes 65536 | tf_op jit(solution)/shard_map/scatter | solution.py:117
  41.6 12.3 %all_to_all.24 = f32[16,1,640]{2,1,0:T(1,128)S(1)} all-to-all(f32[16,1,640]{2,1,0:T(1,128)S(1)} %reshape.235), channel_id=1, replica_groups=mesh['dp'=8,'wide'=16] {'wide'}, dimensions={0} | all-to-all | bytes 81920 | tf_op jit(solution)/shard_map/all_to_all | solution.py:120
  56.2 5.3 %all-to-all-start.1 = ((f32[8,1,1280]{2,1,0:T(1,128)}), f32[8,1,1280]{2,1,0:T(1,128)S(1)}, u32[]{:S(2)}, u32[]{:S(2)}) async-start(f32[8,1,1280]{2,1,0:T(1,128)} %reshape.237), calls=%async_computation.1 | async-start | bytes 81920 | tf_op jit(solution)/shard_map/all_to_all | solution.py:121
  62.2 4.8 %all-to-all-done.1 = f32[8,1,1280]{2,1,0:T(1,128)S(1)} async-done(((f32[8,1,1280]{2,1,0:T(1,128)}), f32[8,1,1280]{2,1,0:T(1,128)S(1)}, u32[]{:S(2)}, u32[]{:S(2)}) %all-to-all-start.1) | async-done | bytes 40992 | tf_op jit(solution)/shard_map/all_to_all | solution.py:121
  68.6 6.6 %gather_fusion = f32[2048,256]{1,0:T(8,128)S(1)} fusion(f32[256,256]{1,0:T(8,128)S(1)} %copy-done, s32[2048]{0:T(1024)S(1)} %broadcast_clamp_fusion), kind=kCustom, calls=%fused_computation | custom fusion | bytes 4202496 | tf_op jit(solution)/shard_map/jvp(jit(_take))/gather | solution.py:128
  84.6 2.3 slice.89
  92.9 4.9 %fusion.27 = (f32[2048,253]{0,1:T(8,128)S(1)}, f32[2048,253]{0,1:T(8,128)S(1)}) fusion(f32[253]{0:T(256)S(1)} %get-tuple-element.26, f32[253,259]{0,1:T(8,128)} %copy.114, f32[253]{0:T(256)S(1)} %rsqrt_multiply_fusion.3, f32[2048,3]{0,1:T(4,128)S(1)} %bitcast.112, f32[2048,256]{0,1:T(8,128)S(1)} %get-tuple-element.36), kind=kOutput, calls=%fused_computation.56 | convolution fusion | flops 1613578240 | bytes 6531012 | tf_op jit(solution)/shard_map/jvp(jvp())/dot_general | solution.py:62
  97.8 7.5 %convolution_add_fusion = f32[2048,512]{1,0:T(8,128)S(1)} fusion(f32[2048,3]{0,1:T(4,128)S(1)} %bitcast.113, f32[2048,256]{0,1:T(8,128)S(1)} %get-tuple-element.36, f32[2048,253]{0,1:T(8,128)S(1)} %get-tuple-element.56, f32[512]{0:T(512)S(1)} %get-tuple-element.23, f32[512,512]{0,1:T(8,128)S(1)} %copy.115, f32[512]{0:T(512)S(1)} %rsqrt_multiply_fusion.1), kind=kOutput, calls=%fused_computation.27 | convolution fusion | flops 6445858816 | bytes 9441280 | tf_op jit(solution)/shard_map/jvp(jvp())/dot_general | solution.py:66
  105.3 4.4 %fusion.36 = f32[1,2048]{1,0:T(1,128)S(1)} fusion(f32[512,1]{0,1:T(1,128)S(1)} %bitcast.121, f32[2048,512]{1,0:T(8,128)S(1)} %convolution_add_fusion), kind=kOutput, calls=%fused_computation.70 | convolution fusion | flops 16777216 | bytes 4204544 | tf_op jit(solution)/shard_map/jvp(jvp())/dot_general | solution.py:68
  111.0 8.8 %fusion.33 = f32[2048,512]{0,1:T(8,128)S(1)} fusion(f32[512,512]{0,1:T(8,128)S(1)} %copy.115, f32[512]{0:T(512)S(1)} %rsqrt_multiply_fusion.1, f32[2048,512]{1,0:T(8,128)S(1)} %convolution_add_fusion, f32[512]{0:T(512)S(1)} %get-tuple-element.22, f32[2048]{0:T(1024)S(1)} %subtract_multiply_fusion.4), kind=kOutput, calls=%fused_computation.68 | convolution fusion | flops 6453198848 | bytes 9449472 | tf_op jit(solution)/shard_map/jvp(transpose(jvp()))/dot_general | solution.py:66
  124.9 2.6 fusion.11
  128.9 6.6 %multiply_add_fusion.1 = (f32[2048,253]{0,1:T(8,128)}, f32[2048,253]{0,1:T(8,128)}) fusion(f32[2048,253]{0,1:T(8,128)} %copy-done.9, f32[253,259]{0,1:T(8,128)} %copy.114, f32[253]{0:T(256)S(1)} %rsqrt_multiply_fusion.3, f32[2048,3]{0,1:T(4,128)S(1)} %add_multiply_fusion), kind=kOutput, calls=%fused_computation.48 | convolution fusion | flops 1615120384 | bytes 6505424 | tf_op jit(solution)/shard_map/transpose(jvp(transpose(jvp())))/dot_general | solution.py:62
  135.5 3.0 copy.103
  138.5 19.4 %fusion.8 = f32[512,512]{1,0:T(8,128)S(1)} fusion(f32[2048,3]{1,0:T(8,128)} %copy.104, f32[2048,253]{1,0:T(8,128)} %copy.103, f32[512]{0:T(512)S(1)} %copy-done.31, f32[2048,512]{1,0:T(8,128)} %copy-done.12, f32[512]{0:T(512)S(1)} %get-tuple-element.22, f32[2048]{0:T(1024)S(1)} %subtract_multiply_fusion.4), kind=kOutput, calls=%fused_computation.25 | convolution fusion | flops 6455033856 | bytes 7352320 | tf_op jit(solution)/shard_map/transpose(jvp(transpose(jvp())))/dot_general | solution.py:66
  158.0 8.4 %multiply_add_fusion = (f32[2048,512]{1,0:T(8,128)S(1)}, f32[2048,512]{1,0:T(8,128)S(1)}) fusion(f32[2048,512]{1,0:T(8,128)S(1)} %copy-done.13, f32[512,512]{0,1:T(8,128)S(1)} %copy.115, f32[512]{0:T(512)S(1)} %rsqrt_multiply_fusion.1, f32[2048,3]{1,0:T(8,128)S(1)} %copy-done.21, f32[2048,253]{1,0:T(8,128)S(1)} %copy-done.17, f32[512]{0:T(512)S(1)} %copy-done.31), kind=kOutput, calls=%fused_computation.20 | convolution fusion | flops 6454247424 | bytes 15732736 | tf_op jit(solution)/shard_map/transpose(jvp(transpose(jvp())))/dot_general | solution.py:66
  166.4 3.6 %fusion.95 = f32[1,2048]{1,0:T(1,128)S(1)} fusion(f32[2048,512]{1,0:T(8,128)S(1)} %get-tuple-element.60, f32[512,1]{0,1:T(1,128)S(1)} %bitcast.122), kind=kOutput, calls=%fused_computation.174 | convolution fusion | flops 12582912 | bytes 4204544 | tf_op jit(solution)/shard_map/transpose(jvp(transpose(jvp())))/dot_general | solution.py:68
  170.0 2.5 fusion.96
  173.8 3.9 %fusion.90 = (f32[512]{0:T(512)S(1)}, f32[2048,512]{1,0:T(8,128)S(1)}) fusion(f32[2048,512]{1,0:T(8,128)S(1)} %get-tuple-element.61, f32[2048,512]{1,0:T(8,128)S(1)} %copy-done.13, f32[2048]{0:T(1024)S(1)} %get-tuple-element.38, f32[512]{0:T(512)S(1)} %get-tuple-element.22, f32[2048]{0:T(1024)S(1)} %subtract_multiply_fusion.4), kind=kLoop, calls=%fused_computation.167 | loop fusion | flops 25165312 | bytes 12603392 | tf_op jit(solution)/shard_map/transpose(jvp(jvp()))/reduce_sum | solution.py:66
  177.8 6.9 %fusion.32 = f32[2048,512]{0,1:T(8,128)S(1)} fusion(f32[2048,512]{1,0:T(8,128)S(1)} %get-tuple-element.40, f32[512,512]{0,1:T(8,128)S(1)} %copy.115, f32[512]{0:T(512)S(1)} %rsqrt_multiply_fusion.1), kind=kOutput, calls=%fused_computation.67 | convolution fusion | flops 6442713088 | bytes 9439232 | tf_op jit(solution)/shard_map/transpose(jvp(jvp()))/dot_general | solution.py:66
  184.7 8.1 %fusion.31 = (f32[512]{0:T(512)S(1)}, f32[512,512]{1,0:T(8,128)}) fusion(f32[512,512]{0,1:T(8,128)S(1)} %copy.115, f32[512,512]{1,0:T(8,128)S(1)} %fusion.8, f32[2048,512]{1,0:T(8,128)S(1)} %get-tuple-element.40, f32[2048,3]{0,1:T(4,128)S(1)} %bitcast.114, f32[2048,256]{0,1:T(8,128)S(1)} %get-tuple-element.36, f32[2048,253]{0,1:T(8,128)S(1)} %copy-done.16), kind=kOutput, calls=%fused_computation.65 | convolution fusion | flops 6445334016 | bytes 11536384 | tf_op jit(solution)/shard_map/transpose(jvp(jvp()))/dot_general | solution.py:66
  196.7 2.8 fusion.34
  209.6 3.0 pad_add_fusion
  212.7 2.6 reshape.187
  215.3 2.9 copy.109
  218.2 4.6 %all-to-all-start.2 = ((f32[16,8,2688]{2,1,0:T(8,128)}), f32[16,8,2688]{2,1,0:T(8,128)}, u32[]{:S(2)}, u32[]{:S(2)}) async-start(f32[16,8,2688]{2,1,0:T(8,128)} %copy.109), calls=%async_computation.2 | async-start | bytes 2752512 | tf_op jit(solution)/shard_map/all_to_all | solution.py:135
  229.1 2.9 copy.111
  232.0 12.1 %scatter_custom_fusion.1 = f32[256,256]{1,0:T(8,128)S(1)} fusion(s32[2048]{0:T(1024)S(1)} %reshape.190, f32[2048,256]{1,0:T(8,128)} %copy.111, f32[]{:T(128)} %constant.134.clone.1), kind=kCustom, calls=%fused_computation.98 | custom fusion | flops 524288 | bytes 262656 | tf_op jit(solution)/shard_map/transpose(jvp(jit(_take)))/scatter-add | solution.py:128
  246.9 3.4 %all-to-all-start.3 = ((f32[8,1,2688]{2,1,0:T(1,128)}), f32[8,1,2688]{2,1,0:T(1,128)S(1)}, u32[]{:S(2)}, u32[]{:S(2)}) async-start(f32[8,1,2688]{2,1,0:T(1,128)} %all_to_all.18), calls=%async_computation.3 | async-start | bytes 172032 | tf_op jit(solution)/shard_map/all_to_all | solution.py:136
  251.0 5.0 %all-to-all-done.3 = f32[8,1,2688]{2,1,0:T(1,128)S(1)} async-done(((f32[8,1,2688]{2,1,0:T(1,128)}), f32[8,1,2688]{2,1,0:T(1,128)S(1)}, u32[]{:S(2)}, u32[]{:S(2)}) %all-to-all-start.3) | async-done | bytes 86048 | tf_op jit(solution)/shard_map/all_to_all | solution.py:136
  258.0 40.7 %psum.14 = f32[2]{0:T(128)S(1)} all-reduce(f32[2]{0:T(128)S(1)} %pad_maximum_fusion.13), channel_id=1, replica_groups=mesh['dp'=8,'wide'=16] {'wide'}, use_global_device_ids=true, to_apply=%region_17.18 | all-reduce | flops 2 | bytes 16 | tf_op jit(solution)/shard_map/psum | solution.py:138
  298.7 12.4 %psum.15 = f32[2]{0:T(128)S(1)} all-reduce(f32[2]{0:T(128)S(1)} %psum.14), channel_id=1, replica_groups=mesh['dp'=8,'wide'=16] {'dp'}, use_global_device_ids=true, to_apply=%region_18.19 | all-reduce | flops 2 | bytes 16 | tf_op jit(solution)/shard_map/psum | solution.py:139
  (149 shorter events, 59.5 us)
Async XLA Ops:
  7.2 29.8 %copy-start.11 = (f32[5,2048]{0,1:T(8,128)S(1)}, f32[5,2048]{0,1:T(8,128)}, u32[]{:S(2)}) copy-start(f32[5,2048]{0,1:T(8,128)} %constant.124.clone.1) | copy-start | bytes 122884
  7.2 72.1 %all-gather.3.cloned.1.call-start = ((), (), s32[]{:S(2)}) async-start(), calls=%async_computation.4 | async-start | bytes 1548288 | tf_op jit(solution)/shard_map/all_gather | solution.py:107
  55.3 13.3 %copy-start = (f32[256,256]{1,0:T(8,128)S(1)}, f32[256,256]{1,0:T(8,128)}, u32[]{:S(2)}) copy-start(f32[256,256]{1,0:T(8,128)} %param.14) | copy-start | bytes 786436
  56.2 10.8 %all-to-all-start.1 = ((f32[8,1,1280]{2,1,0:T(1,128)}), f32[8,1,1280]{2,1,0:T(1,128)S(1)}, u32[]{:S(2)}, u32[]{:S(2)}) async-start(f32[8,1,1280]{2,1,0:T(1,128)} %reshape.237), calls=%async_computation.1 | async-start | bytes 81920 | tf_op jit(solution)/shard_map/all_to_all | solution.py:121
  82.9 4.0 %slice-start = ((f32[344064]{0:T(1024)}), f32[66033]{0:T(1024)S(1)}, s32[]{:S(2)}) async-start(f32[344064]{0:T(1024)} %all-gather.3.cloned.1.call-done), calls=%async_computation.5 | async-start | bytes 532480 | tf_op jit(solution)/shard_map/jvp()/slice | solution.py:30
  88.3 9.5 %copy-start.27 = (f32[253]{0:T(256)}, f32[253]{0:T(256)S(1)}, u32[]{:S(2)}) copy-start(f32[253]{0:T(256)S(1)} %get-tuple-element.25) | copy-start | bytes 3040
  92.8 4.9 %copy-start.29 = (f32[253]{0:T(256)}, f32[253]{0:T(256)S(1)}, u32[]{:S(2)}) copy-start(f32[253]{0:T(256)S(1)} %fusion.42) | copy-start | bytes 3040
  97.8 7.5 %copy-start.15 = (f32[2048,253]{0,1:T(8,128)}, f32[2048,253]{0,1:T(8,128)S(1)}, u32[]{:S(2)}) copy-start(f32[2048,253]{0,1:T(8,128)S(1)} %get-tuple-element.56) | copy-start | bytes 6217732
  97.8 22.2 %copy-start.9 = (f32[2048,253]{0,1:T(8,128)}, f32[2048,253]{0,1:T(8,128)S(1)}, u32[]{:S(2)}) copy-start(f32[2048,253]{0,1:T(8,128)S(1)} %get-tuple-element.57) | copy-start | bytes 6217732
  105.3 5.7 %copy-start.12 = (f32[2048,512]{1,0:T(8,128)}, f32[2048,512]{1,0:T(8,128)S(1)}, u32[]{:S(2)}) copy-start(f32[2048,512]{1,0:T(8,128)S(1)} %convolution_add_fusion) | copy-start | bytes 12582916
  105.3 4.5 %copy-start.19 = (f32[344064]{0:T(1024)S(1)}, f32[344064]{0:T(1024)}, u32[]{:S(2)}) copy-start(f32[344064]{0:T(1024)} %all-gather.3.cloned.1.call-done) | copy-start | bytes 4128772
  135.5 3.0 copy-start.31
  138.5 19.4 %copy-start.13 = (f32[2048,512]{1,0:T(8,128)S(1)}, f32[2048,512]{1,0:T(8,128)}, u32[]{:S(2)}) copy-start(f32[2048,512]{1,0:T(8,128)} %copy-done.12) | copy-start | bytes 12582916
  138.5 19.4 %copy-start.17 = (f32[2048,253]{1,0:T(8,128)S(1)}, f32[2048,253]{1,0:T(8,128)}, u32[]{:S(2)}) copy-start(f32[2048,253]{1,0:T(8,128)} %copy.103) | copy-start | bytes 6217732
  138.5 19.4 %copy-start.21 = (f32[2048,3]{1,0:T(8,128)S(1)}, f32[2048,3]{1,0:T(8,128)}, u32[]{:S(2)}) copy-start(f32[2048,3]{1,0:T(8,128)} %copy.104) | copy-start | bytes 73732
  177.8 6.9 %copy-start.16 = (f32[2048,253]{0,1:T(8,128)S(1)}, f32[2048,253]{0,1:T(8,128)}, u32[]{:S(2)}) copy-start(f32[2048,253]{0,1:T(8,128)} %copy-done.15) | copy-start | bytes 6217732
  184.7 8.2 %copy-start.1 = (f32[2048,512]{0,1:T(8,128)}, f32[2048,512]{0,1:T(8,128)S(1)}, u32[]{:S(2)}) copy-start(f32[2048,512]{0,1:T(8,128)S(1)} %fusion.32) | copy-start | bytes 12582916
  184.7 8.2 %copy-start.8 = (f32[2048,512]{0,1:T(8,128)S(1)}, f32[2048,512]{0,1:T(8,128)}, u32[]{:S(2)}) copy-start(f32[2048,512]{0,1:T(8,128)} %copy-done.7) | copy-start | bytes 12582916
  184.7 8.2 %copy-start.10 = (f32[2048,253]{0,1:T(8,128)S(1)}, f32[2048,253]{0,1:T(8,128)}, u32[]{:S(2)}) copy-start(f32[2048,253]{0,1:T(8,128)} %copy-done.9) | copy-start | bytes 6217732
  184.7 8.2 %copy-start.18 = (f32[2048,253]{0,1:T(8,128)S(1)}, f32[2048,253]{0,1:T(8,128)}, u32[]{:S(2)}) copy-start(f32[2048,253]{0,1:T(8,128)} %get-tuple-element.59) | copy-start | bytes 6217732
  194.7 2.0 copy-start.2
  194.7 2.0 copy-start.28
  194.7 2.0 copy-start.30
  218.2 26.6 %all-to-all-start.2 = ((f32[16,8,2688]{2,1,0:T(8,128)}), f32[16,8,2688]{2,1,0:T(8,128)}, u32[]{:S(2)}, u32[]{:S(2)}) async-start(f32[16,8,2688]{2,1,0:T(8,128)} %copy.109), calls=%async_computation.2 | async-start | bytes 2752512 | tf_op jit(solution)/shard_map/all_to_all | solution.py:135
  222.8 2.2 copy-start.3
  222.8 2.2 copy-start.6
  232.0 80.4 %copy-start.24 = (f32[2688]{0:T(1024)S(1)}, f32[2688]{0:T(1024)}, u32[]{:S(2)}) copy-start(f32[2688]{0:T(1024)} %param.11) | copy-start | bytes 32260
  232.0 80.5 %copy-start.25 = (f32[2688]{0:T(1024)S(1)}, f32[2688]{0:T(1024)}, u32[]{:S(2)}) copy-start(f32[2688]{0:T(1024)} %param.12) | copy-start | bytes 32260
  232.0 80.5 %copy-start.26 = (f32[2688]{0:T(1024)S(1)}, f32[2688]{0:T(1024)}, u32[]{:S(2)}) copy-start(f32[2688]{0:T(1024)} %param.13) | copy-start | bytes 32260
  232.0 81.1 %copy-start.22 = (f32[256,256]{1,0:T(8,128)S(1)}, f32[256,256]{1,0:T(8,128)}, u32[]{:S(2)}) copy-start(f32[256,256]{1,0:T(8,128)} %param.15) | copy-start | bytes 786436
  232.0 81.1 %copy-start.23 = (f32[256,256]{1,0:T(8,128)S(1)}, f32[256,256]{1,0:T(8,128)}, u32[]{:S(2)}) copy-start(f32[256,256]{1,0:T(8,128)} %param.16) | copy-start | bytes 786436
  246.9 9.0 %all-to-all-start.3 = ((f32[8,1,2688]{2,1,0:T(1,128)}), f32[8,1,2688]{2,1,0:T(1,128)S(1)}, u32[]{:S(2)}, u32[]{:S(2)}) async-start(f32[8,1,2688]{2,1,0:T(1,128)} %all_to_all.18), calls=%async_computation.3 | async-start | bytes 172032 | tf_op jit(solution)/shard_map/all_to_all | solution.py:136
  (5 other events, 7.3 us)
Sparse Core Ops, SparseCore 0:
  34.2 24.5 all-gather.2

commit v2 on v0

v2 whole, which is shorter than its diff:
```python
import jax
import jax.numpy as jnp
from jax import lax
from jax.experimental import pallas as pl
from jax.experimental.pallas import tpu as pltpu
from jax.sharding import Mesh
from jax.sharding import PartitionSpec as P

LATENT = 256
HID = 512
MIDDLE = HID - LATENT - 3
STEP = 10

DELTA = 0.1
SMOOTH = 0.01
CODE_WEIGHT = 0.001
EIK_WEIGHT = 0.1
CLIP = 0.001
WEIGHT_RATE = 0.02
CODE_RATE = 0.15
BETA_ONE = 0.9
BETA_TWO = 0.999
ADAM_EPS = 1e-08
DECAY = 0.01

LANES = 128
DEVICES = 128
PEERS = 64
SHARD_ROWS = 21
BOX_ROWS = 24
SLOTS = 16
POINTS_DEV = 1024
CODE_ROWS = 256
FLAT_ROWS = DEVICES * SHARD_ROWS
BLOCK = 256
ALL_POINTS = POINTS_DEV * DEVICES

F32 = jnp.float32
BF16 = jnp.bfloat16
ALL = ("z", "core", "wide")


def rows_of_lanes(lead, shape):
    return lax.broadcasted_iota(jnp.int32, shape, lead)


def halves(v):
    high = v.astype(BF16)
    return high, (v - high.astype(F32)).astype(BF16)


def thirds(v):
    high = v.astype(BF16).astype(F32)
    rest = v - high
    mid = rest.astype(BF16).astype(F32)
    return high, mid, rest - mid


def mm(a, b):
    return lax.dot_general(a, b, (((1,), (0,)), ((), ())), preferred_element_type=F32)


def mm_nt(a, b):
    return lax.dot_general(a, b, (((1,), (1,)), ((), ())), preferred_element_type=F32)


def beside(*parts):
    return jnp.concatenate(parts, axis=1)


def total_of(v):
    return jnp.sum(jnp.sum(v, axis=0, keepdims=True), axis=1, keepdims=True)


def stacked(*parts):
    return jnp.concatenate(parts, axis=0)


def pack_kernel(weights_ref, coords_ref, distances_ref, index_ref, out_ref):
    shard = stacked(weights_ref[...], jnp.zeros((BOX_ROWS - SHARD_ROWS, LANES), F32))
    for peer in range(PEERS):
        out_ref[peer * BOX_ROWS : (peer + 1) * BOX_ROWS, :] = shard
    index = index_ref[...]
    owner = lax.shift_right_logical(index, 8)
    row = lax.bitwise_and(index, CODE_ROWS - 1)
    sent = (rows_of_lanes(0, (DEVICES, POINTS_DEV)) == owner).astype(F32)
    sent_low = sent.astype(BF16)
    width = 256
    earlier = rows_of_lanes(0, (width, width)) < rows_of_lanes(1, (width, width))
    earlier = earlier.astype(F32).astype(BF16)
    ones = jnp.ones((width, width), BF16)
    ranks = [
        mm(sent_low[:, : (part + 1) * width], stacked(*([ones] * part + [earlier])))
        for part in range(POINTS_DEV // width)
    ]
    placed = jnp.sum(sent * beside(*ranks), axis=0, keepdims=True).astype(jnp.int32)
    at_slot = rows_of_lanes(0, (SLOTS, POINTS_DEV)) == placed
    values = [coords_ref[i : i + 1, :] for i in range(3)]
    values += [distances_ref[...], (row + 1).astype(F32)]
    pieces = [[], [], []]
    for value in values:
        for k, third in enumerate(thirds(value)):
            pieces[k].append(jnp.where(at_slot, third, 0.0))
    spare = jnp.zeros((LANES - SLOTS * len(values), POINTS_DEV), F32)
    boxes = mm_nt(
        beside(sent_low, sent_low, sent_low),
        beside(*[stacked(*piece, spare).astype(BF16) for piece in pieces]),
    )
    for z in range(4):
        for core in range(2):
            first = z * 32 + core * 16
            out_ref[pl.ds(z * 16 * BOX_ROWS + SHARD_ROWS + core, 16, stride=BOX_ROWS), :] = boxes[
                first : first + 16, :
            ]


def unit_groups(count, stride_rows, extra, first_entry):
    for group in range(count):
        entry = first_entry + group * 8 * (stride_rows * LANES + extra)
        yield group, entry // LANES, entry % LANES


def unpack_units(flat_ref, out_ref, count, stride_rows, extra, first_entry):
    lane = rows_of_lanes(1, (8, LANES))
    slope = rows_of_lanes(0, (8, LANES)) * extra
    for group, first, shift in unit_groups(count, stride_rows, extra, first_entry):
        start = slope + shift
        wraps = shift + 7 * extra >= LANES
        turn = lax.bitwise_and(lane + start, LANES - 1)
        tiles = []
        for a in range(stride_rows + 2 + wraps):
            tile = flat_ref[pl.ds(first + a, 8, stride=stride_rows), :]
            tiles.append(jnp.take_along_axis(tile, turn, axis=1, mode="promise_in_bounds"))
        for c in range(stride_rows + 1):
            value = jnp.where(lane + start < LANES, tiles[c], tiles[c + 1])
            if wraps:
                value = jnp.where(lane + start < 2 * LANES, value, tiles[c + 2])
            out_ref[group * 8 : group * 8 + 8, c * LANES : (c + 1) * LANES] = value


def pack_units(value_ref, flat_ref, count, stride_rows, extra, first_entry, adding):
    lane = rows_of_lanes(1, (8, LANES))
    slope = rows_of_lanes(0, (8, LANES)) * extra
    zero = jnp.zeros((8, LANES), F32)
    for group, first, shift in unit_groups(count, stride_rows, extra, first_entry):
        start = slope + shift
        wraps = shift + 7 * extra >= LANES
        wanted = range(stride_rows, stride_rows + 1 + wraps + 1) if adding else range(stride_rows)
        rolled = {}

        turn = lax.bitwise_and(lane - start, LANES - 1)

        def tile(c, rolled=rolled, group=group, turn=turn):
            if c < 0 or c > stride_rows:
                return zero
            if c not in rolled:
                value = value_ref[group * 8 : group * 8 + 8, c * LANES : (c + 1) * LANES]
                rolled[c] = jnp.take_along_axis(value, turn, axis=1, mode="promise_in_bounds")
            return rolled[c]

        for a in wanted:
            value = jnp.where(lane >= start, tile(a), tile(a - 1))
            if wraps:
                value = jnp.where(lane >= start - LANES, value, tile(a - 2))
            rows = pl.ds(first + a, 8, stride=stride_rows)
            if adding:
                flat_ref[rows, :] = flat_ref[rows, :] + value
            else:
                flat_ref[rows, :] = value


FIRST_UNITS = (32, 2, 5, 0)
SECOND_UNITS = (64, 4, 3, MIDDLE * (LATENT + 5))
HEAD_ENTRY = MIDDLE * (LATENT + 5) + HID * (HID + 3)


def silu_parts(v):
    gate = 0.5 * jnp.tanh(0.5 * v) + 0.5
    rest = 1.0 - gate
    value = v * gate
    slope = gate + value * rest
    curve = rest * (gate + gate + value * (rest - gate))
    return value, slope, curve


def main_kernel(
    core_ref,
    mine_ref,
    other_ref,
    codes_ref,
    out_ref,
    code_grad_ref,
    flat,
    first_w,
    second_w,
    lhs_one,
    lhs_two,
    lhs_back,
    latent_w,
    coord_w,
    head_w,
    spots,
    sum_two,
    sum_codes,
    sum_coord,
    sum_head,
    sum_count,
    sum_loss,
    act_one,
    slope_one,
    curve_one,
    back_one,
    hid_hi,
    hid_lo,
    hot,
    act_two,
    slope_two,
    curve_two,
    gate_hi,
    gate_lo,
    tang_hi,
    tang_lo,
    near_hi,
    near_lo,
    bar_hi,
    bar_lo,
    low_hi,
    low_lo,
):
    core = core_ref[0]

    for which in range(2):

        @pl.when(core == which)
        def _(which=which):
            for d in range(DEVICES):
                z, c, w = d // 32, d // 16 % 2, d % 16
                box = (z * 16 + w) * BOX_ROWS
                source = mine_ref if c == which else other_ref
                flat[d * SHARD_ROWS : d * SHARD_ROWS + BOX_ROWS, :] = source[box : box + BOX_ROWS, :]
            rows = pl.ds(SHARD_ROWS + which, PEERS, stride=BOX_ROWS)
            spots[...] = stacked(mine_ref[rows, :], other_ref[rows, :]).T

    unpack_units(flat, first_w, *FIRST_UNITS)
    unpack_units(flat, second_w, *SECOND_UNITS)
    head_bias = flat[HEAD_ENTRY // LANES : HEAD_ENTRY // LANES + 1, :][
        :, HEAD_ENTRY % LANES : HEAD_ENTRY % LANES + 1
    ]

    lane = rows_of_lanes(1, (256, LANES))
    unit = rows_of_lanes(0, (256, LANES))
    real = unit < MIDDLE

    first_low = jnp.where(beside(real, real), first_w[:, : 2 * LANES], 0.0)
    first_end = jnp.where(real, first_w[:, 2 * LANES :], 0.0)
    first_near = jnp.where(lane < 3, first_end, 0.0)
    first_gain = first_end[:, 3:4]
    first_bias = first_end[:, 4:5]
    first_w[:, : 2 * LANES] = first_low
    first_w[:, 2 * LANES :] = first_end
    first_root = lax.rsqrt(
        jnp.sum(first_low * first_low, axis=1, keepdims=True)
        + jnp.sum(first_near * first_near, axis=1, keepdims=True)
        + 1e-12
    )
    first_scale = first_gain * first_root
    first_low = first_low * first_scale
    first_near = first_near * first_scale
    latent_w[0:256, :] = first_low
    for i in range(3):
        coord_w[:, i * LANES : (i + 1) * LANES] = jnp.broadcast_to(
            first_near[:, i : i + 1], (256, LANES)
        )

    second_a = second_w[:, 0:256]
    second_b = second_w[:, 256:512]
    second_gain = second_w[:, 512:513]
    second_bias = second_w[:, 513:514]
    head_w[...] = jnp.broadcast_to(second_w[:, 514:515], (HID, LANES))
    second_root = lax.rsqrt(
        jnp.sum(second_a * second_a + second_b * second_b, axis=1, keepdims=True) + 1e-12
    )
    second_scale = second_gain * second_root
    second_a = second_a * second_scale
    second_b = second_b * second_scale
    is_hidden = rows_of_lanes(1, (HID, 256)) < MIDDLE
    hidden_cols = jnp.where(is_hidden, second_a, second_b)
    latent_cols = pltpu.roll(jnp.where(is_hidden, second_b, second_a), 3, 1)
    latent_w[256:768, :] = latent_cols

    hidden_hi, hidden_lo = halves(hidden_cols)
    lhs_two[:, 0:256] = hidden_hi
    lhs_two[:, 256:512] = hidden_hi
    lhs_two[:, 512:768] = hidden_lo
    back_hi, back_lo = halves(hidden_cols.T)
    lhs_back[:, 0:512] = back_hi
    lhs_back[:, 512:1024] = back_hi
    lhs_back[:, 1024:1536] = back_lo

    code_hi, code_lo = halves(codes_ref[...])
    weight_hi, weight_lo = halves(latent_w[...])
    by_code = mm_nt(
        beside(weight_hi, weight_hi, weight_lo), beside(code_hi, code_lo, code_hi)
    )
    one_hi, one_lo = halves(by_code[0:256, :] + first_bias)
    lhs_one[:, 0:256] = one_hi
    lhs_one[:, 256:512] = one_lo
    two_hi, two_lo = halves(by_code[256:768, :] + second_bias)
    lhs_two[:, 768:1024] = two_hi
    lhs_two[:, 1024:1280] = two_lo
    spread = jnp.where((unit - MIDDLE == lane) & (lane < 3), 1.0, first_near)
    near_parts = thirds(spread)
    near_lhs = near_parts[0]
    for place, k in enumerate((0, 0, 1, 1, 2)):
        near_lhs = near_lhs + pltpu.roll(near_parts[k], 8 * (place + 1), 1)
    lhs_one[:, 512:640] = near_lhs.astype(BF16)

    for ref in (sum_two, sum_codes, sum_coord, sum_head, sum_count, sum_loss):
        ref[...] = jnp.zeros(ref.shape, F32)

    def feature(which, step, sub):
        first = which * SLOTS + step * 4 + sub * 2
        return beside(spots[pl.ds(first, 1), :], spots[pl.ds(first + 1, 1), :])

    blank5 = jnp.zeros((5, BLOCK), F32)
    subs = range(2)
    chunk = 32

    def step_body(step, carry):
        place = [[feature(i, step, s) for i in range(3)] for s in subs]
        target = [feature(3, step, s) for s in subs]
        code_row = [feature(4, step, s) for s in subs]
        valid = [(code_row[s] > 0.5).astype(F32) for s in subs]
        near8 = [stacked(*place[s], blank5) for s in subs]
        near_pieces = [thirds(near8[s]) for s in subs]

        for s in subs:
            wanted = code_row[s] - 1.0
            for r in range(0, CODE_ROWS, chunk):
                mark = jnp.where(
                    (rows_of_lanes(0, (chunk, BLOCK)) + r).astype(F32) == wanted, 1.0, 0.0
                )
                hot[s, r : r + chunk, :] = mark.astype(BF16)
                sum_count[r : r + chunk, :] += mark[:, :LANES] + mark[:, LANES:]

        for s in subs:
            high, mid, low = near_pieces[s]
            near_rhs = stacked(
                high, mid, low, high, mid, high, jnp.zeros((80, BLOCK), F32)
            ).astype(BF16)
            act_one[s] = mm(lhs_one[...], stacked(hot[s], hot[s], near_rhs))
        for s in subs:
            for r in range(0, 256, chunk):
                pre = act_one[s, r : r + chunk, :]
                value, slope, curve = silu_parts(pre)
                if r + chunk == 256:
                    inside = rows_of_lanes(0, (chunk, BLOCK)) + r < MIDDLE
                    value = jnp.where(inside, value, pre)
                    slope = jnp.where(inside, slope, 0.0)
                    curve = jnp.where(inside, curve, 0.0)
                high, low = halves(value)
                hid_hi[s, r : r + chunk, :] = high
                hid_lo[s, r : r + chunk, :] = low
                slope_one[s, r : r + chunk, :] = slope
                curve_one[s, r : r + chunk, :] = curve

        for s in subs:
            act_two[s] = mm(
                lhs_two[...], stacked(hid_hi[s], hid_lo[s], hid_hi[s], hot[s], hot[s])
            )
        summed = []
        for s in subs:
            total = jnp.zeros((8, BLOCK), F32)
            for r in range(0, HID, chunk):
                value, slope, curve = silu_parts(act_two[s, r : r + chunk, :])
                head = beside(head_w[r : r + chunk, :], head_w[r : r + chunk, :])
                weighed = head * value
                for k in range(0, chunk, 8):
                    total = total + weighed[k : k + 8, :]
                high, low = halves(head * slope)
                gate_hi[s, r : r + chunk, :] = high
                gate_lo[s, r : r + chunk, :] = low
                act_two[s, r : r + chunk, :] = value
                slope_two[s, r : r + chunk, :] = slope
                curve_two[s, r : r + chunk, :] = curve
            summed.append(jnp.sum(total, axis=0, keepdims=True))

        for s in subs:
            back_one[s] = mm(lhs_back[...], stacked(gate_hi[s], gate_lo[s], gate_hi[s]))
        leads = []
        for s in subs:
            totals = [jnp.zeros((8, BLOCK), F32) for _ in range(3)]
            for r in range(0, 256, chunk):
                grad = back_one[s, r : r + chunk, :] * slope_one[s, r : r + chunk, :]
                high, low = halves(grad)
                near_hi[s, r : r + chunk, :] = high
                near_lo[s, r : r + chunk, :] = low
                for i in range(3):
                    col = coord_w[r : r + chunk, i * LANES : (i + 1) * LANES]
                    weighed = beside(col, col) * grad
                    for k in range(0, chunk, 8):
                        totals[i] = totals[i] + weighed[k : k + 8, :]
            leads.append(
                [
                    jnp.sum(totals[i], axis=0, keepdims=True)
                    + back_one[s, MIDDLE + i : MIDDLE + i + 1, :]
                    for i in range(3)
                ]
            )

        bars, pulls = [], []
        for s in subs:
            predicted = jnp.tanh(summed[s] + head_bias)
            flank = 1.0 - predicted * predicted
            slope = [flank * q for q in leads[s]]
            excess = slope[0] * slope[0] + slope[1] * slope[1] + slope[2] * slope[2] - 1.0
            capped = jnp.tanh(predicted / DELTA)
            misfit = DELTA * capped - DELTA * jnp.tanh(target[s] / DELTA)
            fitting = jnp.sqrt(misfit * misfit + SMOOTH * SMOOTH)
            loss = fitting + EIK_WEIGHT * excess * excess
            sum_loss[0:1, :] += valid[s] * loss
            share = valid[s] * (1.0 / ALL_POINTS)
            pull = [(4.0 * EIK_WEIGHT) * excess * v for v in slope]
            by_flank = sum(p * q for p, q in zip(pull, leads[s]))
            by_predicted = misfit / fitting * (1.0 - capped * capped) - 2.0 * predicted * by_flank
            bars.append(share * by_predicted * flank)
            sum_loss[1:2, :] += bars[s]
            pulls.append([share * flank * p for p in pull])

        for s in subs:
            last = stacked(blank5, *pulls[s])
            for r in range(0, 256, chunk):
                grad = 0.0
                for i in range(3):
                    col = coord_w[r : r + chunk, i * LANES : (i + 1) * LANES]
                    grad = grad + beside(col, col) * pulls[s][i]
                through = grad * slope_one[s, r : r + chunk, :]
                if r + chunk == 256:
                    inside = rows_of_lanes(0, (8, BLOCK)) < MIDDLE - 248
                    through = stacked(
                        through[: chunk - 8], jnp.where(inside, through[chunk - 8 :], last)
                    )
                high, low = halves(through)
                tang_hi[s, r : r + chunk, :] = high
                tang_lo[s, r : r + chunk, :] = low
                curve_one[s, r : r + chunk, :] = (
                    grad * back_one[s, r : r + chunk, :] * curve_one[s, r : r + chunk, :]
                )
        tangents = []
        for s in subs:
            tangents.append(
                mm(lhs_two[:, 0:768], stacked(tang_hi[s], tang_lo[s], tang_hi[s]))
            )
        for s in subs:
            for r in range(0, HID, chunk):
                tangent = tangents[s][r : r + chunk, :]
                slope = slope_two[s, r : r + chunk, :]
                head = beside(head_w[r : r + chunk, :], head_w[r : r + chunk, :])
                bar = head * (bars[s] * slope + tangent * curve_two[s, r : r + chunk, :])
                by_head = act_two[s, r : r + chunk, :] * bars[s] + slope * tangent
                sum_head[r : r + chunk, :] += by_head[:, :LANES] + by_head[:, LANES:]
                high, low = halves(bar)
                bar_hi[s, r : r + chunk, :] = high
                bar_lo[s, r : r + chunk, :] = low

        for s in subs:
            back_one[s] = mm(lhs_back[...], stacked(bar_hi[s], bar_lo[s], bar_hi[s]))
        left, right = [], []
        for s in subs:
            left += [bar_hi[s], bar_hi[s], bar_lo[s], gate_hi[s], gate_hi[s], gate_lo[s]]
            right += [hid_hi[s], hid_lo[s], hid_hi[s], tang_hi[s], tang_lo[s], tang_hi[s]]
        sum_two[...] += mm_nt(beside(*left), beside(*right))
        hots = beside(hot[0], hot[0], hot[1], hot[1])
        sum_codes[256:768, :] += mm_nt(beside(bar_hi[0], bar_lo[0], bar_hi[1], bar_lo[1]), hots)

        for s in subs:
            for r in range(0, 256, chunk):
                bar = (
                    back_one[s, r : r + chunk, :] * slope_one[s, r : r + chunk, :]
                    + curve_one[s, r : r + chunk, :]
                )
                high, low = halves(bar)
                low_hi[s, r : r + chunk, :] = high
                low_lo[s, r : r + chunk, :] = low
        sum_codes[0:256, :] += mm_nt(beside(low_hi[0], low_lo[0], low_hi[1], low_lo[1]), hots)
        left, right = [], []
        for s in subs:
            seen = stacked(near_pieces[s][0], near_pieces[s][1]).astype(BF16)
            pulled = stacked(*pulls[s], blank5)
            high = pulled.astype(BF16).astype(F32)
            pulled = stacked(high, pulled - high).astype(BF16)
            left += [seen, seen, pulled, pulled]
            right += [low_hi[s], low_lo[s], near_hi[s], near_lo[s]]
        sum_coord[...] += mm_nt(beside(*left), beside(*right))
        return carry

    lax.fori_loop(0, SLOTS * DEVICES // (2 * BLOCK), step_body, 0)

    codes = codes_ref[...]
    count = jnp.sum(sum_count[...], axis=1, keepdims=True)
    by_code = sum_codes[...]
    turned_hi, turned_lo = halves(by_code.T)
    weight_hi, weight_lo = halves(latent_w[...])
    code_grad = mm(
        beside(turned_hi, turned_hi, turned_lo), stacked(weight_hi, weight_lo, weight_hi)
    )
    code_grad = code_grad + (2.0 * CODE_WEIGHT / ALL_POINTS) * count * codes
    code_grad_ref[...] = code_grad
    code_squares = total_of(code_grad * code_grad)
    loss = jnp.sum(sum_loss[0:1, :], axis=1, keepdims=True)
    loss = loss + CODE_WEIGHT * total_of(count * codes * codes)
    loss = loss / ALL_POINTS

    code_hi, code_lo = halves(codes)
    by_hi, by_lo = halves(by_code)
    latent_grad = mm(beside(by_hi, by_hi, by_lo), stacked(code_hi, code_lo, code_hi))
    bias_grad = jnp.sum(by_code, axis=1, keepdims=True)

    near_grad = sum_coord[0:8, :] + sum_coord[8:16, :]
    near_grad = stacked(near_grad, jnp.zeros((LANES - 8, 256), F32)).T
    near_grad = jnp.where(lane < 3, near_grad, 0.0)
    low_grad = latent_grad[0:256, :]
    first_low = first_w[:, : 2 * LANES]
    first_near = jnp.where(lane < 3, first_w[:, 2 * LANES :], 0.0)
    along = jnp.sum(first_low * low_grad, axis=1, keepdims=True)
    along = along + jnp.sum(first_near * near_grad, axis=1, keepdims=True)
    inward = first_scale * first_root * first_root * along
    end = first_scale * near_grad - first_near * inward
    end = jnp.where(lane == 3, first_root * along, end)
    end = jnp.where(lane == 4, bias_grad[0:256, :], end)
    low_grad = first_scale * low_grad - first_low * inward
    first_w[:, : 2 * LANES] = jnp.where(beside(real, real), low_grad, 0.0)
    first_w[:, 2 * LANES :] = jnp.where(real, end, 0.0)

    hidden_grad = sum_two[...]
    moved = pltpu.roll(latent_grad[256:768, :], 256 - 3, 1)
    grad_a = jnp.where(is_hidden, hidden_grad, moved)
    grad_b = jnp.where(is_hidden, moved, hidden_grad)
    second_a = second_w[:, 0:256]
    second_b = second_w[:, 256:512]
    along = jnp.sum(second_a * grad_a + second_b * grad_b, axis=1, keepdims=True)
    inward = second_scale * second_root * second_root * along
    second_w[:, 0:256] = second_scale * grad_a - second_a * inward
    second_w[:, 256:512] = second_scale * grad_b - second_b * inward
    head_grad = jnp.sum(sum_head[...], axis=1, keepdims=True)
    lane = rows_of_lanes(1, (HID, LANES))
    end = jnp.where(lane == 0, second_root * along, 0.0)
    end = jnp.where(lane == 1, bias_grad[256:768, :], end)
    second_w[:, 512:640] = jnp.where(lane == 2, head_grad, end)

    flat[...] = jnp.zeros(flat.shape, F32)
    for adding in (False, True):
        pack_units(first_w, flat, *FIRST_UNITS, adding)
        pack_units(second_w, flat, *SECOND_UNITS, adding)
    row = HEAD_ENTRY // LANES
    lane = rows_of_lanes(1, (1, LANES))
    bias_total = jnp.sum(sum_loss[1:2, :], axis=1, keepdims=True)
    flat[row : row + 1, :] = flat[row : row + 1, :] + jnp.where(
        lane == HEAD_ENTRY % LANES, bias_total, 0.0
    )
    sub = rows_of_lanes(0, (8, LANES))
    wide = rows_of_lanes(1, (8, LANES))
    info = jnp.where((sub == 5) & (wide == 0), loss, 0.0)
    info = jnp.where((sub == 5) & (wide == 1), code_squares, info)
    for d in range(DEVICES):
        z, c, w = d // 32, d // 16 % 2, d % 16
        half = jnp.where(core == c, 0, PEERS * BOX_ROWS)
        base = pl.multiple_of(half + (z * 16 + w) * BOX_ROWS, 8)
        first = d * SHARD_ROWS
        out_ref[pl.ds(base, 16), :] = flat[first : first + 16, :]
        out_ref[pl.ds(base + 16, 8), :] = jnp.where(sub < 5, flat[first + 16 : first + 24, :], info)


def vmem(count):
    return [pl.BlockSpec(memory_space=pltpu.VMEM)] * count


PARAMS = pltpu.CompilerParams(vmem_limit_bytes=48 * 1024 * 1024)


def pack_boxes(weights, coords, distances, index):
    return pl.pallas_call(
        pack_kernel,
        out_shape=jax.ShapeDtypeStruct((PEERS * BOX_ROWS, LANES), F32),
        in_specs=vmem(4),
        out_specs=vmem(1)[0],
        compiler_params=PARAMS,
    )(weights, coords, distances, index)


def main_call(core, mine, other, codes):
    pair = (2, 256, BLOCK)
    pair_two = (2, HID, BLOCK)
    scratch = [
        ((FLAT_ROWS + 8, LANES), F32),
        ((256, 3 * LANES), F32),
        ((HID, 5 * LANES), F32),
        ((256, 640), BF16),
        ((HID, 1280), BF16),
        ((256, 1536), BF16),
        ((768, 256), F32),
        ((256, 3 * LANES), F32),
        ((HID, LANES), F32),
        ((LANES, LANES), F32),
        ((HID, 256), F32),
        ((768, 256), F32),
        ((16, 256), F32),
        ((HID, LANES), F32),
        ((CODE_ROWS, LANES), F32),
        ((2, BLOCK), F32),
        (pair, F32),
        (pair, F32),
        (pair, F32),
        (pair, F32),
        (pair, BF16),
        (pair, BF16),
        (pair, BF16),
        (pair_two, F32),
        (pair_two, F32),
        (pair_two, F32),
        (pair_two, BF16),
        (pair_two, BF16),
        (pair, BF16),
        (pair, BF16),
        (pair, BF16),
        (pair, BF16),
        (pair_two, BF16),
        (pair_two, BF16),
        (pair, BF16),
        (pair, BF16),
    ]
    return pl.pallas_call(
        main_kernel,
        out_shape=(
            jax.ShapeDtypeStruct((2 * PEERS * BOX_ROWS, LANES), F32),
            jax.ShapeDtypeStruct((CODE_ROWS, LATENT), F32),
        ),
        in_specs=[pl.BlockSpec(memory_space=pltpu.SMEM)] + vmem(3),
        out_specs=tuple(vmem(2)),
        scratch_shapes=[pltpu.VMEM(shape, dtype) for shape, dtype in scratch],
        compiler_params=PARAMS,
    )(core, mine, other, codes)


def adam_update(value, first, second, grad, rate):
    first_new = BETA_ONE * first + (1.0 - BETA_ONE) * grad
    second_new = BETA_TWO * second + (1.0 - BETA_TWO) * grad * grad
    first_hat = first_new / (1.0 - BETA_ONE**STEP)
    second_hat = second_new / (1.0 - BETA_TWO**STEP)
    value_new = value - rate * (first_hat / (jnp.sqrt(second_hat) + ADAM_EPS) + DECAY * value)
    return (value_new, first_new, second_new)


def swap_cores(v):
    return lax.ppermute(v, "core", [(0, 1), (1, 0)])


def exchange(v):
    return lax.all_to_all(v, ("z", "wide"), split_axis=0, concat_axis=0)


def body(
    weights_flat,
    moment_one,
    moment_two,
    codes,
    code_first,
    code_second,
    coords,
    distances,
    shape_index,
):
    boxes = pack_boxes(
        weights_flat.reshape(SHARD_ROWS, LANES),
        coords,
        distances.reshape(1, POINTS_DEV),
        shape_index.reshape(1, POINTS_DEV),
    )
    mine = exchange(boxes.reshape(PEERS, BOX_ROWS, LANES))
    other = swap_cores(mine)
    core = lax.axis_index("core").astype(jnp.int32).reshape(1)
    grads, code_grad = main_call(
        core,
        mine.reshape(PEERS * BOX_ROWS, LANES),
        other.reshape(PEERS * BOX_ROWS, LANES),
        codes,
    )
    grads = grads.reshape(2, PEERS, BOX_ROWS, LANES)
    pair_sum = grads[0] + swap_cores(grads[1])
    shard = jnp.sum(exchange(pair_sum), axis=0)
    weight_grad = shard[:SHARD_ROWS]
    loss_value = shard[SHARD_ROWS, 0]
    code_squares = shard[SHARD_ROWS, 1]
    squares = jnp.sum(weight_grad * weight_grad)
    seen = exchange(jnp.broadcast_to(squares, (PEERS, 1, LANES)))
    squares = jnp.sum(seen[:, 0, 0]).reshape(1, 1)
    squares = (squares + swap_cores(squares)).reshape(())
    grad_norm = jnp.sqrt(squares + code_squares)
    factor = jnp.minimum(1.0, CLIP / (grad_norm + 1e-06))
    new_weights, first_new, second_new = adam_update(
        weights_flat, moment_one, moment_two, factor * weight_grad.reshape(-1), WEIGHT_RATE
    )
    new_codes, code_first_new, code_second_new = adam_update(
        codes, code_first, code_second, factor * code_grad, CODE_RATE
    )
    return (
        loss_value,
        grad_norm,
        new_weights,
        first_new,
        second_new,
        new_weights.astype(BF16),
        new_codes,
        code_first_new,
        code_second_new,
        new_codes.astype(BF16),
    )


def solution(mesh):
    parts = Mesh(mesh.devices.reshape(4, 2, 16), ALL)
    return jax.shard_map(
        body,
        mesh=parts,
        in_specs=(
            P(ALL),
            P(ALL),
            P(ALL),
            P(ALL, None),
            P(ALL, None),
            P(ALL, None),
            P(None, ALL),
            P(ALL),
            P(ALL),
        ),
        out_specs=(
            P(),
            P(),
            P(ALL),
            P(ALL),
            P(ALL),
            P(ALL),
            P(ALL, None),
            P(ALL, None),
            P(ALL, None),
            P(ALL, None),
        ),
        check_vma=False,
    )
```

time: 452 us -> 106 us (0.23); the launches traced: 446 us -> 105 us
  waiting for transfers between devices: 164 us -> 14.6 us
  matrix products: 94.1 us -> 0 us
  local copies, waits for them, and re-layouts: 51.8 us -> 4.83 us
  other arithmetic: 42.1 us -> 3.11 us
  Pallas kernels: 0 us -> 24.9 us
  blocking collectives: 63.5 us -> 48.2 us
  between operations: 18.9 us -> 3.9 us
  starting transfers between devices: 11.2 us -> 4.95 us
    unnamed x3 -> x0, waiting for transfers between devices: 125 us -> none
    dot_general x16 -> x0, matrix products: 94.1 us -> none  [the longest x6 59.1 us: forward_points(): jnp.dot(widened, normed(second_dir, second_gain), precision=HIGH)]
    psum x1 -> x0, blocking collectives: 63.5 us -> none  [body(): loss_value, squares = lax.psum((loss_part, squares_part), ('dp', 'wide'))]
    all_to_all x0 -> x2, blocking collectives: none -> 48.2 us  [exchange(): return lax.all_to_all(v, ('z', 'wide'), split_axis=0, concat_axis=0)]
    all_gather x1 -> x0, waiting for transfers between devices: 26.2 us -> none  [body(): whole = lax.all_gather(weights_flat, ('dp', 'wide'), axis=0, tiled=True)]
    pallas_call x0 -> x2, Pallas kernels: none -> 24.9 us  [the longest x1 24.1 us: main_call(): pl.pallas_call(main_kernel, out_shape=(jax.ShapeDtypeStruct((2 * PEERS *...]
    scatter-add x1 -> x0, other arithmetic: 12.3 us -> none  [local_loss(): latent = jnp.take(table, safe_rows, axis=0)]
    reduce_sum x10 -> x3, other arithmetic: 12.7 us -> 1.35 us  [the longest x1 0.67 us: body(): squares = jnp.sum(seen[:, 0, 0]).reshape(1, 1)]
  transfers between devices with their start and end apart: 3 -> 4, of which waited for: 3 -> 4; matrix products, arithmetic and copies ran while one was open for 9% -> 1% of each run, Pallas kernels for 0% -> 0%
where the time goes in v2:
time: 106 us; the launch traced here: 105 us
  blocking collectives  48.2 us (45%)
  Pallas kernels  24.9 us (23%)
  waiting for transfers between devices  14.6 us (14%)
  starting transfers between devices  4.95 us (5%)
  local copies, waits for them, and re-layouts  4.83 us (5%)
  between operations  3.9 us (4%)
  other arithmetic  3.11 us (3%)
    all_to_all x2, blocking collectives, exchange(): return lax.all_to_all(v, ('z', 'wide'), split_axis=0, concat_axis=0)  48.2 us
    pallas_call x1, Pallas kernels, main_call(): pl.pallas_call(main_kernel, out_shape=(jax.ShapeDtypeStruct((2 * PEERS *...  24.1 us
    all_to_all x1, waiting for transfers between devices, exchange(): return lax.all_to_all(v, ('z', 'wide'), split_axis=0, concat_axis=0)  8.89 us
    ppermute x3, waiting for transfers between devices, swap_cores(): return lax.ppermute(v, 'core', [(0, 1), (1, 0)])  5.66 us
    all_to_all x1, starting transfers between devices, exchange(): return lax.all_to_all(v, ('z', 'wide'), split_axis=0, concat_axis=0)  4.73 us
    unnamed x20, local copies, waits for them, and re-layouts  2.87 us
  transfers between devices with their start and end apart: 4, of which 4 were waited for; matrix products, arithmetic and copies ran while one was open for 1% of the time, Pallas kernels for 0%

profile of v2, /device:TPU:0, one launch (start us, length us, event | category | flops | bytes accessed | tf_op | source)
XLA Modules:
  0.0 104.5 jit_solution(9717409077455372922)
XLA Ops:
  0.7 0.0 copy-start.1
  0.7 0.7 copy-done.1
  1.4 0.7 copy-done.3
  2.1 0.7 copy-done.4
  2.8 0.7 copy-done.5
  3.5 0.8 shard_map.168
  4.3 27.3 %all_to_all.15 = f32[64,24,128]{2,1,0:T(8,128)S(1)} all-to-all(f32[64,24,128]{2,1,0:T(8,128)S(1)} %bitcast.20), channel_id=1, replica_groups=mesh['z'=4,'core'=2,'wide'=16] {'z','wide'}, dimensions={0} | all-to-all | bytes 1572864 | tf_op jit(solution)/shard_map/all_to_all | solution.py:659
  31.6 0.0 collective-permute-start
  31.6 2.3 %collective-permute-done = f32[64,24,128]{2,1,0:T(8,128)S(1)} collective-permute-done((f32[64,24,128]{2,1,0:T(8,128)S(1)}, f32[64,24,128]{2,1,0:T(8,128)S(1)}, u32[]{:S(2)}, u32[]{:S(2)}) %collective-permute-start) | collective-permute-done | bytes 786464 | tf_op jit(solution)/shard_map/ppermute | solution.py:655
  33.9 0.0 copy-done
  33.9 24.1 %shard_map.169 = (f32[3072,128]{1,0:T(8,128)S(1)}, f32[256,256]{1,0:T(8,128)S(1)}) custom-call(s32[1]{0:T(128)} %bitcast.core_ref, f32[1536,128]{1,0:T(8,128)S(1)} %bitcast.19, f32[1536,128]{1,0:T(8,128)S(1)} %bitcast.21, f32[256,256]{1,0:T(8,128)S(1)} %copy-done), custom_call_target="tpu_custom_call" | custom-call | tf_op jit(solution)/shard_map/pallas_call | solution.py:632
  58.0 0.1 fusion.8
  58.1 0.2 collective-permute-start.1
  58.4 2.1 %collective-permute-done.1 = f32[64,24,128]{2,1,0:T(8,128)S(1)} collective-permute-done((f32[64,24,128]{2,1,0:T(8,128)S(1)}, f32[64,24,128]{2,1,0:T(8,128)S(1)}, u32[]{:S(2)}, u32[]{:S(2)}) %collective-permute-start.1) | collective-permute-done | bytes 786464 | tf_op jit(solution)/shard_map/ppermute | solution.py:655
  60.5 0.1 add.43
  60.6 0.0 copy-start.2
  60.6 0.0 copy-start.8
  60.6 0.0 copy-start.9
  60.6 0.0 copy-start.6
  60.6 0.0 copy-start.7
  60.7 21.0 %all_to_all.16 = f32[64,24,128]{2,1,0:T(8,128)S(1)} all-to-all(f32[64,24,128]{2,1,0:T(8,128)S(1)} %add.43), channel_id=1, replica_groups=mesh['z'=4,'core'=2,'wide'=16] {'z','wide'}, dimensions={0} | all-to-all | bytes 1572864 | tf_op jit(solution)/shard_map/all_to_all | solution.py:659
  81.6 0.1 reduce_sum.27
  81.7 0.6 multiply_reduce_fusion
  82.3 1.3 %broadcast_in_dim.3 = f32[64,1,128]{2,1,0:T(1,128)} broadcast(f32[]{:T(128)} %multiply_reduce_fusion), dimensions={} | broadcast | bytes 32772 | tf_op jit(solution)/shard_map/broadcast_in_dim | solution.py:695
  83.6 4.7 %all-to-all-start.2 = ((f32[64,1,128]{2,1,0:T(1,128)}), f32[64,1,128]{2,1,0:T(1,128)S(1)}, u32[]{:S(2)}, u32[]{:S(2)}) async-start(f32[64,1,128]{2,1,0:T(1,128)} %broadcast_in_dim.3), calls=%async_computation.2 | async-start | bytes 65536 | tf_op jit(solution)/shard_map/all_to_all | solution.py:659
  88.3 0.6 fusion.9
  88.9 8.9 %all-to-all-done.2 = f32[64,1,128]{2,1,0:T(1,128)S(1)} async-done(((f32[64,1,128]{2,1,0:T(1,128)}), f32[64,1,128]{2,1,0:T(1,128)S(1)}, u32[]{:S(2)}, u32[]{:S(2)}) %all-to-all-start.2) | async-done | bytes 32800 | tf_op jit(solution)/shard_map/all_to_all | solution.py:659
  97.8 0.7 slice_reduce_fusion
  98.5 0.0 collective-permute-start.2
  98.5 1.2 %collective-permute-done.2 = f32[1,1]{1,0:T(1,128)} collective-permute-done((f32[1,1]{1,0:T(1,128)}, f32[1,1]{1,0:T(1,128)}, u32[]{:S(2)}, u32[]{:S(2)}) %collective-permute-start.2) | collective-permute-done | bytes 36 | tf_op jit(solution)/shard_map/ppermute | solution.py:655
  101.7 0.6 fusion.5
  102.4 1.0 %fusion.3 = (bf16[256,256]{1,0:T(8,128)(2,1)}, f32[256,256]{1,0:T(8,128)}, f32[256,256]{1,0:T(8,128)}, f32[256,256]{1,0:T(8,128)}) fusion(f32[256,256]{1,0:T(8,128)S(1)} %copy-done, f32[256,256]{1,0:T(8,128)S(1)} %get-tuple-element.13, f32[]{:T(128)S(6)} %min_shard_map.3, f32[256,256]{1,0:T(8,128)S(1)} %copy-done.6, f32[256,256]{1,0:T(8,128)S(1)} %copy-done.7), kind=kLoop, calls=%fused_computation.12 | loop fusion | flops 1114112 | bytes 1966084 | tf_op jit(solution)/shard_map/convert_element_type | solution.py:716
  (9 shorter events, 0.0 us)
Async XLA Ops:
  0.6 33.3 %copy-start = (f32[256,256]{1,0:T(8,128)S(1)}, f32[256,256]{1,0:T(8,128)}, u32[]{:S(2)}) copy-start(f32[256,256]{1,0:T(8,128)} %codes_ref.1) | copy-start | bytes 786436
  0.7 0.8 copy-start.1
  1.4 0.7 copy-start.3
  2.1 0.7 copy-start.4
  2.8 0.7 copy-start.5
  31.6 2.3 %collective-permute-start = (f32[64,24,128]{2,1,0:T(8,128)S(1)}, f32[64,24,128]{2,1,0:T(8,128)S(1)}, u32[]{:S(2)}, u32[]{:S(2)}) collective-permute-start(f32[64,24,128]{2,1,0:T(8,128)S(1)} %all_to_all.15), channel_id=1, source_target_pairs={{0,16},{16,0},{1,17},{17,1},{2,18},{18,2},{3,19},{19,3},{4,20},{20... | collective-permute-start | bytes 2359304 | tf_op jit(solution)/shard_map/ppermute | solution.py:655
  58.1 2.4 %collective-permute-start.1 = (f32[64,24,128]{2,1,0:T(8,128)S(1)}, f32[64,24,128]{2,1,0:T(8,128)S(1)}, u32[]{:S(2)}, u32[]{:S(2)}) collective-permute-start(f32[64,24,128]{2,1,0:T(8,128)S(1)} %bitcast.26), channel_id=1, source_target_pairs={{0,16},{16,0},{1,17},{17,1},{2,18},{18,2},{3,19},{19,3},{4,20},{20... | collective-permute-start | bytes 2359304 | tf_op jit(solution)/shard_map/ppermute | solution.py:655
  60.6 41.1 %copy-start.2 = (f32[2688]{0:T(1024)S(1)}, f32[2688]{0:T(1024)}, u32[]{:S(2)}) copy-start(f32[2688]{0:T(1024)} %param.9) | copy-start | bytes 32260
  60.6 41.1 %copy-start.8 = (f32[2688]{0:T(1024)S(1)}, f32[2688]{0:T(1024)}, u32[]{:S(2)}) copy-start(f32[2688]{0:T(1024)} %param.10) | copy-start | bytes 32260
  60.6 41.1 %copy-start.9 = (f32[2688]{0:T(1024)S(1)}, f32[2688]{0:T(1024)}, u32[]{:S(2)}) copy-start(f32[2688]{0:T(1024)} %param.11) | copy-start | bytes 32260
  60.6 41.7 %copy-start.6 = (f32[256,256]{1,0:T(8,128)S(1)}, f32[256,256]{1,0:T(8,128)}, u32[]{:S(2)}) copy-start(f32[256,256]{1,0:T(8,128)} %param.13) | copy-start | bytes 786436
  60.6 41.7 %copy-start.7 = (f32[256,256]{1,0:T(8,128)S(1)}, f32[256,256]{1,0:T(8,128)}, u32[]{:S(2)}) copy-start(f32[256,256]{1,0:T(8,128)} %param.14) | copy-start | bytes 786436
  83.6 14.2 %all-to-all-start.2 = ((f32[64,1,128]{2,1,0:T(1,128)}), f32[64,1,128]{2,1,0:T(1,128)S(1)}, u32[]{:S(2)}, u32[]{:S(2)}) async-start(f32[64,1,128]{2,1,0:T(1,128)} %broadcast_in_dim.3), calls=%async_computation.2 | async-start | bytes 65536 | tf_op jit(solution)/shard_map/all_to_all | solution.py:659
  98.5 1.2 %collective-permute-start.2 = (f32[1,1]{1,0:T(1,128)}, f32[1,1]{1,0:T(1,128)}, u32[]{:S(2)}, u32[]{:S(2)}) collective-permute-start(f32[1,1]{1,0:T(1,128)} %bitcast.10), channel_id=1, source_target_pairs={{0,16},{16,0},{1,17},{17,1},{2,18},{18,2},{3,19},{19,3},{4,20},{20... | collective-permute-start | bytes 20 | tf_op jit(solution)/shard_map/ppermute | solution.py:655

commit v3 on v2

--- a/solution.py
+++ b/solution.py
@@ -3,7 +3,6 @@
 from jax import lax
 from jax.experimental import pallas as pl
 from jax.experimental.pallas import tpu as pltpu
-from jax.sharding import Mesh
 from jax.sharding import PartitionSpec as P
 
 LATENT = 256
@@ -25,9 +24,13 @@
 
 LANES = 128
 DEVICES = 128
-PEERS = 64
+CHIPS = 64
 SHARD_ROWS = 21
 BOX_ROWS = 24
+RING = 4
+LINE_ROWS = RING * BOX_ROWS
+PLANE_ROWS = RING * LINE_ROWS
+CORE_ROWS = RING * PLANE_ROWS
 SLOTS = 16
 POINTS_DEV = 1024
 CODE_ROWS = 256
@@ -37,7 +40,53 @@
 
 F32 = jnp.float32
 BF16 = jnp.bfloat16
-ALL = ("z", "core", "wide")
+ALL = ("dp", "wide")
+
+
+def coordinates(device):
+    return device // 4 % 4, device % 4, device // 32, device // 16 % 2
+
+
+def device_at(x, y, z, core):
+    return z * 32 + core * 16 + x * 4 + y
+
+
+def neighbour(device, ring, hops):
+    x, y, z, core = coordinates(device)
+    axis = (ring + core) % 3
+    place = [x, y, z]
+    place[axis] = (place[axis] + hops) % RING
+    return device_at(*place, core)
+
+
+def shifted(v, ring, hops):
+    return lax.ppermute(v, ALL, [(d, neighbour(d, ring, hops)) for d in range(DEVICES)])
+
+
+def swap_cores(v):
+    return lax.ppermute(v, ALL, [(d, d ^ 16) for d in range(DEVICES)])
+
+
+def relative_devices(device, shape):
+    row = lax.broadcasted_iota(jnp.int32, shape, 0)
+    ra, rb, rc = row >> 5, (row >> 3) & 3, (row >> 1) & 3
+    x, y = (device >> 2) & 3, device & 3
+    z, core = device >> 5, (device >> 4) & 1
+    first = core == 0
+    dx, dy, dz = (
+        jnp.where(first, ra, rc),
+        jnp.where(first, rb, ra),
+        jnp.where(first, rc, rb),
+    )
+    return ((z + dz) & 3) * 32 + (core ^ (row & 1)) * 16 + ((x + dx) & 3) * 4 + ((y + dy) & 3)
+
+
+def relative_place(device, core, ra, rb, rc, sign):
+    x, y, z = (device >> 2) & 3, device & 3, device >> 5
+    dx, dy, dz = (ra, rb, rc) if core == 0 else (rc, ra, rb)
+    return (
+        ((z + sign * dz) & 3) * 32 + core * 16 + ((x + sign * dx) & 3) * 4 + ((y + sign * dy) & 3)
+    )
 
 
 def rows_of_lanes(lead, shape):
@@ -76,14 +125,30 @@
     return jnp.concatenate(parts, axis=0)
 
 
-def pack_kernel(weights_ref, coords_ref, distances_ref, index_ref, out_ref):
+def pack_kernel(
+    device_ref, weights_hbm, coords_hbm, distances_hbm, index_hbm, *refs
+):
+    outs, (weights_ref, coords_ref, distances_ref, index_ref, sems) = refs[:RING], refs[RING:]
+    copies = [
+        pltpu.make_async_copy(source, target, sems.at[i])
+        for i, (source, target) in enumerate(
+            [
+                (index_hbm, index_ref),
+                (weights_hbm, weights_ref),
+                (coords_hbm, coords_ref),
+                (distances_hbm, distances_ref),
+            ]
+        )
+    ]
+    for copy in copies:
+        copy.start()
+    for copy in copies:
+        copy.wait()
     shard = stacked(weights_ref[...], jnp.zeros((BOX_ROWS - SHARD_ROWS, LANES), F32))
-    for peer in range(PEERS):
-        out_ref[peer * BOX_ROWS : (peer + 1) * BOX_ROWS, :] = shard
     index = index_ref[...]
     owner = lax.shift_right_logical(index, 8)
     row = lax.bitwise_and(index, CODE_ROWS - 1)
-    sent = (rows_of_lanes(0, (DEVICES, POINTS_DEV)) == owner).astype(F32)
+    sent = (relative_devices(device_ref[0], (DEVICES, POINTS_DEV)) == owner).astype(F32)
     sent_low = sent.astype(BF16)
     width = 256
     earlier = rows_of_lanes(0, (width, width)) < rows_of_lanes(1, (width, width))
@@ -106,12 +171,9 @@
         beside(sent_low, sent_low, sent_low),
         beside(*[stacked(*piece, spare).astype(BF16) for piece in pieces]),
     )
-    for z in range(4):
-        for core in range(2):
-            first = z * 32 + core * 16
-            out_ref[pl.ds(z * 16 * BOX_ROWS + SHARD_ROWS + core, 16, stride=BOX_ROWS), :] = boxes[
-                first : first + 16, :
-            ]
+    for r in range(RING):
+        outs[r][0:BOX_ROWS, :] = shard
+        outs[r][BOX_ROWS:, :] = boxes[r * 32 : r * 32 + 32, :]
 
 
 def unit_groups(count, stride_rows, extra, first_entry):
@@ -184,11 +246,12 @@
 
 
 def main_kernel(
-    core_ref,
+    device_ref,
     mine_ref,
     other_ref,
     codes_ref,
-    out_ref,
+    keep_ref,
+    give_ref,
     code_grad_ref,
     flat,
     first_w,
@@ -227,19 +290,25 @@
     low_hi,
     low_lo,
 ):
-    core = core_ref[0]
+    device = device_ref[0]
+    core = (device >> 4) & 1
 
     for which in range(2):
 
         @pl.when(core == which)
         def _(which=which):
-            for d in range(DEVICES):
-                z, c, w = d // 32, d // 16 % 2, d % 16
-                box = (z * 16 + w) * BOX_ROWS
+            for c in range(2):
                 source = mine_ref if c == which else other_ref
-                flat[d * SHARD_ROWS : d * SHARD_ROWS + BOX_ROWS, :] = source[box : box + BOX_ROWS, :]
-            rows = pl.ds(SHARD_ROWS + which, PEERS, stride=BOX_ROWS)
-            spots[...] = stacked(mine_ref[rows, :], other_ref[rows, :]).T
+                for place in range(CHIPS):
+                    rc, rb, ra = place // 16, place // 4 % 4, place % 4
+                    first = relative_place(device, c, ra, rb, rc, -1) * SHARD_ROWS
+                    box = place * BOX_ROWS
+                    flat[pl.ds(first, SHARD_ROWS), :] = source[box : box + SHARD_ROWS, :]
+
+    spots[...] = stacked(
+        mine_ref[pl.ds(CORE_ROWS, CHIPS, stride=2), :],
+        other_ref[pl.ds(CORE_ROWS + 1, CHIPS, stride=2), :],
+    ).T
 
     unpack_units(flat, first_w, *FIRST_UNITS)
     unpack_units(flat, second_w, *SECOND_UNITS)
@@ -562,13 +631,20 @@
     wide = rows_of_lanes(1, (8, LANES))
     info = jnp.where((sub == 5) & (wide == 0), loss, 0.0)
     info = jnp.where((sub == 5) & (wide == 1), code_squares, info)
-    for d in range(DEVICES):
-        z, c, w = d // 32, d // 16 % 2, d % 16
-        half = jnp.where(core == c, 0, PEERS * BOX_ROWS)
-        base = pl.multiple_of(half + (z * 16 + w) * BOX_ROWS, 8)
-        first = d * SHARD_ROWS
-        out_ref[pl.ds(base, 16), :] = flat[first : first + 16, :]
-        out_ref[pl.ds(base + 16, 8), :] = jnp.where(sub < 5, flat[first + 16 : first + 24, :], info)
+    for which in range(2):
+
+        @pl.when(core == which)
+        def _(which=which):
+            for c in range(2):
+                target = keep_ref if c == which else give_ref
+                for place in range(CHIPS):
+                    rc, rb, ra = place // 16, place // 4 % 4, place % 4
+                    first = relative_place(device, c, ra, rb, rc, 1) * SHARD_ROWS
+                    box = place * BOX_ROWS
+                    target[box : box + 16, :] = flat[pl.ds(first, 16), :]
+                    target[box + 16 : box + 24, :] = jnp.where(
+                        sub < 5, flat[pl.ds(first + 16, 8), :], info
+                    )
 
 
 def vmem(count):
@@ -578,17 +654,29 @@
 PARAMS = pltpu.CompilerParams(vmem_limit_bytes=48 * 1024 * 1024)
 
 
-def pack_boxes(weights, coords, distances, index):
+ANY = pl.BlockSpec(memory_space=pl.ANY)
+SMEM = pl.BlockSpec(memory_space=pltpu.SMEM)
+
+
+def pack_boxes(device, weights, coords, distances, index):
+    box = jax.ShapeDtypeStruct((BOX_ROWS + 32, LANES), F32)
     return pl.pallas_call(
         pack_kernel,
-        out_shape=jax.ShapeDtypeStruct((PEERS * BOX_ROWS, LANES), F32),
-        in_specs=vmem(4),
-        out_specs=vmem(1)[0],
+        out_shape=(box,) * RING,
+        in_specs=[SMEM] + [ANY] * 4,
+        out_specs=tuple(vmem(RING)),
+        scratch_shapes=[
+            pltpu.VMEM(weights.shape, F32),
+            pltpu.VMEM(coords.shape, F32),
+            pltpu.VMEM(distances.shape, F32),
+            pltpu.VMEM(index.shape, jnp.int32),
+            pltpu.SemaphoreType.DMA((4,)),
+        ],
         compiler_params=PARAMS,
-    )(weights, coords, distances, index)
-
-
-def main_call(core, mine, other, codes):
+    )(device, weights, coords, distances, index)
+
+
+def main_call(device, mine, other, codes):
     pair = (2, 256, BLOCK)
     pair_two = (2, HID, BLOCK)
     scratch = [
@@ -632,14 +720,15 @@
     return pl.pallas_call(
         main_kernel,
         out_shape=(
-            jax.ShapeDtypeStruct((2 * PEERS * BOX_ROWS, LANES), F32),
+            jax.ShapeDtypeStruct((CORE_ROWS, LANES), F32),
+            jax.ShapeDtypeStruct((CORE_ROWS, LANES), F32),
             jax.ShapeDtypeStruct((CODE_ROWS, LATENT), F32),
         ),
-        in_specs=[pl.BlockSpec(memory_space=pltpu.SMEM)] + vmem(3),
-        out_specs=tuple(vmem(2)),
+        in_specs=[SMEM] + vmem(3),
+        out_specs=tuple(vmem(3)),
         scratch_shapes=[pltpu.VMEM(shape, dtype) for shape, dtype in scratch],
         compiler_params=PARAMS,
-    )(core, mine, other, codes)
+    )(device, mine, other, codes)
 
 
 def adam_update(value, first, second, grad, rate):
@@ -651,12 +740,57 @@
     return (value_new, first_new, second_new)
 
 
-def swap_cores(v):
-    return lax.ppermute(v, "core", [(0, 1), (1, 0)])
-
-
-def exchange(v):
-    return lax.all_to_all(v, ("z", "wide"), split_axis=0, concat_axis=0)
+def gather_rings(boxes):
+    got = [boxes[0]] + [shifted(boxes[r], 0, r) for r in range(1, RING)]
+    line = jnp.concatenate([v[:BOX_ROWS] for v in got])
+    message = [
+        jnp.concatenate([line] + [v[BOX_ROWS + 8 * r : BOX_ROWS + 8 * r + 8] for v in got])
+        for r in range(RING)
+    ]
+    got = [message[0]] + [shifted(message[r], 1, r) for r in range(1, RING)]
+    plane = jnp.concatenate([v[:LINE_ROWS] for v in got])
+    points = jnp.concatenate([v[LINE_ROWS:] for v in got]).reshape(16, RING, 2, LANES)
+    points = [points[:, r].reshape(32, LANES) for r in range(RING)]
+    across = shifted(points[2], 2, 2)
+    behind = shifted(jnp.concatenate([plane, points[1]]), 2, 1)
+    ahead = shifted(jnp.concatenate([plane, points[3]]), 2, 3)
+    half = PLANE_ROWS // 2
+    far_low = shifted(behind[:half], 2, 1)
+    far_high = shifted(ahead[half:PLANE_ROWS], 2, 3)
+    return jnp.concatenate(
+        [
+            plane,
+            behind[:PLANE_ROWS],
+            far_low,
+            far_high,
+            ahead[:PLANE_ROWS],
+            points[0],
+            behind[PLANE_ROWS:],
+            across,
+            ahead[PLANE_ROWS:],
+        ]
+    )
+
+
+def reduce_rings(total):
+    part = [total[r * PLANE_ROWS : (r + 1) * PLANE_ROWS] for r in range(RING)]
+    half = PLANE_ROWS // 2
+    low = shifted(part[2][:half], 2, 1)
+    high = shifted(part[2][half:], 2, 3)
+    onward = jnp.concatenate([part[1][:half] + low, part[1][half:]])
+    back = jnp.concatenate([part[3][:half], part[3][half:] + high])
+    total = part[0] + shifted(onward, 2, 1) + shifted(back, 2, 3)
+    for ring, rows in ((1, LINE_ROWS), (0, BOX_ROWS)):
+        part = [total[r * rows : (r + 1) * rows] for r in range(RING)]
+        total = part[0] + sum(shifted(part[r], ring, r) for r in range(1, RING))
+    return total
+
+
+def sum_everywhere(v):
+    v = v + swap_cores(v)
+    for ring in range(3):
+        v = v + sum(shifted(v, ring, r) for r in range(1, RING))
+    return v
 
 
 def body(
@@ -670,31 +804,22 @@
     distances,
     shape_index,
 ):
+    device = (lax.axis_index("dp") * 16 + lax.axis_index("wide")).astype(jnp.int32).reshape(1)
     boxes = pack_boxes(
+        device,
         weights_flat.reshape(SHARD_ROWS, LANES),
         coords,
         distances.reshape(1, POINTS_DEV),
         shape_index.reshape(1, POINTS_DEV),
     )
-    mine = exchange(boxes.reshape(PEERS, BOX_ROWS, LANES))
+    mine = gather_rings(boxes)
     other = swap_cores(mine)
-    core = lax.axis_index("core").astype(jnp.int32).reshape(1)
-    grads, code_grad = main_call(
-        core,
-        mine.reshape(PEERS * BOX_ROWS, LANES),
-        other.reshape(PEERS * BOX_ROWS, LANES),
-        codes,
-    )
-    grads = grads.reshape(2, PEERS, BOX_ROWS, LANES)
-    pair_sum = grads[0] + swap_cores(grads[1])
-    shard = jnp.sum(exchange(pair_sum), axis=0)
+    keep, give, code_grad = main_call(device, mine, other, codes)
+    shard = reduce_rings(keep + swap_cores(give))
     weight_grad = shard[:SHARD_ROWS]
     loss_value = shard[SHARD_ROWS, 0]
     code_squares = shard[SHARD_ROWS, 1]
-    squares = jnp.sum(weight_grad * weight_grad)
-    seen = exchange(jnp.broadcast_to(squares, (PEERS, 1, LANES)))
-    squares = jnp.sum(seen[:, 0, 0]).reshape(1, 1)
-    squares = (squares + swap_cores(squares)).reshape(())
+    squares = sum_everywhere(jnp.sum(weight_grad * weight_grad).reshape(1, 1)).reshape(())
     grad_norm = jnp.sqrt(squares + code_squares)
     factor = jnp.minimum(1.0, CLIP / (grad_norm + 1e-06))
     new_weights, first_new, second_new = adam_update(
@@ -718,32 +843,11 @@
 
 
 def solution(mesh):
-    parts = Mesh(mesh.devices.reshape(4, 2, 16), ALL)
+    flat, rows = P(ALL), P(ALL, None)
     return jax.shard_map(
         body,
-        mesh=parts,
-        in_specs=(
-            P(ALL),
-            P(ALL),
-            P(ALL),
-            P(ALL, None),
-            P(ALL, None),
-            P(ALL, None),
-            P(None, ALL),
-            P(ALL),
-            P(ALL),
-        ),
-        out_specs=(
-            P(),
-            P(),
-            P(ALL),
-            P(ALL),
-            P(ALL),
-            P(ALL),
-            P(ALL, None),
-            P(ALL, None),
-            P(ALL, None),
-            P(ALL, None),
-        ),
+        mesh=mesh,
+        in_specs=(flat, flat, flat, rows, rows, rows, P(None, ALL), flat, flat),
+        out_specs=(P(), P(), flat, flat, flat, flat, rows, rows, rows, rows),
         check_vma=False,
     )

time: 106 us -> 143 us (1.35)
  blocking collectives: 48.2 us -> 0 us
  starting transfers between devices: 4.95 us -> 51.8 us
  waiting for transfers between devices: 14.6 us -> 50.9 us
  between operations: 3.9 us -> 9.61 us
  local copies, waits for them, and re-layouts: 4.83 us -> 2.25 us
    ppermute x3 -> x33, starting transfers between devices: 0.22 us -> 51.8 us  [the longest x30 51.6 us: shifted(): lax.ppermute(v, ALL, [(d, neighbour(d, ring, hops)) for d in range(DEVICE...]
    all_to_all x2 -> x0, blocking collectives: 48.2 us -> none  [exchange(): return lax.all_to_all(v, ('z', 'wide'), split_axis=0, concat_axis=0)]
    ppermute x3 -> x33, waiting for transfers between devices: 5.66 us -> 50.9 us  [the longest x30 45.1 us: shifted(): lax.ppermute(v, ALL, [(d, neighbour(d, ring, hops)) for d in range(DEVICE...]
    all_to_all x1 -> x0, waiting for transfers between devices: 8.89 us -> none  [exchange(): return lax.all_to_all(v, ('z', 'wide'), split_axis=0, concat_axis=0)]
    all_to_all x1 -> x0, starting transfers between devices: 4.73 us -> none  [exchange(): return lax.all_to_all(v, ('z', 'wide'), split_axis=0, concat_axis=0)]
    unnamed x20 -> x43, local copies, waits for them, and re-layouts: 2.87 us -> 1.59 us
  transfers between devices with their start and end apart: 4 -> 33, of which waited for: 4 -> 25; matrix products, arithmetic and copies ran while one was open for 1% -> 0% of each run, Pallas kernels for 0% -> 0%
where the time goes in v3:
time: 143 us; the launch traced here: 142 us
  starting transfers between devices  51.8 us (36%)
  waiting for transfers between devices  50.9 us (36%)
  Pallas kernels  25.3 us (18%)
  between operations  9.61 us (7%)
  other arithmetic  2.48 us (2%)
  local copies, waits for them, and re-layouts  2.25 us (2%)
    ppermute x30, starting transfers between devices, shifted(): lax.ppermute(v, ALL, [(d, neighbour(d, ring, hops)) for d in range(DEVICE...  51.6 us
    ppermute x30, waiting for transfers between devices, shifted(): lax.ppermute(v, ALL, [(d, neighbour(d, ring, hops)) for d in range(DEVICE...  45.1 us
    pallas_call x1, Pallas kernels, main_call(): pl.pallas_call(main_kernel, out_shape=(jax.ShapeDtypeStruct((CORE_ROWS, L...  24.4 us
    ppermute x3, waiting for transfers between devices, swap_cores(): return lax.ppermute(v, ALL, [(d, d ^ 16) for d in range(DEVICES)])  5.76 us
  transfers between devices with their start and end apart: 33, of which 25 were waited for; matrix products, arithmetic and copies ran while one was open for 0% of the time, Pallas kernels for 0%

profile of v3, /device:TPU:0, one launch (start us, length us, event | category | flops | bytes accessed | tf_op | source)
XLA Modules:
  0.0 142.4 jit_solution(14092978981588684468)
XLA Ops:
  3.0 1.6 %collective-permute-start = (f32[56,128]{1,0:T(8,128)S(1)}, f32[56,128]{1,0:T(8,128)S(1)}, u32[]{:S(2)}, u32[]{:S(2)}) collective-permute-start(f32[56,128]{1,0:T(8,128)S(1)} %get-tuple-element.18), channel_id=1, source_target_pairs={{0,4},{1,5},{2,6},{3,7},{4,8},{5,9},{6,10},{7,11},{8,12},{9,13},{1... | collective-permute-start | bytes 86024 | tf_op jit(solution)/shard_map/ppermute | solution.py:63
  4.7 2.7 %collective-permute-start.1 = (f32[56,128]{1,0:T(8,128)S(1)}, f32[56,128]{1,0:T(8,128)S(1)}, u32[]{:S(2)}, u32[]{:S(2)}) collective-permute-start(f32[56,128]{1,0:T(8,128)S(1)} %get-tuple-element.19), channel_id=1, source_target_pairs={{0,8},{1,9},{2,10},{3,11},{4,12},{5,13},{6,14},{7,15},{8,0},{9,1},... | collective-permute-start | bytes 86024 | tf_op jit(solution)/shard_map/ppermute | solution.py:63
  11.4 1.6 %collective-permute-start.3 = (f32[128,128]{1,0:T(8,128)S(1)}, f32[128,128]{1,0:T(8,128)S(1)}, u32[]{:S(2)}, u32[]{:S(2)}) collective-permute-start(f32[128,128]{1,0:T(8,128)S(1)} %get-tuple-element.55), channel_id=1, source_target_pairs={{0,1},{1,2},{2,3},{3,0},{4,5},{5,6},{6,7},{7,4},{8,9},{9,10},{10,1... | collective-permute-start | bytes 196616 | tf_op jit(solution)/shard_map/ppermute | solution.py:63
  13.0 1.7 %collective-permute-start.5 = (f32[128,128]{1,0:T(8,128)S(1)}, f32[128,128]{1,0:T(8,128)S(1)}, u32[]{:S(2)}, u32[]{:S(2)}) collective-permute-start(f32[128,128]{1,0:T(8,128)S(1)} %get-tuple-element.53), channel_id=1, source_target_pairs={{0,3},{1,0},{2,1},{3,2},{4,7},{5,4},{6,5},{7,6},{8,11},{9,8},{10,9... | collective-permute-start | bytes 196616 | tf_op jit(solution)/shard_map/ppermute | solution.py:63
  14.7 2.0 %collective-permute-start.4 = (f32[128,128]{1,0:T(8,128)S(1)}, f32[128,128]{1,0:T(8,128)S(1)}, u32[]{:S(2)}, u32[]{:S(2)}) collective-permute-start(f32[128,128]{1,0:T(8,128)S(1)} %get-tuple-element.54), channel_id=1, source_target_pairs={{0,2},{1,3},{2,0},{3,1},{4,6},{5,7},{6,4},{7,5},{8,10},{9,11},{10,... | collective-permute-start | bytes 196616 | tf_op jit(solution)/shard_map/ppermute | solution.py:63
  16.9 3.5 %collective-permute-done.4 = f32[128,128]{1,0:T(8,128)S(1)} collective-permute-done((f32[128,128]{1,0:T(8,128)S(1)}, f32[128,128]{1,0:T(8,128)S(1)}, u32[]{:S(2)}, u32[]{:S(2)}) %collective-permute-start.4) | collective-permute-done | bytes 65568 | tf_op jit(solution)/shard_map/ppermute | solution.py:63
  20.6 4.1 %collective-permute-start.8 = (f32[416,128]{1,0:T(8,128)S(1)}, f32[416,128]{1,0:T(8,128)S(1)}, u32[]{:S(2)}, u32[]{:S(2)}) collective-permute-start(f32[416,128]{1,0:T(8,128)S(1)} %constant_dynamic-update-slice_fusion.39), channel_id=1, source_target_pairs={{0,96},{1,97},{2,98},{3,99},{4,100},{5,101},{6,102},{7,103},{8,104... | collective-permute-start | bytes 638984 | tf_op jit(solution)/shard_map/ppermute | solution.py:63
  24.7 1.9 %collective-permute-start.10 = (f32[32,128]{1,0:T(8,128)S(1)}, f32[32,128]{1,0:T(8,128)S(1)}, u32[]{:S(2)}, u32[]{:S(2)}) collective-permute-start(f32[32,128]{1,0:T(8,128)S(1)} %bitcast.30), channel_id=1, source_target_pairs={{0,64},{1,65},{2,66},{3,67},{4,68},{5,69},{6,70},{7,71},{8,72},{9,... | collective-permute-start | bytes 49160 | tf_op jit(solution)/shard_map/ppermute | solution.py:63
  28.0 3.8 %collective-permute-start.9 = (f32[192,128]{1,0:T(8,128)S(1)}, f32[192,128]{1,0:T(8,128)S(1)}, u32[]{:S(2)}, u32[]{:S(2)}) collective-permute-start(f32[192,128]{1,0:T(8,128)S(1)} %slice.250), channel_id=1, source_target_pairs={{0,96},{1,97},{2,98},{3,99},{4,100},{5,101},{6,102},{7,103},{8,104... | collective-permute-start | bytes 294920 | tf_op jit(solution)/shard_map/ppermute | solution.py:63
  32.0 5.8 %collective-permute-done.7 = f32[192,128]{1,0:T(8,128)S(1)} collective-permute-done((f32[192,128]{1,0:T(8,128)S(1)}, f32[192,128]{1,0:T(8,128)S(1)}, u32[]{:S(2)}, u32[]{:S(2)}) %collective-permute-start.7) | collective-permute-done | bytes 98336 | tf_op jit(solution)/shard_map/ppermute | solution.py:63
  38.0 2.4 %collective-permute-done.11.other_ref = f32[1664,128]{1,0:T(8,128)S(1)} collective-permute-done((f32[1664,128]{1,0:T(8,128)S(1)}, f32[1664,128]{1,0:T(8,128)S(1)}, u32[]{:S(2)}, u32[]{:S(2)}) %collective-permute-start.11) | collective-permute-done | bytes 852000 | tf_op jit(solution)/shard_map/ppermute | solution.py:67
  40.4 24.4 %shard_map.169 = (f32[1536,128]{1,0:T(8,128)S(1)}, f32[1536,128]{1,0:T(8,128)S(1)}, f32[256,256]{1,0:T(8,128)S(1)}) custom-call(s32[1]{0:T(128)} %bitcast.device_ref, f32[1664,128]{1,0:T(8,128)S(1)} %constant_dynamic-update-slice_fusion.47.mine_ref, f32[1664,128]{1,0:T(8,128)S(1)} %collective-permute-done.11.other_ref, f32[256,256]{1,0:T(8,128)S(1)} %copy-done), custom_call_target="tpu_custom_call" | custom-call | tf_op jit(solution)/shard_map/pallas_call | solution.py:720
  65.0 2.2 %collective-permute-done.12 = f32[1536,128]{1,0:T(8,128)S(1)} collective-permute-done((f32[1536,128]{1,0:T(8,128)S(1)}, f32[1536,128]{1,0:T(8,128)S(1)}, u32[]{:S(2)}, u32[]{:S(2)}) %collective-permute-start.12) | collective-permute-done | bytes 786464 | tf_op jit(solution)/shard_map/ppermute | solution.py:67
  67.4 5.8 %collective-permute-done.13 = f32[192,128]{1,0:T(8,128)S(1)} collective-permute-done((f32[192,128]{1,0:T(8,128)S(1)}, f32[192,128]{1,0:T(8,128)S(1)}, u32[]{:S(2)}, u32[]{:S(2)}) %collective-permute-start.13) | collective-permute-done | bytes 98336 | tf_op jit(solution)/shard_map/ppermute | solution.py:63
  73.3 2.1 %collective-permute-start.14 = (f32[384,128]{1,0:T(8,128)S(1)}, f32[384,128]{1,0:T(8,128)S(1)}, u32[]{:S(2)}, u32[]{:S(2)}) collective-permute-start(f32[384,128]{1,0:T(8,128)S(1)} %pad_maximum_fusion), channel_id=1, source_target_pairs={{0,32},{1,33},{2,34},{3,35},{4,36},{5,37},{6,38},{7,39},{8,40},{9,... | collective-permute-start | bytes 589832 | tf_op jit(solution)/shard_map/ppermute | solution.py:63
  75.4 2.5 %collective-permute-done.15 = f32[192,128]{1,0:T(8,128)S(1)} collective-permute-done((f32[192,128]{1,0:T(8,128)S(1)}, f32[192,128]{1,0:T(8,128)S(1)}, u32[]{:S(2)}, u32[]{:S(2)}) %collective-permute-start.15) | collective-permute-done | bytes 98336 | tf_op jit(solution)/shard_map/ppermute | solution.py:63
  80.3 4.4 %collective-permute-done.16 = f32[384,128]{1,0:T(8,128)S(1)} collective-permute-done((f32[384,128]{1,0:T(8,128)S(1)}, f32[384,128]{1,0:T(8,128)S(1)}, u32[]{:S(2)}, u32[]{:S(2)}) %collective-permute-start.16) | collective-permute-done | bytes 196640 | tf_op jit(solution)/shard_map/ppermute | solution.py:63
  84.8 2.1 %collective-permute-start.18 = (f32[96,128]{1,0:T(8,128)S(1)}, f32[96,128]{1,0:T(8,128)S(1)}, u32[]{:S(2)}, u32[]{:S(2)}) collective-permute-start(f32[96,128]{1,0:T(8,128)S(1)} %get-tuple-element.36), channel_id=1, source_target_pairs={{0,2},{1,3},{2,0},{3,1},{4,6},{5,7},{6,4},{7,5},{8,10},{9,11},{10,... | collective-permute-start | bytes 147464 | tf_op jit(solution)/shard_map/ppermute | solution.py:63
  88.8 1.6 %collective-permute-done.18 = f32[96,128]{1,0:T(8,128)S(1)} collective-permute-done((f32[96,128]{1,0:T(8,128)S(1)}, f32[96,128]{1,0:T(8,128)S(1)}, u32[]{:S(2)}, u32[]{:S(2)}) %collective-permute-start.18) | collective-permute-done | bytes 49184 | tf_op jit(solution)/shard_map/ppermute | solution.py:63
  91.0 2.3 %collective-permute-done.17 = f32[96,128]{1,0:T(8,128)S(1)} collective-permute-done((f32[96,128]{1,0:T(8,128)S(1)}, f32[96,128]{1,0:T(8,128)S(1)}, u32[]{:S(2)}, u32[]{:S(2)}) %collective-permute-start.17) | collective-permute-done | bytes 49184 | tf_op jit(solution)/shard_map/ppermute | solution.py:63
  94.7 1.7 %collective-permute-start.22 = (f32[24,128]{1,0:T(8,128)S(1)}, f32[24,128]{1,0:T(8,128)S(1)}, u32[]{:S(2)}, u32[]{:S(2)}) collective-permute-start(f32[24,128]{1,0:T(8,128)S(1)} %get-tuple-element.50), channel_id=1, source_target_pairs={{0,12},{1,13},{2,14},{3,15},{4,0},{5,1},{6,2},{7,3},{8,4},{9,5},{1... | collective-permute-start | bytes 36872 | tf_op jit(solution)/shard_map/ppermute | solution.py:63
  96.7 2.1 %collective-permute-done.21 = f32[24,128]{1,0:T(8,128)S(1)} collective-permute-done((f32[24,128]{1,0:T(8,128)S(1)}, f32[24,128]{1,0:T(8,128)S(1)}, u32[]{:S(2)}, u32[]{:S(2)}) %collective-permute-start.21) | collective-permute-done | bytes 12320 | tf_op jit(solution)/shard_map/ppermute | solution.py:63
  98.8 2.4 %collective-permute-done.20 = f32[24,128]{1,0:T(8,128)S(1)} collective-permute-done((f32[24,128]{1,0:T(8,128)S(1)}, f32[24,128]{1,0:T(8,128)S(1)}, u32[]{:S(2)}, u32[]{:S(2)}) %collective-permute-start.20) | collective-permute-done | bytes 12320 | tf_op jit(solution)/shard_map/ppermute | solution.py:63
  105.0 1.6 %collective-permute-start.26 = (f32[1,1]{1,0:T(1,128)}, f32[1,1]{1,0:T(1,128)}, u32[]{:S(2)}, u32[]{:S(2)}) collective-permute-start(f32[1,1]{1,0:T(1,128)} %add.115), channel_id=1, source_target_pairs={{0,12},{1,13},{2,14},{3,15},{4,0},{5,1},{6,2},{7,3},{8,4},{9,5},{1... | collective-permute-start | bytes 20 | tf_op jit(solution)/shard_map/ppermute | solution.py:63
  106.6 2.3 %collective-permute-start.25 = (f32[1,1]{1,0:T(1,128)}, f32[1,1]{1,0:T(1,128)}, u32[]{:S(2)}, u32[]{:S(2)}) collective-permute-start(f32[1,1]{1,0:T(1,128)} %add.115), channel_id=1, source_target_pairs={{0,8},{1,9},{2,10},{3,11},{4,12},{5,13},{6,14},{7,15},{8,0},{9,1},... | collective-permute-start | bytes 20 | tf_op jit(solution)/shard_map/ppermute | solution.py:63
  108.9 2.4 %collective-permute-start.24 = (f32[1,1]{1,0:T(1,128)}, f32[1,1]{1,0:T(1,128)}, u32[]{:S(2)}, u32[]{:S(2)}) collective-permute-start(f32[1,1]{1,0:T(1,128)} %add.115), channel_id=1, source_target_pairs={{0,4},{1,5},{2,6},{3,7},{4,8},{5,9},{6,10},{7,11},{8,12},{9,13},{1... | collective-permute-start | bytes 20 | tf_op jit(solution)/shard_map/ppermute | solution.py:63
  111.7 2.3 %collective-permute-done.24 = f32[1,1]{1,0:T(1,128)} collective-permute-done((f32[1,1]{1,0:T(1,128)}, f32[1,1]{1,0:T(1,128)}, u32[]{:S(2)}, u32[]{:S(2)}) %collective-permute-start.24) | collective-permute-done | bytes 36 | tf_op jit(solution)/shard_map/ppermute | solution.py:63
  117.2 3.1 %collective-permute-start.28 = (f32[1,1]{1,0:T(1,128)}, f32[1,1]{1,0:T(1,128)}, u32[]{:S(2)}, u32[]{:S(2)}) collective-permute-start(f32[1,1]{1,0:T(1,128)} %add.118), channel_id=1, source_target_pairs={{0,2},{1,3},{2,0},{3,1},{4,6},{5,7},{6,4},{7,5},{8,10},{9,11},{10,... | collective-permute-start | bytes 20 | tf_op jit(solution)/shard_map/ppermute | solution.py:63
  122.3 2.8 %collective-permute-done.27 = f32[1,1]{1,0:T(1,128)} collective-permute-done((f32[1,1]{1,0:T(1,128)}, f32[1,1]{1,0:T(1,128)}, u32[]{:S(2)}, u32[]{:S(2)}) %collective-permute-start.27) | collective-permute-done | bytes 36 | tf_op jit(solution)/shard_map/ppermute | solution.py:63
  126.9 4.0 %collective-permute-start.32 = (f32[1,1]{1,0:T(1,128)}, f32[1,1]{1,0:T(1,128)}, u32[]{:S(2)}, u32[]{:S(2)}) collective-permute-start(f32[1,1]{1,0:T(1,128)} %add.121), channel_id=1, source_target_pairs={{0,96},{1,97},{2,98},{3,99},{4,100},{5,101},{6,102},{7,103},{8,104... | collective-permute-start | bytes 20 | tf_op jit(solution)/shard_map/ppermute | solution.py:63
  132.2 2.2 %collective-permute-start.30 = (f32[1,1]{1,0:T(1,128)}, f32[1,1]{1,0:T(1,128)}, u32[]{:S(2)}, u32[]{:S(2)}) collective-permute-start(f32[1,1]{1,0:T(1,128)} %add.121), channel_id=1, source_target_pairs={{0,32},{1,33},{2,34},{3,35},{4,36},{5,37},{6,38},{7,39},{8,40},{9,... | collective-permute-start | bytes 20 | tf_op jit(solution)/shard_map/ppermute | solution.py:63
  134.3 1.7 %collective-permute-done.31 = f32[1,1]{1,0:T(1,128)} collective-permute-done((f32[1,1]{1,0:T(1,128)}, f32[1,1]{1,0:T(1,128)}, u32[]{:S(2)}, u32[]{:S(2)}) %collective-permute-start.31) | collective-permute-done | bytes 36 | tf_op jit(solution)/shard_map/ppermute | solution.py:63
  (101 shorter events, 25.9 us)
Async XLA Ops:
  3.0 5.8 %collective-permute-start = (f32[56,128]{1,0:T(8,128)S(1)}, f32[56,128]{1,0:T(8,128)S(1)}, u32[]{:S(2)}, u32[]{:S(2)}) collective-permute-start(f32[56,128]{1,0:T(8,128)S(1)} %get-tuple-element.18), channel_id=1, source_target_pairs={{0,4},{1,5},{2,6},{3,7},{4,8},{5,9},{6,10},{7,11},{8,12},{9,13},{1... | collective-permute-start | bytes 86024 | tf_op jit(solution)/shard_map/ppermute | solution.py:63
  4.7 5.4 %collective-permute-start.1 = (f32[56,128]{1,0:T(8,128)S(1)}, f32[56,128]{1,0:T(8,128)S(1)}, u32[]{:S(2)}, u32[]{:S(2)}) collective-permute-start(f32[56,128]{1,0:T(8,128)S(1)} %get-tuple-element.19), channel_id=1, source_target_pairs={{0,8},{1,9},{2,10},{3,11},{4,12},{5,13},{6,14},{7,15},{8,0},{9,1},... | collective-permute-start | bytes 86024 | tf_op jit(solution)/shard_map/ppermute | solution.py:63
  7.4 3.9 %collective-permute-start.2 = (f32[56,128]{1,0:T(8,128)S(1)}, f32[56,128]{1,0:T(8,128)S(1)}, u32[]{:S(2)}, u32[]{:S(2)}) collective-permute-start(f32[56,128]{1,0:T(8,128)S(1)} %get-tuple-element.20), channel_id=1, source_target_pairs={{0,12},{1,13},{2,14},{3,15},{4,0},{5,1},{6,2},{7,3},{8,4},{9,5},{1... | collective-permute-start | bytes 86024 | tf_op jit(solution)/shard_map/ppermute | solution.py:63
  11.4 5.5 %collective-permute-start.3 = (f32[128,128]{1,0:T(8,128)S(1)}, f32[128,128]{1,0:T(8,128)S(1)}, u32[]{:S(2)}, u32[]{:S(2)}) collective-permute-start(f32[128,128]{1,0:T(8,128)S(1)} %get-tuple-element.55), channel_id=1, source_target_pairs={{0,1},{1,2},{2,3},{3,0},{4,5},{5,6},{6,7},{7,4},{8,9},{9,10},{10,1... | collective-permute-start | bytes 196616 | tf_op jit(solution)/shard_map/ppermute | solution.py:63
  13.0 7.4 %collective-permute-start.5 = (f32[128,128]{1,0:T(8,128)S(1)}, f32[128,128]{1,0:T(8,128)S(1)}, u32[]{:S(2)}, u32[]{:S(2)}) collective-permute-start(f32[128,128]{1,0:T(8,128)S(1)} %get-tuple-element.53), channel_id=1, source_target_pairs={{0,3},{1,0},{2,1},{3,2},{4,7},{5,4},{6,5},{7,6},{8,11},{9,8},{10,9... | collective-permute-start | bytes 196616 | tf_op jit(solution)/shard_map/ppermute | solution.py:63
  14.7 5.8 %collective-permute-start.4 = (f32[128,128]{1,0:T(8,128)S(1)}, f32[128,128]{1,0:T(8,128)S(1)}, u32[]{:S(2)}, u32[]{:S(2)}) collective-permute-start(f32[128,128]{1,0:T(8,128)S(1)} %get-tuple-element.54), channel_id=1, source_target_pairs={{0,2},{1,3},{2,0},{3,1},{4,6},{5,7},{6,4},{7,5},{8,10},{9,11},{10,... | collective-permute-start | bytes 196616 | tf_op jit(solution)/shard_map/ppermute | solution.py:63
  20.6 7.5 %collective-permute-start.8 = (f32[416,128]{1,0:T(8,128)S(1)}, f32[416,128]{1,0:T(8,128)S(1)}, u32[]{:S(2)}, u32[]{:S(2)}) collective-permute-start(f32[416,128]{1,0:T(8,128)S(1)} %constant_dynamic-update-slice_fusion.39), channel_id=1, source_target_pairs={{0,96},{1,97},{2,98},{3,99},{4,100},{5,101},{6,102},{7,103},{8,104... | collective-permute-start | bytes 638984 | tf_op jit(solution)/shard_map/ppermute | solution.py:63
  24.7 7.2 %collective-permute-start.6 = (f32[416,128]{1,0:T(8,128)S(1)}, f32[416,128]{1,0:T(8,128)S(1)}, u32[]{:S(2)}, u32[]{:S(2)}) collective-permute-start(f32[416,128]{1,0:T(8,128)S(1)} %constant_dynamic-update-slice_fusion.31), channel_id=1, source_target_pairs={{0,32},{1,33},{2,34},{3,35},{4,36},{5,37},{6,38},{7,39},{8,40},{9,... | collective-permute-start | bytes 638984 | tf_op jit(solution)/shard_map/ppermute | solution.py:63
  24.7 13.2 %collective-permute-start.10 = (f32[32,128]{1,0:T(8,128)S(1)}, f32[32,128]{1,0:T(8,128)S(1)}, u32[]{:S(2)}, u32[]{:S(2)}) collective-permute-start(f32[32,128]{1,0:T(8,128)S(1)} %bitcast.30), channel_id=1, source_target_pairs={{0,64},{1,65},{2,66},{3,67},{4,68},{5,69},{6,70},{7,71},{8,72},{9,... | collective-permute-start | bytes 49160 | tf_op jit(solution)/shard_map/ppermute | solution.py:63
  28.0 9.8 %collective-permute-start.9 = (f32[192,128]{1,0:T(8,128)S(1)}, f32[192,128]{1,0:T(8,128)S(1)}, u32[]{:S(2)}, u32[]{:S(2)}) collective-permute-start(f32[192,128]{1,0:T(8,128)S(1)} %slice.250), channel_id=1, source_target_pairs={{0,96},{1,97},{2,98},{3,99},{4,100},{5,101},{6,102},{7,103},{8,104... | collective-permute-start | bytes 294920 | tf_op jit(solution)/shard_map/ppermute | solution.py:63
  31.9 5.9 %collective-permute-start.7 = (f32[192,128]{1,0:T(8,128)S(1)}, f32[192,128]{1,0:T(8,128)S(1)}, u32[]{:S(2)}, u32[]{:S(2)}) collective-permute-start(f32[192,128]{1,0:T(8,128)S(1)} %slice.248), channel_id=1, source_target_pairs={{0,32},{1,33},{2,34},{3,35},{4,36},{5,37},{6,38},{7,39},{8,40},{9,... | collective-permute-start | bytes 294920 | tf_op jit(solution)/shard_map/ppermute | solution.py:63
  37.9 2.5 %collective-permute-start.11 = (f32[1664,128]{1,0:T(8,128)S(1)}, f32[1664,128]{1,0:T(8,128)S(1)}, u32[]{:S(2)}, u32[]{:S(2)}) collective-permute-start(f32[1664,128]{1,0:T(8,128)S(1)} %constant_dynamic-update-slice_fusion.47.mine_ref), channel_id=1, source_target_pairs={{0,16},{1,17},{2,18},{3,19},{4,20},{5,21},{6,22},{7,23},{8,24},{9,... | collective-permute-start | bytes 2555912 | tf_op jit(solution)/shard_map/ppermute | solution.py:67
  64.8 2.4 %collective-permute-start.12 = (f32[1536,128]{1,0:T(8,128)S(1)}, f32[1536,128]{1,0:T(8,128)S(1)}, u32[]{:S(2)}, u32[]{:S(2)}) collective-permute-start(f32[1536,128]{1,0:T(8,128)S(1)} %get-tuple-element.22), channel_id=1, source_target_pairs={{0,16},{1,17},{2,18},{3,19},{4,20},{5,21},{6,22},{7,23},{8,24},{9,... | collective-permute-start | bytes 2359304 | tf_op jit(solution)/shard_map/ppermute | solution.py:67
  67.3 5.9 %collective-permute-start.13 = (f32[192,128]{1,0:T(8,128)S(1)}, f32[192,128]{1,0:T(8,128)S(1)}, u32[]{:S(2)}, u32[]{:S(2)}) collective-permute-start(f32[192,128]{1,0:T(8,128)S(1)} %slice.258), channel_id=1, source_target_pairs={{0,32},{1,33},{2,34},{3,35},{4,36},{5,37},{6,38},{7,39},{8,40},{9,... | collective-permute-start | bytes 294920 | tf_op jit(solution)/shard_map/ppermute | solution.py:63
  73.2 4.7 %collective-permute-start.15 = (f32[192,128]{1,0:T(8,128)S(1)}, f32[192,128]{1,0:T(8,128)S(1)}, u32[]{:S(2)}, u32[]{:S(2)}) collective-permute-start(f32[192,128]{1,0:T(8,128)S(1)} %get-tuple-element.33), channel_id=1, source_target_pairs={{0,96},{1,97},{2,98},{3,99},{4,100},{5,101},{6,102},{7,103},{8,104... | collective-permute-start | bytes 294920 | tf_op jit(solution)/shard_map/ppermute | solution.py:63
  73.3 7.0 %collective-permute-start.14 = (f32[384,128]{1,0:T(8,128)S(1)}, f32[384,128]{1,0:T(8,128)S(1)}, u32[]{:S(2)}, u32[]{:S(2)}) collective-permute-start(f32[384,128]{1,0:T(8,128)S(1)} %pad_maximum_fusion), channel_id=1, source_target_pairs={{0,32},{1,33},{2,34},{3,35},{4,36},{5,37},{6,38},{7,39},{8,40},{9,... | collective-permute-start | bytes 589832 | tf_op jit(solution)/shard_map/ppermute | solution.py:63
  77.9 6.7 %collective-permute-start.16 = (f32[384,128]{1,0:T(8,128)S(1)}, f32[384,128]{1,0:T(8,128)S(1)}, u32[]{:S(2)}, u32[]{:S(2)}) collective-permute-start(f32[384,128]{1,0:T(8,128)S(1)} %pad_maximum_fusion.1), channel_id=1, source_target_pairs={{0,96},{1,97},{2,98},{3,99},{4,100},{5,101},{6,102},{7,103},{8,104... | collective-permute-start | bytes 589832 | tf_op jit(solution)/shard_map/ppermute | solution.py:63
  84.8 5.7 %collective-permute-start.18 = (f32[96,128]{1,0:T(8,128)S(1)}, f32[96,128]{1,0:T(8,128)S(1)}, u32[]{:S(2)}, u32[]{:S(2)}) collective-permute-start(f32[96,128]{1,0:T(8,128)S(1)} %get-tuple-element.36), channel_id=1, source_target_pairs={{0,2},{1,3},{2,0},{3,1},{4,6},{5,7},{6,4},{7,5},{8,10},{9,11},{10,... | collective-permute-start | bytes 147464 | tf_op jit(solution)/shard_map/ppermute | solution.py:63
  86.8 4.2 %collective-permute-start.19 = (f32[96,128]{1,0:T(8,128)S(1)}, f32[96,128]{1,0:T(8,128)S(1)}, u32[]{:S(2)}, u32[]{:S(2)}) collective-permute-start(f32[96,128]{1,0:T(8,128)S(1)} %get-tuple-element.37), channel_id=1, source_target_pairs={{0,3},{1,0},{2,1},{3,2},{4,7},{5,4},{6,5},{7,6},{8,11},{9,8},{10,9... | collective-permute-start | bytes 147464 | tf_op jit(solution)/shard_map/ppermute | solution.py:63
  87.9 5.4 %collective-permute-start.17 = (f32[96,128]{1,0:T(8,128)S(1)}, f32[96,128]{1,0:T(8,128)S(1)}, u32[]{:S(2)}, u32[]{:S(2)}) collective-permute-start(f32[96,128]{1,0:T(8,128)S(1)} %get-tuple-element.38), channel_id=1, source_target_pairs={{0,1},{1,2},{2,3},{3,0},{4,5},{5,6},{6,7},{7,4},{8,9},{9,10},{10,1... | collective-permute-start | bytes 147464 | tf_op jit(solution)/shard_map/ppermute | solution.py:63
  93.3 5.5 %collective-permute-start.21 = (f32[24,128]{1,0:T(8,128)S(1)}, f32[24,128]{1,0:T(8,128)S(1)}, u32[]{:S(2)}, u32[]{:S(2)}) collective-permute-start(f32[24,128]{1,0:T(8,128)S(1)} %get-tuple-element.49), channel_id=1, source_target_pairs={{0,8},{1,9},{2,10},{3,11},{4,12},{5,13},{6,14},{7,15},{8,0},{9,1},... | collective-permute-start | bytes 36872 | tf_op jit(solution)/shard_map/ppermute | solution.py:63
  94.7 4.2 %collective-permute-start.22 = (f32[24,128]{1,0:T(8,128)S(1)}, f32[24,128]{1,0:T(8,128)S(1)}, u32[]{:S(2)}, u32[]{:S(2)}) collective-permute-start(f32[24,128]{1,0:T(8,128)S(1)} %get-tuple-element.50), channel_id=1, source_target_pairs={{0,12},{1,13},{2,14},{3,15},{4,0},{5,1},{6,2},{7,3},{8,4},{9,5},{1... | collective-permute-start | bytes 36872 | tf_op jit(solution)/shard_map/ppermute | solution.py:63
  96.3 4.9 %collective-permute-start.20 = (f32[24,128]{1,0:T(8,128)S(1)}, f32[24,128]{1,0:T(8,128)S(1)}, u32[]{:S(2)}, u32[]{:S(2)}) collective-permute-start(f32[24,128]{1,0:T(8,128)S(1)} %get-tuple-element.51), channel_id=1, source_target_pairs={{0,4},{1,5},{2,6},{3,7},{4,8},{5,9},{6,10},{7,11},{8,12},{9,13},{1... | collective-permute-start | bytes 36872 | tf_op jit(solution)/shard_map/ppermute | solution.py:63
  105.0 10.1 %collective-permute-start.26 = (f32[1,1]{1,0:T(1,128)}, f32[1,1]{1,0:T(1,128)}, u32[]{:S(2)}, u32[]{:S(2)}) collective-permute-start(f32[1,1]{1,0:T(1,128)} %add.115), channel_id=1, source_target_pairs={{0,12},{1,13},{2,14},{3,15},{4,0},{5,1},{6,2},{7,3},{8,4},{9,5},{1... | collective-permute-start | bytes 20 | tf_op jit(solution)/shard_map/ppermute | solution.py:63
  106.6 5.2 %collective-permute-start.25 = (f32[1,1]{1,0:T(1,128)}, f32[1,1]{1,0:T(1,128)}, u32[]{:S(2)}, u32[]{:S(2)}) collective-permute-start(f32[1,1]{1,0:T(1,128)} %add.115), channel_id=1, source_target_pairs={{0,8},{1,9},{2,10},{3,11},{4,12},{5,13},{6,14},{7,15},{8,0},{9,1},... | collective-permute-start | bytes 20 | tf_op jit(solution)/shard_map/ppermute | solution.py:63
  108.9 5.1 %collective-permute-start.24 = (f32[1,1]{1,0:T(1,128)}, f32[1,1]{1,0:T(1,128)}, u32[]{:S(2)}, u32[]{:S(2)}) collective-permute-start(f32[1,1]{1,0:T(1,128)} %add.115), channel_id=1, source_target_pairs={{0,4},{1,5},{2,6},{3,7},{4,8},{5,9},{6,10},{7,11},{8,12},{9,13},{1... | collective-permute-start | bytes 20 | tf_op jit(solution)/shard_map/ppermute | solution.py:63
  115.8 10.5 %collective-permute-start.29 = (f32[1,1]{1,0:T(1,128)}, f32[1,1]{1,0:T(1,128)}, u32[]{:S(2)}, u32[]{:S(2)}) collective-permute-start(f32[1,1]{1,0:T(1,128)} %add.118), channel_id=1, source_target_pairs={{0,3},{1,0},{2,1},{3,2},{4,7},{5,4},{6,5},{7,6},{8,11},{9,8},{10,9... | collective-permute-start | bytes 20 | tf_op jit(solution)/shard_map/ppermute | solution.py:63
  117.2 5.2 %collective-permute-start.28 = (f32[1,1]{1,0:T(1,128)}, f32[1,1]{1,0:T(1,128)}, u32[]{:S(2)}, u32[]{:S(2)}) collective-permute-start(f32[1,1]{1,0:T(1,128)} %add.118), channel_id=1, source_target_pairs={{0,2},{1,3},{2,0},{3,1},{4,6},{5,7},{6,4},{7,5},{8,10},{9,11},{10,... | collective-permute-start | bytes 20 | tf_op jit(solution)/shard_map/ppermute | solution.py:63
  120.3 4.9 %collective-permute-start.27 = (f32[1,1]{1,0:T(1,128)}, f32[1,1]{1,0:T(1,128)}, u32[]{:S(2)}, u32[]{:S(2)}) collective-permute-start(f32[1,1]{1,0:T(1,128)} %add.118), channel_id=1, source_target_pairs={{0,1},{1,2},{2,3},{3,0},{4,5},{5,6},{6,7},{7,4},{8,9},{9,10},{10,1... | collective-permute-start | bytes 20 | tf_op jit(solution)/shard_map/ppermute | solution.py:63
  126.9 11.3 %collective-permute-start.32 = (f32[1,1]{1,0:T(1,128)}, f32[1,1]{1,0:T(1,128)}, u32[]{:S(2)}, u32[]{:S(2)}) collective-permute-start(f32[1,1]{1,0:T(1,128)} %add.121), channel_id=1, source_target_pairs={{0,96},{1,97},{2,98},{3,99},{4,100},{5,101},{6,102},{7,103},{8,104... | collective-permute-start | bytes 20 | tf_op jit(solution)/shard_map/ppermute | solution.py:63
  130.9 5.2 %collective-permute-start.31 = (f32[1,1]{1,0:T(1,128)}, f32[1,1]{1,0:T(1,128)}, u32[]{:S(2)}, u32[]{:S(2)}) collective-permute-start(f32[1,1]{1,0:T(1,128)} %add.121), channel_id=1, source_target_pairs={{0,64},{1,65},{2,66},{3,67},{4,68},{5,69},{6,70},{7,71},{8,72},{9,... | collective-permute-start | bytes 20 | tf_op jit(solution)/shard_map/ppermute | solution.py:63
  132.2 4.9 %collective-permute-start.30 = (f32[1,1]{1,0:T(1,128)}, f32[1,1]{1,0:T(1,128)}, u32[]{:S(2)}, u32[]{:S(2)}) collective-permute-start(f32[1,1]{1,0:T(1,128)} %add.121), channel_id=1, source_target_pairs={{0,32},{1,33},{2,34},{3,35},{4,36},{5,37},{6,38},{7,39},{8,40},{9,... | collective-permute-start | bytes 20 | tf_op jit(solution)/shard_map/ppermute | solution.py:63
  (10 other events, 221.0 us)

commit v4 on v2

--- a/solution.py
+++ b/solution.py
@@ -33,6 +33,7 @@
 CODE_ROWS = 256
 FLAT_ROWS = DEVICES * SHARD_ROWS
 BLOCK = 256
+SUBS = 4
 ALL_POINTS = POINTS_DEV * DEVICES
 
 F32 = jnp.float32
@@ -76,7 +77,32 @@
     return jnp.concatenate(parts, axis=0)
 
 
-def pack_kernel(weights_ref, coords_ref, distances_ref, index_ref, out_ref):
+def pack_kernel(
+    weights_hbm,
+    coords_hbm,
+    distances_hbm,
+    index_hbm,
+    out_ref,
+    weights_ref,
+    coords_ref,
+    distances_ref,
+    index_ref,
+    sems,
+):
+    pairs = [
+        (index_hbm, index_ref),
+        (weights_hbm, weights_ref),
+        (coords_hbm, coords_ref),
+        (distances_hbm, distances_ref),
+    ]
+    copies = [
+        pltpu.make_async_copy(source, target, sems.at[i])
+        for i, (source, target) in enumerate(pairs)
+    ]
+    for copy in copies:
+        copy.start()
+    for copy in copies:
+        copy.wait()
     shard = stacked(weights_ref[...], jnp.zeros((BOX_ROWS - SHARD_ROWS, LANES), F32))
     for peer in range(PEERS):
         out_ref[peer * BOX_ROWS : (peer + 1) * BOX_ROWS, :] = shard
@@ -188,7 +214,8 @@
     mine_ref,
     other_ref,
     codes_ref,
-    out_ref,
+    keep_ref,
+    give_ref,
     code_grad_ref,
     flat,
     first_w,
@@ -319,11 +346,11 @@
         ref[...] = jnp.zeros(ref.shape, F32)
 
     def feature(which, step, sub):
-        first = which * SLOTS + step * 4 + sub * 2
+        first = which * SLOTS + (step * SUBS + sub) * 2
         return beside(spots[pl.ds(first, 1), :], spots[pl.ds(first + 1, 1), :])
 
     blank5 = jnp.zeros((5, BLOCK), F32)
-    subs = range(2)
+    subs = range(SUBS)
     chunk = 32
 
     def step_body(step, carry):
@@ -470,8 +497,9 @@
             left += [bar_hi[s], bar_hi[s], bar_lo[s], gate_hi[s], gate_hi[s], gate_lo[s]]
             right += [hid_hi[s], hid_lo[s], hid_hi[s], tang_hi[s], tang_lo[s], tang_hi[s]]
         sum_two[...] += mm_nt(beside(*left), beside(*right))
-        hots = beside(hot[0], hot[0], hot[1], hot[1])
-        sum_codes[256:768, :] += mm_nt(beside(bar_hi[0], bar_lo[0], bar_hi[1], bar_lo[1]), hots)
+        hots = beside(*[hot[s // 2] for s in range(2 * SUBS)])
+        bars = beside(*[(bar_hi, bar_lo)[s % 2][s // 2] for s in range(2 * SUBS)])
+        sum_codes[256:768, :] += mm_nt(bars, hots)
 
         for s in subs:
             for r in range(0, 256, chunk):
@@ -482,7 +510,8 @@
                 high, low = halves(bar)
                 low_hi[s, r : r + chunk, :] = high
                 low_lo[s, r : r + chunk, :] = low
-        sum_codes[0:256, :] += mm_nt(beside(low_hi[0], low_lo[0], low_hi[1], low_lo[1]), hots)
+        bars = beside(*[(low_hi, low_lo)[s % 2][s // 2] for s in range(2 * SUBS)])
+        sum_codes[0:256, :] += mm_nt(bars, hots)
         left, right = [], []
         for s in subs:
             seen = stacked(near_pieces[s][0], near_pieces[s][1]).astype(BF16)
@@ -494,7 +523,7 @@
         sum_coord[...] += mm_nt(beside(*left), beside(*right))
         return carry
 
-    lax.fori_loop(0, SLOTS * DEVICES // (2 * BLOCK), step_body, 0)
+    lax.fori_loop(0, SLOTS * DEVICES // (SUBS * BLOCK), step_body, 0)
 
     codes = codes_ref[...]
     count = jnp.sum(sum_count[...], axis=1, keepdims=True)
@@ -562,13 +591,19 @@
     wide = rows_of_lanes(1, (8, LANES))
     info = jnp.where((sub == 5) & (wide == 0), loss, 0.0)
     info = jnp.where((sub == 5) & (wide == 1), code_squares, info)
-    for d in range(DEVICES):
-        z, c, w = d // 32, d // 16 % 2, d % 16
-        half = jnp.where(core == c, 0, PEERS * BOX_ROWS)
-        base = pl.multiple_of(half + (z * 16 + w) * BOX_ROWS, 8)
-        first = d * SHARD_ROWS
-        out_ref[pl.ds(base, 16), :] = flat[first : first + 16, :]
-        out_ref[pl.ds(base + 16, 8), :] = jnp.where(sub < 5, flat[first + 16 : first + 24, :], info)
+    for which in range(2):
+
+        @pl.when(core == which)
+        def _(which=which):
+            for d in range(DEVICES):
+                z, c, w = d // 32, d // 16 % 2, d % 16
+                target = keep_ref if c == which else give_ref
+                box = (z * 16 + w) * BOX_ROWS
+                first = d * SHARD_ROWS
+                target[box : box + 16, :] = flat[first : first + 16, :]
+                target[box + 16 : box + 24, :] = jnp.where(
+                    sub < 5, flat[first + 16 : first + 24, :], info
+                )
 
 
 def vmem(count):
@@ -576,21 +611,31 @@
 
 
 PARAMS = pltpu.CompilerParams(vmem_limit_bytes=48 * 1024 * 1024)
+
+
+HBM = pl.BlockSpec(memory_space=pltpu.HBM)
 
 
 def pack_boxes(weights, coords, distances, index):
     return pl.pallas_call(
         pack_kernel,
         out_shape=jax.ShapeDtypeStruct((PEERS * BOX_ROWS, LANES), F32),
-        in_specs=vmem(4),
+        in_specs=[HBM] * 4,
         out_specs=vmem(1)[0],
+        scratch_shapes=[
+            pltpu.VMEM(weights.shape, F32),
+            pltpu.VMEM(coords.shape, F32),
+            pltpu.VMEM(distances.shape, F32),
+            pltpu.VMEM(index.shape, jnp.int32),
+            pltpu.SemaphoreType.DMA((4,)),
+        ],
         compiler_params=PARAMS,
     )(weights, coords, distances, index)
 
 
 def main_call(core, mine, other, codes):
-    pair = (2, 256, BLOCK)
-    pair_two = (2, HID, BLOCK)
+    pair = (SUBS, 256, BLOCK)
+    pair_two = (SUBS, HID, BLOCK)
     scratch = [
         ((FLAT_ROWS + 8, LANES), F32),
         ((256, 3 * LANES), F32),
@@ -632,11 +677,12 @@
     return pl.pallas_call(
         main_kernel,
         out_shape=(
-            jax.ShapeDtypeStruct((2 * PEERS * BOX_ROWS, LANES), F32),
+            jax.ShapeDtypeStruct((PEERS * BOX_ROWS, LANES), F32),
+            jax.ShapeDtypeStruct((PEERS * BOX_ROWS, LANES), F32),
             jax.ShapeDtypeStruct((CODE_ROWS, LATENT), F32),
         ),
         in_specs=[pl.BlockSpec(memory_space=pltpu.SMEM)] + vmem(3),
-        out_specs=tuple(vmem(2)),
+        out_specs=tuple(vmem(3)),
         scratch_shapes=[pltpu.VMEM(shape, dtype) for shape, dtype in scratch],
         compiler_params=PARAMS,
     )(core, mine, other, codes)
@@ -649,6 +695,95 @@
     second_hat = second_new / (1.0 - BETA_TWO**STEP)
     value_new = value - rate * (first_hat / (jnp.sqrt(second_hat) + ADAM_EPS) + DECAY * value)
     return (value_new, first_new, second_new)
+
+
+def shard_kernel(parts_ref, shard_ref, squares_ref):
+    total = parts_ref[0:BOX_ROWS, :]
+    for peer in range(1, PEERS):
+        total = total + parts_ref[peer * BOX_ROWS : (peer + 1) * BOX_ROWS, :]
+    shard_ref[...] = total
+    grad = total[:SHARD_ROWS, :]
+    squares_ref[...] = jnp.broadcast_to(total_of(grad * grad), squares_ref.shape)
+
+
+def sum_shards(parts):
+    return pl.pallas_call(
+        shard_kernel,
+        out_shape=(
+            jax.ShapeDtypeStruct((BOX_ROWS, LANES), F32),
+            jax.ShapeDtypeStruct((8, LANES), F32),
+        ),
+        in_specs=vmem(1),
+        out_specs=tuple(vmem(2)),
+        compiler_params=PARAMS,
+    )(parts)
+
+
+def update_kernel(
+    seen_ref,
+    shard_ref,
+    weights_ref,
+    moment_one_ref,
+    moment_two_ref,
+    codes_ref,
+    code_first_ref,
+    code_second_ref,
+    code_grad_ref,
+    loss_out,
+    norm_out,
+    weights_out,
+    moment_one_out,
+    moment_two_out,
+    weights_copy_out,
+    codes_out,
+    code_first_out,
+    code_second_out,
+    codes_copy_out,
+):
+    total = seen_ref[0:8, :]
+    for peer in range(1, PEERS):
+        total = total + seen_ref[peer * 8 : peer * 8 + 8, :]
+    loss_out[...] = shard_ref[SHARD_ROWS : SHARD_ROWS + 1, 0:1]
+    norm = jnp.sqrt(total[0:1, 0:1] + shard_ref[SHARD_ROWS : SHARD_ROWS + 1, 1:2])
+    norm_out[...] = norm
+    factor = jnp.minimum(1.0, CLIP / (norm + 1e-06))
+    value, first, second = adam_update(
+        weights_ref[...],
+        moment_one_ref[...],
+        moment_two_ref[...],
+        factor * shard_ref[0:SHARD_ROWS, :],
+        WEIGHT_RATE,
+    )
+    weights_out[...] = value
+    moment_one_out[...] = first
+    moment_two_out[...] = second
+    weights_copy_out[...] = value.astype(BF16)
+    for r in range(0, CODE_ROWS, 32):
+        rows = slice(r, r + 32)
+        value, first, second = adam_update(
+            codes_ref[rows, :],
+            code_first_ref[rows, :],
+            code_second_ref[rows, :],
+            factor * code_grad_ref[rows, :],
+            CODE_RATE,
+        )
+        codes_out[rows, :] = value
+        code_first_out[rows, :] = first
+        code_second_out[rows, :] = second
+        codes_copy_out[rows, :] = value.astype(BF16)
+
+
+def update_all(*args):
+    scalar = jax.ShapeDtypeStruct((1, 1), F32)
+    shard = [jax.ShapeDtypeStruct((SHARD_ROWS, LANES), t) for t in (F32, F32, F32, BF16)]
+    table = [jax.ShapeDtypeStruct((CODE_ROWS, LATENT), t) for t in (F32, F32, F32, BF16)]
+    return pl.pallas_call(
+        update_kernel,
+        out_shape=(scalar, scalar, *shard, *table),
+        in_specs=vmem(9),
+        out_specs=tuple(vmem(10)),
+        compiler_params=PARAMS,
+    )(*args)
 
 
 def swap_cores(v):
@@ -679,41 +814,33 @@
     mine = exchange(boxes.reshape(PEERS, BOX_ROWS, LANES))
     other = swap_cores(mine)
     core = lax.axis_index("core").astype(jnp.int32).reshape(1)
-    grads, code_grad = main_call(
+    keep, give, code_grad = main_call(
         core,
         mine.reshape(PEERS * BOX_ROWS, LANES),
         other.reshape(PEERS * BOX_ROWS, LANES),
         codes,
     )
-    grads = grads.reshape(2, PEERS, BOX_ROWS, LANES)
-    pair_sum = grads[0] + swap_cores(grads[1])
-    shard = jnp.sum(exchange(pair_sum), axis=0)
-    weight_grad = shard[:SHARD_ROWS]
-    loss_value = shard[SHARD_ROWS, 0]
-    code_squares = shard[SHARD_ROWS, 1]
-    squares = jnp.sum(weight_grad * weight_grad)
-    seen = exchange(jnp.broadcast_to(squares, (PEERS, 1, LANES)))
-    squares = jnp.sum(seen[:, 0, 0]).reshape(1, 1)
-    squares = (squares + swap_cores(squares)).reshape(())
-    grad_norm = jnp.sqrt(squares + code_squares)
-    factor = jnp.minimum(1.0, CLIP / (grad_norm + 1e-06))
-    new_weights, first_new, second_new = adam_update(
-        weights_flat, moment_one, moment_two, factor * weight_grad.reshape(-1), WEIGHT_RATE
-    )
-    new_codes, code_first_new, code_second_new = adam_update(
-        codes, code_first, code_second, factor * code_grad, CODE_RATE
+    pair_sum = (keep + swap_cores(give)).reshape(PEERS, BOX_ROWS, LANES)
+    shard, squares = sum_shards(exchange(pair_sum).reshape(PEERS * BOX_ROWS, LANES))
+    squares = squares + swap_cores(squares)
+    seen = exchange(jnp.broadcast_to(squares, (PEERS, 8, LANES)))
+    flat = lambda v: v.reshape(SHARD_ROWS, LANES)
+    out = update_all(
+        seen.reshape(PEERS * 8, LANES),
+        shard,
+        flat(weights_flat),
+        flat(moment_one),
+        flat(moment_two),
+        codes,
+        code_first,
+        code_second,
+        code_grad,
     )
     return (
-        loss_value,
-        grad_norm,
-        new_weights,
-        first_new,
-        second_new,
-        new_weights.astype(BF16),
-        new_codes,
-        code_first_new,
-        code_second_new,
-        new_codes.astype(BF16),
+        out[0].reshape(()),
+        out[1].reshape(()),
+        *[v.reshape(weights_flat.shape) for v in out[2:6]],
+        *out[6:],
     )
 
 

time: 106 us -> 98.7 us (0.931)
  blocking collectives: 48.2 us -> 63.8 us
  waiting for transfers between devices: 14.6 us -> 5.56 us
  starting transfers between devices: 4.95 us -> 0.25 us
  between operations: 3.9 us -> 0.75 us
  other arithmetic: 3.11 us -> 0.08 us
  local copies, waits for them, and re-layouts: 4.83 us -> 2.84 us
    all_to_all x2 -> x3, blocking collectives: 48.2 us -> 63.8 us  [exchange(): return lax.all_to_all(v, ('z', 'wide'), split_axis=0, concat_axis=0)]
    all_to_all x1 -> x0, waiting for transfers between devices: 8.89 us -> none  [exchange(): return lax.all_to_all(v, ('z', 'wide'), split_axis=0, concat_axis=0)]
    all_to_all x1 -> x0, starting transfers between devices: 4.73 us -> none  [exchange(): return lax.all_to_all(v, ('z', 'wide'), split_axis=0, concat_axis=0)]
    convert_element_type x2 -> x0, other arithmetic: 1.68 us -> none  [the longest x1 1.05 us: body(): new_codes.astype(BF16)]
    reduce_sum x3 -> x0, other arithmetic: 1.35 us -> none  [the longest x1 0.67 us: body(): squares = jnp.sum(seen[:, 0, 0]).reshape(1, 1)]
    broadcast_in_dim x1, local copies, waits for them, and re-layouts: 1.28 us -> 0.02 us  [body(): seen = exchange(jnp.broadcast_to(squares, (PEERS, 8, LANES)))]
    pallas_call x1 -> x3, Pallas kernels: 24.1 us -> 24 us  [the longest x1 22.6 us: main_call(): pl.pallas_call(main_kernel, out_shape=(jax.ShapeDtypeStruct((PEERS * BOX_...]
  transfers between devices with their start and end apart: 4 -> 3, of which waited for: 4 -> 3; matrix products, arithmetic and copies ran while one was open for 1% -> 0% of each run, Pallas kernels for 0% -> 0%
where the time goes in v4:
time: 98.7 us; the launch traced here: 98.2 us
  blocking collectives  63.8 us (65%)
  Pallas kernels  24.9 us (25%)
  waiting for transfers between devices  5.56 us (6%)
  local copies, waits for them, and re-layouts  2.84 us (3%)
    all_to_all x3, blocking collectives, exchange(): return lax.all_to_all(v, ('z', 'wide'), split_axis=0, concat_axis=0)  63.8 us
    pallas_call x1, Pallas kernels, main_call(): pl.pallas_call(main_kernel, out_shape=(jax.ShapeDtypeStruct((PEERS * BOX_...  22.6 us
    ppermute x3, waiting for transfers between devices, swap_cores(): return lax.ppermute(v, 'core', [(0, 1), (1, 0)])  5.56 us
    unnamed x20, local copies, waits for them, and re-layouts  2.82 us
  transfers between devices with their start and end apart: 3, of which 3 were waited for; matrix products, arithmetic and copies ran while one was open for 0% of the time, Pallas kernels for 0%

profile of v4, /device:TPU:0, one launch (start us, length us, event | category | flops | bytes accessed | tf_op | source)
XLA Modules:
  0.0 98.2 jit_solution(9314597374561562245)
XLA Ops:
  0.6 0.0 copy-start.8
  0.7 0.7 copy-done.8
  1.3 0.0 copy-start.3
  1.3 0.7 copy-done.3
  2.0 0.0 copy-start.5
  2.0 0.7 copy-done.5
  2.8 0.0 copy-start.9
  2.8 0.7 copy-done.9
  3.4 0.9 shard_map.168
  4.4 0.0 copy-start
  4.4 27.4 %all_to_all.15 = f32[64,24,128]{2,1,0:T(8,128)S(1)} all-to-all(f32[64,24,128]{2,1,0:T(8,128)S(1)} %bitcast.20), channel_id=1, replica_groups=mesh['z'=4,'core'=2,'wide'=16] {'z','wide'}, dimensions={0} | all-to-all | bytes 1572864 | tf_op jit(solution)/shard_map/all_to_all | solution.py:794
  31.8 0.0 collective-permute-start
  31.8 2.3 %collective-permute-done = f32[64,24,128]{2,1,0:T(8,128)S(1)} collective-permute-done((f32[64,24,128]{2,1,0:T(8,128)S(1)}, f32[64,24,128]{2,1,0:T(8,128)S(1)}, u32[]{:S(2)}, u32[]{:S(2)}) %collective-permute-start) | collective-permute-done | bytes 786464 | tf_op jit(solution)/shard_map/ppermute | solution.py:790
  34.1 0.0 copy-done
  34.1 22.6 %shard_map.169 = (f32[1536,128]{1,0:T(8,128)S(1)}, f32[1536,128]{1,0:T(8,128)S(1)}, f32[256,256]{1,0:T(8,128)S(1)}) custom-call(s32[1]{0:T(128)} %bitcast.core_ref, f32[1536,128]{1,0:T(8,128)S(1)} %bitcast.18, f32[1536,128]{1,0:T(8,128)S(1)} %bitcast.22, f32[256,256]{1,0:T(8,128)S(1)} %copy-done), custom_call_target="tpu_custom_call" | custom-call | tf_op jit(solution)/shard_map/pallas_call | solution.py:677
  56.8 0.2 collective-permute-start.1
  57.0 2.1 %collective-permute-done.1 = f32[1536,128]{1,0:T(8,128)S(1)} collective-permute-done((f32[1536,128]{1,0:T(8,128)S(1)}, f32[1536,128]{1,0:T(8,128)S(1)}, u32[]{:S(2)}, u32[]{:S(2)}) %collective-permute-start.1) | collective-permute-done | bytes 786464 | tf_op jit(solution)/shard_map/ppermute | solution.py:790
  59.1 0.1 add.6
  59.2 20.9 %all_to_all.16 = f32[64,24,128]{2,1,0:T(8,128)S(1)} all-to-all(f32[64,24,128]{2,1,0:T(8,128)S(1)} %bitcast.29), channel_id=1, replica_groups=mesh['z'=4,'core'=2,'wide'=16] {'z','wide'}, dimensions={0} | all-to-all | bytes 1572864 | tf_op jit(solution)/shard_map/all_to_all | solution.py:794
  80.1 0.2 shard_map.170
  80.2 0.0 collective-permute-start.2
  80.2 1.2 %collective-permute-done.2 = f32[8,128]{1,0:T(8,128)S(1)} collective-permute-done((f32[8,128]{1,0:T(8,128)S(1)}, f32[8,128]{1,0:T(8,128)S(1)}, u32[]{:S(2)}, u32[]{:S(2)}) %collective-permute-start.2) | collective-permute-done | bytes 4128 | tf_op jit(solution)/shard_map/ppermute | solution.py:790
  81.4 0.0 copy-start.6
  81.4 0.0 copy-start.1
  81.4 0.0 copy-start.2
  81.5 15.5 %all_to_all.17 = f32[64,8,128]{2,1,0:T(8,128)S(1)} all-to-all(f32[64,8,128]{2,1,0:T(8,128)S(1)} %broadcast_in_dim.3), channel_id=1, replica_groups=mesh['z'=4,'core'=2,'wide'=16] {'z','wide'}, dimensions={0} | all-to-all | bytes 524288 | tf_op jit(solution)/shard_map/all_to_all | solution.py:794
  97.0 0.0 copy-done.4
  97.0 0.0 copy-done.6
  97.0 0.0 copy-done.7
  97.0 0.0 copy-done.1
  97.0 0.0 copy-done.2
  97.0 1.2 %shard_map.171 = (f32[1,1]{1,0:T(1,128)}, f32[1,1]{1,0:T(1,128)}, f32[21,128]{1,0:T(8,128)}, f32[21,128]{1,0:T(8,128)}, f32[21,128]{1,0:T(8,128)}, /*index=5*/bf...) custom-call(f32[512,128]{1,0:T(8,128)S(1)} %bitcast.21, ...), custom_call_target="tpu_custom_call" | custom-call | tf_op jit(solution)/shard_map/pallas_call | solution.py:780
  (4 shorter events, 0.0 us)
Async XLA Ops:
  0.6 0.7 copy-start.8
  1.3 0.7 copy-start.3
  2.0 0.7 copy-start.5
  2.8 0.7 copy-start.9
  4.4 29.7 %copy-start = (f32[256,256]{1,0:T(8,128)S(1)}, f32[256,256]{1,0:T(8,128)}, u32[]{:S(2)}) copy-start(f32[256,256]{1,0:T(8,128)} %codes_ref.3) | copy-start | bytes 786436
  31.8 2.3 %collective-permute-start = (f32[64,24,128]{2,1,0:T(8,128)S(1)}, f32[64,24,128]{2,1,0:T(8,128)S(1)}, u32[]{:S(2)}, u32[]{:S(2)}) collective-permute-start(f32[64,24,128]{2,1,0:T(8,128)S(1)} %all_to_all.15), channel_id=1, source_target_pairs={{0,16},{16,0},{1,17},{17,1},{2,18},{18,2},{3,19},{19,3},{4,20},{20... | collective-permute-start | bytes 2359304 | tf_op jit(solution)/shard_map/ppermute | solution.py:790
  56.8 2.4 %collective-permute-start.1 = (f32[1536,128]{1,0:T(8,128)S(1)}, f32[1536,128]{1,0:T(8,128)S(1)}, u32[]{:S(2)}, u32[]{:S(2)}) collective-permute-start(f32[1536,128]{1,0:T(8,128)S(1)} %get-tuple-element.26), channel_id=1, source_target_pairs={{0,16},{16,0},{1,17},{17,1},{2,18},{18,2},{3,19},{19,3},{4,20},{20... | collective-permute-start | bytes 2359304 | tf_op jit(solution)/shard_map/ppermute | solution.py:790
  80.2 1.2 %collective-permute-start.2 = (f32[8,128]{1,0:T(8,128)S(1)}, f32[8,128]{1,0:T(8,128)S(1)}, u32[]{:S(2)}, u32[]{:S(2)}) collective-permute-start(f32[8,128]{1,0:T(8,128)S(1)} %get-tuple-element.27), channel_id=1, source_target_pairs={{0,16},{16,0},{1,17},{17,1},{2,18},{18,2},{3,19},{19,3},{4,20},{20... | collective-permute-start | bytes 12296 | tf_op jit(solution)/shard_map/ppermute | solution.py:790
  81.4 15.6 %copy-start.4 = (f32[2688]{0:T(1024)S(1)}, f32[2688]{0:T(1024)}, u32[]{:S(2)}) copy-start(f32[2688]{0:T(1024)} %param.9) | copy-start | bytes 32260
  81.4 15.6 %copy-start.6 = (f32[2688]{0:T(1024)S(1)}, f32[2688]{0:T(1024)}, u32[]{:S(2)}) copy-start(f32[2688]{0:T(1024)} %param.10) | copy-start | bytes 32260
  81.4 15.6 %copy-start.7 = (f32[2688]{0:T(1024)S(1)}, f32[2688]{0:T(1024)}, u32[]{:S(2)}) copy-start(f32[2688]{0:T(1024)} %param.11) | copy-start | bytes 32260
  81.4 15.6 %copy-start.1 = (f32[256,256]{1,0:T(8,128)S(1)}, f32[256,256]{1,0:T(8,128)}, u32[]{:S(2)}) copy-start(f32[256,256]{1,0:T(8,128)} %code_first_ref.1) | copy-start | bytes 786436
  81.4 15.6 %copy-start.2 = (f32[256,256]{1,0:T(8,128)S(1)}, f32[256,256]{1,0:T(8,128)}, u32[]{:S(2)}) copy-start(f32[256,256]{1,0:T(8,128)} %code_second_ref.1) | copy-start | bytes 786436

commit v5 on v4

--- a/solution.py
+++ b/solution.py
@@ -32,8 +32,9 @@
 POINTS_DEV = 1024
 CODE_ROWS = 256
 FLAT_ROWS = DEVICES * SHARD_ROWS
-BLOCK = 256
-SUBS = 4
+BLOCK = 512
+SUBS = 2
+TILES = BLOCK // LANES
 ALL_POINTS = POINTS_DEV * DEVICES
 
 F32 = jnp.float32
@@ -200,13 +201,27 @@
 HEAD_ENTRY = MIDDLE * (LATENT + 5) + HID * (HID + 3)
 
 
-def silu_parts(v):
-    gate = 0.5 * jnp.tanh(0.5 * v) + 0.5
-    rest = 1.0 - gate
-    value = v * gate
-    slope = gate + value * rest
-    curve = rest * (gate + gate + value * (rest - gate))
-    return value, slope, curve
+def across(column):
+    return beside(*[column] * TILES)
+
+
+def folded(v):
+    return sum(v[:, i * LANES : (i + 1) * LANES] for i in range(TILES))
+
+
+def silu_parts(half):
+    gate = jnp.tanh(half)
+    low = 0.5 * gate
+    bend = 0.5 - gate * low
+    bent = half * gate
+    return half + bent, (0.5 + low) + half * bend, bend * (1.0 - bent)
+
+
+def silu_parts_twice(half):
+    gate = jnp.tanh(half)
+    bend = 1.0 - gate * gate
+    bent = half * gate
+    return half + bent, (1.0 + gate) + half * bend, bend * (1.0 - bent)
 
 
 def main_kernel(
@@ -303,7 +318,9 @@
     second_b = second_w[:, 256:512]
     second_gain = second_w[:, 512:513]
     second_bias = second_w[:, 513:514]
-    head_w[...] = jnp.broadcast_to(second_w[:, 514:515], (HID, LANES))
+    head = jnp.broadcast_to(second_w[:, 514:515], (HID, LANES))
+    head_w[:, :LANES] = 0.5 * head
+    head_w[:, LANES:] = head
     second_root = lax.rsqrt(
         jnp.sum(second_a * second_a + second_b * second_b, axis=1, keepdims=True) + 1e-12
     )
@@ -315,7 +332,7 @@
     latent_cols = pltpu.roll(jnp.where(is_hidden, second_b, second_a), 3, 1)
     latent_w[256:768, :] = latent_cols
 
-    hidden_hi, hidden_lo = halves(hidden_cols)
+    hidden_hi, hidden_lo = halves(0.5 * hidden_cols)
     lhs_two[:, 0:256] = hidden_hi
     lhs_two[:, 256:512] = hidden_hi
     lhs_two[:, 512:768] = hidden_lo
@@ -329,14 +346,14 @@
     by_code = mm_nt(
         beside(weight_hi, weight_hi, weight_lo), beside(code_hi, code_lo, code_hi)
     )
-    one_hi, one_lo = halves(by_code[0:256, :] + first_bias)
+    one_hi, one_lo = halves(0.5 * (by_code[0:256, :] + first_bias))
     lhs_one[:, 0:256] = one_hi
     lhs_one[:, 256:512] = one_lo
-    two_hi, two_lo = halves(by_code[256:768, :] + second_bias)
+    two_hi, two_lo = halves(0.5 * (by_code[256:768, :] + second_bias))
     lhs_two[:, 768:1024] = two_hi
     lhs_two[:, 1024:1280] = two_lo
     spread = jnp.where((unit - MIDDLE == lane) & (lane < 3), 1.0, first_near)
-    near_parts = thirds(spread)
+    near_parts = thirds(0.5 * spread)
     near_lhs = near_parts[0]
     for place, k in enumerate((0, 0, 1, 1, 2)):
         near_lhs = near_lhs + pltpu.roll(near_parts[k], 8 * (place + 1), 1)
@@ -346,12 +363,12 @@
         ref[...] = jnp.zeros(ref.shape, F32)
 
     def feature(which, step, sub):
-        first = which * SLOTS + (step * SUBS + sub) * 2
-        return beside(spots[pl.ds(first, 1), :], spots[pl.ds(first + 1, 1), :])
+        first = which * SLOTS + (step * SUBS + sub) * TILES
+        return beside(*[spots[pl.ds(first + i, 1), :] for i in range(TILES)])
 
     blank5 = jnp.zeros((5, BLOCK), F32)
     subs = range(SUBS)
-    chunk = 32
+    chunk = 8192 // BLOCK
 
     def step_body(step, carry):
         place = [[feature(i, step, s) for i in range(3)] for s in subs]
@@ -368,7 +385,7 @@
                     (rows_of_lanes(0, (chunk, BLOCK)) + r).astype(F32) == wanted, 1.0, 0.0
                 )
                 hot[s, r : r + chunk, :] = mark.astype(BF16)
-                sum_count[r : r + chunk, :] += mark[:, :LANES] + mark[:, LANES:]
+                sum_count[r : r + chunk, :] += folded(mark)
 
         for s in subs:
             high, mid, low = near_pieces[s]
@@ -382,7 +399,7 @@
                 value, slope, curve = silu_parts(pre)
                 if r + chunk == 256:
                     inside = rows_of_lanes(0, (chunk, BLOCK)) + r < MIDDLE
-                    value = jnp.where(inside, value, pre)
+                    value = jnp.where(inside, value, pre + pre)
                     slope = jnp.where(inside, slope, 0.0)
                     curve = jnp.where(inside, curve, 0.0)
                 high, low = halves(value)
@@ -399,8 +416,8 @@
         for s in subs:
             total = jnp.zeros((8, BLOCK), F32)
             for r in range(0, HID, chunk):
-                value, slope, curve = silu_parts(act_two[s, r : r + chunk, :])
-                head = beside(head_w[r : r + chunk, :], head_w[r : r + chunk, :])
+                value, slope, curve = silu_parts_twice(act_two[s, r : r + chunk, :])
+                head = across(head_w[r : r + chunk, :LANES])
                 weighed = head * value
                 for k in range(0, chunk, 8):
                     total = total + weighed[k : k + 8, :]
@@ -424,7 +441,7 @@
                 near_lo[s, r : r + chunk, :] = low
                 for i in range(3):
                     col = coord_w[r : r + chunk, i * LANES : (i + 1) * LANES]
-                    weighed = beside(col, col) * grad
+                    weighed = across(col) * grad
                     for k in range(0, chunk, 8):
                         totals[i] = totals[i] + weighed[k : k + 8, :]
             leads.append(
@@ -437,7 +454,7 @@
 
         bars, pulls = [], []
         for s in subs:
-            predicted = jnp.tanh(summed[s] + head_bias)
+            predicted = jnp.tanh(2.0 * summed[s] + head_bias)
             flank = 1.0 - predicted * predicted
             slope = [flank * q for q in leads[s]]
             excess = slope[0] * slope[0] + slope[1] * slope[1] + slope[2] * slope[2] - 1.0
@@ -454,13 +471,15 @@
             sum_loss[1:2, :] += bars[s]
             pulls.append([share * flank * p for p in pull])
 
+        half_bars = [0.5 * bar for bar in bars]
+
         for s in subs:
             last = stacked(blank5, *pulls[s])
             for r in range(0, 256, chunk):
                 grad = 0.0
                 for i in range(3):
                     col = coord_w[r : r + chunk, i * LANES : (i + 1) * LANES]
-                    grad = grad + beside(col, col) * pulls[s][i]
+                    grad = grad + across(col) * pulls[s][i]
                 through = grad * slope_one[s, r : r + chunk, :]
                 if r + chunk == 256:
                     inside = rows_of_lanes(0, (8, BLOCK)) < MIDDLE - 248
@@ -482,10 +501,10 @@
             for r in range(0, HID, chunk):
                 tangent = tangents[s][r : r + chunk, :]
                 slope = slope_two[s, r : r + chunk, :]
-                head = beside(head_w[r : r + chunk, :], head_w[r : r + chunk, :])
-                bar = head * (bars[s] * slope + tangent * curve_two[s, r : r + chunk, :])
+                head = across(head_w[r : r + chunk, LANES:])
+                bar = head * (half_bars[s] * slope + tangent * curve_two[s, r : r + chunk, :])
                 by_head = act_two[s, r : r + chunk, :] * bars[s] + slope * tangent
-                sum_head[r : r + chunk, :] += by_head[:, :LANES] + by_head[:, LANES:]
+                sum_head[r : r + chunk, :] += folded(by_head)
                 high, low = halves(bar)
                 bar_hi[s, r : r + chunk, :] = high
                 bar_lo[s, r : r + chunk, :] = low
@@ -629,7 +648,7 @@
             pltpu.VMEM(index.shape, jnp.int32),
             pltpu.SemaphoreType.DMA((4,)),
         ],
-        compiler_params=PARAMS,
+        compiler_params=pltpu.CompilerParams(vmem_limit_bytes=60 * 1024 * 1024),
     )(weights, coords, distances, index)
 
 
@@ -645,7 +664,7 @@
         ((256, 1536), BF16),
         ((768, 256), F32),
         ((256, 3 * LANES), F32),
-        ((HID, LANES), F32),
+        ((HID, 2 * LANES), F32),
         ((LANES, LANES), F32),
         ((HID, 256), F32),
         ((768, 256), F32),

time: 98.7 us -> 97.8 us (level)
  local copies, waits for them, and re-layouts: 2.84 us -> 0.05 us
  Pallas kernels: 24.9 us -> 26.8 us
    unnamed x20 -> x12, local copies, waits for them, and re-layouts: 2.82 us -> 0.03 us
    pallas_call x1, Pallas kernels: 0.94 us -> 2.52 us  [pack_boxes(): pl.pallas_call(pack_kernel, out_shape=jax.ShapeDtypeStruct((PEERS * BOX_R...]
where the time goes in v5:
time: 97.8 us; the launch traced here: 97.5 us
  blocking collectives  64 us (65%)
  Pallas kernels  26.8 us (27%)
  waiting for transfers between devices  5.57 us (6%)
    all_to_all x3, blocking collectives, exchange(): return lax.all_to_all(v, ('z', 'wide'), split_axis=0, concat_axis=0)  64 us
    pallas_call x1, Pallas kernels, main_call(): pl.pallas_call(main_kernel, out_shape=(jax.ShapeDtypeStruct((PEERS * BOX_...  22.9 us
    ppermute x3, waiting for transfers between devices, swap_cores(): return lax.ppermute(v, 'core', [(0, 1), (1, 0)])  5.57 us
    pallas_call x1, Pallas kernels, pack_boxes(): pl.pallas_call(pack_kernel, out_shape=jax.ShapeDtypeStruct((PEERS * BOX_R...  2.52 us
  transfers between devices with their start and end apart: 3, of which 3 were waited for; matrix products, arithmetic and copies ran while one was open for 0% of the time, Pallas kernels for 0%

profile of v5, /device:TPU:0, one launch (start us, length us, event | category | flops | bytes accessed | tf_op | source)
XLA Modules:
  0.0 97.5 jit_solution(4256886943300061729)
XLA Ops:
  0.6 2.5 %shard_map.168 = f32[1536,128]{1,0:T(8,128)} custom-call(f32[21,128]{1,0:T(8,128)} %bitcast.22, f32[3,1024]{1,0:T(4,128)} %coords_hbm.1, f32[1,1024]{1,0:T(1,128)} %bitcast.28, s32[1,1024]{1,0:T(1,128)} %bitcast.29), custom_call_target="tpu_custom_call" | custom-call | tf_op jit(solution)/shard_map/pallas_call | solution.py:639
  3.2 0.0 copy-start
  3.2 27.6 %all_to_all.15 = f32[64,24,128]{2,1,0:T(8,128)S(1)} all-to-all(f32[64,24,128]{2,1,0:T(8,128)} %bitcast.26), channel_id=1, replica_groups=mesh['z'=4,'core'=2,'wide'=16] {'z','wide'}, dimensions={0} | all-to-all | bytes 1572864 | tf_op jit(solution)/shard_map/all_to_all | solution.py:813
  30.8 0.0 collective-permute-start
  30.8 2.3 %collective-permute-done = f32[64,24,128]{2,1,0:T(8,128)S(1)} collective-permute-done((f32[64,24,128]{2,1,0:T(8,128)S(1)}, f32[64,24,128]{2,1,0:T(8,128)S(1)}, u32[]{:S(2)}, u32[]{:S(2)}) %collective-permute-start) | collective-permute-done | bytes 786464 | tf_op jit(solution)/shard_map/ppermute | solution.py:809
  33.1 0.0 copy-done
  33.1 22.9 %shard_map.169 = (f32[1536,128]{1,0:T(8,128)S(1)}, f32[1536,128]{1,0:T(8,128)S(1)}, f32[256,256]{1,0:T(8,128)S(1)}) custom-call(s32[1]{0:T(128)} %bitcast.core_ref, f32[1536,128]{1,0:T(8,128)S(1)} %bitcast.18, f32[1536,128]{1,0:T(8,128)S(1)} %bitcast.21, f32[256,256]{1,0:T(8,128)S(1)} %copy-done), custom_call_target="tpu_custom_call" | custom-call | tf_op jit(solution)/shard_map/pallas_call | solution.py:696
  56.0 0.2 collective-permute-start.1
  56.3 2.1 %collective-permute-done.1 = f32[1536,128]{1,0:T(8,128)S(1)} collective-permute-done((f32[1536,128]{1,0:T(8,128)S(1)}, f32[1536,128]{1,0:T(8,128)S(1)}, u32[]{:S(2)}, u32[]{:S(2)}) %collective-permute-start.1) | collective-permute-done | bytes 786464 | tf_op jit(solution)/shard_map/ppermute | solution.py:809
  58.4 0.1 add.6
  58.5 20.9 %all_to_all.16 = f32[64,24,128]{2,1,0:T(8,128)S(1)} all-to-all(f32[64,24,128]{2,1,0:T(8,128)S(1)} %bitcast.27), channel_id=1, replica_groups=mesh['z'=4,'core'=2,'wide'=16] {'z','wide'}, dimensions={0} | all-to-all | bytes 1572864 | tf_op jit(solution)/shard_map/all_to_all | solution.py:813
  79.3 0.2 shard_map.170
  79.5 0.0 collective-permute-start.2
  79.5 1.2 %collective-permute-done.2 = f32[8,128]{1,0:T(8,128)S(1)} collective-permute-done((f32[8,128]{1,0:T(8,128)S(1)}, f32[8,128]{1,0:T(8,128)S(1)}, u32[]{:S(2)}, u32[]{:S(2)}) %collective-permute-start.2) | collective-permute-done | bytes 4128 | tf_op jit(solution)/shard_map/ppermute | solution.py:809
  80.7 0.0 copy-start.3
  80.7 0.0 copy-start.4
  80.7 0.0 copy-start.5
  80.7 0.0 copy-start.1
  80.7 0.0 copy-start.2
  80.7 15.5 %all_to_all.17 = f32[64,8,128]{2,1,0:T(8,128)S(1)} all-to-all(f32[64,8,128]{2,1,0:T(8,128)S(1)} %broadcast_in_dim.3), channel_id=1, replica_groups=mesh['z'=4,'core'=2,'wide'=16] {'z','wide'}, dimensions={0} | all-to-all | bytes 524288 | tf_op jit(solution)/shard_map/all_to_all | solution.py:813
  96.3 0.0 copy-done.3
  96.3 0.0 copy-done.4
  96.3 0.0 copy-done.5
  96.3 0.0 copy-done.1
  96.3 0.0 copy-done.2
  96.3 1.2 %shard_map.171 = (f32[1,1]{1,0:T(1,128)}, f32[1,1]{1,0:T(1,128)}, f32[21,128]{1,0:T(8,128)}, f32[21,128]{1,0:T(8,128)}, f32[21,128]{1,0:T(8,128)}, /*index=5*/bf...) custom-call(f32[512,128]{1,0:T(8,128)S(1)} %bitcast.20, ...), custom_call_target="tpu_custom_call" | custom-call | tf_op jit(solution)/shard_map/pallas_call | solution.py:799
  (2 shorter events, 0.0 us)
Async XLA Ops:
  3.2 29.9 %copy-start = (f32[256,256]{1,0:T(8,128)S(1)}, f32[256,256]{1,0:T(8,128)}, u32[]{:S(2)}) copy-start(f32[256,256]{1,0:T(8,128)} %codes_ref.3) | copy-start | bytes 786436
  30.8 2.3 %collective-permute-start = (f32[64,24,128]{2,1,0:T(8,128)S(1)}, f32[64,24,128]{2,1,0:T(8,128)S(1)}, u32[]{:S(2)}, u32[]{:S(2)}) collective-permute-start(f32[64,24,128]{2,1,0:T(8,128)S(1)} %all_to_all.15), channel_id=1, source_target_pairs={{0,16},{16,0},{1,17},{17,1},{2,18},{18,2},{3,19},{19,3},{4,20},{20... | collective-permute-start | bytes 2359304 | tf_op jit(solution)/shard_map/ppermute | solution.py:809
  56.0 2.4 %collective-permute-start.1 = (f32[1536,128]{1,0:T(8,128)S(1)}, f32[1536,128]{1,0:T(8,128)S(1)}, u32[]{:S(2)}, u32[]{:S(2)}) collective-permute-start(f32[1536,128]{1,0:T(8,128)S(1)} %get-tuple-element.26), channel_id=1, source_target_pairs={{0,16},{16,0},{1,17},{17,1},{2,18},{18,2},{3,19},{19,3},{4,20},{20... | collective-permute-start | bytes 2359304 | tf_op jit(solution)/shard_map/ppermute | solution.py:809
  79.5 1.2 %collective-permute-start.2 = (f32[8,128]{1,0:T(8,128)S(1)}, f32[8,128]{1,0:T(8,128)S(1)}, u32[]{:S(2)}, u32[]{:S(2)}) collective-permute-start(f32[8,128]{1,0:T(8,128)S(1)} %get-tuple-element.27), channel_id=1, source_target_pairs={{0,16},{16,0},{1,17},{17,1},{2,18},{18,2},{3,19},{19,3},{4,20},{20... | collective-permute-start | bytes 12296 | tf_op jit(solution)/shard_map/ppermute | solution.py:809
  80.7 15.6 %copy-start.3 = (f32[2688]{0:T(1024)S(1)}, f32[2688]{0:T(1024)}, u32[]{:S(2)}) copy-start(f32[2688]{0:T(1024)} %param.9) | copy-start | bytes 32260
  80.7 15.6 %copy-start.4 = (f32[2688]{0:T(1024)S(1)}, f32[2688]{0:T(1024)}, u32[]{:S(2)}) copy-start(f32[2688]{0:T(1024)} %param.10) | copy-start | bytes 32260
  80.7 15.6 %copy-start.5 = (f32[2688]{0:T(1024)S(1)}, f32[2688]{0:T(1024)}, u32[]{:S(2)}) copy-start(f32[2688]{0:T(1024)} %param.11) | copy-start | bytes 32260
  80.7 15.6 %copy-start.1 = (f32[256,256]{1,0:T(8,128)S(1)}, f32[256,256]{1,0:T(8,128)}, u32[]{:S(2)}) copy-start(f32[256,256]{1,0:T(8,128)} %code_first_ref.1) | copy-start | bytes 786436
  80.7 15.6 %copy-start.2 = (f32[256,256]{1,0:T(8,128)S(1)}, f32[256,256]{1,0:T(8,128)}, u32[]{:S(2)}) copy-start(f32[256,256]{1,0:T(8,128)} %code_second_ref.1) | copy-start | bytes 786436

commit v6 on v5

--- a/solution.py
+++ b/solution.py
@@ -32,8 +32,8 @@
 POINTS_DEV = 1024
 CODE_ROWS = 256
 FLAT_ROWS = DEVICES * SHARD_ROWS
-BLOCK = 512
-SUBS = 2
+BLOCK = 256
+SUBS = 4
 TILES = BLOCK // LANES
 ALL_POINTS = POINTS_DEV * DEVICES
 
@@ -258,6 +258,7 @@
     act_two,
     slope_two,
     curve_two,
+    act_tang,
     gate_hi,
     gate_lo,
     tang_hi,
@@ -367,179 +368,163 @@
         return beside(*[spots[pl.ds(first + i, 1), :] for i in range(TILES)])
 
     blank5 = jnp.zeros((5, BLOCK), F32)
-    subs = range(SUBS)
     chunk = 8192 // BLOCK
+    low_chunks = range(0, 256, chunk)
+    high_chunks = range(0, HID, chunk)
+
+    def block_stages(step, s):
+        place = [feature(i, step, s) for i in range(3)]
+        target = feature(3, step, s)
+        code_row = feature(4, step, s)
+        valid = (code_row > 0.5).astype(F32)
+        near_pieces = thirds(stacked(*place, blank5))
+
+        wanted = code_row - 1.0
+        for r in range(0, CODE_ROWS, chunk):
+            row = (rows_of_lanes(0, (chunk, BLOCK)) + r).astype(F32)
+            mark = jnp.where(row == wanted, 1.0, 0.0)
+            hot[s, r : r + chunk, :] = mark.astype(BF16)
+            sum_count[r : r + chunk, :] += folded(mark)
+        yield
+
+        high, mid, low = near_pieces
+        near_rhs = stacked(high, mid, low, high, mid, high, jnp.zeros((80, BLOCK), F32))
+        act_one[s] = mm(lhs_one[...], stacked(hot[s], hot[s], near_rhs.astype(BF16)))
+        yield
+        for r in low_chunks:
+            pre = act_one[s, r : r + chunk, :]
+            value, slope, curve = silu_parts(pre)
+            if r + chunk == 256:
+                inside = rows_of_lanes(0, (chunk, BLOCK)) + r < MIDDLE
+                value = jnp.where(inside, value, pre + pre)
+                slope = jnp.where(inside, slope, 0.0)
+                curve = jnp.where(inside, curve, 0.0)
+            high, low = halves(value)
+            hid_hi[s, r : r + chunk, :] = high
+            hid_lo[s, r : r + chunk, :] = low
+            slope_one[s, r : r + chunk, :] = slope
+            curve_one[s, r : r + chunk, :] = curve
+        yield
+
+        act_two[s] = mm(lhs_two[...], stacked(hid_hi[s], hid_lo[s], hid_hi[s], hot[s], hot[s]))
+        yield
+        total = jnp.zeros((8, BLOCK), F32)
+        for r in high_chunks:
+            value, slope, curve = silu_parts_twice(act_two[s, r : r + chunk, :])
+            head = across(head_w[r : r + chunk, :LANES])
+            weighed = head * value
+            for k in range(0, chunk, 8):
+                total = total + weighed[k : k + 8, :]
+            high, low = halves(head * slope)
+            gate_hi[s, r : r + chunk, :] = high
+            gate_lo[s, r : r + chunk, :] = low
+            act_two[s, r : r + chunk, :] = value
+            slope_two[s, r : r + chunk, :] = slope
+            curve_two[s, r : r + chunk, :] = curve
+        summed = jnp.sum(total, axis=0, keepdims=True)
+        yield
+
+        back_one[s] = mm(lhs_back[...], stacked(gate_hi[s], gate_lo[s], gate_hi[s]))
+        yield
+        totals = [jnp.zeros((8, BLOCK), F32) for _ in range(3)]
+        for r in low_chunks:
+            grad = back_one[s, r : r + chunk, :] * slope_one[s, r : r + chunk, :]
+            high, low = halves(grad)
+            near_hi[s, r : r + chunk, :] = high
+            near_lo[s, r : r + chunk, :] = low
+            for i in range(3):
+                weighed = across(coord_w[r : r + chunk, i * LANES : (i + 1) * LANES]) * grad
+                for k in range(0, chunk, 8):
+                    totals[i] = totals[i] + weighed[k : k + 8, :]
+        lead = [
+            jnp.sum(totals[i], axis=0, keepdims=True)
+            + back_one[s, MIDDLE + i : MIDDLE + i + 1, :]
+            for i in range(3)
+        ]
+
+        predicted = jnp.tanh(2.0 * summed + head_bias)
+        flank = 1.0 - predicted * predicted
+        slope = [flank * q for q in lead]
+        excess = slope[0] * slope[0] + slope[1] * slope[1] + slope[2] * slope[2] - 1.0
+        capped = jnp.tanh(predicted / DELTA)
+        misfit = DELTA * capped - DELTA * jnp.tanh(target / DELTA)
+        fitting = jnp.sqrt(misfit * misfit + SMOOTH * SMOOTH)
+        sum_loss[0:1, :] += valid * (fitting + EIK_WEIGHT * excess * excess)
+        share = valid * (1.0 / ALL_POINTS)
+        pull = [(4.0 * EIK_WEIGHT) * excess * v for v in slope]
+        by_flank = sum(p * q for p, q in zip(pull, lead))
+        by_predicted = misfit / fitting * (1.0 - capped * capped) - 2.0 * predicted * by_flank
+        bar_out = share * by_predicted * flank
+        sum_loss[1:2, :] += bar_out
+        half_bar = 0.5 * bar_out
+        pull = [share * flank * p for p in pull]
+
+        last = stacked(blank5, *pull)
+        for r in low_chunks:
+            grad = 0.0
+            for i in range(3):
+                grad = grad + across(coord_w[r : r + chunk, i * LANES : (i + 1) * LANES]) * pull[i]
+            through = grad * slope_one[s, r : r + chunk, :]
+            if r + chunk == 256:
+                inside = rows_of_lanes(0, (8, BLOCK)) < MIDDLE - 248
+                end = jnp.where(inside, through[chunk - 8 :], last)
+                through = stacked(through[: chunk - 8], end)
+            high, low = halves(through)
+            tang_hi[s, r : r + chunk, :] = high
+            tang_lo[s, r : r + chunk, :] = low
+            curve_one[s, r : r + chunk, :] = (
+                grad * back_one[s, r : r + chunk, :] * curve_one[s, r : r + chunk, :]
+            )
+        yield
+        act_tang[s] = mm(lhs_two[:, 0:768], stacked(tang_hi[s], tang_lo[s], tang_hi[s]))
+        yield
+        for r in high_chunks:
+            tangent = act_tang[s, r : r + chunk, :]
+            slope = slope_two[s, r : r + chunk, :]
+            head = across(head_w[r : r + chunk, LANES:])
+            bar = head * (half_bar * slope + tangent * curve_two[s, r : r + chunk, :])
+            by_head = act_two[s, r : r + chunk, :] * bar_out + slope * tangent
+            sum_head[r : r + chunk, :] += folded(by_head)
+            high, low = halves(bar)
+            bar_hi[s, r : r + chunk, :] = high
+            bar_lo[s, r : r + chunk, :] = low
+        yield
+
+        back_one[s] = mm(lhs_back[...], stacked(bar_hi[s], bar_lo[s], bar_hi[s]))
+        yield
+        for r in low_chunks:
+            bar = (
+                back_one[s, r : r + chunk, :] * slope_one[s, r : r + chunk, :]
+                + curve_one[s, r : r + chunk, :]
+            )
+            high, low = halves(bar)
+            low_hi[s, r : r + chunk, :] = high
+            low_lo[s, r : r + chunk, :] = low
+        yield
+
+        sum_two[...] += mm_nt(
+            beside(bar_hi[s], bar_hi[s], bar_lo[s], gate_hi[s], gate_hi[s], gate_lo[s]),
+            beside(hid_hi[s], hid_lo[s], hid_hi[s], tang_hi[s], tang_lo[s], tang_hi[s]),
+        )
+        hots = beside(hot[s], hot[s])
+        sum_codes[256:768, :] += mm_nt(beside(bar_hi[s], bar_lo[s]), hots)
+        sum_codes[0:256, :] += mm_nt(beside(low_hi[s], low_lo[s]), hots)
+        seen = stacked(near_pieces[0], near_pieces[1]).astype(BF16)
+        pulled = stacked(*pull, blank5)
+        high = pulled.astype(BF16).astype(F32)
+        pulled = stacked(high, pulled - high).astype(BF16)
+        sum_coord[...] += mm_nt(
+            beside(seen, seen, pulled, pulled),
+            beside(low_hi[s], low_lo[s], near_hi[s], near_lo[s]),
+        )
 
     def step_body(step, carry):
-        place = [[feature(i, step, s) for i in range(3)] for s in subs]
-        target = [feature(3, step, s) for s in subs]
-        code_row = [feature(4, step, s) for s in subs]
-        valid = [(code_row[s] > 0.5).astype(F32) for s in subs]
-        near8 = [stacked(*place[s], blank5) for s in subs]
-        near_pieces = [thirds(near8[s]) for s in subs]
-
-        for s in subs:
-            wanted = code_row[s] - 1.0
-            for r in range(0, CODE_ROWS, chunk):
-                mark = jnp.where(
-                    (rows_of_lanes(0, (chunk, BLOCK)) + r).astype(F32) == wanted, 1.0, 0.0
-                )
-                hot[s, r : r + chunk, :] = mark.astype(BF16)
-                sum_count[r : r + chunk, :] += folded(mark)
-
-        for s in subs:
-            high, mid, low = near_pieces[s]
-            near_rhs = stacked(
-                high, mid, low, high, mid, high, jnp.zeros((80, BLOCK), F32)
-            ).astype(BF16)
-            act_one[s] = mm(lhs_one[...], stacked(hot[s], hot[s], near_rhs))
-        for s in subs:
-            for r in range(0, 256, chunk):
-                pre = act_one[s, r : r + chunk, :]
-                value, slope, curve = silu_parts(pre)
-                if r + chunk == 256:
-                    inside = rows_of_lanes(0, (chunk, BLOCK)) + r < MIDDLE
-                    value = jnp.where(inside, value, pre + pre)
-                    slope = jnp.where(inside, slope, 0.0)
-                    curve = jnp.where(inside, curve, 0.0)
-                high, low = halves(value)
-                hid_hi[s, r : r + chunk, :] = high
-                hid_lo[s, r : r + chunk, :] = low
-                slope_one[s, r : r + chunk, :] = slope
-                curve_one[s, r : r + chunk, :] = curve
-
-        for s in subs:
-            act_two[s] = mm(
-                lhs_two[...], stacked(hid_hi[s], hid_lo[s], hid_hi[s], hot[s], hot[s])
-            )
-        summed = []
-        for s in subs:
-            total = jnp.zeros((8, BLOCK), F32)
-            for r in range(0, HID, chunk):
-                value, slope, curve = silu_parts_twice(act_two[s, r : r + chunk, :])
-                head = across(head_w[r : r + chunk, :LANES])
-                weighed = head * value
-                for k in range(0, chunk, 8):
-                    total = total + weighed[k : k + 8, :]
-                high, low = halves(head * slope)
-                gate_hi[s, r : r + chunk, :] = high
-                gate_lo[s, r : r + chunk, :] = low
-                act_two[s, r : r + chunk, :] = value
-                slope_two[s, r : r + chunk, :] = slope
-                curve_two[s, r : r + chunk, :] = curve
-            summed.append(jnp.sum(total, axis=0, keepdims=True))
-
-        for s in subs:
-            back_one[s] = mm(lhs_back[...], stacked(gate_hi[s], gate_lo[s], gate_hi[s]))
-        leads = []
-        for s in subs:
-            totals = [jnp.zeros((8, BLOCK), F32) for _ in range(3)]
-            for r in range(0, 256, chunk):
-                grad = back_one[s, r : r + chunk, :] * slope_one[s, r : r + chunk, :]
-                high, low = halves(grad)
-                near_hi[s, r : r + chunk, :] = high
-                near_lo[s, r : r + chunk, :] = low
-                for i in range(3):
-                    col = coord_w[r : r + chunk, i * LANES : (i + 1) * LANES]
-                    weighed = across(col) * grad
-                    for k in range(0, chunk, 8):
-                        totals[i] = totals[i] + weighed[k : k + 8, :]
-            leads.append(
-                [
-                    jnp.sum(totals[i], axis=0, keepdims=True)
-                    + back_one[s, MIDDLE + i : MIDDLE + i + 1, :]
-                    for i in range(3)
-                ]
-            )
-
-        bars, pulls = [], []
-        for s in subs:
-            predicted = jnp.tanh(2.0 * summed[s] + head_bias)
-            flank = 1.0 - predicted * predicted
-            slope = [flank * q for q in leads[s]]
-            excess = slope[0] * slope[0] + slope[1] * slope[1] + slope[2] * slope[2] - 1.0
-            capped = jnp.tanh(predicted / DELTA)
-            misfit = DELTA * capped - DELTA * jnp.tanh(target[s] / DELTA)
-            fitting = jnp.sqrt(misfit * misfit + SMOOTH * SMOOTH)
-            loss = fitting + EIK_WEIGHT * excess * excess
-            sum_loss[0:1, :] += valid[s] * loss
-            share = valid[s] * (1.0 / ALL_POINTS)
-            pull = [(4.0 * EIK_WEIGHT) * excess * v for v in slope]
-            by_flank = sum(p * q for p, q in zip(pull, leads[s]))
-            by_predicted = misfit / fitting * (1.0 - capped * capped) - 2.0 * predicted * by_flank
-            bars.append(share * by_predicted * flank)
-            sum_loss[1:2, :] += bars[s]
-            pulls.append([share * flank * p for p in pull])
-
-        half_bars = [0.5 * bar for bar in bars]
-
-        for s in subs:
-            last = stacked(blank5, *pulls[s])
-            for r in range(0, 256, chunk):
-                grad = 0.0
-                for i in range(3):
-                    col = coord_w[r : r + chunk, i * LANES : (i + 1) * LANES]
-                    grad = grad + across(col) * pulls[s][i]
-                through = grad * slope_one[s, r : r + chunk, :]
-                if r + chunk == 256:
-                    inside = rows_of_lanes(0, (8, BLOCK)) < MIDDLE - 248
-                    through = stacked(
-                        through[: chunk - 8], jnp.where(inside, through[chunk - 8 :], last)
-                    )
-                high, low = halves(through)
-                tang_hi[s, r : r + chunk, :] = high
-                tang_lo[s, r : r + chunk, :] = low
-                curve_one[s, r : r + chunk, :] = (
-                    grad * back_one[s, r : r + chunk, :] * curve_one[s, r : r + chunk, :]
-                )
-        tangents = []
-        for s in subs:
-            tangents.append(
-                mm(lhs_two[:, 0:768], stacked(tang_hi[s], tang_lo[s], tang_hi[s]))
-            )
-        for s in subs:
-            for r in range(0, HID, chunk):
-                tangent = tangents[s][r : r + chunk, :]
-                slope = slope_two[s, r : r + chunk, :]
-                head = across(head_w[r : r + chunk, LANES:])
-                bar = head * (half_bars[s] * slope + tangent * curve_two[s, r : r + chunk, :])
-                by_head = act_two[s, r : r + chunk, :] * bars[s] + slope * tangent
-                sum_head[r : r + chunk, :] += folded(by_head)
-                high, low = halves(bar)
-                bar_hi[s, r : r + chunk, :] = high
-                bar_lo[s, r : r + chunk, :] = low
-
-        for s in subs:
-            back_one[s] = mm(lhs_back[...], stacked(bar_hi[s], bar_lo[s], bar_hi[s]))
-        left, right = [], []
-        for s in subs:
-            left += [bar_hi[s], bar_hi[s], bar_lo[s], gate_hi[s], gate_hi[s], gate_lo[s]]
-            right += [hid_hi[s], hid_lo[s], hid_hi[s], tang_hi[s], tang_lo[s], tang_hi[s]]
-        sum_two[...] += mm_nt(beside(*left), beside(*right))
-        hots = beside(*[hot[s // 2] for s in range(2 * SUBS)])
-        bars = beside(*[(bar_hi, bar_lo)[s % 2][s // 2] for s in range(2 * SUBS)])
-        sum_codes[256:768, :] += mm_nt(bars, hots)
-
-        for s in subs:
-            for r in range(0, 256, chunk):
-                bar = (
-                    back_one[s, r : r + chunk, :] * slope_one[s, r : r + chunk, :]
-                    + curve_one[s, r : r + chunk, :]
-                )
-                high, low = halves(bar)
-                low_hi[s, r : r + chunk, :] = high
-                low_lo[s, r : r + chunk, :] = low
-        bars = beside(*[(low_hi, low_lo)[s % 2][s // 2] for s in range(2 * SUBS)])
-        sum_codes[0:256, :] += mm_nt(bars, hots)
-        left, right = [], []
-        for s in subs:
-            seen = stacked(near_pieces[s][0], near_pieces[s][1]).astype(BF16)
-            pulled = stacked(*pulls[s], blank5)
-            high = pulled.astype(BF16).astype(F32)
-            pulled = stacked(high, pulled - high).astype(BF16)
-            left += [seen, seen, pulled, pulled]
-            right += [low_hi[s], low_lo[s], near_hi[s], near_lo[s]]
-        sum_coord[...] += mm_nt(beside(*left), beside(*right))
+        waiting = [block_stages(step, s) for s in range(SUBS)]
+        active = []
+        while waiting or active:
+            if waiting:
+                active.append(waiting.pop(0))
+            active = [work for work in active if next(work, work) is not work]
         return carry
 
     lax.fori_loop(0, SLOTS * DEVICES // (SUBS * BLOCK), step_body, 0)
@@ -679,6 +664,7 @@
         (pair, BF16),
         (pair, BF16),
         (pair, BF16),
+        (pair_two, F32),
         (pair_two, F32),
         (pair_two, F32),
         (pair_two, F32),

time: 97.8 us -> 97.4 us (level)
  no operation moved by 1% of the time
where the time goes in v6:
time: 97.4 us; the launch traced here: 97 us
  blocking collectives  64 us (66%)
  Pallas kernels  26.3 us (27%)
  waiting for transfers between devices  5.56 us (6%)
    all_to_all x3, blocking collectives, exchange(): return lax.all_to_all(v, ('z', 'wide'), split_axis=0, concat_axis=0)  64 us
    pallas_call x1, Pallas kernels, main_call(): pl.pallas_call(main_kernel, out_shape=(jax.ShapeDtypeStruct((PEERS * BOX_...  22.5 us
    ppermute x3, waiting for transfers between devices, swap_cores(): return lax.ppermute(v, 'core', [(0, 1), (1, 0)])  5.56 us
    pallas_call x1, Pallas kernels, pack_boxes(): pl.pallas_call(pack_kernel, out_shape=jax.ShapeDtypeStruct((PEERS * BOX_R...  2.52 us
  transfers between devices with their start and end apart: 3, of which 3 were waited for; matrix products, arithmetic and copies ran while one was open for 0% of the time, Pallas kernels for 0%

profile of v6, /device:TPU:0, one launch (start us, length us, event | category | flops | bytes accessed | tf_op | source)
XLA Modules:
  0.0 97.0 jit_solution(16644860718257829631)
XLA Ops:
  0.6 2.5 %shard_map.168 = f32[1536,128]{1,0:T(8,128)} custom-call(f32[21,128]{1,0:T(8,128)} %bitcast.22, f32[3,1024]{1,0:T(4,128)} %coords_hbm.1, f32[1,1024]{1,0:T(1,128)} %bitcast.28, s32[1,1024]{1,0:T(1,128)} %bitcast.29), custom_call_target="tpu_custom_call" | custom-call | tf_op jit(solution)/shard_map/pallas_call | solution.py:624
  3.2 0.0 copy-start
  3.2 27.6 %all_to_all.15 = f32[64,24,128]{2,1,0:T(8,128)S(1)} all-to-all(f32[64,24,128]{2,1,0:T(8,128)} %bitcast.26), channel_id=1, replica_groups=mesh['z'=4,'core'=2,'wide'=16] {'z','wide'}, dimensions={0} | all-to-all | bytes 1572864 | tf_op jit(solution)/shard_map/all_to_all | solution.py:799
  30.8 0.0 collective-permute-start
  30.8 2.3 %collective-permute-done = f32[64,24,128]{2,1,0:T(8,128)S(1)} collective-permute-done((f32[64,24,128]{2,1,0:T(8,128)S(1)}, f32[64,24,128]{2,1,0:T(8,128)S(1)}, u32[]{:S(2)}, u32[]{:S(2)}) %collective-permute-start) | collective-permute-done | bytes 786464 | tf_op jit(solution)/shard_map/ppermute | solution.py:795
  33.1 0.0 copy-done
  33.1 22.5 %shard_map.169 = (f32[1536,128]{1,0:T(8,128)S(1)}, f32[1536,128]{1,0:T(8,128)S(1)}, f32[256,256]{1,0:T(8,128)S(1)}) custom-call(s32[1]{0:T(128)} %bitcast.core_ref, f32[1536,128]{1,0:T(8,128)S(1)} %bitcast.18, f32[1536,128]{1,0:T(8,128)S(1)} %bitcast.21, f32[256,256]{1,0:T(8,128)S(1)} %copy-done), custom_call_target="tpu_custom_call" | custom-call | tf_op jit(solution)/shard_map/pallas_call | solution.py:682
  55.6 0.2 collective-permute-start.1
  55.8 2.1 %collective-permute-done.1 = f32[1536,128]{1,0:T(8,128)S(1)} collective-permute-done((f32[1536,128]{1,0:T(8,128)S(1)}, f32[1536,128]{1,0:T(8,128)S(1)}, u32[]{:S(2)}, u32[]{:S(2)}) %collective-permute-start.1) | collective-permute-done | bytes 786464 | tf_op jit(solution)/shard_map/ppermute | solution.py:795
  57.9 0.1 add.6
  58.0 20.9 %all_to_all.16 = f32[64,24,128]{2,1,0:T(8,128)S(1)} all-to-all(f32[64,24,128]{2,1,0:T(8,128)S(1)} %bitcast.27), channel_id=1, replica_groups=mesh['z'=4,'core'=2,'wide'=16] {'z','wide'}, dimensions={0} | all-to-all | bytes 1572864 | tf_op jit(solution)/shard_map/all_to_all | solution.py:799
  78.9 0.2 shard_map.170
  79.0 0.0 collective-permute-start.2
  79.0 1.2 %collective-permute-done.2 = f32[8,128]{1,0:T(8,128)S(1)} collective-permute-done((f32[8,128]{1,0:T(8,128)S(1)}, f32[8,128]{1,0:T(8,128)S(1)}, u32[]{:S(2)}, u32[]{:S(2)}) %collective-permute-start.2) | collective-permute-done | bytes 4128 | tf_op jit(solution)/shard_map/ppermute | solution.py:795
  80.2 0.0 copy-start.3
  80.2 0.0 copy-start.4
  80.2 0.0 copy-start.5
  80.2 0.0 copy-start.1
  80.3 0.0 copy-start.2
  80.3 15.5 %all_to_all.17 = f32[64,8,128]{2,1,0:T(8,128)S(1)} all-to-all(f32[64,8,128]{2,1,0:T(8,128)S(1)} %broadcast_in_dim.3), channel_id=1, replica_groups=mesh['z'=4,'core'=2,'wide'=16] {'z','wide'}, dimensions={0} | all-to-all | bytes 524288 | tf_op jit(solution)/shard_map/all_to_all | solution.py:799
  95.8 0.0 copy-done.3
  95.8 0.0 copy-done.4
  95.8 0.0 copy-done.5
  95.8 0.0 copy-done.1
  95.8 0.0 copy-done.2
  95.8 1.2 %shard_map.171 = (f32[1,1]{1,0:T(1,128)}, f32[1,1]{1,0:T(1,128)}, f32[21,128]{1,0:T(8,128)}, f32[21,128]{1,0:T(8,128)}, f32[21,128]{1,0:T(8,128)}, /*index=5*/bf...) custom-call(f32[512,128]{1,0:T(8,128)S(1)} %bitcast.20, ...), custom_call_target="tpu_custom_call" | custom-call | tf_op jit(solution)/shard_map/pallas_call | solution.py:785
  (2 shorter events, 0.0 us)
Async XLA Ops:
  3.2 29.9 %copy-start = (f32[256,256]{1,0:T(8,128)S(1)}, f32[256,256]{1,0:T(8,128)}, u32[]{:S(2)}) copy-start(f32[256,256]{1,0:T(8,128)} %codes_ref.3) | copy-start | bytes 786436
  30.8 2.3 %collective-permute-start = (f32[64,24,128]{2,1,0:T(8,128)S(1)}, f32[64,24,128]{2,1,0:T(8,128)S(1)}, u32[]{:S(2)}, u32[]{:S(2)}) collective-permute-start(f32[64,24,128]{2,1,0:T(8,128)S(1)} %all_to_all.15), channel_id=1, source_target_pairs={{0,16},{16,0},{1,17},{17,1},{2,18},{18,2},{3,19},{19,3},{4,20},{20... | collective-permute-start | bytes 2359304 | tf_op jit(solution)/shard_map/ppermute | solution.py:795
  55.6 2.4 %collective-permute-start.1 = (f32[1536,128]{1,0:T(8,128)S(1)}, f32[1536,128]{1,0:T(8,128)S(1)}, u32[]{:S(2)}, u32[]{:S(2)}) collective-permute-start(f32[1536,128]{1,0:T(8,128)S(1)} %get-tuple-element.26), channel_id=1, source_target_pairs={{0,16},{16,0},{1,17},{17,1},{2,18},{18,2},{3,19},{19,3},{4,20},{20... | collective-permute-start | bytes 2359304 | tf_op jit(solution)/shard_map/ppermute | solution.py:795
  79.0 1.2 %collective-permute-start.2 = (f32[8,128]{1,0:T(8,128)S(1)}, f32[8,128]{1,0:T(8,128)S(1)}, u32[]{:S(2)}, u32[]{:S(2)}) collective-permute-start(f32[8,128]{1,0:T(8,128)S(1)} %get-tuple-element.27), channel_id=1, source_target_pairs={{0,16},{16,0},{1,17},{17,1},{2,18},{18,2},{3,19},{19,3},{4,20},{20... | collective-permute-start | bytes 12296 | tf_op jit(solution)/shard_map/ppermute | solution.py:795
  80.2 15.6 %copy-start.3 = (f32[2688]{0:T(1024)S(1)}, f32[2688]{0:T(1024)}, u32[]{:S(2)}) copy-start(f32[2688]{0:T(1024)} %param.9) | copy-start | bytes 32260
  80.2 15.6 %copy-start.4 = (f32[2688]{0:T(1024)S(1)}, f32[2688]{0:T(1024)}, u32[]{:S(2)}) copy-start(f32[2688]{0:T(1024)} %param.10) | copy-start | bytes 32260
  80.2 15.6 %copy-start.5 = (f32[2688]{0:T(1024)S(1)}, f32[2688]{0:T(1024)}, u32[]{:S(2)}) copy-start(f32[2688]{0:T(1024)} %param.11) | copy-start | bytes 32260
  80.2 15.6 %copy-start.1 = (f32[256,256]{1,0:T(8,128)S(1)}, f32[256,256]{1,0:T(8,128)}, u32[]{:S(2)}) copy-start(f32[256,256]{1,0:T(8,128)} %code_first_ref.1) | copy-start | bytes 786436
  80.3 15.6 %copy-start.2 = (f32[256,256]{1,0:T(8,128)S(1)}, f32[256,256]{1,0:T(8,128)}, u32[]{:S(2)}) copy-start(f32[256,256]{1,0:T(8,128)} %code_second_ref.1) | copy-start | bytes 786436

commit v7 on v6

--- a/solution.py
+++ b/solution.py
@@ -224,30 +224,27 @@
     return half + bent, (1.0 + gate) + half * bend, bend * (1.0 - bent)
 
 
-def main_kernel(
+def loop_kernel(
     core_ref,
     mine_ref,
     other_ref,
     codes_ref,
-    keep_ref,
-    give_ref,
-    code_grad_ref,
-    flat,
     first_w,
     second_w,
-    lhs_one,
-    lhs_two,
-    lhs_back,
     latent_w,
-    coord_w,
-    head_w,
-    spots,
     sum_two,
     sum_codes,
     sum_coord,
     sum_head,
     sum_count,
     sum_loss,
+    flat,
+    lhs_one,
+    lhs_two,
+    lhs_back,
+    coord_w,
+    head_w,
+    spots,
     act_one,
     slope_one,
     curve_one,
@@ -301,12 +298,7 @@
     first_bias = first_end[:, 4:5]
     first_w[:, : 2 * LANES] = first_low
     first_w[:, 2 * LANES :] = first_end
-    first_root = lax.rsqrt(
-        jnp.sum(first_low * first_low, axis=1, keepdims=True)
-        + jnp.sum(first_near * first_near, axis=1, keepdims=True)
-        + 1e-12
-    )
-    first_scale = first_gain * first_root
+    _, first_scale = norm_parts(beside(first_low, first_near), first_gain)
     first_low = first_low * first_scale
     first_near = first_near * first_scale
     latent_w[0:256, :] = first_low
@@ -322,10 +314,7 @@
     head = jnp.broadcast_to(second_w[:, 514:515], (HID, LANES))
     head_w[:, :LANES] = 0.5 * head
     head_w[:, LANES:] = head
-    second_root = lax.rsqrt(
-        jnp.sum(second_a * second_a + second_b * second_b, axis=1, keepdims=True) + 1e-12
-    )
-    second_scale = second_gain * second_root
+    _, second_scale = norm_parts(second_w[:, 0:512], second_gain)
     second_a = second_a * second_scale
     second_b = second_b * second_scale
     is_hidden = rows_of_lanes(1, (HID, 256)) < MIDDLE
@@ -529,17 +518,46 @@
 
     lax.fori_loop(0, SLOTS * DEVICES // (SUBS * BLOCK), step_body, 0)
 
+
+def code_kernel(codes_ref, latent_w, sum_codes, sum_count, code_grad_ref, squares_ref):
     codes = codes_ref[...]
     count = jnp.sum(sum_count[...], axis=1, keepdims=True)
-    by_code = sum_codes[...]
-    turned_hi, turned_lo = halves(by_code.T)
+    turned_hi, turned_lo = halves(sum_codes[...].T)
     weight_hi, weight_lo = halves(latent_w[...])
     code_grad = mm(
         beside(turned_hi, turned_hi, turned_lo), stacked(weight_hi, weight_lo, weight_hi)
     )
     code_grad = code_grad + (2.0 * CODE_WEIGHT / ALL_POINTS) * count * codes
     code_grad_ref[...] = code_grad
-    code_squares = total_of(code_grad * code_grad)
+    squares_ref[...] = jnp.broadcast_to(total_of(code_grad * code_grad), squares_ref.shape)
+
+
+def norm_parts(direction, gain):
+    root = lax.rsqrt(jnp.sum(direction * direction, axis=1, keepdims=True) + 1e-12)
+    return root, gain * root
+
+
+def weight_kernel(
+    core_ref,
+    codes_ref,
+    first_w,
+    second_w,
+    sum_two,
+    sum_codes,
+    sum_coord,
+    sum_head,
+    sum_count,
+    sum_loss,
+    keep_ref,
+    give_ref,
+    flat,
+    first_grad,
+    second_grad,
+):
+    core = core_ref[0]
+    codes = codes_ref[...]
+    by_code = sum_codes[...]
+    count = jnp.sum(sum_count[...], axis=1, keepdims=True)
     loss = jnp.sum(sum_loss[0:1, :], axis=1, keepdims=True)
     loss = loss + CODE_WEIGHT * total_of(count * codes * codes)
     loss = loss / ALL_POINTS
@@ -549,42 +567,47 @@
     latent_grad = mm(beside(by_hi, by_hi, by_lo), stacked(code_hi, code_lo, code_hi))
     bias_grad = jnp.sum(by_code, axis=1, keepdims=True)
 
+    lane = rows_of_lanes(1, (256, LANES))
+    real = rows_of_lanes(0, (256, LANES)) < MIDDLE
     near_grad = sum_coord[0:8, :] + sum_coord[8:16, :]
     near_grad = stacked(near_grad, jnp.zeros((LANES - 8, 256), F32)).T
     near_grad = jnp.where(lane < 3, near_grad, 0.0)
     low_grad = latent_grad[0:256, :]
     first_low = first_w[:, : 2 * LANES]
     first_near = jnp.where(lane < 3, first_w[:, 2 * LANES :], 0.0)
+    root, scale = norm_parts(beside(first_low, first_near), first_w[:, 2 * LANES + 3 : 2 * LANES + 4])
     along = jnp.sum(first_low * low_grad, axis=1, keepdims=True)
     along = along + jnp.sum(first_near * near_grad, axis=1, keepdims=True)
-    inward = first_scale * first_root * first_root * along
-    end = first_scale * near_grad - first_near * inward
-    end = jnp.where(lane == 3, first_root * along, end)
+    inward = scale * root * root * along
+    end = scale * near_grad - first_near * inward
+    end = jnp.where(lane == 3, root * along, end)
     end = jnp.where(lane == 4, bias_grad[0:256, :], end)
-    low_grad = first_scale * low_grad - first_low * inward
-    first_w[:, : 2 * LANES] = jnp.where(beside(real, real), low_grad, 0.0)
-    first_w[:, 2 * LANES :] = jnp.where(real, end, 0.0)
-
+    low_grad = scale * low_grad - first_low * inward
+    first_grad[:, : 2 * LANES] = jnp.where(beside(real, real), low_grad, 0.0)
+    first_grad[:, 2 * LANES :] = jnp.where(real, end, 0.0)
+
+    is_hidden = rows_of_lanes(1, (HID, 256)) < MIDDLE
     hidden_grad = sum_two[...]
     moved = pltpu.roll(latent_grad[256:768, :], 256 - 3, 1)
     grad_a = jnp.where(is_hidden, hidden_grad, moved)
     grad_b = jnp.where(is_hidden, moved, hidden_grad)
     second_a = second_w[:, 0:256]
     second_b = second_w[:, 256:512]
+    root, scale = norm_parts(second_w[:, 0:512], second_w[:, 512:513])
     along = jnp.sum(second_a * grad_a + second_b * grad_b, axis=1, keepdims=True)
-    inward = second_scale * second_root * second_root * along
-    second_w[:, 0:256] = second_scale * grad_a - second_a * inward
-    second_w[:, 256:512] = second_scale * grad_b - second_b * inward
+    inward = scale * root * root * along
+    second_grad[:, 0:256] = scale * grad_a - second_a * inward
+    second_grad[:, 256:512] = scale * grad_b - second_b * inward
     head_grad = jnp.sum(sum_head[...], axis=1, keepdims=True)
     lane = rows_of_lanes(1, (HID, LANES))
-    end = jnp.where(lane == 0, second_root * along, 0.0)
+    end = jnp.where(lane == 0, root * along, 0.0)
     end = jnp.where(lane == 1, bias_grad[256:768, :], end)
-    second_w[:, 512:640] = jnp.where(lane == 2, head_grad, end)
+    second_grad[:, 512:640] = jnp.where(lane == 2, head_grad, end)
 
     flat[...] = jnp.zeros(flat.shape, F32)
     for adding in (False, True):
-        pack_units(first_w, flat, *FIRST_UNITS, adding)
-        pack_units(second_w, flat, *SECOND_UNITS, adding)
+        pack_units(first_grad, flat, *FIRST_UNITS, adding)
+        pack_units(second_grad, flat, *SECOND_UNITS, adding)
     row = HEAD_ENTRY // LANES
     lane = rows_of_lanes(1, (1, LANES))
     bias_total = jnp.sum(sum_loss[1:2, :], axis=1, keepdims=True)
@@ -594,7 +617,6 @@
     sub = rows_of_lanes(0, (8, LANES))
     wide = rows_of_lanes(1, (8, LANES))
     info = jnp.where((sub == 5) & (wide == 0), loss, 0.0)
-    info = jnp.where((sub == 5) & (wide == 1), code_squares, info)
     for which in range(2):
 
         @pl.when(core == which)
@@ -618,6 +640,7 @@
 
 
 HBM = pl.BlockSpec(memory_space=pltpu.HBM)
+SMEM = pl.BlockSpec(memory_space=pltpu.SMEM)
 
 
 def pack_boxes(weights, coords, distances, index):
@@ -637,26 +660,21 @@
     )(weights, coords, distances, index)
 
 
-def main_call(core, mine, other, codes):
+def f32(*shape):
+    return jax.ShapeDtypeStruct(shape, F32)
+
+
+def run_loop(core, mine, other, codes):
     pair = (SUBS, 256, BLOCK)
     pair_two = (SUBS, HID, BLOCK)
     scratch = [
         ((FLAT_ROWS + 8, LANES), F32),
-        ((256, 3 * LANES), F32),
-        ((HID, 5 * LANES), F32),
         ((256, 640), BF16),
         ((HID, 1280), BF16),
         ((256, 1536), BF16),
-        ((768, 256), F32),
         ((256, 3 * LANES), F32),
         ((HID, 2 * LANES), F32),
         ((LANES, LANES), F32),
-        ((HID, 256), F32),
-        ((768, 256), F32),
-        ((16, 256), F32),
-        ((HID, LANES), F32),
-        ((CODE_ROWS, LANES), F32),
-        ((2, BLOCK), F32),
         (pair, F32),
         (pair, F32),
         (pair, F32),
@@ -680,17 +698,51 @@
         (pair, BF16),
     ]
     return pl.pallas_call(
-        main_kernel,
+        loop_kernel,
         out_shape=(
-            jax.ShapeDtypeStruct((PEERS * BOX_ROWS, LANES), F32),
-            jax.ShapeDtypeStruct((PEERS * BOX_ROWS, LANES), F32),
-            jax.ShapeDtypeStruct((CODE_ROWS, LATENT), F32),
+            f32(256, 3 * LANES),
+            f32(HID, 5 * LANES),
+            f32(768, 256),
+            f32(HID, 256),
+            f32(768, 256),
+            f32(16, 256),
+            f32(HID, LANES),
+            f32(CODE_ROWS, LANES),
+            f32(2, BLOCK),
         ),
-        in_specs=[pl.BlockSpec(memory_space=pltpu.SMEM)] + vmem(3),
-        out_specs=tuple(vmem(3)),
+        in_specs=[SMEM] + vmem(3),
+        out_specs=tuple(vmem(9)),
         scratch_shapes=[pltpu.VMEM(shape, dtype) for shape, dtype in scratch],
         compiler_params=PARAMS,
     )(core, mine, other, codes)
+
+
+def weight_boxes(core, codes, first_w, second_w, *sums):
+    return pl.pallas_call(
+        weight_kernel,
+        out_shape=(f32(PEERS * BOX_ROWS, LANES),) * 2,
+        in_specs=[SMEM] + vmem(9),
+        out_specs=tuple(vmem(2)),
+        scratch_shapes=[
+            pltpu.VMEM((FLAT_ROWS + 8, LANES), F32),
+            pltpu.VMEM((256, 3 * LANES), F32),
+            pltpu.VMEM((HID, 5 * LANES), F32),
+        ],
+        compiler_params=PARAMS,
+    )(core, codes, first_w, second_w, *sums)
+
+
+def code_grads(*args):
+    return pl.pallas_call(
+        code_kernel,
+        out_shape=(f32(CODE_ROWS, LATENT), f32(8, LANES)),
+        in_specs=vmem(4),
+        out_specs=tuple(vmem(2)),
+        compiler_params=PARAMS,
+        cost_estimate=pl.CostEstimate(
+            flops=2 * 3 * 768 * 256 * 256, bytes_accessed=3 << 20, transcendentals=0
+        ),
+    )(*args)
 
 
 def adam_update(value, first, second, grad, rate):
@@ -702,26 +754,26 @@
     return (value_new, first_new, second_new)
 
 
-def shard_kernel(parts_ref, shard_ref, squares_ref):
+def shard_kernel(parts_ref, code_squares_ref, shard_ref, squares_ref):
     total = parts_ref[0:BOX_ROWS, :]
     for peer in range(1, PEERS):
         total = total + parts_ref[peer * BOX_ROWS : (peer + 1) * BOX_ROWS, :]
     shard_ref[...] = total
     grad = total[:SHARD_ROWS, :]
-    squares_ref[...] = jnp.broadcast_to(total_of(grad * grad), squares_ref.shape)
-
-
-def sum_shards(parts):
+    squares_ref[...] = code_squares_ref[...] + total_of(grad * grad)
+
+
+def sum_shards(parts, code_squares):
     return pl.pallas_call(
         shard_kernel,
         out_shape=(
             jax.ShapeDtypeStruct((BOX_ROWS, LANES), F32),
             jax.ShapeDtypeStruct((8, LANES), F32),
         ),
-        in_specs=vmem(1),
+        in_specs=vmem(2),
         out_specs=tuple(vmem(2)),
         compiler_params=PARAMS,
-    )(parts)
+    )(parts, code_squares)
 
 
 def update_kernel(
@@ -749,7 +801,7 @@
     for peer in range(1, PEERS):
         total = total + seen_ref[peer * 8 : peer * 8 + 8, :]
     loss_out[...] = shard_ref[SHARD_ROWS : SHARD_ROWS + 1, 0:1]
-    norm = jnp.sqrt(total[0:1, 0:1] + shard_ref[SHARD_ROWS : SHARD_ROWS + 1, 1:2])
+    norm = jnp.sqrt(total[0:1, 0:1])
     norm_out[...] = norm
     factor = jnp.minimum(1.0, CLIP / (norm + 1e-06))
     value, first, second = adam_update(
@@ -819,14 +871,16 @@
     mine = exchange(boxes.reshape(PEERS, BOX_ROWS, LANES))
     other = swap_cores(mine)
     core = lax.axis_index("core").astype(jnp.int32).reshape(1)
-    keep, give, code_grad = main_call(
+    first_w, second_w, latent_w, *sums = run_loop(
         core,
         mine.reshape(PEERS * BOX_ROWS, LANES),
         other.reshape(PEERS * BOX_ROWS, LANES),
         codes,
     )
+    keep, give = weight_boxes(core, codes, first_w, second_w, *sums)
     pair_sum = (keep + swap_cores(give)).reshape(PEERS, BOX_ROWS, LANES)
-    shard, squares = sum_shards(exchange(pair_sum).reshape(PEERS * BOX_ROWS, LANES))
+    code_grad, code_squares = code_grads(codes, latent_w, sums[1], sums[4])
+    shard, squares = sum_shards(exchange(pair_sum).reshape(PEERS * BOX_ROWS, LANES), code_squares)
     squares = squares + swap_cores(squares)
     seen = exchange(jnp.broadcast_to(squares, (PEERS, 8, LANES)))
     flat = lambda v: v.reshape(SHARD_ROWS, LANES)

time: 97.4 us -> 98.2 us (level)
  blocking collectives: 64 us -> 42.9 us
  waiting for transfers between devices: 5.56 us -> 21.4 us
  starting transfers between devices: 0.25 us -> 5.17 us
    all_to_all x3 -> x2, blocking collectives: 64 us -> 42.9 us  [exchange(): return lax.all_to_all(v, ('z', 'wide'), split_axis=0, concat_axis=0)]
    all_to_all x0 -> x1, waiting for transfers between devices: none -> 15.8 us  [exchange(): return lax.all_to_all(v, ('z', 'wide'), split_axis=0, concat_axis=0)]
    all_to_all x0 -> x1, starting transfers between devices: none -> 4.74 us  [exchange(): return lax.all_to_all(v, ('z', 'wide'), split_axis=0, concat_axis=0)]
    pallas_call x1 -> x3, Pallas kernels: 22.5 us -> 22.6 us  [the longest x1 19.4 us: run_loop(): pl.pallas_call(loop_kernel, out_shape=(f32(256, 3 * LANES), f32(HID, 5 *...]
  transfers between devices with their start and end apart: 3 -> 4, of which waited for: 3 -> 4; matrix products, arithmetic and copies ran while one was open for 0% -> 0% of each run, Pallas kernels for 0% -> 1%
where the time goes in v7:
time: 98.2 us; the launch traced here: 97.8 us
  blocking collectives  42.9 us (44%)
  Pallas kernels  26.6 us (27%)
  waiting for transfers between devices  21.4 us (22%)
  starting transfers between devices  5.17 us (5%)
  other arithmetic  0.99 us (1%)
    all_to_all x2, blocking collectives, exchange(): return lax.all_to_all(v, ('z', 'wide'), split_axis=0, concat_axis=0)  42.9 us
    pallas_call x1, Pallas kernels, run_loop(): pl.pallas_call(loop_kernel, out_shape=(f32(256, 3 * LANES), f32(HID, 5 *...  19.4 us
    all_to_all x1, waiting for transfers between devices, exchange(): return lax.all_to_all(v, ('z', 'wide'), split_axis=0, concat_axis=0)  15.8 us
    ppermute x3, waiting for transfers between devices, swap_cores(): return lax.ppermute(v, 'core', [(0, 1), (1, 0)])  5.56 us
    all_to_all x1, starting transfers between devices, exchange(): return lax.all_to_all(v, ('z', 'wide'), split_axis=0, concat_axis=0)  4.74 us
    pallas_call x1, Pallas kernels, pack_boxes(): pl.pallas_call(pack_kernel, out_shape=jax.ShapeDtypeStruct((PEERS * BOX_R...  2.58 us
    pallas_call x1, Pallas kernels, weight_boxes(): pl.pallas_call(weight_kernel, out_shape=(f32(PEERS * BOX_ROWS, LANES),) *...  2.57 us
  transfers between devices with their start and end apart: 4, of which 4 were waited for; matrix products, arithmetic and copies ran while one was open for 0% of the time, Pallas kernels for 1%

profile of v7, /device:TPU:0, one launch (start us, length us, event | category | flops | bytes accessed | tf_op | source)
XLA Modules:
  0.0 97.8 jit_solution(12543715214718642283)
XLA Ops:
  0.6 0.0 copy-start
  0.7 2.6 %shard_map.168 = f32[1536,128]{1,0:T(8,128)} custom-call(f32[21,128]{1,0:T(8,128)} %bitcast.22, f32[3,1024]{1,0:T(4,128)} %coords_hbm.1, f32[1,1024]{1,0:T(1,128)} %bitcast.27, s32[1,1024]{1,0:T(1,128)} %bitcast.28), custom_call_target="tpu_custom_call" | custom-call | tf_op jit(solution)/shard_map/pallas_call | solution.py:647
  3.2 27.5 %all_to_all.15 = f32[64,24,128]{2,1,0:T(8,128)S(1)} all-to-all(f32[64,24,128]{2,1,0:T(8,128)} %bitcast.26), channel_id=1, replica_groups=mesh['z'=4,'core'=2,'wide'=16] {'z','wide'}, dimensions={0} | all-to-all | bytes 1572864 | tf_op jit(solution)/shard_map/all_to_all | solution.py:851
  30.7 0.0 collective-permute-start
  30.8 2.3 %collective-permute-done = f32[64,24,128]{2,1,0:T(8,128)S(1)} collective-permute-done((f32[64,24,128]{2,1,0:T(8,128)S(1)}, f32[64,24,128]{2,1,0:T(8,128)S(1)}, u32[]{:S(2)}, u32[]{:S(2)}) %collective-permute-start) | collective-permute-done | bytes 786464 | tf_op jit(solution)/shard_map/ppermute | solution.py:847
  33.0 0.0 copy-done
  33.0 19.4 %shard_map.169 = (f32[256,384]{1,0:T(8,128)S(1)}, f32[512,640]{1,0:T(8,128)S(1)}, f32[768,256]{1,0:T(8,128)S(1)}, f32[512,256]{1,0:T(8,128)S(1)}, f32[768,256]{1...) custom-call(s32[1]{0:T(128)} %bitcast.core_ref, ...), custom_call_target="tpu_custom_call" | custom-call | tf_op jit(solution)/shard_map/pallas_call | solution.py:700
  52.5 2.6 %shard_map.170 = (f32[1536,128]{1,0:T(8,128)S(1)}, f32[1536,128]{1,0:T(8,128)S(1)}) custom-call(s32[1]{0:T(128)} %bitcast.core_ref, f32[256,256]{1,0:T(8,128)S(1)} %copy-done, f32[256,384]{1,0:T(8,128)S(1)} %get-tuple-element.35.first_w, f32[512,640]{1,0:T(8,128)S(1)} %get-tuple-element.36.second_w, f32[512,256]{1,0:T(8,128)S(1)} %get-tuple-element.37.sum_two, ...), custom_call_target="tpu_custom_call" | custom-call | tf_op jit(solution)/shard_map/pallas_call | solution.py:721
  55.0 0.4 collective-permute-start.1
  55.5 2.1 %collective-permute-done.1 = f32[1536,128]{1,0:T(8,128)S(1)} collective-permute-done((f32[1536,128]{1,0:T(8,128)S(1)}, f32[1536,128]{1,0:T(8,128)S(1)}, u32[]{:S(2)}, u32[]{:S(2)}) %collective-permute-start.1) | collective-permute-done | bytes 786464 | tf_op jit(solution)/shard_map/ppermute | solution.py:847
  57.6 1.0 %add.6 = f32[1536,128]{1,0:T(8,128)} add(f32[1536,128]{1,0:T(8,128)S(1)} %get-tuple-element.43, f32[1536,128]{1,0:T(8,128)S(1)} %collective-permute-done.1) | non-fusion elementwise | flops 196608 | bytes 2359296 | tf_op jit(solution)/shard_map/add | solution.py:881
  58.6 4.7 %all-to-all-start.1 = ((f32[64,24,128]{2,1,0:T(8,128)}), f32[64,24,128]{2,1,0:T(8,128)S(1)}, u32[]{:S(2)}, u32[]{:S(2)}) async-start(f32[64,24,128]{2,1,0:T(8,128)} %bitcast.7), calls=%async_computation.1 | async-start | bytes 1572864 | tf_op jit(solution)/shard_map/all_to_all | solution.py:851
  63.3 0.0 copy-start.1
  63.3 0.0 copy-start.2
  63.3 0.0 copy-start.3
  63.3 0.7 shard_map.171
  64.0 0.0 copy-start.4
  64.0 0.0 copy-start.5
  64.0 15.8 %all-to-all-done.1 = f32[64,24,128]{2,1,0:T(8,128)S(1)} async-done(((f32[64,24,128]{2,1,0:T(8,128)}), f32[64,24,128]{2,1,0:T(8,128)S(1)}, u32[]{:S(2)}, u32[]{:S(2)}) %all-to-all-start.1) | async-done | bytes 786464 | tf_op jit(solution)/shard_map/all_to_all | solution.py:851
  79.8 0.2 shard_map.172
  80.0 0.0 collective-permute-start.2
  80.0 1.2 %collective-permute-done.2 = f32[8,128]{1,0:T(8,128)S(1)} collective-permute-done((f32[8,128]{1,0:T(8,128)S(1)}, f32[8,128]{1,0:T(8,128)S(1)}, u32[]{:S(2)}, u32[]{:S(2)}) %collective-permute-start.2) | collective-permute-done | bytes 4128 | tf_op jit(solution)/shard_map/ppermute | solution.py:847
  81.2 15.4 %all_to_all.16 = f32[64,8,128]{2,1,0:T(8,128)S(1)} all-to-all(f32[64,8,128]{2,1,0:T(8,128)S(1)} %broadcast_in_dim.3), channel_id=1, replica_groups=mesh['z'=4,'core'=2,'wide'=16] {'z','wide'}, dimensions={0} | all-to-all | bytes 524288 | tf_op jit(solution)/shard_map/all_to_all | solution.py:851
  96.6 0.0 copy-done.1
  96.6 0.0 copy-done.2
  96.6 0.0 copy-done.3
  96.6 0.0 copy-done.4
  96.6 0.0 copy-done.5
  96.6 1.2 %shard_map.173 = (f32[1,1]{1,0:T(1,128)}, f32[1,1]{1,0:T(1,128)}, f32[21,128]{1,0:T(8,128)}, f32[21,128]{1,0:T(8,128)}, f32[21,128]{1,0:T(8,128)}, /*index=5*/bf...) custom-call(f32[512,128]{1,0:T(8,128)S(1)} %bitcast.20, ...), custom_call_target="tpu_custom_call" | custom-call | tf_op jit(solution)/shard_map/pallas_call | solution.py:837
  (2 shorter events, 0.0 us)
Async XLA Ops:
  0.6 32.4 %copy-start = (f32[256,256]{1,0:T(8,128)S(1)}, f32[256,256]{1,0:T(8,128)}, u32[]{:S(2)}) copy-start(f32[256,256]{1,0:T(8,128)} %codes_ref.7) | copy-start | bytes 786436
  30.7 2.3 %collective-permute-start = (f32[64,24,128]{2,1,0:T(8,128)S(1)}, f32[64,24,128]{2,1,0:T(8,128)S(1)}, u32[]{:S(2)}, u32[]{:S(2)}) collective-permute-start(f32[64,24,128]{2,1,0:T(8,128)S(1)} %all_to_all.15), channel_id=1, source_target_pairs={{0,16},{16,0},{1,17},{17,1},{2,18},{18,2},{3,19},{19,3},{4,20},{20... | collective-permute-start | bytes 2359304 | tf_op jit(solution)/shard_map/ppermute | solution.py:847
  55.0 2.5 %collective-permute-start.1 = (f32[1536,128]{1,0:T(8,128)S(1)}, f32[1536,128]{1,0:T(8,128)S(1)}, u32[]{:S(2)}, u32[]{:S(2)}) collective-permute-start(f32[1536,128]{1,0:T(8,128)S(1)} %get-tuple-element.44), channel_id=1, source_target_pairs={{0,16},{16,0},{1,17},{17,1},{2,18},{18,2},{3,19},{19,3},{4,20},{20... | collective-permute-start | bytes 2359304 | tf_op jit(solution)/shard_map/ppermute | solution.py:847
  58.6 21.3 %all-to-all-start.1 = ((f32[64,24,128]{2,1,0:T(8,128)}), f32[64,24,128]{2,1,0:T(8,128)S(1)}, u32[]{:S(2)}, u32[]{:S(2)}) async-start(f32[64,24,128]{2,1,0:T(8,128)} %bitcast.7), calls=%async_computation.1 | async-start | bytes 1572864 | tf_op jit(solution)/shard_map/all_to_all | solution.py:851
  63.3 33.3 %copy-start.1 = (f32[256,256]{1,0:T(8,128)S(1)}, f32[256,256]{1,0:T(8,128)}, u32[]{:S(2)}) copy-start(f32[256,256]{1,0:T(8,128)} %code_first_ref.1) | copy-start | bytes 786436
  63.3 33.3 %copy-start.2 = (f32[256,256]{1,0:T(8,128)S(1)}, f32[256,256]{1,0:T(8,128)}, u32[]{:S(2)}) copy-start(f32[256,256]{1,0:T(8,128)} %code_second_ref.1) | copy-start | bytes 786436
  63.3 33.3 %copy-start.3 = (f32[2688]{0:T(1024)S(1)}, f32[2688]{0:T(1024)}, u32[]{:S(2)}) copy-start(f32[2688]{0:T(1024)} %param.9) | copy-start | bytes 32260
  64.0 32.6 %copy-start.4 = (f32[2688]{0:T(1024)S(1)}, f32[2688]{0:T(1024)}, u32[]{:S(2)}) copy-start(f32[2688]{0:T(1024)} %param.10) | copy-start | bytes 32260
  64.0 32.6 %copy-start.5 = (f32[2688]{0:T(1024)S(1)}, f32[2688]{0:T(1024)}, u32[]{:S(2)}) copy-start(f32[2688]{0:T(1024)} %param.11) | copy-start | bytes 32260
  80.0 1.2 %collective-permute-start.2 = (f32[8,128]{1,0:T(8,128)S(1)}, f32[8,128]{1,0:T(8,128)S(1)}, u32[]{:S(2)}, u32[]{:S(2)}) collective-permute-start(f32[8,128]{1,0:T(8,128)S(1)} %get-tuple-element.47), channel_id=1, source_target_pairs={{0,16},{16,0},{1,17},{17,1},{2,18},{18,2},{3,19},{19,3},{4,20},{20... | collective-permute-start | bytes 12296 | tf_op jit(solution)/shard_map/ppermute | solution.py:847

commit v8 on v7

--- a/solution.py
+++ b/solution.py
@@ -252,6 +252,7 @@
     hid_hi,
     hid_lo,
     hot,
+    hot_turned,
     act_two,
     slope_two,
     curve_two,
@@ -260,8 +261,6 @@
     gate_lo,
     tang_hi,
     tang_lo,
-    near_hi,
-    near_lo,
     bar_hi,
     bar_lo,
     low_hi,
@@ -304,7 +303,7 @@
     latent_w[0:256, :] = first_low
     for i in range(3):
         coord_w[:, i * LANES : (i + 1) * LANES] = jnp.broadcast_to(
-            first_near[:, i : i + 1], (256, LANES)
+            0.5 * first_near[:, i : i + 1], (256, LANES)
         )
 
     second_a = second_w[:, 0:256]
@@ -342,12 +341,6 @@
     two_hi, two_lo = halves(0.5 * (by_code[256:768, :] + second_bias))
     lhs_two[:, 768:1024] = two_hi
     lhs_two[:, 1024:1280] = two_lo
-    spread = jnp.where((unit - MIDDLE == lane) & (lane < 3), 1.0, first_near)
-    near_parts = thirds(0.5 * spread)
-    near_lhs = near_parts[0]
-    for place, k in enumerate((0, 0, 1, 1, 2)):
-        near_lhs = near_lhs + pltpu.roll(near_parts[k], 8 * (place + 1), 1)
-    lhs_one[:, 512:640] = near_lhs.astype(BF16)
 
     for ref in (sum_two, sum_codes, sum_coord, sum_head, sum_count, sum_loss):
         ref[...] = jnp.zeros(ref.shape, F32)
@@ -366,7 +359,6 @@
         target = feature(3, step, s)
         code_row = feature(4, step, s)
         valid = (code_row > 0.5).astype(F32)
-        near_pieces = thirds(stacked(*place, blank5))
 
         wanted = code_row - 1.0
         for r in range(0, CODE_ROWS, chunk):
@@ -374,18 +366,26 @@
             mark = jnp.where(row == wanted, 1.0, 0.0)
             hot[s, r : r + chunk, :] = mark.astype(BF16)
             sum_count[r : r + chunk, :] += folded(mark)
-        yield
-
-        high, mid, low = near_pieces
-        near_rhs = stacked(high, mid, low, high, mid, high, jnp.zeros((80, BLOCK), F32))
-        act_one[s] = mm(lhs_one[...], stacked(hot[s], hot[s], near_rhs.astype(BF16)))
-        yield
+        for i in range(TILES):
+            wanted = jnp.broadcast_to(code_row[:, i * LANES : (i + 1) * LANES] - 1.0, (LANES, LANES)).T
+            for c in range(0, CODE_ROWS, LANES):
+                code = (rows_of_lanes(1, (LANES, LANES)) + c).astype(F32)
+                mark = jnp.where(code == wanted, 1.0, 0.0).astype(BF16)
+                hot_turned[s, i * LANES : (i + 1) * LANES, c : c + LANES] = mark
+        yield
+
+        act_one[s] = mm(lhs_one[...], stacked(hot[s], hot[s]))
+        yield
+        last = stacked(blank5, *place)
         for r in low_chunks:
             pre = act_one[s, r : r + chunk, :]
+            for i in range(3):
+                pre = pre + across(coord_w[r : r + chunk, i * LANES : (i + 1) * LANES]) * place[i]
             value, slope, curve = silu_parts(pre)
             if r + chunk == 256:
                 inside = rows_of_lanes(0, (chunk, BLOCK)) + r < MIDDLE
-                value = jnp.where(inside, value, pre + pre)
+                end = jnp.where(inside[chunk - 8 :], value[chunk - 8 :], last)
+                value = stacked(value[: chunk - 8], end)
                 slope = jnp.where(inside, slope, 0.0)
                 curve = jnp.where(inside, curve, 0.0)
             high, low = halves(value)
@@ -418,15 +418,12 @@
         totals = [jnp.zeros((8, BLOCK), F32) for _ in range(3)]
         for r in low_chunks:
             grad = back_one[s, r : r + chunk, :] * slope_one[s, r : r + chunk, :]
-            high, low = halves(grad)
-            near_hi[s, r : r + chunk, :] = high
-            near_lo[s, r : r + chunk, :] = low
             for i in range(3):
                 weighed = across(coord_w[r : r + chunk, i * LANES : (i + 1) * LANES]) * grad
                 for k in range(0, chunk, 8):
                     totals[i] = totals[i] + weighed[k : k + 8, :]
         lead = [
-            jnp.sum(totals[i], axis=0, keepdims=True)
+            2.0 * jnp.sum(totals[i], axis=0, keepdims=True)
             + back_one[s, MIDDLE + i : MIDDLE + i + 1, :]
             for i in range(3)
         ]
@@ -449,11 +446,17 @@
         pull = [share * flank * p for p in pull]
 
         last = stacked(blank5, *pull)
+        twice = [2.0 * p for p in pull]
         for r in low_chunks:
             grad = 0.0
             for i in range(3):
-                grad = grad + across(coord_w[r : r + chunk, i * LANES : (i + 1) * LANES]) * pull[i]
-            through = grad * slope_one[s, r : r + chunk, :]
+                grad = grad + across(coord_w[r : r + chunk, i * LANES : (i + 1) * LANES]) * twice[i]
+            slope = slope_one[s, r : r + chunk, :]
+            back = back_one[s, r : r + chunk, :]
+            near = back * slope
+            for i in range(3):
+                sum_coord[r : r + chunk, i * LANES : (i + 1) * LANES] += folded(near * pull[i])
+            through = grad * slope
             if r + chunk == 256:
                 inside = rows_of_lanes(0, (8, BLOCK)) < MIDDLE - 248
                 end = jnp.where(inside, through[chunk - 8 :], last)
@@ -462,7 +465,7 @@
             tang_hi[s, r : r + chunk, :] = high
             tang_lo[s, r : r + chunk, :] = low
             curve_one[s, r : r + chunk, :] = (
-                grad * back_one[s, r : r + chunk, :] * curve_one[s, r : r + chunk, :]
+                grad * back * curve_one[s, r : r + chunk, :]
             )
         yield
         act_tang[s] = mm(lhs_two[:, 0:768], stacked(tang_hi[s], tang_lo[s], tang_hi[s]))
@@ -486,6 +489,8 @@
                 back_one[s, r : r + chunk, :] * slope_one[s, r : r + chunk, :]
                 + curve_one[s, r : r + chunk, :]
             )
+            for i in range(3):
+                sum_coord[r : r + chunk, i * LANES : (i + 1) * LANES] += folded(bar * place[i])
             high, low = halves(bar)
             low_hi[s, r : r + chunk, :] = high
             low_lo[s, r : r + chunk, :] = low
@@ -495,17 +500,9 @@
             beside(bar_hi[s], bar_hi[s], bar_lo[s], gate_hi[s], gate_hi[s], gate_lo[s]),
             beside(hid_hi[s], hid_lo[s], hid_hi[s], tang_hi[s], tang_lo[s], tang_hi[s]),
         )
-        hots = beside(hot[s], hot[s])
-        sum_codes[256:768, :] += mm_nt(beside(bar_hi[s], bar_lo[s]), hots)
-        sum_codes[0:256, :] += mm_nt(beside(low_hi[s], low_lo[s]), hots)
-        seen = stacked(near_pieces[0], near_pieces[1]).astype(BF16)
-        pulled = stacked(*pull, blank5)
-        high = pulled.astype(BF16).astype(F32)
-        pulled = stacked(high, pulled - high).astype(BF16)
-        sum_coord[...] += mm_nt(
-            beside(seen, seen, pulled, pulled),
-            beside(low_hi[s], low_lo[s], near_hi[s], near_lo[s]),
-        )
+        turned = stacked(hot_turned[s], hot_turned[s])
+        sum_codes[256:768, :] += mm(beside(bar_hi[s], bar_lo[s]), turned)
+        sum_codes[0:256, :] += mm(beside(low_hi[s], low_lo[s]), turned)
 
     def step_body(step, carry):
         waiting = [block_stages(step, s) for s in range(SUBS)]
@@ -569,9 +566,10 @@
 
     lane = rows_of_lanes(1, (256, LANES))
     real = rows_of_lanes(0, (256, LANES)) < MIDDLE
-    near_grad = sum_coord[0:8, :] + sum_coord[8:16, :]
-    near_grad = stacked(near_grad, jnp.zeros((LANES - 8, 256), F32)).T
-    near_grad = jnp.where(lane < 3, near_grad, 0.0)
+    near_grad = 0.0
+    for i in range(3):
+        column = jnp.sum(sum_coord[:, i * LANES : (i + 1) * LANES], axis=1, keepdims=True)
+        near_grad = jnp.where(lane == i, column, near_grad)
     low_grad = latent_grad[0:256, :]
     first_low = first_w[:, : 2 * LANES]
     first_near = jnp.where(lane < 3, first_w[:, 2 * LANES :], 0.0)
@@ -669,7 +667,7 @@
     pair_two = (SUBS, HID, BLOCK)
     scratch = [
         ((FLAT_ROWS + 8, LANES), F32),
-        ((256, 640), BF16),
+        ((256, 512), BF16),
         ((HID, 1280), BF16),
         ((256, 1536), BF16),
         ((256, 3 * LANES), F32),
@@ -682,14 +680,13 @@
         (pair, BF16),
         (pair, BF16),
         (pair, BF16),
+        ((SUBS, BLOCK, CODE_ROWS), BF16),
         (pair_two, F32),
         (pair_two, F32),
         (pair_two, F32),
         (pair_two, F32),
         (pair_two, BF16),
         (pair_two, BF16),
-        (pair, BF16),
-        (pair, BF16),
         (pair, BF16),
         (pair, BF16),
         (pair_two, BF16),
@@ -705,7 +702,7 @@
             f32(768, 256),
             f32(HID, 256),
             f32(768, 256),
-            f32(16, 256),
+            f32(256, 3 * LANES),
             f32(HID, LANES),
             f32(CODE_ROWS, LANES),
             f32(2, BLOCK),
@@ -880,6 +877,7 @@
     keep, give = weight_boxes(core, codes, first_w, second_w, *sums)
     pair_sum = (keep + swap_cores(give)).reshape(PEERS, BOX_ROWS, LANES)
     code_grad, code_squares = code_grads(codes, latent_w, sums[1], sums[4])
+    pair_sum, code_grad, code_squares = lax.optimization_barrier((pair_sum, code_grad, code_squares))
     shard, squares = sum_shards(exchange(pair_sum).reshape(PEERS * BOX_ROWS, LANES), code_squares)
     squares = squares + swap_cores(squares)
     seen = exchange(jnp.broadcast_to(squares, (PEERS, 8, LANES)))

time: 98.2 us -> 98.1 us (level)
  blocking collectives: 42.9 us -> 63.9 us
  waiting for transfers between devices: 21.4 us -> 4.89 us
  starting transfers between devices: 5.17 us -> 0.44 us
  local copies, waits for them, and re-layouts: 0.05 us -> 1.37 us
    all_to_all x2 -> x3, blocking collectives: 42.9 us -> 63.9 us  [exchange(): return lax.all_to_all(v, ('z', 'wide'), split_axis=0, concat_axis=0)]
    all_to_all x1 -> x0, waiting for transfers between devices: 15.8 us -> none  [exchange(): return lax.all_to_all(v, ('z', 'wide'), split_axis=0, concat_axis=0)]
    all_to_all x1 -> x0, starting transfers between devices: 4.74 us -> none  [exchange(): return lax.all_to_all(v, ('z', 'wide'), split_axis=0, concat_axis=0)]
    unnamed x12 -> x14, local copies, waits for them, and re-layouts: 0.03 us -> 1.35 us
  transfers between devices with their start and end apart: 4 -> 3, of which waited for: 4 -> 3; matrix products, arithmetic and copies ran while one was open for 0% -> 0% of each run, Pallas kernels for 1% -> 1%
where the time goes in v8:
time: 98.1 us; the launch traced here: 97.8 us
  blocking collectives  63.9 us (65%)
  Pallas kernels  26.4 us (27%)
  waiting for transfers between devices  4.89 us (5%)
  local copies, waits for them, and re-layouts  1.37 us (1%)
    all_to_all x3, blocking collectives, exchange(): return lax.all_to_all(v, ('z', 'wide'), split_axis=0, concat_axis=0)  63.9 us
    pallas_call x1, Pallas kernels, run_loop(): pl.pallas_call(loop_kernel, out_shape=(f32(256, 3 * LANES), f32(HID, 5 *...  19.1 us
    ppermute x3, waiting for transfers between devices, swap_cores(): return lax.ppermute(v, 'core', [(0, 1), (1, 0)])  4.89 us
    pallas_call x1, Pallas kernels, weight_boxes(): pl.pallas_call(weight_kernel, out_shape=(f32(PEERS * BOX_ROWS, LANES),) *...  2.63 us
    pallas_call x1, Pallas kernels, pack_boxes(): pl.pallas_call(pack_kernel, out_shape=jax.ShapeDtypeStruct((PEERS * BOX_R...  2.59 us
  transfers between devices with their start and end apart: 3, of which 3 were waited for; matrix products, arithmetic and copies ran while one was open for 0% of the time, Pallas kernels for 1%

profile of v8, /device:TPU:0, one launch (start us, length us, event | category | flops | bytes accessed | tf_op | source)
XLA Modules:
  0.0 97.8 jit_solution(15157060010586988065)
XLA Ops:
  0.6 0.0 copy-start
  0.7 2.6 %shard_map.168 = f32[1536,128]{1,0:T(8,128)} custom-call(f32[21,128]{1,0:T(8,128)} %bitcast.22, f32[3,1024]{1,0:T(4,128)} %coords_hbm.1, f32[1,1024]{1,0:T(1,128)} %bitcast.28, s32[1,1024]{1,0:T(1,128)} %bitcast.29), custom_call_target="tpu_custom_call" | custom-call | tf_op jit(solution)/shard_map/pallas_call | solution.py:645
  3.2 27.5 %all_to_all.15 = f32[64,24,128]{2,1,0:T(8,128)S(1)} all-to-all(f32[64,24,128]{2,1,0:T(8,128)} %bitcast.26), channel_id=1, replica_groups=mesh['z'=4,'core'=2,'wide'=16] {'z','wide'}, dimensions={0} | all-to-all | bytes 1572864 | tf_op jit(solution)/shard_map/all_to_all | solution.py:848
  30.8 0.0 collective-permute-start
  30.8 2.3 %collective-permute-done = f32[64,24,128]{2,1,0:T(8,128)S(1)} collective-permute-done((f32[64,24,128]{2,1,0:T(8,128)S(1)}, f32[64,24,128]{2,1,0:T(8,128)S(1)}, u32[]{:S(2)}, u32[]{:S(2)}) %collective-permute-start) | collective-permute-done | bytes 786464 | tf_op jit(solution)/shard_map/ppermute | solution.py:844
  33.0 0.0 copy-done
  33.0 19.1 %shard_map.169 = (f32[256,384]{1,0:T(8,128)S(1)}, f32[512,640]{1,0:T(8,128)}, f32[768,256]{1,0:T(8,128)S(1)}, f32[512,256]{1,0:T(8,128)S(1)}, f32[768,256]{1,0:T...) custom-call(s32[1]{0:T(128)} %bitcast.core_ref, ...), custom_call_target="tpu_custom_call" | custom-call | tf_op jit(solution)/shard_map/pallas_call | solution.py:697
  52.2 0.0 copy-start.1
  52.2 1.3 %copy-done.1 = f32[512,640]{1,0:T(8,128)S(1)} copy-done((f32[512,640]{1,0:T(8,128)S(1)}, f32[512,640]{1,0:T(8,128)}, u32[]{:S(2)}) %copy-start.1) | copy-done | bytes 1310744
  53.5 2.6 %shard_map.170 = (f32[1536,128]{1,0:T(8,128)S(1)}, f32[1536,128]{1,0:T(8,128)S(1)}) custom-call(s32[1]{0:T(128)} %bitcast.core_ref, f32[256,256]{1,0:T(8,128)S(1)} %copy-done, f32[256,384]{1,0:T(8,128)S(1)} %get-tuple-element.38.first_w, f32[512,640]{1,0:T(8,128)S(1)} %copy-done.1, f32[512,256]{1,0:T(8,128)S(1)} %get-tuple-element.40.sum_two, ...), custom_call_target="tpu_custom_call" | custom-call | tf_op jit(solution)/shard_map/pallas_call | solution.py:718
  56.1 0.4 collective-permute-start.1
  56.6 0.7 shard_map.171
  57.2 1.5 %collective-permute-done.1 = f32[1536,128]{1,0:T(8,128)S(1)} collective-permute-done((f32[1536,128]{1,0:T(8,128)S(1)}, f32[1536,128]{1,0:T(8,128)S(1)}, u32[]{:S(2)}, u32[]{:S(2)}) %collective-permute-start.1) | collective-permute-done | bytes 786464 | tf_op jit(solution)/shard_map/ppermute | solution.py:844
  58.7 0.1 add.6
  58.8 0.0 copy-start.2
  58.8 0.0 copy-start.3
  58.8 0.0 copy-start.4
  58.8 0.0 copy-start.5
  58.8 0.0 copy-start.6
  58.8 21.0 %all_to_all.16 = f32[64,24,128]{2,1,0:T(8,128)S(1)} all-to-all(f32[64,24,128]{2,1,0:T(8,128)S(1)} %bitcast.27), channel_id=1, replica_groups=mesh['z'=4,'core'=2,'wide'=16] {'z','wide'}, dimensions={0} | all-to-all | bytes 1572864 | tf_op jit(solution)/shard_map/all_to_all | solution.py:848
  79.8 0.2 shard_map.172
  80.0 0.0 collective-permute-start.2
  80.0 1.2 %collective-permute-done.2 = f32[8,128]{1,0:T(8,128)S(1)} collective-permute-done((f32[8,128]{1,0:T(8,128)S(1)}, f32[8,128]{1,0:T(8,128)S(1)}, u32[]{:S(2)}, u32[]{:S(2)}) %collective-permute-start.2) | collective-permute-done | bytes 4128 | tf_op jit(solution)/shard_map/ppermute | solution.py:844
  81.2 15.4 %all_to_all.17 = f32[64,8,128]{2,1,0:T(8,128)S(1)} all-to-all(f32[64,8,128]{2,1,0:T(8,128)S(1)} %broadcast_in_dim.3), channel_id=1, replica_groups=mesh['z'=4,'core'=2,'wide'=16] {'z','wide'}, dimensions={0} | all-to-all | bytes 524288 | tf_op jit(solution)/shard_map/all_to_all | solution.py:848
  96.6 0.0 copy-done.2
  96.6 0.0 copy-done.3
  96.6 0.0 copy-done.4
  96.6 0.0 copy-done.5
  96.6 0.0 copy-done.6
  96.6 1.2 %shard_map.173 = (f32[1,1]{1,0:T(1,128)}, f32[1,1]{1,0:T(1,128)}, f32[21,128]{1,0:T(8,128)}, f32[21,128]{1,0:T(8,128)}, f32[21,128]{1,0:T(8,128)}, /*index=5*/bf...) custom-call(f32[512,128]{1,0:T(8,128)S(1)} %bitcast.20, ...), custom_call_target="tpu_custom_call" | custom-call | tf_op jit(solution)/shard_map/pallas_call | solution.py:834
  (2 shorter events, 0.0 us)
Async XLA Ops:
  0.6 32.4 %copy-start = (f32[256,256]{1,0:T(8,128)S(1)}, f32[256,256]{1,0:T(8,128)}, u32[]{:S(2)}) copy-start(f32[256,256]{1,0:T(8,128)} %codes_ref.7) | copy-start | bytes 786436
  30.8 2.3 %collective-permute-start = (f32[64,24,128]{2,1,0:T(8,128)S(1)}, f32[64,24,128]{2,1,0:T(8,128)S(1)}, u32[]{:S(2)}, u32[]{:S(2)}) collective-permute-start(f32[64,24,128]{2,1,0:T(8,128)S(1)} %all_to_all.15), channel_id=1, source_target_pairs={{0,16},{16,0},{1,17},{17,1},{2,18},{18,2},{3,19},{19,3},{4,20},{20... | collective-permute-start | bytes 2359304 | tf_op jit(solution)/shard_map/ppermute | solution.py:844
  52.2 1.3 %copy-start.1 = (f32[512,640]{1,0:T(8,128)S(1)}, f32[512,640]{1,0:T(8,128)}, u32[]{:S(2)}) copy-start(f32[512,640]{1,0:T(8,128)} %get-tuple-element.39.second_w) | copy-start | bytes 3932164
  56.1 2.5 %collective-permute-start.1 = (f32[1536,128]{1,0:T(8,128)S(1)}, f32[1536,128]{1,0:T(8,128)S(1)}, u32[]{:S(2)}, u32[]{:S(2)}) collective-permute-start(f32[1536,128]{1,0:T(8,128)S(1)} %get-tuple-element.47), channel_id=1, source_target_pairs={{0,16},{16,0},{1,17},{17,1},{2,18},{18,2},{3,19},{19,3},{4,20},{20... | collective-permute-start | bytes 2359304 | tf_op jit(solution)/shard_map/ppermute | solution.py:844
  58.8 37.8 %copy-start.2 = (f32[256,256]{1,0:T(8,128)S(1)}, f32[256,256]{1,0:T(8,128)}, u32[]{:S(2)}) copy-start(f32[256,256]{1,0:T(8,128)} %code_first_ref.1) | copy-start | bytes 786436
  58.8 37.8 %copy-start.3 = (f32[256,256]{1,0:T(8,128)S(1)}, f32[256,256]{1,0:T(8,128)}, u32[]{:S(2)}) copy-start(f32[256,256]{1,0:T(8,128)} %code_second_ref.1) | copy-start | bytes 786436
  58.8 37.8 %copy-start.4 = (f32[2688]{0:T(1024)S(1)}, f32[2688]{0:T(1024)}, u32[]{:S(2)}) copy-start(f32[2688]{0:T(1024)} %param.9) | copy-start | bytes 32260
  58.8 37.8 %copy-start.5 = (f32[2688]{0:T(1024)S(1)}, f32[2688]{0:T(1024)}, u32[]{:S(2)}) copy-start(f32[2688]{0:T(1024)} %param.10) | copy-start | bytes 32260
  58.8 37.8 %copy-start.6 = (f32[2688]{0:T(1024)S(1)}, f32[2688]{0:T(1024)}, u32[]{:S(2)}) copy-start(f32[2688]{0:T(1024)} %param.11) | copy-start | bytes 32260
  80.0 1.2 %collective-permute-start.2 = (f32[8,128]{1,0:T(8,128)S(1)}, f32[8,128]{1,0:T(8,128)S(1)}, u32[]{:S(2)}, u32[]{:S(2)}) collective-permute-start(f32[8,128]{1,0:T(8,128)S(1)} %get-tuple-element.53), channel_id=1, source_target_pairs={{0,16},{16,0},{1,17},{17,1},{2,18},{18,2},{3,19},{19,3},{4,20},{20... | collective-permute-start | bytes 12296 | tf_op jit(solution)/shard_map/ppermute | solution.py:844

commit v9 on v8

--- a/solution.py
+++ b/solution.py
@@ -32,7 +32,7 @@
 POINTS_DEV = 1024
 CODE_ROWS = 256
 FLAT_ROWS = DEVICES * SHARD_ROWS
-BLOCK = 256
+BLOCK = 512
 SUBS = 4
 TILES = BLOCK // LANES
 ALL_POINTS = POINTS_DEV * DEVICES
@@ -83,11 +83,12 @@
     coords_hbm,
     distances_hbm,
     index_hbm,
-    out_ref,
+    out_hbm,
     weights_ref,
     coords_ref,
     distances_ref,
     index_ref,
+    staged,
     sems,
 ):
     pairs = [
@@ -102,11 +103,16 @@
     ]
     for copy in copies:
         copy.start()
-    for copy in copies:
-        copy.wait()
+    copies[1].wait()
     shard = stacked(weights_ref[...], jnp.zeros((BOX_ROWS - SHARD_ROWS, LANES), F32))
     for peer in range(PEERS):
-        out_ref[peer * BOX_ROWS : (peer + 1) * BOX_ROWS, :] = shard
+        staged[peer] = shard
+    early = pltpu.make_async_copy(
+        staged.at[:, pl.ds(0, 16), :], out_hbm.at[:, pl.ds(0, 16), :], sems.at[4]
+    )
+    early.start()
+    for i in (0, 2, 3):
+        copies[i].wait()
     index = index_ref[...]
     owner = lax.shift_right_logical(index, 8)
     row = lax.bitwise_and(index, CODE_ROWS - 1)
@@ -133,12 +139,16 @@
         beside(sent_low, sent_low, sent_low),
         beside(*[stacked(*piece, spare).astype(BF16) for piece in pieces]),
     )
-    for z in range(4):
-        for core in range(2):
-            first = z * 32 + core * 16
-            out_ref[pl.ds(z * 16 * BOX_ROWS + SHARD_ROWS + core, 16, stride=BOX_ROWS), :] = boxes[
-                first : first + 16, :
-            ]
+    for d in range(DEVICES):
+        z, core, w = d // 32, d // 16 % 2, d % 16
+        row = SHARD_ROWS + core
+        staged[z * 16 + w, row : row + 1, :] = boxes[d : d + 1, :]
+    late = pltpu.make_async_copy(
+        staged.at[:, pl.ds(16, 8), :], out_hbm.at[:, pl.ds(16, 8), :], sems.at[5]
+    )
+    late.start()
+    early.wait()
+    late.wait()
 
 
 def unit_groups(count, stride_rows, extra, first_entry):
@@ -513,7 +523,11 @@
             active = [work for work in active if next(work, work) is not work]
         return carry
 
-    lax.fori_loop(0, SLOTS * DEVICES // (SUBS * BLOCK), step_body, 0)
+    steps = SLOTS * DEVICES // (SUBS * BLOCK)
+    if steps == 1:
+        step_body(0, 0)
+    else:
+        lax.fori_loop(0, steps, step_body, 0)
 
 
 def code_kernel(codes_ref, latent_w, sum_codes, sum_count, code_grad_ref, squares_ref):
@@ -641,32 +655,56 @@
 SMEM = pl.BlockSpec(memory_space=pltpu.SMEM)
 
 
+def f32(*shape):
+    return jax.ShapeDtypeStruct(shape, F32)
+
+
 def pack_boxes(weights, coords, distances, index):
     return pl.pallas_call(
         pack_kernel,
-        out_shape=jax.ShapeDtypeStruct((PEERS * BOX_ROWS, LANES), F32),
+        out_shape=f32(PEERS, BOX_ROWS, LANES),
         in_specs=[HBM] * 4,
-        out_specs=vmem(1)[0],
+        out_specs=HBM,
         scratch_shapes=[
             pltpu.VMEM(weights.shape, F32),
             pltpu.VMEM(coords.shape, F32),
             pltpu.VMEM(distances.shape, F32),
             pltpu.VMEM(index.shape, jnp.int32),
-            pltpu.SemaphoreType.DMA((4,)),
+            pltpu.VMEM((PEERS, BOX_ROWS, LANES), F32),
+            pltpu.SemaphoreType.DMA((6,)),
         ],
         compiler_params=pltpu.CompilerParams(vmem_limit_bytes=60 * 1024 * 1024),
     )(weights, coords, distances, index)
 
 
-def f32(*shape):
-    return jax.ShapeDtypeStruct(shape, F32)
-
-
-def run_loop(core, mine, other, codes):
+def main_kernel(
+    core_ref, mine_ref, other_ref, codes_ref, keep_ref, give_ref, code_grad_ref, squares_ref, *scratch
+):
+    first_w, second_w, latent_w, *sums = scratch[:9]
+    flat, first_grad, second_grad = scratch[9:12]
+    loop_kernel(core_ref, mine_ref, other_ref, codes_ref, *scratch[:9], flat, *scratch[12:])
+    code_kernel(codes_ref, latent_w, sums[1], sums[4], code_grad_ref, squares_ref)
+    weight_kernel(
+        core_ref, codes_ref, first_w, second_w, *sums, keep_ref, give_ref, flat, first_grad, second_grad
+    )
+
+
+def main_call(core, mine, other, codes):
     pair = (SUBS, 256, BLOCK)
     pair_two = (SUBS, HID, BLOCK)
     scratch = [
+        ((256, 3 * LANES), F32),
+        ((HID, 5 * LANES), F32),
+        ((768, 256), F32),
+        ((HID, 256), F32),
+        ((768, 256), F32),
+        ((256, 3 * LANES), F32),
+        ((HID, LANES), F32),
+        ((CODE_ROWS, LANES), F32),
+        ((2, BLOCK), F32),
         ((FLAT_ROWS + 8, LANES), F32),
+        ((256, 3 * LANES), F32),
+        ((HID, 5 * LANES), F32),
         ((256, 512), BF16),
         ((HID, 1280), BF16),
         ((256, 1536), BF16),
@@ -694,52 +732,15 @@
         (pair, BF16),
         (pair, BF16),
     ]
+    boxes = f32(PEERS * BOX_ROWS, LANES)
     return pl.pallas_call(
-        loop_kernel,
-        out_shape=(
-            f32(256, 3 * LANES),
-            f32(HID, 5 * LANES),
-            f32(768, 256),
-            f32(HID, 256),
-            f32(768, 256),
-            f32(256, 3 * LANES),
-            f32(HID, LANES),
-            f32(CODE_ROWS, LANES),
-            f32(2, BLOCK),
-        ),
+        main_kernel,
+        out_shape=(boxes, boxes, f32(CODE_ROWS, LATENT), f32(8, LANES)),
         in_specs=[SMEM] + vmem(3),
-        out_specs=tuple(vmem(9)),
+        out_specs=tuple(vmem(4)),
         scratch_shapes=[pltpu.VMEM(shape, dtype) for shape, dtype in scratch],
         compiler_params=PARAMS,
     )(core, mine, other, codes)
-
-
-def weight_boxes(core, codes, first_w, second_w, *sums):
-    return pl.pallas_call(
-        weight_kernel,
-        out_shape=(f32(PEERS * BOX_ROWS, LANES),) * 2,
-        in_specs=[SMEM] + vmem(9),
-        out_specs=tuple(vmem(2)),
-        scratch_shapes=[
-            pltpu.VMEM((FLAT_ROWS + 8, LANES), F32),
-            pltpu.VMEM((256, 3 * LANES), F32),
-            pltpu.VMEM((HID, 5 * LANES), F32),
-        ],
-        compiler_params=PARAMS,
-    )(core, codes, first_w, second_w, *sums)
-
-
-def code_grads(*args):
-    return pl.pallas_call(
-        code_kernel,
-        out_shape=(f32(CODE_ROWS, LATENT), f32(8, LANES)),
-        in_specs=vmem(4),
-        out_specs=tuple(vmem(2)),
-        compiler_params=PARAMS,
-        cost_estimate=pl.CostEstimate(
-            flops=2 * 3 * 768 * 256 * 256, bytes_accessed=3 << 20, transcendentals=0
-        ),
-    )(*args)
 
 
 def adam_update(value, first, second, grad, rate):
@@ -774,7 +775,7 @@
 
 
 def update_kernel(
-    seen_ref,
+    squares_ref,
     shard_ref,
     weights_ref,
     moment_one_ref,
@@ -794,11 +795,8 @@
     code_second_out,
     codes_copy_out,
 ):
-    total = seen_ref[0:8, :]
-    for peer in range(1, PEERS):
-        total = total + seen_ref[peer * 8 : peer * 8 + 8, :]
     loss_out[...] = shard_ref[SHARD_ROWS : SHARD_ROWS + 1, 0:1]
-    norm = jnp.sqrt(total[0:1, 0:1])
+    norm = jnp.sqrt(squares_ref[0:1, 0:1])
     norm_out[...] = norm
     factor = jnp.minimum(1.0, CLIP / (norm + 1e-06))
     value, first, second = adam_update(
@@ -848,6 +846,18 @@
     return lax.all_to_all(v, ("z", "wide"), split_axis=0, concat_axis=0)
 
 
+def sum_everywhere(v):
+    v = v + swap_cores(v)
+    flip = [1, 0, 3, 2], [3, 2, 1, 0]
+    for pairs in flip:
+        v = v + lax.ppermute(v, "z", list(enumerate(pairs)))
+    for stride in (4, 1):
+        for pairs in flip:
+            moves = [(d, d + (pairs[d // stride % 4] - d // stride % 4) * stride) for d in range(16)]
+            v = v + lax.ppermute(v, "wide", moves)
+    return v
+
+
 def body(
     weights_flat,
     moment_one,
@@ -865,25 +875,21 @@
         distances.reshape(1, POINTS_DEV),
         shape_index.reshape(1, POINTS_DEV),
     )
-    mine = exchange(boxes.reshape(PEERS, BOX_ROWS, LANES))
+    mine = exchange(boxes)
     other = swap_cores(mine)
     core = lax.axis_index("core").astype(jnp.int32).reshape(1)
-    first_w, second_w, latent_w, *sums = run_loop(
+    keep, give, code_grad, code_squares = main_call(
         core,
         mine.reshape(PEERS * BOX_ROWS, LANES),
         other.reshape(PEERS * BOX_ROWS, LANES),
         codes,
     )
-    keep, give = weight_boxes(core, codes, first_w, second_w, *sums)
     pair_sum = (keep + swap_cores(give)).reshape(PEERS, BOX_ROWS, LANES)
-    code_grad, code_squares = code_grads(codes, latent_w, sums[1], sums[4])
-    pair_sum, code_grad, code_squares = lax.optimization_barrier((pair_sum, code_grad, code_squares))
     shard, squares = sum_shards(exchange(pair_sum).reshape(PEERS * BOX_ROWS, LANES), code_squares)
-    squares = squares + swap_cores(squares)
-    seen = exchange(jnp.broadcast_to(squares, (PEERS, 8, LANES)))
+    squares = sum_everywhere(squares)
     flat = lambda v: v.reshape(SHARD_ROWS, LANES)
     out = update_all(
-        seen.reshape(PEERS * 8, LANES),
+        squares,
         shard,
         flat(weights_flat),
         flat(moment_one),

time: 98.1 us -> 109 us (1.11)
  waiting for transfers between devices: 4.89 us -> 27.5 us
  blocking collectives: 63.9 us -> 48.5 us
  starting transfers between devices: 0.44 us -> 3.69 us
  Pallas kernels: 26.4 us -> 27.8 us
  local copies, waits for them, and re-layouts: 1.37 us -> 0.02 us
    ppermute x0 -> x6, waiting for transfers between devices: none -> 21.9 us  [the longest x4 14.4 us: sum_everywhere(): v = v + lax.ppermute(v, 'wide', moves)]
    all_to_all x3 -> x2, blocking collectives: 63.9 us -> 48.5 us  [exchange(): return lax.all_to_all(v, ('z', 'wide'), split_axis=0, concat_axis=0)]
    ppermute x0 -> x6, starting transfers between devices: none -> 3.44 us  [the longest x4 2.48 us: sum_everywhere(): v = v + lax.ppermute(v, 'wide', moves)]
    pallas_call x4 -> x2, Pallas kernels: 25 us -> 26.6 us  [the longest x1 24.1 us: main_call(): pl.pallas_call(main_kernel, out_shape=(boxes, boxes, f32(CODE_ROWS, LATEN...]
    unnamed x14 -> x12, local copies, waits for them, and re-layouts: 1.35 us -> 0.02 us
  transfers between devices with their start and end apart: 3 -> 9, of which waited for: 3 -> 9; matrix products, arithmetic and copies ran while one was open for 0% -> 0% of each run, Pallas kernels for 1% -> 0%
where the time goes in v9:
time: 109 us; the launch traced here: 108 us
  blocking collectives  48.5 us (44%)
  Pallas kernels  27.8 us (26%)
  waiting for transfers between devices  27.5 us (25%)
  starting transfers between devices  3.69 us (3%)
    all_to_all x2, blocking collectives, exchange(): return lax.all_to_all(v, ('z', 'wide'), split_axis=0, concat_axis=0)  48.5 us
    pallas_call x1, Pallas kernels, main_call(): pl.pallas_call(main_kernel, out_shape=(boxes, boxes, f32(CODE_ROWS, LATEN...  24.1 us
    ppermute x4, waiting for transfers between devices, sum_everywhere(): v = v + lax.ppermute(v, 'wide', moves)  14.4 us
    ppermute x2, waiting for transfers between devices, sum_everywhere(): v = v + lax.ppermute(v, 'z', list(enumerate(pairs)))  7.46 us
    ppermute x3, waiting for transfers between devices, swap_cores(): return lax.ppermute(v, 'core', [(0, 1), (1, 0)])  5.56 us
    ppermute x4, starting transfers between devices, sum_everywhere(): v = v + lax.ppermute(v, 'wide', moves)  2.48 us
    pallas_call x1, Pallas kernels, pack_boxes(): pl.pallas_call(pack_kernel, out_shape=f32(PEERS, BOX_ROWS, LANES), in_spe...  2.44 us
  transfers between devices with their start and end apart: 9, of which 9 were waited for; matrix products, arithmetic and copies ran while one was open for 0% of the time, Pallas kernels for 0%

profile of v9, /device:TPU:0, one launch (start us, length us, event | category | flops | bytes accessed | tf_op | source)
XLA Modules:
  0.0 108.3 jit_solution(5406237417376053394)
XLA Ops:
  0.6 2.4 %shard_map.168 = f32[64,24,128]{2,1,0:T(8,128)} custom-call(f32[21,128]{1,0:T(8,128)} %bitcast.19, f32[3,1024]{1,0:T(4,128)} %coords_hbm.1, f32[1,1024]{1,0:T(1,128)} %bitcast.24, s32[1,1024]{1,0:T(1,128)} %bitcast.25), custom_call_target="tpu_custom_call" | custom-call | tf_op jit(solution)/shard_map/pallas_call | solution.py:663
  3.1 0.0 copy-start
  3.1 27.6 %all_to_all.10 = f32[64,24,128]{2,1,0:T(8,128)S(1)} all-to-all(f32[64,24,128]{2,1,0:T(8,128)} %shard_map.168), channel_id=1, replica_groups=mesh['z'=4,'core'=2,'wide'=16] {'z','wide'}, dimensions={0} | all-to-all | bytes 1572864 | tf_op jit(solution)/shard_map/all_to_all | solution.py:846
  30.7 0.0 collective-permute-start
  30.7 2.3 %collective-permute-done = f32[64,24,128]{2,1,0:T(8,128)S(1)} collective-permute-done((f32[64,24,128]{2,1,0:T(8,128)S(1)}, f32[64,24,128]{2,1,0:T(8,128)S(1)}, u32[]{:S(2)}, u32[]{:S(2)}) %collective-permute-start) | collective-permute-done | bytes 786464 | tf_op jit(solution)/shard_map/ppermute | solution.py:842
  33.0 0.0 copy-done
  33.0 24.1 %shard_map.169 = (f32[1536,128]{1,0:T(8,128)S(1)}, f32[1536,128]{1,0:T(8,128)S(1)}, f32[256,256]{1,0:T(8,128)S(1)}, f32[8,128]{1,0:T(8,128)S(1)}) custom-call(s32[1]{0:T(128)} %bitcast.core_ref, f32[1536,128]{1,0:T(8,128)S(1)} %bitcast.16, f32[1536,128]{1,0:T(8,128)S(1)} %bitcast.18, f32[256,256]{1,0:T(8,128)S(1)} %copy-done), custom_call_target="tpu_custom_call" | custom-call | tf_op jit(solution)/shard_map/pallas_call | solution.py:736
  57.2 0.2 collective-permute-start.1
  57.4 2.1 %collective-permute-done.1 = f32[1536,128]{1,0:T(8,128)S(1)} collective-permute-done((f32[1536,128]{1,0:T(8,128)S(1)}, f32[1536,128]{1,0:T(8,128)S(1)}, u32[]{:S(2)}, u32[]{:S(2)}) %collective-permute-start.1) | collective-permute-done | bytes 786464 | tf_op jit(solution)/shard_map/ppermute | solution.py:842
  59.5 0.1 add.24
  59.6 20.8 %all_to_all.11 = f32[64,24,128]{2,1,0:T(8,128)S(1)} all-to-all(f32[64,24,128]{2,1,0:T(8,128)S(1)} %bitcast.23), channel_id=1, replica_groups=mesh['z'=4,'core'=2,'wide'=16] {'z','wide'}, dimensions={0} | all-to-all | bytes 1572864 | tf_op jit(solution)/shard_map/all_to_all | solution.py:846
  80.5 0.2 shard_map.170
  80.6 0.0 collective-permute-start.2
  80.6 1.2 %collective-permute-done.2 = f32[8,128]{1,0:T(8,128)S(1)} collective-permute-done((f32[8,128]{1,0:T(8,128)S(1)}, f32[8,128]{1,0:T(8,128)S(1)}, u32[]{:S(2)}, u32[]{:S(2)}) %collective-permute-start.2) | collective-permute-done | bytes 4128 | tf_op jit(solution)/shard_map/ppermute | solution.py:842
  81.8 0.2 collective-permute-start.3
  82.0 3.4 %collective-permute-done.3 = f32[8,128]{1,0:T(8,128)S(1)} collective-permute-done((f32[8,128]{1,0:T(8,128)S(1)}, f32[8,128]{1,0:T(8,128)S(1)}, u32[]{:S(2)}, u32[]{:S(2)}) %collective-permute-start.3) | collective-permute-done | bytes 4128 | tf_op jit(solution)/shard_map/ppermute | solution.py:853
  85.4 0.7 collective-permute-start.4
  86.1 4.1 %collective-permute-done.4 = f32[8,128]{1,0:T(8,128)S(1)} collective-permute-done((f32[8,128]{1,0:T(8,128)S(1)}, f32[8,128]{1,0:T(8,128)S(1)}, u32[]{:S(2)}, u32[]{:S(2)}) %collective-permute-start.4) | collective-permute-done | bytes 4128 | tf_op jit(solution)/shard_map/ppermute | solution.py:853
  90.2 0.6 collective-permute-start.5
  90.8 3.0 %collective-permute-done.5 = f32[8,128]{1,0:T(8,128)S(1)} collective-permute-done((f32[8,128]{1,0:T(8,128)S(1)}, f32[8,128]{1,0:T(8,128)S(1)}, u32[]{:S(2)}, u32[]{:S(2)}) %collective-permute-start.5) | collective-permute-done | bytes 4128 | tf_op jit(solution)/shard_map/ppermute | solution.py:857
  93.8 0.6 collective-permute-start.6
  94.4 4.2 %collective-permute-done.6 = f32[8,128]{1,0:T(8,128)S(1)} collective-permute-done((f32[8,128]{1,0:T(8,128)S(1)}, f32[8,128]{1,0:T(8,128)S(1)}, u32[]{:S(2)}, u32[]{:S(2)}) %collective-permute-start.6) | collective-permute-done | bytes 4128 | tf_op jit(solution)/shard_map/ppermute | solution.py:857
  98.7 0.7 collective-permute-start.7
  99.4 2.9 %collective-permute-done.7 = f32[8,128]{1,0:T(8,128)S(1)} collective-permute-done((f32[8,128]{1,0:T(8,128)S(1)}, f32[8,128]{1,0:T(8,128)S(1)}, u32[]{:S(2)}, u32[]{:S(2)}) %collective-permute-start.7) | collective-permute-done | bytes 4128 | tf_op jit(solution)/shard_map/ppermute | solution.py:857
  102.3 0.6 collective-permute-start.8
  102.8 4.3 %collective-permute-done.8 = f32[8,128]{1,0:T(8,128)S(1)} collective-permute-done((f32[8,128]{1,0:T(8,128)S(1)}, f32[8,128]{1,0:T(8,128)S(1)}, u32[]{:S(2)}, u32[]{:S(2)}) %collective-permute-start.8) | collective-permute-done | bytes 4128 | tf_op jit(solution)/shard_map/ppermute | solution.py:857
  107.2 0.0 copy-done.1
  107.2 0.0 copy-done.2
  107.2 0.0 copy-done.5
  107.2 0.0 copy-done.4
  107.2 0.0 copy-done.3
  107.2 1.1 %shard_map.171 = (f32[1,1]{1,0:T(1,128)}, f32[1,1]{1,0:T(1,128)}, f32[21,128]{1,0:T(8,128)}, f32[21,128]{1,0:T(8,128)}, f32[21,128]{1,0:T(8,128)}, /*index=5*/bf...) custom-call(f32[8,128]{1,0:T(8,128)S(1)} %add.31.squares_ref, ...), custom_call_target="tpu_custom_call" | custom-call | tf_op jit(solution)/shard_map/pallas_call | solution.py:832
  (12 shorter events, 0.0 us)
Async XLA Ops:
  3.1 29.9 %copy-start = (f32[256,256]{1,0:T(8,128)S(1)}, f32[256,256]{1,0:T(8,128)}, u32[]{:S(2)}) copy-start(f32[256,256]{1,0:T(8,128)} %codes_ref.3) | copy-start | bytes 786436
  30.7 2.3 %collective-permute-start = (f32[64,24,128]{2,1,0:T(8,128)S(1)}, f32[64,24,128]{2,1,0:T(8,128)S(1)}, u32[]{:S(2)}, u32[]{:S(2)}) collective-permute-start(f32[64,24,128]{2,1,0:T(8,128)S(1)} %all_to_all.10), channel_id=1, source_target_pairs={{0,16},{16,0},{1,17},{17,1},{2,18},{18,2},{3,19},{19,3},{4,20},{20... | collective-permute-start | bytes 2359304 | tf_op jit(solution)/shard_map/ppermute | solution.py:842
  57.2 2.4 %collective-permute-start.1 = (f32[1536,128]{1,0:T(8,128)S(1)}, f32[1536,128]{1,0:T(8,128)S(1)}, u32[]{:S(2)}, u32[]{:S(2)}) collective-permute-start(f32[1536,128]{1,0:T(8,128)S(1)} %get-tuple-element.27), channel_id=1, source_target_pairs={{0,16},{16,0},{1,17},{17,1},{2,18},{18,2},{3,19},{19,3},{4,20},{20... | collective-permute-start | bytes 2359304 | tf_op jit(solution)/shard_map/ppermute | solution.py:842
  80.5 26.7 %copy-start.1 = (f32[256,256]{1,0:T(8,128)S(1)}, f32[256,256]{1,0:T(8,128)}, u32[]{:S(2)}) copy-start(f32[256,256]{1,0:T(8,128)} %code_first_ref.1) | copy-start | bytes 786436
  80.5 26.7 %copy-start.2 = (f32[256,256]{1,0:T(8,128)S(1)}, f32[256,256]{1,0:T(8,128)}, u32[]{:S(2)}) copy-start(f32[256,256]{1,0:T(8,128)} %code_second_ref.1) | copy-start | bytes 786436
  80.6 1.2 %collective-permute-start.2 = (f32[8,128]{1,0:T(8,128)S(1)}, f32[8,128]{1,0:T(8,128)S(1)}, u32[]{:S(2)}, u32[]{:S(2)}) collective-permute-start(f32[8,128]{1,0:T(8,128)S(1)} %get-tuple-element.29), channel_id=1, source_target_pairs={{0,16},{16,0},{1,17},{17,1},{2,18},{18,2},{3,19},{19,3},{4,20},{20... | collective-permute-start | bytes 12296 | tf_op jit(solution)/shard_map/ppermute | solution.py:842
  81.8 3.6 %collective-permute-start.3 = (f32[8,128]{1,0:T(8,128)S(1)}, f32[8,128]{1,0:T(8,128)S(1)}, u32[]{:S(2)}, u32[]{:S(2)}) collective-permute-start(f32[8,128]{1,0:T(8,128)S(1)} %add.25), channel_id=1, source_target_pairs={{0,32},{32,0},{64,96},{96,64},{1,33},{33,1},{65,97},{97,65},{2,34}... | collective-permute-start | bytes 12296 | tf_op jit(solution)/shard_map/ppermute | solution.py:853
  85.4 4.8 %collective-permute-start.4 = (f32[8,128]{1,0:T(8,128)S(1)}, f32[8,128]{1,0:T(8,128)S(1)}, u32[]{:S(2)}, u32[]{:S(2)}) collective-permute-start(f32[8,128]{1,0:T(8,128)S(1)} %add.26), channel_id=1, source_target_pairs={{0,96},{32,64},{64,32},{96,0},{1,97},{33,65},{65,33},{97,1},{2,98}... | collective-permute-start | bytes 12296 | tf_op jit(solution)/shard_map/ppermute | solution.py:853
  90.2 3.6 %collective-permute-start.5 = (f32[8,128]{1,0:T(8,128)S(1)}, f32[8,128]{1,0:T(8,128)S(1)}, u32[]{:S(2)}, u32[]{:S(2)}) collective-permute-start(f32[8,128]{1,0:T(8,128)S(1)} %add.27), channel_id=1, source_target_pairs={{0,4},{1,5},{2,6},{3,7},{4,0},{5,1},{6,2},{7,3},{8,12},{9,13},{10,... | collective-permute-start | bytes 12296 | tf_op jit(solution)/shard_map/ppermute | solution.py:857
  93.8 4.8 %collective-permute-start.6 = (f32[8,128]{1,0:T(8,128)S(1)}, f32[8,128]{1,0:T(8,128)S(1)}, u32[]{:S(2)}, u32[]{:S(2)}) collective-permute-start(f32[8,128]{1,0:T(8,128)S(1)} %add.28), channel_id=1, source_target_pairs={{0,12},{1,13},{2,14},{3,15},{4,8},{5,9},{6,10},{7,11},{8,4},{9,5},... | collective-permute-start | bytes 12296 | tf_op jit(solution)/shard_map/ppermute | solution.py:857
  98.6 8.5 %copy-start.5 = (f32[2688]{0:T(1024)S(1)}, f32[2688]{0:T(1024)}, u32[]{:S(2)}) copy-start(f32[2688]{0:T(1024)} %param.11) | copy-start | bytes 32260
  98.7 3.6 %collective-permute-start.7 = (f32[8,128]{1,0:T(8,128)S(1)}, f32[8,128]{1,0:T(8,128)S(1)}, u32[]{:S(2)}, u32[]{:S(2)}) collective-permute-start(f32[8,128]{1,0:T(8,128)S(1)} %add.29), channel_id=1, source_target_pairs={{0,1},{1,0},{2,3},{3,2},{4,5},{5,4},{6,7},{7,6},{8,9},{9,8},{10,11... | collective-permute-start | bytes 12296 | tf_op jit(solution)/shard_map/ppermute | solution.py:857
  102.3 4.9 %copy-start.4 = (f32[2688]{0:T(1024)S(1)}, f32[2688]{0:T(1024)}, u32[]{:S(2)}) copy-start(f32[2688]{0:T(1024)} %param.10) | copy-start | bytes 32260
  102.3 4.9 %copy-start.3 = (f32[2688]{0:T(1024)S(1)}, f32[2688]{0:T(1024)}, u32[]{:S(2)}) copy-start(f32[2688]{0:T(1024)} %param.9) | copy-start | bytes 32260
  102.3 4.9 %collective-permute-start.8 = (f32[8,128]{1,0:T(8,128)S(1)}, f32[8,128]{1,0:T(8,128)S(1)}, u32[]{:S(2)}, u32[]{:S(2)}) collective-permute-start(f32[8,128]{1,0:T(8,128)S(1)} %add.30), channel_id=1, source_target_pairs={{0,3},{1,2},{2,1},{3,0},{4,7},{5,6},{6,5},{7,4},{8,11},{9,10},{10,... | collective-permute-start | bytes 12296 | tf_op jit(solution)/shard_map/ppermute | solution.py:857

commit v10 on v9

--- a/solution.py
+++ b/solution.py
@@ -32,7 +32,7 @@
 POINTS_DEV = 1024
 CODE_ROWS = 256
 FLAT_ROWS = DEVICES * SHARD_ROWS
-BLOCK = 512
+BLOCK = 256
 SUBS = 4
 TILES = BLOCK // LANES
 ALL_POINTS = POINTS_DEV * DEVICES
@@ -175,35 +175,23 @@
             out_ref[group * 8 : group * 8 + 8, c * LANES : (c + 1) * LANES] = value
 
 
-def pack_units(value_ref, flat_ref, count, stride_rows, extra, first_entry, adding):
+def pack_group(flat_ref, tiles, first, shift, stride_rows, extra):
     lane = rows_of_lanes(1, (8, LANES))
-    slope = rows_of_lanes(0, (8, LANES)) * extra
+    start = rows_of_lanes(0, (8, LANES)) * extra + shift
+    wraps = shift + 7 * extra >= LANES
+    turn = lax.bitwise_and(lane - start, LANES - 1)
     zero = jnp.zeros((8, LANES), F32)
-    for group, first, shift in unit_groups(count, stride_rows, extra, first_entry):
-        start = slope + shift
-        wraps = shift + 7 * extra >= LANES
-        wanted = range(stride_rows, stride_rows + 1 + wraps + 1) if adding else range(stride_rows)
-        rolled = {}
-
-        turn = lax.bitwise_and(lane - start, LANES - 1)
-
-        def tile(c, rolled=rolled, group=group, turn=turn):
-            if c < 0 or c > stride_rows:
-                return zero
-            if c not in rolled:
-                value = value_ref[group * 8 : group * 8 + 8, c * LANES : (c + 1) * LANES]
-                rolled[c] = jnp.take_along_axis(value, turn, axis=1, mode="promise_in_bounds")
-            return rolled[c]
-
-        for a in wanted:
-            value = jnp.where(lane >= start, tile(a), tile(a - 1))
-            if wraps:
-                value = jnp.where(lane >= start - LANES, value, tile(a - 2))
-            rows = pl.ds(first + a, 8, stride=stride_rows)
-            if adding:
-                flat_ref[rows, :] = flat_ref[rows, :] + value
-            else:
-                flat_ref[rows, :] = value
+    turned = [jnp.take_along_axis(v, turn, axis=1, mode="promise_in_bounds") for v in tiles]
+    turned = [zero, zero] + turned + [zero, zero]
+    for a in range(stride_rows + 2 + wraps):
+        value = jnp.where(lane >= start, turned[a + 2], turned[a + 1])
+        if wraps:
+            value = jnp.where(lane >= start - LANES, value, turned[a])
+        rows = pl.ds(first + a, 8, stride=stride_rows)
+        if 1 + wraps <= a < stride_rows:
+            flat_ref[rows, :] = value
+        else:
+            flat_ref[rows, :] = flat_ref[rows, :] + value
 
 
 FIRST_UNITS = (32, 2, 5, 0)
@@ -530,7 +518,7 @@
         lax.fori_loop(0, steps, step_body, 0)
 
 
-def code_kernel(codes_ref, latent_w, sum_codes, sum_count, code_grad_ref, squares_ref):
+def code_kernel(codes_ref, latent_w, sum_codes, sum_count, sum_loss, code_grad_ref, facts_ref):
     codes = codes_ref[...]
     count = jnp.sum(sum_count[...], axis=1, keepdims=True)
     turned_hi, turned_lo = halves(sum_codes[...].T)
@@ -540,7 +528,10 @@
     )
     code_grad = code_grad + (2.0 * CODE_WEIGHT / ALL_POINTS) * count * codes
     code_grad_ref[...] = code_grad
-    squares_ref[...] = jnp.broadcast_to(total_of(code_grad * code_grad), squares_ref.shape)
+    loss = jnp.sum(sum_loss[0:1, :], axis=1, keepdims=True)
+    loss = (loss + CODE_WEIGHT * total_of(count * codes * codes)) / ALL_POINTS
+    left = rows_of_lanes(1, facts_ref.shape) < LANES // 2
+    facts_ref[...] = jnp.where(left, total_of(code_grad * code_grad), loss)
 
 
 def norm_parts(direction, gain):
@@ -557,91 +548,91 @@
     sum_codes,
     sum_coord,
     sum_head,
-    sum_count,
+    _,
     sum_loss,
     keep_ref,
     give_ref,
     flat,
-    first_grad,
-    second_grad,
 ):
     core = core_ref[0]
     codes = codes_ref[...]
     by_code = sum_codes[...]
-    count = jnp.sum(sum_count[...], axis=1, keepdims=True)
-    loss = jnp.sum(sum_loss[0:1, :], axis=1, keepdims=True)
-    loss = loss + CODE_WEIGHT * total_of(count * codes * codes)
-    loss = loss / ALL_POINTS
-
     code_hi, code_lo = halves(codes)
     by_hi, by_lo = halves(by_code)
     latent_grad = mm(beside(by_hi, by_hi, by_lo), stacked(code_hi, code_lo, code_hi))
-    bias_grad = jnp.sum(by_code, axis=1, keepdims=True)
-
-    lane = rows_of_lanes(1, (256, LANES))
-    real = rows_of_lanes(0, (256, LANES)) < MIDDLE
-    near_grad = 0.0
-    for i in range(3):
-        column = jnp.sum(sum_coord[:, i * LANES : (i + 1) * LANES], axis=1, keepdims=True)
-        near_grad = jnp.where(lane == i, column, near_grad)
-    low_grad = latent_grad[0:256, :]
-    first_low = first_w[:, : 2 * LANES]
-    first_near = jnp.where(lane < 3, first_w[:, 2 * LANES :], 0.0)
-    root, scale = norm_parts(beside(first_low, first_near), first_w[:, 2 * LANES + 3 : 2 * LANES + 4])
-    along = jnp.sum(first_low * low_grad, axis=1, keepdims=True)
-    along = along + jnp.sum(first_near * near_grad, axis=1, keepdims=True)
-    inward = scale * root * root * along
-    end = scale * near_grad - first_near * inward
-    end = jnp.where(lane == 3, root * along, end)
-    end = jnp.where(lane == 4, bias_grad[0:256, :], end)
-    low_grad = scale * low_grad - first_low * inward
-    first_grad[:, : 2 * LANES] = jnp.where(beside(real, real), low_grad, 0.0)
-    first_grad[:, 2 * LANES :] = jnp.where(real, end, 0.0)
-
-    is_hidden = rows_of_lanes(1, (HID, 256)) < MIDDLE
-    hidden_grad = sum_two[...]
-    moved = pltpu.roll(latent_grad[256:768, :], 256 - 3, 1)
-    grad_a = jnp.where(is_hidden, hidden_grad, moved)
-    grad_b = jnp.where(is_hidden, moved, hidden_grad)
-    second_a = second_w[:, 0:256]
-    second_b = second_w[:, 256:512]
-    root, scale = norm_parts(second_w[:, 0:512], second_w[:, 512:513])
-    along = jnp.sum(second_a * grad_a + second_b * grad_b, axis=1, keepdims=True)
-    inward = scale * root * root * along
-    second_grad[:, 0:256] = scale * grad_a - second_a * inward
-    second_grad[:, 256:512] = scale * grad_b - second_b * inward
-    head_grad = jnp.sum(sum_head[...], axis=1, keepdims=True)
-    lane = rows_of_lanes(1, (HID, LANES))
-    end = jnp.where(lane == 0, root * along, 0.0)
-    end = jnp.where(lane == 1, bias_grad[256:768, :], end)
-    second_grad[:, 512:640] = jnp.where(lane == 2, head_grad, end)
 
     flat[...] = jnp.zeros(flat.shape, F32)
-    for adding in (False, True):
-        pack_units(first_grad, flat, *FIRST_UNITS, adding)
-        pack_units(second_grad, flat, *SECOND_UNITS, adding)
+    lane = rows_of_lanes(1, (8, LANES))
+    line = rows_of_lanes(0, (8, LANES))
+
+    def lane_sum(v):
+        return jnp.sum(v, axis=1, keepdims=True)
+
+    for group, first, shift in unit_groups(*FIRST_UNITS):
+        rows = slice(group * 8, group * 8 + 8)
+        raw = [first_w[rows, c * LANES : (c + 1) * LANES] for c in range(3)]
+        gain = raw[2][:, 3:4]
+        raw[2] = jnp.where(lane < 3, raw[2], 0.0)
+        grad = [latent_grad[rows, c * LANES : (c + 1) * LANES] for c in range(2)]
+        near = 0.0
+        for i in range(3):
+            near = jnp.where(
+                lane == i, lane_sum(sum_coord[rows, i * LANES : (i + 1) * LANES]), near
+            )
+        grad.append(near)
+        root = lax.rsqrt(lane_sum(sum(v * v for v in raw)) + 1e-12)
+        scale = gain * root
+        along = lane_sum(sum(v * g for v, g in zip(raw, grad)))
+        inward = scale * root * root * along
+        tiles = [scale * g - v * inward for v, g in zip(raw, grad)]
+        tiles[2] = jnp.where(lane == 3, root * along, tiles[2])
+        bias = lane_sum(by_code[rows, :LANES] + by_code[rows, LANES:])
+        tiles[2] = jnp.where(lane == 4, bias, tiles[2])
+        if group * 8 + 8 > MIDDLE:
+            tiles = [jnp.where(line < MIDDLE - group * 8, v, 0.0) for v in tiles]
+        pack_group(flat, tiles, first, shift, *FIRST_UNITS[1:3])
+
+    edge = lane < MIDDLE - LANES
+    for group, first, shift in unit_groups(*SECOND_UNITS):
+        rows = slice(group * 8, group * 8 + 8)
+        low = slice(256 + group * 8, 256 + group * 8 + 8)
+        raw = [second_w[rows, c * LANES : (c + 1) * LANES] for c in range(4)]
+        gain = second_w[rows, 512:513]
+        hidden = [sum_two[rows, c * LANES : (c + 1) * LANES] for c in range(2)]
+        moved = pltpu.roll(latent_grad[low, :], 256 - 3, 1)
+        moved = [moved[:, :LANES], moved[:, LANES:]]
+        grad = [
+            hidden[0],
+            jnp.where(edge, hidden[1], moved[1]),
+            moved[0],
+            jnp.where(edge, moved[1], hidden[1]),
+        ]
+        root = lax.rsqrt(lane_sum(sum(v * v for v in raw)) + 1e-12)
+        scale = gain * root
+        along = lane_sum(sum(v * g for v, g in zip(raw, grad)))
+        inward = scale * root * root * along
+        tiles = [scale * g - v * inward for v, g in zip(raw, grad)]
+        end = jnp.where(lane == 0, root * along, 0.0)
+        end = jnp.where(lane == 1, lane_sum(by_code[low, :LANES] + by_code[low, LANES:]), end)
+        tiles.append(jnp.where(lane == 2, lane_sum(sum_head[rows, :]), end))
+        pack_group(flat, tiles, first, shift, *SECOND_UNITS[1:3])
+
     row = HEAD_ENTRY // LANES
     lane = rows_of_lanes(1, (1, LANES))
     bias_total = jnp.sum(sum_loss[1:2, :], axis=1, keepdims=True)
     flat[row : row + 1, :] = flat[row : row + 1, :] + jnp.where(
         lane == HEAD_ENTRY % LANES, bias_total, 0.0
     )
-    sub = rows_of_lanes(0, (8, LANES))
-    wide = rows_of_lanes(1, (8, LANES))
-    info = jnp.where((sub == 5) & (wide == 0), loss, 0.0)
+    size = 16 * SHARD_ROWS
     for which in range(2):
 
         @pl.when(core == which)
         def _(which=which):
-            for d in range(DEVICES):
-                z, c, w = d // 32, d // 16 % 2, d % 16
-                target = keep_ref if c == which else give_ref
-                box = (z * 16 + w) * BOX_ROWS
-                first = d * SHARD_ROWS
-                target[box : box + 16, :] = flat[first : first + 16, :]
-                target[box + 16 : box + 24, :] = jnp.where(
-                    sub < 5, flat[first + 16 : first + 24, :], info
-                )
+            for z in range(4):
+                for c in range(2):
+                    target = keep_ref if c == which else give_ref
+                    first = (z * 2 + c) * size
+                    target[z * size : (z + 1) * size, :] = flat[first : first + size, :]
 
 
 def vmem(count):
@@ -678,15 +669,13 @@
 
 
 def main_kernel(
-    core_ref, mine_ref, other_ref, codes_ref, keep_ref, give_ref, code_grad_ref, squares_ref, *scratch
+    core_ref, mine_ref, other_ref, codes_ref, keep_ref, give_ref, code_grad_ref, facts_ref, *scratch
 ):
     first_w, second_w, latent_w, *sums = scratch[:9]
-    flat, first_grad, second_grad = scratch[9:12]
-    loop_kernel(core_ref, mine_ref, other_ref, codes_ref, *scratch[:9], flat, *scratch[12:])
-    code_kernel(codes_ref, latent_w, sums[1], sums[4], code_grad_ref, squares_ref)
-    weight_kernel(
-        core_ref, codes_ref, first_w, second_w, *sums, keep_ref, give_ref, flat, first_grad, second_grad
-    )
+    flat = scratch[9]
+    loop_kernel(core_ref, mine_ref, other_ref, codes_ref, *scratch)
+    code_kernel(codes_ref, latent_w, sums[1], sums[4], sums[5], code_grad_ref, facts_ref)
+    weight_kernel(core_ref, codes_ref, first_w, second_w, *sums, keep_ref, give_ref, flat)
 
 
 def main_call(core, mine, other, codes):
@@ -703,8 +692,6 @@
         ((CODE_ROWS, LANES), F32),
         ((2, BLOCK), F32),
         ((FLAT_ROWS + 8, LANES), F32),
-        ((256, 3 * LANES), F32),
-        ((HID, 5 * LANES), F32),
         ((256, 512), BF16),
         ((HID, 1280), BF16),
         ((256, 1536), BF16),
@@ -732,7 +719,7 @@
         (pair, BF16),
         (pair, BF16),
     ]
-    boxes = f32(PEERS * BOX_ROWS, LANES)
+    boxes = f32(PEERS * SHARD_ROWS, LANES)
     return pl.pallas_call(
         main_kernel,
         out_shape=(boxes, boxes, f32(CODE_ROWS, LATENT), f32(8, LANES)),
@@ -752,30 +739,28 @@
     return (value_new, first_new, second_new)
 
 
-def shard_kernel(parts_ref, code_squares_ref, shard_ref, squares_ref):
-    total = parts_ref[0:BOX_ROWS, :]
+def shard_kernel(parts_ref, facts_ref, shard_ref, all_facts_ref):
+    total = parts_ref[0:SHARD_ROWS, :]
     for peer in range(1, PEERS):
-        total = total + parts_ref[peer * BOX_ROWS : (peer + 1) * BOX_ROWS, :]
+        total = total + parts_ref[peer * SHARD_ROWS : (peer + 1) * SHARD_ROWS, :]
     shard_ref[...] = total
-    grad = total[:SHARD_ROWS, :]
-    squares_ref[...] = code_squares_ref[...] + total_of(grad * grad)
-
-
-def sum_shards(parts, code_squares):
+    facts = facts_ref[...]
+    left = rows_of_lanes(1, facts.shape) < LANES // 2
+    all_facts_ref[...] = facts + jnp.where(left, total_of(total * total), 0.0)
+
+
+def sum_shards(parts, facts):
     return pl.pallas_call(
         shard_kernel,
-        out_shape=(
-            jax.ShapeDtypeStruct((BOX_ROWS, LANES), F32),
-            jax.ShapeDtypeStruct((8, LANES), F32),
-        ),
+        out_shape=(f32(SHARD_ROWS, LANES), f32(8, LANES)),
         in_specs=vmem(2),
         out_specs=tuple(vmem(2)),
         compiler_params=PARAMS,
-    )(parts, code_squares)
+    )(parts, facts)
 
 
 def update_kernel(
-    squares_ref,
+    seen_ref,
     shard_ref,
     weights_ref,
     moment_one_ref,
@@ -795,15 +780,16 @@
     code_second_out,
     codes_copy_out,
 ):
-    loss_out[...] = shard_ref[SHARD_ROWS : SHARD_ROWS + 1, 0:1]
-    norm = jnp.sqrt(squares_ref[0:1, 0:1])
+    total = jnp.sum(seen_ref[...], axis=0, keepdims=True)
+    loss_out[...] = total[:, LANES // 2 : LANES // 2 + 1]
+    norm = jnp.sqrt(total[:, 0:1])
     norm_out[...] = norm
     factor = jnp.minimum(1.0, CLIP / (norm + 1e-06))
     value, first, second = adam_update(
         weights_ref[...],
         moment_one_ref[...],
         moment_two_ref[...],
-        factor * shard_ref[0:SHARD_ROWS, :],
+        factor * shard_ref[...],
         WEIGHT_RATE,
     )
     weights_out[...] = value
@@ -846,18 +832,6 @@
     return lax.all_to_all(v, ("z", "wide"), split_axis=0, concat_axis=0)
 
 
-def sum_everywhere(v):
-    v = v + swap_cores(v)
-    flip = [1, 0, 3, 2], [3, 2, 1, 0]
-    for pairs in flip:
-        v = v + lax.ppermute(v, "z", list(enumerate(pairs)))
-    for stride in (4, 1):
-        for pairs in flip:
-            moves = [(d, d + (pairs[d // stride % 4] - d // stride % 4) * stride) for d in range(16)]
-            v = v + lax.ppermute(v, "wide", moves)
-    return v
-
-
 def body(
     weights_flat,
     moment_one,
@@ -878,18 +852,20 @@
     mine = exchange(boxes)
     other = swap_cores(mine)
     core = lax.axis_index("core").astype(jnp.int32).reshape(1)
-    keep, give, code_grad, code_squares = main_call(
+    keep, give, code_grad, facts = main_call(
         core,
         mine.reshape(PEERS * BOX_ROWS, LANES),
         other.reshape(PEERS * BOX_ROWS, LANES),
         codes,
     )
-    pair_sum = (keep + swap_cores(give)).reshape(PEERS, BOX_ROWS, LANES)
-    shard, squares = sum_shards(exchange(pair_sum).reshape(PEERS * BOX_ROWS, LANES), code_squares)
-    squares = sum_everywhere(squares)
+    pair_sum = (keep + swap_cores(give)).reshape(PEERS, 1, SHARD_ROWS * LANES)
+    parts = exchange(pair_sum).reshape(PEERS * SHARD_ROWS, LANES)
+    shard, facts = sum_shards(parts, facts)
+    facts = facts + swap_cores(facts)
+    facts = jnp.broadcast_to(facts[0:1], (PEERS, LANES)).reshape(PEERS, 1, LANES)
     flat = lambda v: v.reshape(SHARD_ROWS, LANES)
     out = update_all(
-        squares,
+        exchange(facts).reshape(PEERS, LANES),
         shard,
         flat(weights_flat),
         flat(moment_one),

time: 109 us -> 105 us (0.963)
  waiting for transfers between devices: 27.5 us -> 5.36 us
  blocking collectives: 48.5 us -> 62 us
  Pallas kernels: 27.8 us -> 36.5 us
  starting transfers between devices: 3.69 us -> 0.31 us
    ppermute x6 -> x0, waiting for transfers between devices: 21.9 us -> none  [the longest x4 14.4 us: sum_everywhere(): v = v + lax.ppermute(v, 'wide', moves)]
    all_to_all x2 -> x3, blocking collectives: 48.5 us -> 62 us  [exchange(): return lax.all_to_all(v, ('z', 'wide'), split_axis=0, concat_axis=0)]
    pallas_call x1, Pallas kernels: 24.1 us -> 32.7 us  [main_call(): pl.pallas_call(main_kernel, out_shape=(boxes, boxes, f32(CODE_ROWS, LATEN...]
    ppermute x6 -> x0, starting transfers between devices: 3.44 us -> none  [the longest x4 2.48 us: sum_everywhere(): v = v + lax.ppermute(v, 'wide', moves)]
  transfers between devices with their start and end apart: 9 -> 3, of which waited for: 9 -> 3; matrix products, arithmetic and copies ran while one was open for 0% -> 0% of each run, Pallas kernels for 0% -> 0%
where the time goes in v10:
time: 105 us
  blocking collectives  62 us (59%)
  Pallas kernels  36.5 us (35%)
  waiting for transfers between devices  5.36 us (5%)
    all_to_all x3, blocking collectives, exchange(): return lax.all_to_all(v, ('z', 'wide'), split_axis=0, concat_axis=0)  62 us
    pallas_call x1, Pallas kernels, main_call(): pl.pallas_call(main_kernel, out_shape=(boxes, boxes, f32(CODE_ROWS, LATEN...  32.7 us
    ppermute x3, waiting for transfers between devices, swap_cores(): return lax.ppermute(v, 'core', [(0, 1), (1, 0)])  5.36 us
    pallas_call x1, Pallas kernels, pack_boxes(): pl.pallas_call(pack_kernel, out_shape=f32(PEERS, BOX_ROWS, LANES), in_spe...  2.43 us
  transfers between devices with their start and end apart: 3, of which 3 were waited for; matrix products, arithmetic and copies ran while one was open for 0% of the time, Pallas kernels for 0%

profile of v10, /device:TPU:0, one launch (start us, length us, event | category | flops | bytes accessed | tf_op | source)
XLA Modules:
  0.0 105.0 jit_solution(4280971437846871262)
XLA Ops:
  0.6 2.4 %shard_map.168 = f32[64,24,128]{2,1,0:T(8,128)} custom-call(f32[21,128]{1,0:T(8,128)} %bitcast.23, f32[3,1024]{1,0:T(4,128)} %coords_hbm.1, f32[1,1024]{1,0:T(1,128)} %bitcast.28, s32[1,1024]{1,0:T(1,128)} %bitcast.29), custom_call_target="tpu_custom_call" | custom-call | tf_op jit(solution)/shard_map/pallas_call | solution.py:654
  3.1 0.0 copy-start
  3.1 27.6 %all_to_all.15 = f32[64,24,128]{2,1,0:T(8,128)S(1)} all-to-all(f32[64,24,128]{2,1,0:T(8,128)} %shard_map.168), channel_id=1, replica_groups=mesh['z'=4,'core'=2,'wide'=16] {'z','wide'}, dimensions={0} | all-to-all | bytes 1572864 | tf_op jit(solution)/shard_map/all_to_all | solution.py:832
  30.7 0.0 collective-permute-start
  30.7 2.3 %collective-permute-done = f32[64,24,128]{2,1,0:T(8,128)S(1)} collective-permute-done((f32[64,24,128]{2,1,0:T(8,128)S(1)}, f32[64,24,128]{2,1,0:T(8,128)S(1)}, u32[]{:S(2)}, u32[]{:S(2)}) %collective-permute-start) | collective-permute-done | bytes 786464 | tf_op jit(solution)/shard_map/ppermute | solution.py:828
  33.0 0.0 copy-done
  33.0 32.7 %shard_map.169 = (f32[1344,128]{1,0:T(8,128)S(1)}, f32[1344,128]{1,0:T(8,128)S(1)}, f32[256,256]{1,0:T(8,128)S(1)}, f32[8,128]{1,0:T(8,128)S(1)}) custom-call(s32[1]{0:T(128)} %bitcast.core_ref, f32[1536,128]{1,0:T(8,128)S(1)} %bitcast.19, f32[1536,128]{1,0:T(8,128)S(1)} %bitcast.21, f32[256,256]{1,0:T(8,128)S(1)} %copy-done), custom_call_target="tpu_custom_call" | custom-call | tf_op jit(solution)/shard_map/pallas_call | solution.py:723
  65.7 0.3 collective-permute-start.1
  66.0 1.9 %collective-permute-done.1 = f32[1344,128]{1,0:T(8,128)S(1)} collective-permute-done((f32[1344,128]{1,0:T(8,128)S(1)}, f32[1344,128]{1,0:T(8,128)S(1)}, u32[]{:S(2)}, u32[]{:S(2)}) %collective-permute-start.1) | collective-permute-done | bytes 688160 | tf_op jit(solution)/shard_map/ppermute | solution.py:828
  68.0 0.1 add.6
  68.0 20.1 %all_to_all.16 = f32[64,1,2688]{2,1,0:T(1,128)S(1)} all-to-all(f32[64,1,2688]{2,1,0:T(1,128)S(1)} %bitcast.27), channel_id=1, replica_groups=mesh['z'=4,'core'=2,'wide'=16] {'z','wide'}, dimensions={0} | all-to-all | bytes 1376256 | tf_op jit(solution)/shard_map/all_to_all | solution.py:832
  88.2 0.0 copy-start.1
  88.2 0.0 copy-start.2
  88.2 0.2 shard_map.170
  88.3 0.0 collective-permute-start.2
  88.3 1.2 %collective-permute-done.2 = f32[8,128]{1,0:T(8,128)S(1)} collective-permute-done((f32[8,128]{1,0:T(8,128)S(1)}, f32[8,128]{1,0:T(8,128)S(1)}, u32[]{:S(2)}, u32[]{:S(2)}) %collective-permute-start.2) | collective-permute-done | bytes 4128 | tf_op jit(solution)/shard_map/ppermute | solution.py:828
  89.5 0.0 copy-start.3
  89.5 0.0 copy-start.4
  89.5 0.0 copy-start.5
  89.6 14.2 %all_to_all.17 = f32[64,1,128]{2,1,0:T(1,128)S(1)} all-to-all(f32[64,1,128]{2,1,0:T(1,128)S(1)} %reshape.83), channel_id=1, replica_groups=mesh['z'=4,'core'=2,'wide'=16] {'z','wide'}, dimensions={0} | all-to-all | bytes 65536 | tf_op jit(solution)/shard_map/all_to_all | solution.py:832
  103.8 0.0 copy-done.1
  103.8 0.0 copy-done.2
  103.8 0.0 copy-done.3
  103.8 0.0 copy-done.4
  103.8 0.0 copy-done.5
  103.8 1.2 %shard_map.171 = (f32[1,1]{1,0:T(1,128)}, f32[1,1]{1,0:T(1,128)}, f32[21,128]{1,0:T(8,128)}, f32[21,128]{1,0:T(8,128)}, f32[21,128]{1,0:T(8,128)}, /*index=5*/bf...) custom-call(f32[64,128]{1,0:T(8,128)S(1)} %bitcast.22, ...), custom_call_target="tpu_custom_call" | custom-call | tf_op jit(solution)/shard_map/pallas_call | solution.py:818
  (3 shorter events, 0.0 us)
Async XLA Ops:
  3.1 29.9 %copy-start = (f32[256,256]{1,0:T(8,128)S(1)}, f32[256,256]{1,0:T(8,128)}, u32[]{:S(2)}) copy-start(f32[256,256]{1,0:T(8,128)} %codes_ref.3) | copy-start | bytes 786436
  30.7 2.3 %collective-permute-start = (f32[64,24,128]{2,1,0:T(8,128)S(1)}, f32[64,24,128]{2,1,0:T(8,128)S(1)}, u32[]{:S(2)}, u32[]{:S(2)}) collective-permute-start(f32[64,24,128]{2,1,0:T(8,128)S(1)} %all_to_all.15), channel_id=1, source_target_pairs={{0,16},{16,0},{1,17},{17,1},{2,18},{18,2},{3,19},{19,3},{4,20},{20... | collective-permute-start | bytes 2359304 | tf_op jit(solution)/shard_map/ppermute | solution.py:828
  65.7 2.2 %collective-permute-start.1 = (f32[1344,128]{1,0:T(8,128)S(1)}, f32[1344,128]{1,0:T(8,128)S(1)}, u32[]{:S(2)}, u32[]{:S(2)}) collective-permute-start(f32[1344,128]{1,0:T(8,128)S(1)} %get-tuple-element.27), channel_id=1, source_target_pairs={{0,16},{16,0},{1,17},{17,1},{2,18},{18,2},{3,19},{19,3},{4,20},{20... | collective-permute-start | bytes 2064392 | tf_op jit(solution)/shard_map/ppermute | solution.py:828
  88.2 15.6 %copy-start.1 = (f32[256,256]{1,0:T(8,128)S(1)}, f32[256,256]{1,0:T(8,128)}, u32[]{:S(2)}) copy-start(f32[256,256]{1,0:T(8,128)} %code_first_ref.1) | copy-start | bytes 786436
  88.2 15.6 %copy-start.2 = (f32[256,256]{1,0:T(8,128)S(1)}, f32[256,256]{1,0:T(8,128)}, u32[]{:S(2)}) copy-start(f32[256,256]{1,0:T(8,128)} %code_second_ref.1) | copy-start | bytes 786436
  88.3 1.2 %collective-permute-start.2 = (f32[8,128]{1,0:T(8,128)S(1)}, f32[8,128]{1,0:T(8,128)S(1)}, u32[]{:S(2)}, u32[]{:S(2)}) collective-permute-start(f32[8,128]{1,0:T(8,128)S(1)} %get-tuple-element.29), channel_id=1, source_target_pairs={{0,16},{16,0},{1,17},{17,1},{2,18},{18,2},{3,19},{19,3},{4,20},{20... | collective-permute-start | bytes 12296 | tf_op jit(solution)/shard_map/ppermute | solution.py:828
  89.5 14.3 %copy-start.3 = (f32[2688]{0:T(1024)S(1)}, f32[2688]{0:T(1024)}, u32[]{:S(2)}) copy-start(f32[2688]{0:T(1024)} %param.9) | copy-start | bytes 32260
  89.5 14.3 %copy-start.4 = (f32[2688]{0:T(1024)S(1)}, f32[2688]{0:T(1024)}, u32[]{:S(2)}) copy-start(f32[2688]{0:T(1024)} %param.10) | copy-start | bytes 32260
  89.5 14.3 %copy-start.5 = (f32[2688]{0:T(1024)S(1)}, f32[2688]{0:T(1024)}, u32[]{:S(2)}) copy-start(f32[2688]{0:T(1024)} %param.11) | copy-start | bytes 32260

commit v11 on v9

--- a/solution.py
+++ b/solution.py
@@ -32,7 +32,7 @@
 POINTS_DEV = 1024
 CODE_ROWS = 256
 FLAT_ROWS = DEVICES * SHARD_ROWS
-BLOCK = 512
+BLOCK = 256
 SUBS = 4
 TILES = BLOCK // LANES
 ALL_POINTS = POINTS_DEV * DEVICES
@@ -175,17 +175,15 @@
             out_ref[group * 8 : group * 8 + 8, c * LANES : (c + 1) * LANES] = value
 
 
-def pack_units(value_ref, flat_ref, count, stride_rows, extra, first_entry, adding):
+def pack_units(value_ref, flat_ref, count, stride_rows, extra, first_entry, tails):
     lane = rows_of_lanes(1, (8, LANES))
     slope = rows_of_lanes(0, (8, LANES)) * extra
     zero = jnp.zeros((8, LANES), F32)
     for group, first, shift in unit_groups(count, stride_rows, extra, first_entry):
         start = slope + shift
         wraps = shift + 7 * extra >= LANES
-        wanted = range(stride_rows, stride_rows + 1 + wraps + 1) if adding else range(stride_rows)
+        turn = lax.bitwise_and(lane - start, LANES - 1)
         rolled = {}
-
-        turn = lax.bitwise_and(lane - start, LANES - 1)
 
         def tile(c, rolled=rolled, group=group, turn=turn):
             if c < 0 or c > stride_rows:
@@ -195,15 +193,11 @@
                 rolled[c] = jnp.take_along_axis(value, turn, axis=1, mode="promise_in_bounds")
             return rolled[c]
 
-        for a in wanted:
+        for a in range(stride_rows, stride_rows + 2) if tails else range(stride_rows):
             value = jnp.where(lane >= start, tile(a), tile(a - 1))
             if wraps:
                 value = jnp.where(lane >= start - LANES, value, tile(a - 2))
-            rows = pl.ds(first + a, 8, stride=stride_rows)
-            if adding:
-                flat_ref[rows, :] = flat_ref[rows, :] + value
-            else:
-                flat_ref[rows, :] = value
+            flat_ref[pl.ds(first + a, 8, stride=stride_rows), :] = value
 
 
 FIRST_UNITS = (32, 2, 5, 0)
@@ -530,7 +524,7 @@
         lax.fori_loop(0, steps, step_body, 0)
 
 
-def code_kernel(codes_ref, latent_w, sum_codes, sum_count, code_grad_ref, squares_ref):
+def code_kernel(codes_ref, latent_w, sum_codes, sum_count, sum_loss, code_grad_ref, facts_ref):
     codes = codes_ref[...]
     count = jnp.sum(sum_count[...], axis=1, keepdims=True)
     turned_hi, turned_lo = halves(sum_codes[...].T)
@@ -540,7 +534,10 @@
     )
     code_grad = code_grad + (2.0 * CODE_WEIGHT / ALL_POINTS) * count * codes
     code_grad_ref[...] = code_grad
-    squares_ref[...] = jnp.broadcast_to(total_of(code_grad * code_grad), squares_ref.shape)
+    loss = jnp.sum(sum_loss[0:1, :], axis=1, keepdims=True)
+    loss = (loss + CODE_WEIGHT * total_of(count * codes * codes)) / ALL_POINTS
+    left = rows_of_lanes(1, facts_ref.shape) < LANES // 2
+    facts_ref[...] = jnp.where(left, total_of(code_grad * code_grad), loss)
 
 
 def norm_parts(direction, gain):
@@ -557,27 +554,23 @@
     sum_codes,
     sum_coord,
     sum_head,
-    sum_count,
+    _,
     sum_loss,
     keep_ref,
     give_ref,
     flat,
+    tails,
     first_grad,
     second_grad,
 ):
     core = core_ref[0]
     codes = codes_ref[...]
     by_code = sum_codes[...]
-    count = jnp.sum(sum_count[...], axis=1, keepdims=True)
-    loss = jnp.sum(sum_loss[0:1, :], axis=1, keepdims=True)
-    loss = loss + CODE_WEIGHT * total_of(count * codes * codes)
-    loss = loss / ALL_POINTS
-
     code_hi, code_lo = halves(codes)
     by_hi, by_lo = halves(by_code)
     latent_grad = mm(beside(by_hi, by_hi, by_lo), stacked(code_hi, code_lo, code_hi))
+
     bias_grad = jnp.sum(by_code, axis=1, keepdims=True)
-
     lane = rows_of_lanes(1, (256, LANES))
     real = rows_of_lanes(0, (256, LANES)) < MIDDLE
     near_grad = 0.0
@@ -616,32 +609,28 @@
     end = jnp.where(lane == 1, bias_grad[256:768, :], end)
     second_grad[:, 512:640] = jnp.where(lane == 2, head_grad, end)
 
-    flat[...] = jnp.zeros(flat.shape, F32)
-    for adding in (False, True):
-        pack_units(first_grad, flat, *FIRST_UNITS, adding)
-        pack_units(second_grad, flat, *SECOND_UNITS, adding)
+    for ref in (flat, tails):
+        ref[...] = jnp.zeros(ref.shape, F32)
+    pack_units(first_grad, flat, *FIRST_UNITS, False)
+    pack_units(second_grad, flat, *SECOND_UNITS, False)
+    pack_units(first_grad, tails, *FIRST_UNITS, True)
+    pack_units(second_grad, tails, *SECOND_UNITS, True)
     row = HEAD_ENTRY // LANES
     lane = rows_of_lanes(1, (1, LANES))
     bias_total = jnp.sum(sum_loss[1:2, :], axis=1, keepdims=True)
-    flat[row : row + 1, :] = flat[row : row + 1, :] + jnp.where(
-        lane == HEAD_ENTRY % LANES, bias_total, 0.0
-    )
-    sub = rows_of_lanes(0, (8, LANES))
-    wide = rows_of_lanes(1, (8, LANES))
-    info = jnp.where((sub == 5) & (wide == 0), loss, 0.0)
+    flat[row : row + 1, :] += jnp.where(lane == HEAD_ENTRY % LANES, bias_total, 0.0)
+    size = 16 * SHARD_ROWS
     for which in range(2):
 
         @pl.when(core == which)
         def _(which=which):
-            for d in range(DEVICES):
-                z, c, w = d // 32, d // 16 % 2, d % 16
-                target = keep_ref if c == which else give_ref
-                box = (z * 16 + w) * BOX_ROWS
-                first = d * SHARD_ROWS
-                target[box : box + 16, :] = flat[first : first + 16, :]
-                target[box + 16 : box + 24, :] = jnp.where(
-                    sub < 5, flat[first + 16 : first + 24, :], info
-                )
+            for z in range(4):
+                for c in range(2):
+                    target = keep_ref if c == which else give_ref
+                    first = (z * 2 + c) * size
+                    target[z * size : (z + 1) * size, :] = (
+                        flat[first : first + size, :] + tails[first : first + size, :]
+                    )
 
 
 def vmem(count):
@@ -678,15 +667,13 @@
 
 
 def main_kernel(
-    core_ref, mine_ref, other_ref, codes_ref, keep_ref, give_ref, code_grad_ref, squares_ref, *scratch
+    core_ref, mine_ref, other_ref, codes_ref, keep_ref, give_ref, code_grad_ref, facts_ref, *scratch
 ):
     first_w, second_w, latent_w, *sums = scratch[:9]
-    flat, first_grad, second_grad = scratch[9:12]
-    loop_kernel(core_ref, mine_ref, other_ref, codes_ref, *scratch[:9], flat, *scratch[12:])
-    code_kernel(codes_ref, latent_w, sums[1], sums[4], code_grad_ref, squares_ref)
-    weight_kernel(
-        core_ref, codes_ref, first_w, second_w, *sums, keep_ref, give_ref, flat, first_grad, second_grad
-    )
+    flat = scratch[9]
+    loop_kernel(core_ref, mine_ref, other_ref, codes_ref, *scratch[:-3])
+    code_kernel(codes_ref, latent_w, sums[1], sums[4], sums[5], code_grad_ref, facts_ref)
+    weight_kernel(core_ref, codes_ref, first_w, second_w, *sums, keep_ref, give_ref, flat, *scratch[-3:])
 
 
 def main_call(core, mine, other, codes):
@@ -703,8 +690,6 @@
         ((CODE_ROWS, LANES), F32),
         ((2, BLOCK), F32),
         ((FLAT_ROWS + 8, LANES), F32),
-        ((256, 3 * LANES), F32),
-        ((HID, 5 * LANES), F32),
         ((256, 512), BF16),
         ((HID, 1280), BF16),
         ((256, 1536), BF16),
@@ -731,8 +716,11 @@
         (pair_two, BF16),
         (pair, BF16),
         (pair, BF16),
+        ((FLAT_ROWS + 8, LANES), F32),
+        ((256, 3 * LANES), F32),
+        ((HID, 5 * LANES), F32),
     ]
-    boxes = f32(PEERS * BOX_ROWS, LANES)
+    boxes = f32(PEERS * SHARD_ROWS, LANES)
     return pl.pallas_call(
         main_kernel,
         out_shape=(boxes, boxes, f32(CODE_ROWS, LATENT), f32(8, LANES)),
@@ -752,30 +740,28 @@
     return (value_new, first_new, second_new)
 
 
-def shard_kernel(parts_ref, code_squares_ref, shard_ref, squares_ref):
-    total = parts_ref[0:BOX_ROWS, :]
+def shard_kernel(parts_ref, facts_ref, shard_ref, all_facts_ref):
+    total = parts_ref[0:SHARD_ROWS, :]
     for peer in range(1, PEERS):
-        total = total + parts_ref[peer * BOX_ROWS : (peer + 1) * BOX_ROWS, :]
+        total = total + parts_ref[peer * SHARD_ROWS : (peer + 1) * SHARD_ROWS, :]
     shard_ref[...] = total
-    grad = total[:SHARD_ROWS, :]
-    squares_ref[...] = code_squares_ref[...] + total_of(grad * grad)
-
-
-def sum_shards(parts, code_squares):
+    facts = facts_ref[...]
+    left = rows_of_lanes(1, facts.shape) < LANES // 2
+    all_facts_ref[...] = facts + jnp.where(left, total_of(total * total), 0.0)
+
+
+def sum_shards(parts, facts):
     return pl.pallas_call(
         shard_kernel,
-        out_shape=(
-            jax.ShapeDtypeStruct((BOX_ROWS, LANES), F32),
-            jax.ShapeDtypeStruct((8, LANES), F32),
-        ),
+        out_shape=(f32(SHARD_ROWS, LANES), f32(8, LANES)),
         in_specs=vmem(2),
         out_specs=tuple(vmem(2)),
         compiler_params=PARAMS,
-    )(parts, code_squares)
+    )(parts, facts)
 
 
 def update_kernel(
-    squares_ref,
+    seen_ref,
     shard_ref,
     weights_ref,
     moment_one_ref,
@@ -795,15 +781,16 @@
     code_second_out,
     codes_copy_out,
 ):
-    loss_out[...] = shard_ref[SHARD_ROWS : SHARD_ROWS + 1, 0:1]
-    norm = jnp.sqrt(squares_ref[0:1, 0:1])
+    total = jnp.sum(seen_ref[...], axis=0, keepdims=True)
+    loss_out[...] = total[:, LANES // 2 : LANES // 2 + 1]
+    norm = jnp.sqrt(total[:, 0:1])
     norm_out[...] = norm
     factor = jnp.minimum(1.0, CLIP / (norm + 1e-06))
     value, first, second = adam_update(
         weights_ref[...],
         moment_one_ref[...],
         moment_two_ref[...],
-        factor * shard_ref[0:SHARD_ROWS, :],
+        factor * shard_ref[...],
         WEIGHT_RATE,
     )
     weights_out[...] = value
@@ -846,18 +833,6 @@
     return lax.all_to_all(v, ("z", "wide"), split_axis=0, concat_axis=0)
 
 
-def sum_everywhere(v):
-    v = v + swap_cores(v)
-    flip = [1, 0, 3, 2], [3, 2, 1, 0]
-    for pairs in flip:
-        v = v + lax.ppermute(v, "z", list(enumerate(pairs)))
-    for stride in (4, 1):
-        for pairs in flip:
-            moves = [(d, d + (pairs[d // stride % 4] - d // stride % 4) * stride) for d in range(16)]
-            v = v + lax.ppermute(v, "wide", moves)
-    return v
-
-
 def body(
     weights_flat,
     moment_one,
@@ -878,18 +853,20 @@
     mine = exchange(boxes)
     other = swap_cores(mine)
     core = lax.axis_index("core").astype(jnp.int32).reshape(1)
-    keep, give, code_grad, code_squares = main_call(
+    keep, give, code_grad, facts = main_call(
         core,
         mine.reshape(PEERS * BOX_ROWS, LANES),
         other.reshape(PEERS * BOX_ROWS, LANES),
         codes,
     )
-    pair_sum = (keep + swap_cores(give)).reshape(PEERS, BOX_ROWS, LANES)
-    shard, squares = sum_shards(exchange(pair_sum).reshape(PEERS * BOX_ROWS, LANES), code_squares)
-    squares = sum_everywhere(squares)
+    pair_sum = (keep + swap_cores(give)).reshape(PEERS, 1, SHARD_ROWS * LANES)
+    parts = exchange(pair_sum).reshape(PEERS * SHARD_ROWS, LANES)
+    shard, facts = sum_shards(parts, facts)
+    facts = facts + swap_cores(facts)
+    facts = jnp.broadcast_to(facts[0:1], (PEERS, LANES)).reshape(PEERS, 1, LANES)
     flat = lambda v: v.reshape(SHARD_ROWS, LANES)
     out = update_all(
-        squares,
+        exchange(facts).reshape(PEERS, LANES),
         shard,
         flat(weights_flat),
         flat(moment_one),

time: 109 us -> 94.5 us (0.87)
  waiting for transfers between devices: 27.5 us -> 5.42 us
  blocking collectives: 48.5 us -> 61.7 us
  starting transfers between devices: 3.69 us -> 0.25 us
  Pallas kernels: 27.8 us -> 25.8 us
    ppermute x6 -> x0, waiting for transfers between devices: 21.9 us -> none  [the longest x4 14.4 us: sum_everywhere(): v = v + lax.ppermute(v, 'wide', moves)]
    all_to_all x2 -> x3, blocking collectives: 48.5 us -> 61.7 us  [exchange(): return lax.all_to_all(v, ('z', 'wide'), split_axis=0, concat_axis=0)]
    ppermute x6 -> x0, starting transfers between devices: 3.44 us -> none  [the longest x4 2.48 us: sum_everywhere(): v = v + lax.ppermute(v, 'wide', moves)]
    pallas_call x1, Pallas kernels: 24.1 us -> 22.1 us  [main_call(): pl.pallas_call(main_kernel, out_shape=(boxes, boxes, f32(CODE_ROWS, LATEN...]
  transfers between devices with their start and end apart: 9 -> 3, of which waited for: 9 -> 3; matrix products, arithmetic and copies ran while one was open for 0% -> 0% of each run, Pallas kernels for 0% -> 0%
where the time goes in v11:
time: 94.5 us; the launch traced here: 94.1 us
  blocking collectives  61.7 us (65%)
  Pallas kernels  25.8 us (27%)
  waiting for transfers between devices  5.42 us (6%)
    all_to_all x3, blocking collectives, exchange(): return lax.all_to_all(v, ('z', 'wide'), split_axis=0, concat_axis=0)  61.7 us
    pallas_call x1, Pallas kernels, main_call(): pl.pallas_call(main_kernel, out_shape=(boxes, boxes, f32(CODE_ROWS, LATEN...  22.1 us
    ppermute x3, waiting for transfers between devices, swap_cores(): return lax.ppermute(v, 'core', [(0, 1), (1, 0)])  5.42 us
    pallas_call x1, Pallas kernels, pack_boxes(): pl.pallas_call(pack_kernel, out_shape=f32(PEERS, BOX_ROWS, LANES), in_spe...  2.43 us
  transfers between devices with their start and end apart: 3, of which 3 were waited for; matrix products, arithmetic and copies ran while one was open for 0% of the time, Pallas kernels for 0%

profile of v11, /device:TPU:0, one launch (start us, length us, event | category | flops | bytes accessed | tf_op | source)
XLA Modules:
  0.0 94.1 jit_solution(2351892794064909436)
XLA Ops:
  0.6 2.4 %shard_map.168 = f32[64,24,128]{2,1,0:T(8,128)} custom-call(f32[21,128]{1,0:T(8,128)} %bitcast.23, f32[3,1024]{1,0:T(4,128)} %coords_hbm.1, f32[1,1024]{1,0:T(1,128)} %bitcast.28, s32[1,1024]{1,0:T(1,128)} %bitcast.29), custom_call_target="tpu_custom_call" | custom-call | tf_op jit(solution)/shard_map/pallas_call | solution.py:652
  3.1 0.0 copy-start
  3.1 27.6 %all_to_all.15 = f32[64,24,128]{2,1,0:T(8,128)S(1)} all-to-all(f32[64,24,128]{2,1,0:T(8,128)} %shard_map.168), channel_id=1, replica_groups=mesh['z'=4,'core'=2,'wide'=16] {'z','wide'}, dimensions={0} | all-to-all | bytes 1572864 | tf_op jit(solution)/shard_map/all_to_all | solution.py:833
  30.7 0.0 collective-permute-start
  30.7 2.3 %collective-permute-done = f32[64,24,128]{2,1,0:T(8,128)S(1)} collective-permute-done((f32[64,24,128]{2,1,0:T(8,128)S(1)}, f32[64,24,128]{2,1,0:T(8,128)S(1)}, u32[]{:S(2)}, u32[]{:S(2)}) %collective-permute-start) | collective-permute-done | bytes 786464 | tf_op jit(solution)/shard_map/ppermute | solution.py:829
  33.0 0.0 copy-done
  33.0 22.1 %shard_map.169 = (f32[1344,128]{1,0:T(8,128)S(1)}, f32[1344,128]{1,0:T(8,128)S(1)}, f32[256,256]{1,0:T(8,128)S(1)}, f32[8,128]{1,0:T(8,128)S(1)}) custom-call(s32[1]{0:T(128)} %bitcast.core_ref, f32[1536,128]{1,0:T(8,128)S(1)} %bitcast.19, f32[1536,128]{1,0:T(8,128)S(1)} %bitcast.21, f32[256,256]{1,0:T(8,128)S(1)} %copy-done), custom_call_target="tpu_custom_call" | custom-call | tf_op jit(solution)/shard_map/pallas_call | solution.py:724
  55.1 0.2 collective-permute-start.1
  55.4 2.0 %collective-permute-done.1 = f32[1344,128]{1,0:T(8,128)S(1)} collective-permute-done((f32[1344,128]{1,0:T(8,128)S(1)}, f32[1344,128]{1,0:T(8,128)S(1)}, u32[]{:S(2)}, u32[]{:S(2)}) %collective-permute-start.1) | collective-permute-done | bytes 688160 | tf_op jit(solution)/shard_map/ppermute | solution.py:829
  57.3 0.1 add.6
  57.4 19.8 %all_to_all.16 = f32[64,1,2688]{2,1,0:T(1,128)S(1)} all-to-all(f32[64,1,2688]{2,1,0:T(1,128)S(1)} %bitcast.27), channel_id=1, replica_groups=mesh['z'=4,'core'=2,'wide'=16] {'z','wide'}, dimensions={0} | all-to-all | bytes 1376256 | tf_op jit(solution)/shard_map/all_to_all | solution.py:833
  77.2 0.0 copy-start.1
  77.3 0.0 copy-start.2
  77.3 0.2 shard_map.170
  77.4 0.0 collective-permute-start.2
  77.4 1.2 %collective-permute-done.2 = f32[8,128]{1,0:T(8,128)S(1)} collective-permute-done((f32[8,128]{1,0:T(8,128)S(1)}, f32[8,128]{1,0:T(8,128)S(1)}, u32[]{:S(2)}, u32[]{:S(2)}) %collective-permute-start.2) | collective-permute-done | bytes 4128 | tf_op jit(solution)/shard_map/ppermute | solution.py:829
  78.6 0.0 copy-start.3
  78.6 0.0 copy-start.4
  78.6 0.0 copy-start.5
  78.6 14.2 %all_to_all.17 = f32[64,1,128]{2,1,0:T(1,128)S(1)} all-to-all(f32[64,1,128]{2,1,0:T(1,128)S(1)} %reshape.83), channel_id=1, replica_groups=mesh['z'=4,'core'=2,'wide'=16] {'z','wide'}, dimensions={0} | all-to-all | bytes 65536 | tf_op jit(solution)/shard_map/all_to_all | solution.py:833
  92.9 0.0 copy-done.1
  92.9 0.0 copy-done.2
  92.9 0.0 copy-done.3
  92.9 0.0 copy-done.4
  92.9 0.0 copy-done.5
  92.9 1.2 %shard_map.171 = (f32[1,1]{1,0:T(1,128)}, f32[1,1]{1,0:T(1,128)}, f32[21,128]{1,0:T(8,128)}, f32[21,128]{1,0:T(8,128)}, f32[21,128]{1,0:T(8,128)}, /*index=5*/bf...) custom-call(f32[64,128]{1,0:T(8,128)S(1)} %bitcast.22, ...), custom_call_target="tpu_custom_call" | custom-call | tf_op jit(solution)/shard_map/pallas_call | solution.py:819
  (3 shorter events, 0.0 us)
Async XLA Ops:
  3.1 29.9 %copy-start = (f32[256,256]{1,0:T(8,128)S(1)}, f32[256,256]{1,0:T(8,128)}, u32[]{:S(2)}) copy-start(f32[256,256]{1,0:T(8,128)} %codes_ref.3) | copy-start | bytes 786436
  30.7 2.3 %collective-permute-start = (f32[64,24,128]{2,1,0:T(8,128)S(1)}, f32[64,24,128]{2,1,0:T(8,128)S(1)}, u32[]{:S(2)}, u32[]{:S(2)}) collective-permute-start(f32[64,24,128]{2,1,0:T(8,128)S(1)} %all_to_all.15), channel_id=1, source_target_pairs={{0,16},{16,0},{1,17},{17,1},{2,18},{18,2},{3,19},{19,3},{4,20},{20... | collective-permute-start | bytes 2359304 | tf_op jit(solution)/shard_map/ppermute | solution.py:829
  55.1 2.2 %collective-permute-start.1 = (f32[1344,128]{1,0:T(8,128)S(1)}, f32[1344,128]{1,0:T(8,128)S(1)}, u32[]{:S(2)}, u32[]{:S(2)}) collective-permute-start(f32[1344,128]{1,0:T(8,128)S(1)} %get-tuple-element.27), channel_id=1, source_target_pairs={{0,16},{16,0},{1,17},{17,1},{2,18},{18,2},{3,19},{19,3},{4,20},{20... | collective-permute-start | bytes 2064392 | tf_op jit(solution)/shard_map/ppermute | solution.py:829
  77.2 15.6 %copy-start.1 = (f32[256,256]{1,0:T(8,128)S(1)}, f32[256,256]{1,0:T(8,128)}, u32[]{:S(2)}) copy-start(f32[256,256]{1,0:T(8,128)} %code_first_ref.1) | copy-start | bytes 786436
  77.3 15.6 %copy-start.2 = (f32[256,256]{1,0:T(8,128)S(1)}, f32[256,256]{1,0:T(8,128)}, u32[]{:S(2)}) copy-start(f32[256,256]{1,0:T(8,128)} %code_second_ref.1) | copy-start | bytes 786436
  77.4 1.2 %collective-permute-start.2 = (f32[8,128]{1,0:T(8,128)S(1)}, f32[8,128]{1,0:T(8,128)S(1)}, u32[]{:S(2)}, u32[]{:S(2)}) collective-permute-start(f32[8,128]{1,0:T(8,128)S(1)} %get-tuple-element.29), channel_id=1, source_target_pairs={{0,16},{16,0},{1,17},{17,1},{2,18},{18,2},{3,19},{19,3},{4,20},{20... | collective-permute-start | bytes 12296 | tf_op jit(solution)/shard_map/ppermute | solution.py:829
  78.6 14.3 %copy-start.3 = (f32[2688]{0:T(1024)S(1)}, f32[2688]{0:T(1024)}, u32[]{:S(2)}) copy-start(f32[2688]{0:T(1024)} %param.9) | copy-start | bytes 32260
  78.6 14.3 %copy-start.4 = (f32[2688]{0:T(1024)S(1)}, f32[2688]{0:T(1024)}, u32[]{:S(2)}) copy-start(f32[2688]{0:T(1024)} %param.10) | copy-start | bytes 32260
  78.6 14.3 %copy-start.5 = (f32[2688]{0:T(1024)S(1)}, f32[2688]{0:T(1024)}, u32[]{:S(2)}) copy-start(f32[2688]{0:T(1024)} %param.11) | copy-start | bytes 32260

commit v12 on v11

--- a/solution.py
+++ b/solution.py
@@ -243,20 +243,18 @@
     sum_count,
     sum_loss,
     flat,
-    lhs_one,
+    table,
     lhs_two,
     lhs_back,
     coord_w,
     head_w,
     spots,
-    act_one,
     slope_one,
     curve_one,
     back_one,
     hid_hi,
     hid_lo,
     hot,
-    hot_turned,
     act_two,
     slope_two,
     curve_two,
@@ -339,12 +337,8 @@
     by_code = mm_nt(
         beside(weight_hi, weight_hi, weight_lo), beside(code_hi, code_lo, code_hi)
     )
-    one_hi, one_lo = halves(0.5 * (by_code[0:256, :] + first_bias))
-    lhs_one[:, 0:256] = one_hi
-    lhs_one[:, 256:512] = one_lo
-    two_hi, two_lo = halves(0.5 * (by_code[256:768, :] + second_bias))
-    lhs_two[:, 768:1024] = two_hi
-    lhs_two[:, 1024:1280] = two_lo
+    table[0:256, :] = 0.5 * (by_code[0:256, :] + first_bias)
+    table[256:768, :] = 0.5 * (by_code[256:768, :] + second_bias)
 
     for ref in (sum_two, sum_codes, sum_coord, sum_head, sum_count, sum_loss):
         ref[...] = jnp.zeros(ref.shape, F32)
@@ -364,25 +358,38 @@
         code_row = feature(4, step, s)
         valid = (code_row > 0.5).astype(F32)
 
-        wanted = code_row - 1.0
-        for r in range(0, CODE_ROWS, chunk):
-            row = (rows_of_lanes(0, (chunk, BLOCK)) + r).astype(F32)
-            mark = jnp.where(row == wanted, 1.0, 0.0)
-            hot[s, r : r + chunk, :] = mark.astype(BF16)
-            sum_count[r : r + chunk, :] += folded(mark)
-        for i in range(TILES):
-            wanted = jnp.broadcast_to(code_row[:, i * LANES : (i + 1) * LANES] - 1.0, (LANES, LANES)).T
-            for c in range(0, CODE_ROWS, LANES):
-                code = (rows_of_lanes(1, (LANES, LANES)) + c).astype(F32)
-                mark = jnp.where(code == wanted, 1.0, 0.0).astype(BF16)
-                hot_turned[s, i * LANES : (i + 1) * LANES, c : c + LANES] = mark
-        yield
-
-        act_one[s] = mm(lhs_one[...], stacked(hot[s], hot[s]))
-        yield
+        for c in range(0, CODE_ROWS, LANES):
+            code = (rows_of_lanes(1, (LANES, LANES)) + c).astype(F32)
+            seen = jnp.zeros((8, LANES), F32)
+            for i in range(TILES):
+                wanted = code_row[:, i * LANES : (i + 1) * LANES] - 1.0
+                mark = jnp.where(code == jnp.broadcast_to(wanted, (LANES, LANES)).T, 1.0, 0.0)
+                hot[s, i * LANES : (i + 1) * LANES, c : c + LANES] = mark.astype(BF16)
+                for k in range(0, LANES, 8):
+                    seen = seen + mark[k : k + 8, :]
+            sum_count[:, c : c + LANES] += seen
+
+        code = jnp.broadcast_to(jnp.maximum(code_row - 1.0, 0.0).astype(jnp.int32), (chunk, BLOCK))
+        upper = code >= LANES
+        code = lax.bitwise_and(code, LANES - 1)
+
+        def picked(first):
+            rows = slice(first, first + chunk)
+            tiles = []
+            for i in range(TILES):
+                part = slice(i * LANES, (i + 1) * LANES)
+                both = [
+                    jnp.take_along_axis(
+                        table[rows, c : c + LANES], code[:, part], axis=1, mode="promise_in_bounds"
+                    )
+                    for c in (0, LANES)
+                ]
+                tiles.append(jnp.where(upper[:, part], both[1], both[0]))
+            return beside(*tiles)
+
         last = stacked(blank5, *place)
         for r in low_chunks:
-            pre = act_one[s, r : r + chunk, :]
+            pre = picked(r)
             for i in range(3):
                 pre = pre + across(coord_w[r : r + chunk, i * LANES : (i + 1) * LANES]) * place[i]
             value, slope, curve = silu_parts(pre)
@@ -399,11 +406,11 @@
             curve_one[s, r : r + chunk, :] = curve
         yield
 
-        act_two[s] = mm(lhs_two[...], stacked(hid_hi[s], hid_lo[s], hid_hi[s], hot[s], hot[s]))
+        act_two[s] = mm(lhs_two[...], stacked(hid_hi[s], hid_lo[s], hid_hi[s]))
         yield
         total = jnp.zeros((8, BLOCK), F32)
         for r in high_chunks:
-            value, slope, curve = silu_parts_twice(act_two[s, r : r + chunk, :])
+            value, slope, curve = silu_parts_twice(act_two[s, r : r + chunk, :] + picked(256 + r))
             head = across(head_w[r : r + chunk, :LANES])
             weighed = head * value
             for k in range(0, chunk, 8):
@@ -472,7 +479,7 @@
                 grad * back * curve_one[s, r : r + chunk, :]
             )
         yield
-        act_tang[s] = mm(lhs_two[:, 0:768], stacked(tang_hi[s], tang_lo[s], tang_hi[s]))
+        act_tang[s] = mm(lhs_two[...], stacked(tang_hi[s], tang_lo[s], tang_hi[s]))
         yield
         for r in high_chunks:
             tangent = act_tang[s, r : r + chunk, :]
@@ -504,9 +511,9 @@
             beside(bar_hi[s], bar_hi[s], bar_lo[s], gate_hi[s], gate_hi[s], gate_lo[s]),
             beside(hid_hi[s], hid_lo[s], hid_hi[s], tang_hi[s], tang_lo[s], tang_hi[s]),
         )
-        turned = stacked(hot_turned[s], hot_turned[s])
-        sum_codes[256:768, :] += mm(beside(bar_hi[s], bar_lo[s]), turned)
-        sum_codes[0:256, :] += mm(beside(low_hi[s], low_lo[s]), turned)
+        marks = stacked(hot[s], hot[s])
+        sum_codes[256:768, :] += mm(beside(bar_hi[s], bar_lo[s]), marks)
+        sum_codes[0:256, :] += mm(beside(low_hi[s], low_lo[s]), marks)
 
     def step_body(step, carry):
         waiting = [block_stages(step, s) for s in range(SUBS)]
@@ -526,7 +533,8 @@
 
 def code_kernel(codes_ref, latent_w, sum_codes, sum_count, sum_loss, code_grad_ref, facts_ref):
     codes = codes_ref[...]
-    count = jnp.sum(sum_count[...], axis=1, keepdims=True)
+    count = jnp.sum(sum_count[...], axis=0, keepdims=True)
+    count = jnp.broadcast_to(count, (LANES, CODE_ROWS)).T[:, 0:1]
     turned_hi, turned_lo = halves(sum_codes[...].T)
     weight_hi, weight_lo = halves(latent_w[...])
     code_grad = mm(
@@ -687,11 +695,11 @@
         ((768, 256), F32),
         ((256, 3 * LANES), F32),
         ((HID, LANES), F32),
-        ((CODE_ROWS, LANES), F32),
+        ((8, CODE_ROWS), F32),
         ((2, BLOCK), F32),
         ((FLAT_ROWS + 8, LANES), F32),
-        ((256, 512), BF16),
-        ((HID, 1280), BF16),
+        ((768, CODE_ROWS), F32),
+        ((HID, 768), BF16),
         ((256, 1536), BF16),
         ((256, 3 * LANES), F32),
         ((HID, 2 * LANES), F32),
@@ -699,8 +707,6 @@
         (pair, F32),
         (pair, F32),
         (pair, F32),
-        (pair, F32),
-        (pair, BF16),
         (pair, BF16),
         (pair, BF16),
         ((SUBS, BLOCK, CODE_ROWS), BF16),

time: 94.5 us -> 93.2 us (0.986)
  Pallas kernels: 25.8 us -> 24.4 us
    pallas_call x1, Pallas kernels: 22.1 us -> 20.6 us  [main_call(): pl.pallas_call(main_kernel, out_shape=(boxes, boxes, f32(CODE_ROWS, LATEN...]
where the time goes in v12:
time: 93.2 us; the launch traced here: 92.8 us
  blocking collectives  61.7 us (66%)
  Pallas kernels  24.4 us (26%)
  waiting for transfers between devices  5.42 us (6%)
    all_to_all x3, blocking collectives, exchange(): return lax.all_to_all(v, ('z', 'wide'), split_axis=0, concat_axis=0)  61.7 us
    pallas_call x1, Pallas kernels, main_call(): pl.pallas_call(main_kernel, out_shape=(boxes, boxes, f32(CODE_ROWS, LATEN...  20.6 us
    ppermute x3, waiting for transfers between devices, swap_cores(): return lax.ppermute(v, 'core', [(0, 1), (1, 0)])  5.42 us
    pallas_call x1, Pallas kernels, pack_boxes(): pl.pallas_call(pack_kernel, out_shape=f32(PEERS, BOX_ROWS, LANES), in_spe...  2.43 us
  transfers between devices with their start and end apart: 3, of which 3 were waited for; matrix products, arithmetic and copies ran while one was open for 0% of the time, Pallas kernels for 0%

profile of v12, /device:TPU:0, one launch (start us, length us, event | category | flops | bytes accessed | tf_op | source)
XLA Modules:
  0.0 92.8 jit_solution(477751143041330367)
XLA Ops:
  0.6 2.4 %shard_map.168 = f32[64,24,128]{2,1,0:T(8,128)} custom-call(f32[21,128]{1,0:T(8,128)} %bitcast.23, f32[3,1024]{1,0:T(4,128)} %coords_hbm.1, f32[1,1024]{1,0:T(1,128)} %bitcast.28, s32[1,1024]{1,0:T(1,128)} %bitcast.29), custom_call_target="tpu_custom_call" | custom-call | tf_op jit(solution)/shard_map/pallas_call | solution.py:660
  3.1 0.0 copy-start
  3.1 27.6 %all_to_all.15 = f32[64,24,128]{2,1,0:T(8,128)S(1)} all-to-all(f32[64,24,128]{2,1,0:T(8,128)} %shard_map.168), channel_id=1, replica_groups=mesh['z'=4,'core'=2,'wide'=16] {'z','wide'}, dimensions={0} | all-to-all | bytes 1572864 | tf_op jit(solution)/shard_map/all_to_all | solution.py:839
  30.7 0.0 collective-permute-start
  30.7 2.3 %collective-permute-done = f32[64,24,128]{2,1,0:T(8,128)S(1)} collective-permute-done((f32[64,24,128]{2,1,0:T(8,128)S(1)}, f32[64,24,128]{2,1,0:T(8,128)S(1)}, u32[]{:S(2)}, u32[]{:S(2)}) %collective-permute-start) | collective-permute-done | bytes 786464 | tf_op jit(solution)/shard_map/ppermute | solution.py:835
  33.0 0.0 copy-done
  33.0 20.6 %shard_map.169 = (f32[1344,128]{1,0:T(8,128)S(1)}, f32[1344,128]{1,0:T(8,128)S(1)}, f32[256,256]{1,0:T(8,128)S(1)}, f32[8,128]{1,0:T(8,128)S(1)}) custom-call(s32[1]{0:T(128)} %bitcast.core_ref, f32[1536,128]{1,0:T(8,128)S(1)} %bitcast.19, f32[1536,128]{1,0:T(8,128)S(1)} %bitcast.21, f32[256,256]{1,0:T(8,128)S(1)} %copy-done), custom_call_target="tpu_custom_call" | custom-call | tf_op jit(solution)/shard_map/pallas_call | solution.py:730
  53.6 0.4 collective-permute-start.1
  54.1 2.0 %collective-permute-done.1 = f32[1344,128]{1,0:T(8,128)S(1)} collective-permute-done((f32[1344,128]{1,0:T(8,128)S(1)}, f32[1344,128]{1,0:T(8,128)S(1)}, u32[]{:S(2)}, u32[]{:S(2)}) %collective-permute-start.1) | collective-permute-done | bytes 688160 | tf_op jit(solution)/shard_map/ppermute | solution.py:835
  56.0 0.1 add.6
  56.1 19.8 %all_to_all.16 = f32[64,1,2688]{2,1,0:T(1,128)S(1)} all-to-all(f32[64,1,2688]{2,1,0:T(1,128)S(1)} %bitcast.27), channel_id=1, replica_groups=mesh['z'=4,'core'=2,'wide'=16] {'z','wide'}, dimensions={0} | all-to-all | bytes 1376256 | tf_op jit(solution)/shard_map/all_to_all | solution.py:839
  76.0 0.0 copy-start.1
  76.0 0.0 copy-start.2
  76.0 0.2 shard_map.170
  76.1 0.0 collective-permute-start.2
  76.1 1.2 %collective-permute-done.2 = f32[8,128]{1,0:T(8,128)S(1)} collective-permute-done((f32[8,128]{1,0:T(8,128)S(1)}, f32[8,128]{1,0:T(8,128)S(1)}, u32[]{:S(2)}, u32[]{:S(2)}) %collective-permute-start.2) | collective-permute-done | bytes 4128 | tf_op jit(solution)/shard_map/ppermute | solution.py:835
  77.3 0.0 copy-start.3
  77.3 0.0 copy-start.4
  77.3 0.0 copy-start.5
  77.4 14.2 %all_to_all.17 = f32[64,1,128]{2,1,0:T(1,128)S(1)} all-to-all(f32[64,1,128]{2,1,0:T(1,128)S(1)} %reshape.83), channel_id=1, replica_groups=mesh['z'=4,'core'=2,'wide'=16] {'z','wide'}, dimensions={0} | all-to-all | bytes 65536 | tf_op jit(solution)/shard_map/all_to_all | solution.py:839
  91.6 0.0 copy-done.1
  91.6 0.0 copy-done.2
  91.6 0.0 copy-done.3
  91.6 0.0 copy-done.4
  91.6 0.0 copy-done.5
  91.6 1.2 %shard_map.171 = (f32[1,1]{1,0:T(1,128)}, f32[1,1]{1,0:T(1,128)}, f32[21,128]{1,0:T(8,128)}, f32[21,128]{1,0:T(8,128)}, f32[21,128]{1,0:T(8,128)}, /*index=5*/bf...) custom-call(f32[64,128]{1,0:T(8,128)S(1)} %bitcast.22, ...), custom_call_target="tpu_custom_call" | custom-call | tf_op jit(solution)/shard_map/pallas_call | solution.py:825
  (3 shorter events, 0.0 us)
Async XLA Ops:
  3.1 29.9 %copy-start = (f32[256,256]{1,0:T(8,128)S(1)}, f32[256,256]{1,0:T(8,128)}, u32[]{:S(2)}) copy-start(f32[256,256]{1,0:T(8,128)} %codes_ref.3) | copy-start | bytes 786436
  30.7 2.3 %collective-permute-start = (f32[64,24,128]{2,1,0:T(8,128)S(1)}, f32[64,24,128]{2,1,0:T(8,128)S(1)}, u32[]{:S(2)}, u32[]{:S(2)}) collective-permute-start(f32[64,24,128]{2,1,0:T(8,128)S(1)} %all_to_all.15), channel_id=1, source_target_pairs={{0,16},{16,0},{1,17},{17,1},{2,18},{18,2},{3,19},{19,3},{4,20},{20... | collective-permute-start | bytes 2359304 | tf_op jit(solution)/shard_map/ppermute | solution.py:835
  53.6 2.4 %collective-permute-start.1 = (f32[1344,128]{1,0:T(8,128)S(1)}, f32[1344,128]{1,0:T(8,128)S(1)}, u32[]{:S(2)}, u32[]{:S(2)}) collective-permute-start(f32[1344,128]{1,0:T(8,128)S(1)} %get-tuple-element.27), channel_id=1, source_target_pairs={{0,16},{16,0},{1,17},{17,1},{2,18},{18,2},{3,19},{19,3},{4,20},{20... | collective-permute-start | bytes 2064392 | tf_op jit(solution)/shard_map/ppermute | solution.py:835
  76.0 15.6 %copy-start.1 = (f32[256,256]{1,0:T(8,128)S(1)}, f32[256,256]{1,0:T(8,128)}, u32[]{:S(2)}) copy-start(f32[256,256]{1,0:T(8,128)} %code_first_ref.1) | copy-start | bytes 786436
  76.0 15.6 %copy-start.2 = (f32[256,256]{1,0:T(8,128)S(1)}, f32[256,256]{1,0:T(8,128)}, u32[]{:S(2)}) copy-start(f32[256,256]{1,0:T(8,128)} %code_second_ref.1) | copy-start | bytes 786436
  76.1 1.2 %collective-permute-start.2 = (f32[8,128]{1,0:T(8,128)S(1)}, f32[8,128]{1,0:T(8,128)S(1)}, u32[]{:S(2)}, u32[]{:S(2)}) collective-permute-start(f32[8,128]{1,0:T(8,128)S(1)} %get-tuple-element.29), channel_id=1, source_target_pairs={{0,16},{16,0},{1,17},{17,1},{2,18},{18,2},{3,19},{19,3},{4,20},{20... | collective-permute-start | bytes 12296 | tf_op jit(solution)/shard_map/ppermute | solution.py:835
  77.3 14.3 %copy-start.3 = (f32[2688]{0:T(1024)S(1)}, f32[2688]{0:T(1024)}, u32[]{:S(2)}) copy-start(f32[2688]{0:T(1024)} %param.9) | copy-start | bytes 32260
  77.3 14.3 %copy-start.4 = (f32[2688]{0:T(1024)S(1)}, f32[2688]{0:T(1024)}, u32[]{:S(2)}) copy-start(f32[2688]{0:T(1024)} %param.10) | copy-start | bytes 32260
  77.3 14.3 %copy-start.5 = (f32[2688]{0:T(1024)S(1)}, f32[2688]{0:T(1024)}, u32[]{:S(2)}) copy-start(f32[2688]{0:T(1024)} %param.11) | copy-start | bytes 32260

commit v13 on v12

--- a/solution.py
+++ b/solution.py
@@ -33,7 +33,7 @@
 CODE_ROWS = 256
 FLAT_ROWS = DEVICES * SHARD_ROWS
 BLOCK = 256
-SUBS = 4
+SUBS = 8
 TILES = BLOCK // LANES
 ALL_POINTS = POINTS_DEV * DEVICES
 

time: 93.2 us -> 96.2 us (1.032)
  Pallas kernels: 24.4 us -> 27.6 us
    pallas_call x1, Pallas kernels: 20.6 us -> 23.8 us  [main_call(): pl.pallas_call(main_kernel, out_shape=(boxes, boxes, f32(CODE_ROWS, LATEN...]
where the time goes in v13:
time: 96.2 us; the launch traced here: 95.8 us
  blocking collectives  61.7 us (64%)
  Pallas kernels  27.6 us (29%)
  waiting for transfers between devices  5.41 us (6%)
    all_to_all x3, blocking collectives, exchange(): return lax.all_to_all(v, ('z', 'wide'), split_axis=0, concat_axis=0)  61.7 us
    pallas_call x1, Pallas kernels, main_call(): pl.pallas_call(main_kernel, out_shape=(boxes, boxes, f32(CODE_ROWS, LATEN...  23.8 us
    ppermute x3, waiting for transfers between devices, swap_cores(): return lax.ppermute(v, 'core', [(0, 1), (1, 0)])  5.41 us
    pallas_call x1, Pallas kernels, pack_boxes(): pl.pallas_call(pack_kernel, out_shape=f32(PEERS, BOX_ROWS, LANES), in_spe...  2.43 us
  transfers between devices with their start and end apart: 3, of which 3 were waited for; matrix products, arithmetic and copies ran while one was open for 0% of the time, Pallas kernels for 0%

profile of v13, /device:TPU:0, one launch (start us, length us, event | category | flops | bytes accessed | tf_op | source)
XLA Modules:
  0.0 95.8 jit_solution(8916126409950676853)
XLA Ops:
  0.6 2.4 %shard_map.168 = f32[64,24,128]{2,1,0:T(8,128)} custom-call(f32[21,128]{1,0:T(8,128)} %bitcast.23, f32[3,1024]{1,0:T(4,128)} %coords_hbm.1, f32[1,1024]{1,0:T(1,128)} %bitcast.28, s32[1,1024]{1,0:T(1,128)} %bitcast.29), custom_call_target="tpu_custom_call" | custom-call | tf_op jit(solution)/shard_map/pallas_call | solution.py:660
  3.1 0.0 copy-start
  3.1 27.6 %all_to_all.15 = f32[64,24,128]{2,1,0:T(8,128)S(1)} all-to-all(f32[64,24,128]{2,1,0:T(8,128)} %shard_map.168), channel_id=1, replica_groups=mesh['z'=4,'core'=2,'wide'=16] {'z','wide'}, dimensions={0} | all-to-all | bytes 1572864 | tf_op jit(solution)/shard_map/all_to_all | solution.py:839
  30.7 0.0 collective-permute-start
  30.7 2.3 %collective-permute-done = f32[64,24,128]{2,1,0:T(8,128)S(1)} collective-permute-done((f32[64,24,128]{2,1,0:T(8,128)S(1)}, f32[64,24,128]{2,1,0:T(8,128)S(1)}, u32[]{:S(2)}, u32[]{:S(2)}) %collective-permute-start) | collective-permute-done | bytes 786464 | tf_op jit(solution)/shard_map/ppermute | solution.py:835
  33.0 0.0 copy-done
  33.0 23.8 %shard_map.169 = (f32[1344,128]{1,0:T(8,128)S(1)}, f32[1344,128]{1,0:T(8,128)S(1)}, f32[256,256]{1,0:T(8,128)S(1)}, f32[8,128]{1,0:T(8,128)S(1)}) custom-call(s32[1]{0:T(128)} %bitcast.core_ref, f32[1536,128]{1,0:T(8,128)S(1)} %bitcast.19, f32[1536,128]{1,0:T(8,128)S(1)} %bitcast.21, f32[256,256]{1,0:T(8,128)S(1)} %copy-done), custom_call_target="tpu_custom_call" | custom-call | tf_op jit(solution)/shard_map/pallas_call | solution.py:730
  56.8 0.2 collective-permute-start.1
  57.1 2.0 %collective-permute-done.1 = f32[1344,128]{1,0:T(8,128)S(1)} collective-permute-done((f32[1344,128]{1,0:T(8,128)S(1)}, f32[1344,128]{1,0:T(8,128)S(1)}, u32[]{:S(2)}, u32[]{:S(2)}) %collective-permute-start.1) | collective-permute-done | bytes 688160 | tf_op jit(solution)/shard_map/ppermute | solution.py:835
  59.1 0.1 add.6
  59.1 19.8 %all_to_all.16 = f32[64,1,2688]{2,1,0:T(1,128)S(1)} all-to-all(f32[64,1,2688]{2,1,0:T(1,128)S(1)} %bitcast.27), channel_id=1, replica_groups=mesh['z'=4,'core'=2,'wide'=16] {'z','wide'}, dimensions={0} | all-to-all | bytes 1376256 | tf_op jit(solution)/shard_map/all_to_all | solution.py:839
  79.0 0.0 copy-start.1
  79.0 0.0 copy-start.2
  79.0 0.2 shard_map.170
  79.1 0.0 collective-permute-start.2
  79.2 1.2 %collective-permute-done.2 = f32[8,128]{1,0:T(8,128)S(1)} collective-permute-done((f32[8,128]{1,0:T(8,128)S(1)}, f32[8,128]{1,0:T(8,128)S(1)}, u32[]{:S(2)}, u32[]{:S(2)}) %collective-permute-start.2) | collective-permute-done | bytes 4128 | tf_op jit(solution)/shard_map/ppermute | solution.py:835
  80.3 0.0 copy-start.3
  80.4 0.0 copy-start.4
  80.4 0.0 copy-start.5
  80.4 14.2 %all_to_all.17 = f32[64,1,128]{2,1,0:T(1,128)S(1)} all-to-all(f32[64,1,128]{2,1,0:T(1,128)S(1)} %reshape.83), channel_id=1, replica_groups=mesh['z'=4,'core'=2,'wide'=16] {'z','wide'}, dimensions={0} | all-to-all | bytes 65536 | tf_op jit(solution)/shard_map/all_to_all | solution.py:839
  94.6 0.0 copy-done.1
  94.6 0.0 copy-done.2
  94.6 0.0 copy-done.3
  94.6 0.0 copy-done.4
  94.6 0.0 copy-done.5
  94.7 1.2 %shard_map.171 = (f32[1,1]{1,0:T(1,128)}, f32[1,1]{1,0:T(1,128)}, f32[21,128]{1,0:T(8,128)}, f32[21,128]{1,0:T(8,128)}, f32[21,128]{1,0:T(8,128)}, /*index=5*/bf...) custom-call(f32[64,128]{1,0:T(8,128)S(1)} %bitcast.22, ...), custom_call_target="tpu_custom_call" | custom-call | tf_op jit(solution)/shard_map/pallas_call | solution.py:825
  (3 shorter events, 0.0 us)
Async XLA Ops:
  3.1 29.9 %copy-start = (f32[256,256]{1,0:T(8,128)S(1)}, f32[256,256]{1,0:T(8,128)}, u32[]{:S(2)}) copy-start(f32[256,256]{1,0:T(8,128)} %codes_ref.3) | copy-start | bytes 786436
  30.7 2.3 %collective-permute-start = (f32[64,24,128]{2,1,0:T(8,128)S(1)}, f32[64,24,128]{2,1,0:T(8,128)S(1)}, u32[]{:S(2)}, u32[]{:S(2)}) collective-permute-start(f32[64,24,128]{2,1,0:T(8,128)S(1)} %all_to_all.15), channel_id=1, source_target_pairs={{0,16},{16,0},{1,17},{17,1},{2,18},{18,2},{3,19},{19,3},{4,20},{20... | collective-permute-start | bytes 2359304 | tf_op jit(solution)/shard_map/ppermute | solution.py:835
  56.8 2.2 %collective-permute-start.1 = (f32[1344,128]{1,0:T(8,128)S(1)}, f32[1344,128]{1,0:T(8,128)S(1)}, u32[]{:S(2)}, u32[]{:S(2)}) collective-permute-start(f32[1344,128]{1,0:T(8,128)S(1)} %get-tuple-element.27), channel_id=1, source_target_pairs={{0,16},{16,0},{1,17},{17,1},{2,18},{18,2},{3,19},{19,3},{4,20},{20... | collective-permute-start | bytes 2064392 | tf_op jit(solution)/shard_map/ppermute | solution.py:835
  79.0 15.6 %copy-start.1 = (f32[256,256]{1,0:T(8,128)S(1)}, f32[256,256]{1,0:T(8,128)}, u32[]{:S(2)}) copy-start(f32[256,256]{1,0:T(8,128)} %code_first_ref.1) | copy-start | bytes 786436
  79.0 15.6 %copy-start.2 = (f32[256,256]{1,0:T(8,128)S(1)}, f32[256,256]{1,0:T(8,128)}, u32[]{:S(2)}) copy-start(f32[256,256]{1,0:T(8,128)} %code_second_ref.1) | copy-start | bytes 786436
  79.1 1.2 %collective-permute-start.2 = (f32[8,128]{1,0:T(8,128)S(1)}, f32[8,128]{1,0:T(8,128)S(1)}, u32[]{:S(2)}, u32[]{:S(2)}) collective-permute-start(f32[8,128]{1,0:T(8,128)S(1)} %get-tuple-element.29), channel_id=1, source_target_pairs={{0,16},{16,0},{1,17},{17,1},{2,18},{18,2},{3,19},{19,3},{4,20},{20... | collective-permute-start | bytes 12296 | tf_op jit(solution)/shard_map/ppermute | solution.py:835
  80.3 14.3 %copy-start.3 = (f32[2688]{0:T(1024)S(1)}, f32[2688]{0:T(1024)}, u32[]{:S(2)}) copy-start(f32[2688]{0:T(1024)} %param.9) | copy-start | bytes 32260
  80.4 14.3 %copy-start.4 = (f32[2688]{0:T(1024)S(1)}, f32[2688]{0:T(1024)}, u32[]{:S(2)}) copy-start(f32[2688]{0:T(1024)} %param.10) | copy-start | bytes 32260
  80.4 14.3 %copy-start.5 = (f32[2688]{0:T(1024)S(1)}, f32[2688]{0:T(1024)}, u32[]{:S(2)}) copy-start(f32[2688]{0:T(1024)} %param.11) | copy-start | bytes 32260

commit v14 on v13

--- a/solution.py
+++ b/solution.py
@@ -33,7 +33,7 @@
 CODE_ROWS = 256
 FLAT_ROWS = DEVICES * SHARD_ROWS
 BLOCK = 256
-SUBS = 8
+SUBS = 2
 TILES = BLOCK // LANES
 ALL_POINTS = POINTS_DEV * DEVICES
 
@@ -175,7 +175,7 @@
             out_ref[group * 8 : group * 8 + 8, c * LANES : (c + 1) * LANES] = value
 
 
-def pack_units(value_ref, flat_ref, count, stride_rows, extra, first_entry, tails):
+def pack_units(value_ref, heads_ref, tails_ref, count, stride_rows, extra, first_entry):
     lane = rows_of_lanes(1, (8, LANES))
     slope = rows_of_lanes(0, (8, LANES)) * extra
     zero = jnp.zeros((8, LANES), F32)
@@ -183,21 +183,26 @@
         start = slope + shift
         wraps = shift + 7 * extra >= LANES
         turn = lax.bitwise_and(lane - start, LANES - 1)
-        rolled = {}
-
-        def tile(c, rolled=rolled, group=group, turn=turn):
-            if c < 0 or c > stride_rows:
-                return zero
-            if c not in rolled:
-                value = value_ref[group * 8 : group * 8 + 8, c * LANES : (c + 1) * LANES]
-                rolled[c] = jnp.take_along_axis(value, turn, axis=1, mode="promise_in_bounds")
-            return rolled[c]
-
-        for a in range(stride_rows, stride_rows + 2) if tails else range(stride_rows):
-            value = jnp.where(lane >= start, tile(a), tile(a - 1))
+        tiles = [zero, zero]
+        for c in range(stride_rows + 1):
+            value = value_ref[group * 8 : group * 8 + 8, c * LANES : (c + 1) * LANES]
+            tiles.append(jnp.take_along_axis(value, turn, axis=1, mode="promise_in_bounds"))
+        tiles.append(zero)
+        for a in range(stride_rows + 2):
+            value = jnp.where(lane >= start, tiles[a + 2], tiles[a + 1])
             if wraps:
-                value = jnp.where(lane >= start - LANES, value, tile(a - 2))
-            flat_ref[pl.ds(first + a, 8, stride=stride_rows), :] = value
+                value = jnp.where(lane >= start - LANES, value, tiles[a])
+            target = heads_ref if a < stride_rows else tails_ref
+            target[pl.ds(first + a, 8, stride=stride_rows), :] = value
+
+
+def clear(ref, rows):
+    def step(i, carry):
+        place = pl.ds(pl.multiple_of(i * rows, 8), rows)
+        ref[place, :] = jnp.zeros((rows, ref.shape[1]), F32)
+        return carry
+
+    lax.fori_loop(0, ref.shape[0] // rows, step, 0)
 
 
 FIRST_UNITS = (32, 2, 5, 0)
@@ -340,8 +345,10 @@
     table[0:256, :] = 0.5 * (by_code[0:256, :] + first_bias)
     table[256:768, :] = 0.5 * (by_code[256:768, :] + second_bias)
 
-    for ref in (sum_two, sum_codes, sum_coord, sum_head, sum_count, sum_loss):
-        ref[...] = jnp.zeros(ref.shape, F32)
+    for ref in (sum_two, sum_codes, sum_coord, sum_head):
+        clear(ref, 64)
+    sum_count[...] = jnp.zeros(sum_count.shape, F32)
+    sum_loss[...] = jnp.zeros(sum_loss.shape, F32)
 
     def feature(which, step, sub):
         first = which * SLOTS + (step * SUBS + sub) * TILES
@@ -618,11 +625,9 @@
     second_grad[:, 512:640] = jnp.where(lane == 2, head_grad, end)
 
     for ref in (flat, tails):
-        ref[...] = jnp.zeros(ref.shape, F32)
-    pack_units(first_grad, flat, *FIRST_UNITS, False)
-    pack_units(second_grad, flat, *SECOND_UNITS, False)
-    pack_units(first_grad, tails, *FIRST_UNITS, True)
-    pack_units(second_grad, tails, *SECOND_UNITS, True)
+        clear(ref, 128)
+    pack_units(first_grad, flat, tails, *FIRST_UNITS)
+    pack_units(second_grad, flat, tails, *SECOND_UNITS)
     row = HEAD_ENTRY // LANES
     lane = rows_of_lanes(1, (1, LANES))
     bias_total = jnp.sum(sum_loss[1:2, :], axis=1, keepdims=True)

time: 96.2 us -> 95.6 us (level)
  no operation moved by 1% of the time
where the time goes in v14:
time: 95.6 us; the launch traced here: 95.2 us
  blocking collectives  61.7 us (65%)
  Pallas kernels  27 us (28%)
  waiting for transfers between devices  5.4 us (6%)
    all_to_all x3, blocking collectives, exchange(): return lax.all_to_all(v, ('z', 'wide'), split_axis=0, concat_axis=0)  61.7 us
    pallas_call x1, Pallas kernels, main_call(): pl.pallas_call(main_kernel, out_shape=(boxes, boxes, f32(CODE_ROWS, LATEN...  23.2 us
    ppermute x3, waiting for transfers between devices, swap_cores(): return lax.ppermute(v, 'core', [(0, 1), (1, 0)])  5.4 us
    pallas_call x1, Pallas kernels, pack_boxes(): pl.pallas_call(pack_kernel, out_shape=f32(PEERS, BOX_ROWS, LANES), in_spe...  2.43 us
  transfers between devices with their start and end apart: 3, of which 3 were waited for; matrix products, arithmetic and copies ran while one was open for 0% of the time, Pallas kernels for 0%

profile of v14, /device:TPU:0, one launch (start us, length us, event | category | flops | bytes accessed | tf_op | source)
XLA Modules:
  0.0 95.2 jit_solution(9431919699572005479)
XLA Ops:
  0.6 2.4 %shard_map.168 = f32[64,24,128]{2,1,0:T(8,128)} custom-call(f32[21,128]{1,0:T(8,128)} %bitcast.23, f32[3,1024]{1,0:T(4,128)} %coords_hbm.1, f32[1,1024]{1,0:T(1,128)} %bitcast.28, s32[1,1024]{1,0:T(1,128)} %bitcast.29), custom_call_target="tpu_custom_call" | custom-call | tf_op jit(solution)/shard_map/pallas_call | solution.py:665
  3.1 0.0 copy-start
  3.1 27.6 %all_to_all.15 = f32[64,24,128]{2,1,0:T(8,128)S(1)} all-to-all(f32[64,24,128]{2,1,0:T(8,128)} %shard_map.168), channel_id=1, replica_groups=mesh['z'=4,'core'=2,'wide'=16] {'z','wide'}, dimensions={0} | all-to-all | bytes 1572864 | tf_op jit(solution)/shard_map/all_to_all | solution.py:844
  30.7 0.0 collective-permute-start
  30.7 2.3 %collective-permute-done = f32[64,24,128]{2,1,0:T(8,128)S(1)} collective-permute-done((f32[64,24,128]{2,1,0:T(8,128)S(1)}, f32[64,24,128]{2,1,0:T(8,128)S(1)}, u32[]{:S(2)}, u32[]{:S(2)}) %collective-permute-start) | collective-permute-done | bytes 786464 | tf_op jit(solution)/shard_map/ppermute | solution.py:840
  33.0 0.0 copy-done
  33.0 23.2 %shard_map.169 = (f32[1344,128]{1,0:T(8,128)S(1)}, f32[1344,128]{1,0:T(8,128)S(1)}, f32[256,256]{1,0:T(8,128)S(1)}, f32[8,128]{1,0:T(8,128)S(1)}) custom-call(s32[1]{0:T(128)} %bitcast.core_ref, f32[1536,128]{1,0:T(8,128)S(1)} %bitcast.19, f32[1536,128]{1,0:T(8,128)S(1)} %bitcast.21, f32[256,256]{1,0:T(8,128)S(1)} %copy-done), custom_call_target="tpu_custom_call" | custom-call | tf_op jit(solution)/shard_map/pallas_call | solution.py:735
  56.3 0.3 collective-permute-start.1
  56.5 2.0 %collective-permute-done.1 = f32[1344,128]{1,0:T(8,128)S(1)} collective-permute-done((f32[1344,128]{1,0:T(8,128)S(1)}, f32[1344,128]{1,0:T(8,128)S(1)}, u32[]{:S(2)}, u32[]{:S(2)}) %collective-permute-start.1) | collective-permute-done | bytes 688160 | tf_op jit(solution)/shard_map/ppermute | solution.py:840
  58.5 0.1 add.6
  58.6 19.8 %all_to_all.16 = f32[64,1,2688]{2,1,0:T(1,128)S(1)} all-to-all(f32[64,1,2688]{2,1,0:T(1,128)S(1)} %bitcast.27), channel_id=1, replica_groups=mesh['z'=4,'core'=2,'wide'=16] {'z','wide'}, dimensions={0} | all-to-all | bytes 1376256 | tf_op jit(solution)/shard_map/all_to_all | solution.py:844
  78.4 0.0 copy-start.1
  78.4 0.0 copy-start.2
  78.4 0.2 shard_map.170
  78.6 0.0 collective-permute-start.2
  78.6 1.2 %collective-permute-done.2 = f32[8,128]{1,0:T(8,128)S(1)} collective-permute-done((f32[8,128]{1,0:T(8,128)S(1)}, f32[8,128]{1,0:T(8,128)S(1)}, u32[]{:S(2)}, u32[]{:S(2)}) %collective-permute-start.2) | collective-permute-done | bytes 4128 | tf_op jit(solution)/shard_map/ppermute | solution.py:840
  79.8 0.0 copy-start.3
  79.8 0.0 copy-start.4
  79.8 0.0 copy-start.5
  79.8 14.2 %all_to_all.17 = f32[64,1,128]{2,1,0:T(1,128)S(1)} all-to-all(f32[64,1,128]{2,1,0:T(1,128)S(1)} %reshape.83), channel_id=1, replica_groups=mesh['z'=4,'core'=2,'wide'=16] {'z','wide'}, dimensions={0} | all-to-all | bytes 65536 | tf_op jit(solution)/shard_map/all_to_all | solution.py:844
  94.1 0.0 copy-done.1
  94.1 0.0 copy-done.2
  94.1 0.0 copy-done.3
  94.1 0.0 copy-done.4
  94.1 0.0 copy-done.5
  94.1 1.2 %shard_map.171 = (f32[1,1]{1,0:T(1,128)}, f32[1,1]{1,0:T(1,128)}, f32[21,128]{1,0:T(8,128)}, f32[21,128]{1,0:T(8,128)}, f32[21,128]{1,0:T(8,128)}, /*index=5*/bf...) custom-call(f32[64,128]{1,0:T(8,128)S(1)} %bitcast.22, ...), custom_call_target="tpu_custom_call" | custom-call | tf_op jit(solution)/shard_map/pallas_call | solution.py:830
  (3 shorter events, 0.0 us)
Async XLA Ops:
  3.1 29.9 %copy-start = (f32[256,256]{1,0:T(8,128)S(1)}, f32[256,256]{1,0:T(8,128)}, u32[]{:S(2)}) copy-start(f32[256,256]{1,0:T(8,128)} %codes_ref.3) | copy-start | bytes 786436
  30.7 2.3 %collective-permute-start = (f32[64,24,128]{2,1,0:T(8,128)S(1)}, f32[64,24,128]{2,1,0:T(8,128)S(1)}, u32[]{:S(2)}, u32[]{:S(2)}) collective-permute-start(f32[64,24,128]{2,1,0:T(8,128)S(1)} %all_to_all.15), channel_id=1, source_target_pairs={{0,16},{16,0},{1,17},{17,1},{2,18},{18,2},{3,19},{19,3},{4,20},{20... | collective-permute-start | bytes 2359304 | tf_op jit(solution)/shard_map/ppermute | solution.py:840
  56.3 2.2 %collective-permute-start.1 = (f32[1344,128]{1,0:T(8,128)S(1)}, f32[1344,128]{1,0:T(8,128)S(1)}, u32[]{:S(2)}, u32[]{:S(2)}) collective-permute-start(f32[1344,128]{1,0:T(8,128)S(1)} %get-tuple-element.27), channel_id=1, source_target_pairs={{0,16},{16,0},{1,17},{17,1},{2,18},{18,2},{3,19},{19,3},{4,20},{20... | collective-permute-start | bytes 2064392 | tf_op jit(solution)/shard_map/ppermute | solution.py:840
  78.4 15.6 %copy-start.1 = (f32[256,256]{1,0:T(8,128)S(1)}, f32[256,256]{1,0:T(8,128)}, u32[]{:S(2)}) copy-start(f32[256,256]{1,0:T(8,128)} %code_first_ref.1) | copy-start | bytes 786436
  78.4 15.6 %copy-start.2 = (f32[256,256]{1,0:T(8,128)S(1)}, f32[256,256]{1,0:T(8,128)}, u32[]{:S(2)}) copy-start(f32[256,256]{1,0:T(8,128)} %code_second_ref.1) | copy-start | bytes 786436
  78.6 1.2 %collective-permute-start.2 = (f32[8,128]{1,0:T(8,128)S(1)}, f32[8,128]{1,0:T(8,128)S(1)}, u32[]{:S(2)}, u32[]{:S(2)}) collective-permute-start(f32[8,128]{1,0:T(8,128)S(1)} %get-tuple-element.29), channel_id=1, source_target_pairs={{0,16},{16,0},{1,17},{17,1},{2,18},{18,2},{3,19},{19,3},{4,20},{20... | collective-permute-start | bytes 12296 | tf_op jit(solution)/shard_map/ppermute | solution.py:840
  79.8 14.3 %copy-start.3 = (f32[2688]{0:T(1024)S(1)}, f32[2688]{0:T(1024)}, u32[]{:S(2)}) copy-start(f32[2688]{0:T(1024)} %param.9) | copy-start | bytes 32260
  79.8 14.3 %copy-start.4 = (f32[2688]{0:T(1024)S(1)}, f32[2688]{0:T(1024)}, u32[]{:S(2)}) copy-start(f32[2688]{0:T(1024)} %param.10) | copy-start | bytes 32260
  79.8 14.3 %copy-start.5 = (f32[2688]{0:T(1024)S(1)}, f32[2688]{0:T(1024)}, u32[]{:S(2)}) copy-start(f32[2688]{0:T(1024)} %param.11) | copy-start | bytes 32260

commit v15 on v14

--- a/solution.py
+++ b/solution.py
@@ -33,7 +33,7 @@
 CODE_ROWS = 256
 FLAT_ROWS = DEVICES * SHARD_ROWS
 BLOCK = 256
-SUBS = 2
+SUBS = 4
 TILES = BLOCK // LANES
 ALL_POINTS = POINTS_DEV * DEVICES
 
@@ -105,12 +105,14 @@
         copy.start()
     copies[1].wait()
     shard = stacked(weights_ref[...], jnp.zeros((BOX_ROWS - SHARD_ROWS, LANES), F32))
-    for peer in range(PEERS):
-        staged[peer] = shard
-    early = pltpu.make_async_copy(
-        staged.at[:, pl.ds(0, 16), :], out_hbm.at[:, pl.ds(0, 16), :], sems.at[4]
-    )
-    early.start()
+
+    def fill(i, carry):
+        for k in range(8):
+            place = pl.ds(pl.multiple_of((i * 8 + k) * BOX_ROWS, 8), BOX_ROWS)
+            staged[place, :] = shard
+        return carry
+
+    lax.fori_loop(0, PEERS // 8, fill, 0)
     for i in (0, 2, 3):
         copies[i].wait()
     index = index_ref[...]
@@ -139,16 +141,14 @@
         beside(sent_low, sent_low, sent_low),
         beside(*[stacked(*piece, spare).astype(BF16) for piece in pieces]),
     )
-    for d in range(DEVICES):
-        z, core, w = d // 32, d // 16 % 2, d % 16
-        row = SHARD_ROWS + core
-        staged[z * 16 + w, row : row + 1, :] = boxes[d : d + 1, :]
-    late = pltpu.make_async_copy(
-        staged.at[:, pl.ds(16, 8), :], out_hbm.at[:, pl.ds(16, 8), :], sems.at[5]
-    )
-    late.start()
-    early.wait()
-    late.wait()
+    for z in range(4):
+        for core in range(2):
+            place = pl.ds(z * 16 * BOX_ROWS + SHARD_ROWS + core, 16, stride=BOX_ROWS)
+            first = z * 32 + core * 16
+            staged[place, :] = boxes[first : first + 16, :]
+    out = pltpu.make_async_copy(staged, out_hbm, sems.at[4])
+    out.start()
+    out.wait()
 
 
 def unit_groups(count, stride_rows, extra, first_entry):
@@ -365,17 +365,6 @@
         code_row = feature(4, step, s)
         valid = (code_row > 0.5).astype(F32)
 
-        for c in range(0, CODE_ROWS, LANES):
-            code = (rows_of_lanes(1, (LANES, LANES)) + c).astype(F32)
-            seen = jnp.zeros((8, LANES), F32)
-            for i in range(TILES):
-                wanted = code_row[:, i * LANES : (i + 1) * LANES] - 1.0
-                mark = jnp.where(code == jnp.broadcast_to(wanted, (LANES, LANES)).T, 1.0, 0.0)
-                hot[s, i * LANES : (i + 1) * LANES, c : c + LANES] = mark.astype(BF16)
-                for k in range(0, LANES, 8):
-                    seen = seen + mark[k : k + 8, :]
-            sum_count[:, c : c + LANES] += seen
-
         code = jnp.broadcast_to(jnp.maximum(code_row - 1.0, 0.0).astype(jnp.int32), (chunk, BLOCK))
         upper = code >= LANES
         code = lax.bitwise_and(code, LANES - 1)
@@ -487,6 +476,17 @@
             )
         yield
         act_tang[s] = mm(lhs_two[...], stacked(tang_hi[s], tang_lo[s], tang_hi[s]))
+
+        for c in range(0, CODE_ROWS, LANES):
+            code = (rows_of_lanes(1, (LANES, LANES)) + c).astype(F32)
+            seen = jnp.zeros((8, LANES), F32)
+            for i in range(TILES):
+                wanted = code_row[:, i * LANES : (i + 1) * LANES] - 1.0
+                mark = jnp.where(code == jnp.broadcast_to(wanted, (LANES, LANES)).T, 1.0, 0.0)
+                hot[s, i * LANES : (i + 1) * LANES, c : c + LANES] = mark.astype(BF16)
+                for k in range(0, LANES, 8):
+                    seen = seen + mark[k : k + 8, :]
+            sum_count[:, c : c + LANES] += seen
         yield
         for r in high_chunks:
             tangent = act_tang[s, r : r + chunk, :]
@@ -664,7 +664,7 @@
 def pack_boxes(weights, coords, distances, index):
     return pl.pallas_call(
         pack_kernel,
-        out_shape=f32(PEERS, BOX_ROWS, LANES),
+        out_shape=f32(PEERS * BOX_ROWS, LANES),
         in_specs=[HBM] * 4,
         out_specs=HBM,
         scratch_shapes=[
@@ -672,8 +672,8 @@
             pltpu.VMEM(coords.shape, F32),
             pltpu.VMEM(distances.shape, F32),
             pltpu.VMEM(index.shape, jnp.int32),
-            pltpu.VMEM((PEERS, BOX_ROWS, LANES), F32),
-            pltpu.SemaphoreType.DMA((6,)),
+            pltpu.VMEM((PEERS * BOX_ROWS, LANES), F32),
+            pltpu.SemaphoreType.DMA((5,)),
         ],
         compiler_params=pltpu.CompilerParams(vmem_limit_bytes=60 * 1024 * 1024),
     )(weights, coords, distances, index)
@@ -808,8 +808,9 @@
     moment_one_out[...] = first
     moment_two_out[...] = second
     weights_copy_out[...] = value.astype(BF16)
-    for r in range(0, CODE_ROWS, 32):
-        rows = slice(r, r + 32)
+
+    def step(i, carry):
+        rows = pl.ds(pl.multiple_of(i * 64, 8), 64)
         value, first, second = adam_update(
             codes_ref[rows, :],
             code_first_ref[rows, :],
@@ -821,6 +822,9 @@
         code_first_out[rows, :] = first
         code_second_out[rows, :] = second
         codes_copy_out[rows, :] = value.astype(BF16)
+        return carry
+
+    lax.fori_loop(0, CODE_ROWS // 64, step, 0)
 
 
 def update_all(*args):
@@ -861,7 +865,7 @@
         distances.reshape(1, POINTS_DEV),
         shape_index.reshape(1, POINTS_DEV),
     )
-    mine = exchange(boxes)
+    mine = exchange(boxes.reshape(PEERS, BOX_ROWS, LANES))
     other = swap_cores(mine)
     core = lax.axis_index("core").astype(jnp.int32).reshape(1)
     keep, give, code_grad, facts = main_call(

time: 95.6 us -> 93.3 us (0.976)
  Pallas kernels: 27 us -> 24.6 us
    pallas_call x1, Pallas kernels: 23.2 us -> 20.5 us  [main_call(): pl.pallas_call(main_kernel, out_shape=(boxes, boxes, f32(CODE_ROWS, LATEN...]
where the time goes in v15:
time: 93.3 us; the launch traced here: 92.9 us
  blocking collectives  61.7 us (66%)
  Pallas kernels  24.6 us (26%)
  waiting for transfers between devices  5.4 us (6%)
    all_to_all x3, blocking collectives, exchange(): return lax.all_to_all(v, ('z', 'wide'), split_axis=0, concat_axis=0)  61.7 us
    pallas_call x1, Pallas kernels, main_call(): pl.pallas_call(main_kernel, out_shape=(boxes, boxes, f32(CODE_ROWS, LATEN...  20.5 us
    ppermute x3, waiting for transfers between devices, swap_cores(): return lax.ppermute(v, 'core', [(0, 1), (1, 0)])  5.4 us
    pallas_call x1, Pallas kernels, pack_boxes(): pl.pallas_call(pack_kernel, out_shape=f32(PEERS * BOX_ROWS, LANES), in_sp...  2.56 us
  transfers between devices with their start and end apart: 3, of which 3 were waited for; matrix products, arithmetic and copies ran while one was open for 0% of the time, Pallas kernels for 0%

profile of v15, /device:TPU:0, one launch (start us, length us, event | category | flops | bytes accessed | tf_op | source)
XLA Modules:
  0.0 92.9 jit_solution(11391741165479588545)
XLA Ops:
  0.6 2.6 %shard_map.168 = f32[1536,128]{1,0:T(8,128)} custom-call(f32[21,128]{1,0:T(8,128)} %bitcast.24, f32[3,1024]{1,0:T(4,128)} %coords_hbm.1, f32[1,1024]{1,0:T(1,128)} %bitcast.30, s32[1,1024]{1,0:T(1,128)} %bitcast.31), custom_call_target="tpu_custom_call" | custom-call | tf_op jit(solution)/shard_map/pallas_call | solution.py:665
  3.2 0.0 copy-start
  3.2 27.6 %all_to_all.15 = f32[64,24,128]{2,1,0:T(8,128)S(1)} all-to-all(f32[64,24,128]{2,1,0:T(8,128)} %bitcast.28), channel_id=1, replica_groups=mesh['z'=4,'core'=2,'wide'=16] {'z','wide'}, dimensions={0} | all-to-all | bytes 1572864 | tf_op jit(solution)/shard_map/all_to_all | solution.py:848
  30.9 0.0 collective-permute-start
  30.9 2.3 %collective-permute-done = f32[64,24,128]{2,1,0:T(8,128)S(1)} collective-permute-done((f32[64,24,128]{2,1,0:T(8,128)S(1)}, f32[64,24,128]{2,1,0:T(8,128)S(1)}, u32[]{:S(2)}, u32[]{:S(2)}) %collective-permute-start) | collective-permute-done | bytes 786464 | tf_op jit(solution)/shard_map/ppermute | solution.py:844
  33.1 0.0 copy-done
  33.1 20.5 %shard_map.169 = (f32[1344,128]{1,0:T(8,128)S(1)}, f32[1344,128]{1,0:T(8,128)S(1)}, f32[256,256]{1,0:T(8,128)S(1)}, f32[8,128]{1,0:T(8,128)S(1)}) custom-call(s32[1]{0:T(128)} %bitcast.core_ref, f32[1536,128]{1,0:T(8,128)S(1)} %bitcast.20, f32[1536,128]{1,0:T(8,128)S(1)} %bitcast.22, f32[256,256]{1,0:T(8,128)S(1)} %copy-done), custom_call_target="tpu_custom_call" | custom-call | tf_op jit(solution)/shard_map/pallas_call | solution.py:735
  53.7 0.3 collective-permute-start.1
  54.0 2.0 %collective-permute-done.1 = f32[1344,128]{1,0:T(8,128)S(1)} collective-permute-done((f32[1344,128]{1,0:T(8,128)S(1)}, f32[1344,128]{1,0:T(8,128)S(1)}, u32[]{:S(2)}, u32[]{:S(2)}) %collective-permute-start.1) | collective-permute-done | bytes 688160 | tf_op jit(solution)/shard_map/ppermute | solution.py:844
  55.9 0.1 add.6
  56.0 19.8 %all_to_all.16 = f32[64,1,2688]{2,1,0:T(1,128)S(1)} all-to-all(f32[64,1,2688]{2,1,0:T(1,128)S(1)} %bitcast.29), channel_id=1, replica_groups=mesh['z'=4,'core'=2,'wide'=16] {'z','wide'}, dimensions={0} | all-to-all | bytes 1376256 | tf_op jit(solution)/shard_map/all_to_all | solution.py:848
  75.9 0.0 copy-start.1
  75.9 0.0 copy-start.2
  75.9 0.2 shard_map.170
  76.0 0.0 collective-permute-start.2
  76.0 1.2 %collective-permute-done.2 = f32[8,128]{1,0:T(8,128)S(1)} collective-permute-done((f32[8,128]{1,0:T(8,128)S(1)}, f32[8,128]{1,0:T(8,128)S(1)}, u32[]{:S(2)}, u32[]{:S(2)}) %collective-permute-start.2) | collective-permute-done | bytes 4128 | tf_op jit(solution)/shard_map/ppermute | solution.py:844
  77.2 0.0 copy-start.3
  77.2 0.0 copy-start.4
  77.3 0.0 copy-start.5
  77.3 14.2 %all_to_all.17 = f32[64,1,128]{2,1,0:T(1,128)S(1)} all-to-all(f32[64,1,128]{2,1,0:T(1,128)S(1)} %reshape.87), channel_id=1, replica_groups=mesh['z'=4,'core'=2,'wide'=16] {'z','wide'}, dimensions={0} | all-to-all | bytes 65536 | tf_op jit(solution)/shard_map/all_to_all | solution.py:848
  91.5 0.0 copy-done.1
  91.5 0.0 copy-done.2
  91.5 0.0 copy-done.3
  91.5 0.0 copy-done.4
  91.5 0.0 copy-done.5
  91.5 1.3 %shard_map.171 = (f32[1,1]{1,0:T(1,128)}, f32[1,1]{1,0:T(1,128)}, f32[21,128]{1,0:T(8,128)}, f32[21,128]{1,0:T(8,128)}, f32[21,128]{1,0:T(8,128)}, /*index=5*/bf...) custom-call(f32[64,128]{1,0:T(8,128)S(1)} %bitcast.23, ...), custom_call_target="tpu_custom_call" | custom-call | tf_op jit(solution)/shard_map/pallas_call | solution.py:834
  (3 shorter events, 0.0 us)
Async XLA Ops:
  3.2 29.9 %copy-start = (f32[256,256]{1,0:T(8,128)S(1)}, f32[256,256]{1,0:T(8,128)}, u32[]{:S(2)}) copy-start(f32[256,256]{1,0:T(8,128)} %codes_ref.3) | copy-start | bytes 786436
  30.9 2.3 %collective-permute-start = (f32[64,24,128]{2,1,0:T(8,128)S(1)}, f32[64,24,128]{2,1,0:T(8,128)S(1)}, u32[]{:S(2)}, u32[]{:S(2)}) collective-permute-start(f32[64,24,128]{2,1,0:T(8,128)S(1)} %all_to_all.15), channel_id=1, source_target_pairs={{0,16},{16,0},{1,17},{17,1},{2,18},{18,2},{3,19},{19,3},{4,20},{20... | collective-permute-start | bytes 2359304 | tf_op jit(solution)/shard_map/ppermute | solution.py:844
  53.7 2.2 %collective-permute-start.1 = (f32[1344,128]{1,0:T(8,128)S(1)}, f32[1344,128]{1,0:T(8,128)S(1)}, u32[]{:S(2)}, u32[]{:S(2)}) collective-permute-start(f32[1344,128]{1,0:T(8,128)S(1)} %get-tuple-element.27), channel_id=1, source_target_pairs={{0,16},{16,0},{1,17},{17,1},{2,18},{18,2},{3,19},{19,3},{4,20},{20... | collective-permute-start | bytes 2064392 | tf_op jit(solution)/shard_map/ppermute | solution.py:844
  75.9 15.6 %copy-start.1 = (f32[256,256]{1,0:T(8,128)S(1)}, f32[256,256]{1,0:T(8,128)}, u32[]{:S(2)}) copy-start(f32[256,256]{1,0:T(8,128)} %code_first_ref.1) | copy-start | bytes 786436
  75.9 15.6 %copy-start.2 = (f32[256,256]{1,0:T(8,128)S(1)}, f32[256,256]{1,0:T(8,128)}, u32[]{:S(2)}) copy-start(f32[256,256]{1,0:T(8,128)} %code_second_ref.1) | copy-start | bytes 786436
  76.0 1.2 %collective-permute-start.2 = (f32[8,128]{1,0:T(8,128)S(1)}, f32[8,128]{1,0:T(8,128)S(1)}, u32[]{:S(2)}, u32[]{:S(2)}) collective-permute-start(f32[8,128]{1,0:T(8,128)S(1)} %get-tuple-element.29), channel_id=1, source_target_pairs={{0,16},{16,0},{1,17},{17,1},{2,18},{18,2},{3,19},{19,3},{4,20},{20... | collective-permute-start | bytes 12296 | tf_op jit(solution)/shard_map/ppermute | solution.py:844
  77.2 14.3 %copy-start.3 = (f32[2688]{0:T(1024)S(1)}, f32[2688]{0:T(1024)}, u32[]{:S(2)}) copy-start(f32[2688]{0:T(1024)} %param.9) | copy-start | bytes 32260
  77.2 14.3 %copy-start.4 = (f32[2688]{0:T(1024)S(1)}, f32[2688]{0:T(1024)}, u32[]{:S(2)}) copy-start(f32[2688]{0:T(1024)} %param.10) | copy-start | bytes 32260
  77.3 14.3 %copy-start.5 = (f32[2688]{0:T(1024)S(1)}, f32[2688]{0:T(1024)}, u32[]{:S(2)}) copy-start(f32[2688]{0:T(1024)} %param.11) | copy-start | bytes 32260

commit v16 on v15

--- a/solution.py
+++ b/solution.py
@@ -68,6 +68,24 @@
 
 def beside(*parts):
     return jnp.concatenate(parts, axis=1)
+
+
+def row_sums(v):
+    high, low = halves(v)
+    return mm(beside(high, low), jnp.ones((2 * v.shape[1], LANES), BF16))
+
+
+def picked_lanes(v, count):
+    shape = (LANES, count * LANES)
+    row, column = rows_of_lanes(0, shape), rows_of_lanes(1, shape)
+    chosen = jnp.where(column >> 7 == row, 1.0, 0.0).astype(BF16)
+    parts = beside(*[part.astype(BF16) for part in thirds(v)])
+    wide = mm(parts, stacked(chosen, chosen, chosen))
+    return [wide[:, i * LANES : (i + 1) * LANES] for i in range(count)]
+
+
+def twice(v):
+    return beside(v, v)
 
 
 def total_of(v):
@@ -241,6 +259,8 @@
     first_w,
     second_w,
     latent_w,
+    roots,
+    scales,
     sum_two,
     sum_codes,
     sum_coord,
@@ -300,29 +320,31 @@
     first_low = jnp.where(beside(real, real), first_w[:, : 2 * LANES], 0.0)
     first_end = jnp.where(real, first_w[:, 2 * LANES :], 0.0)
     first_near = jnp.where(lane < 3, first_end, 0.0)
-    first_gain = first_end[:, 3:4]
-    first_bias = first_end[:, 4:5]
     first_w[:, : 2 * LANES] = first_low
     first_w[:, 2 * LANES :] = first_end
-    _, first_scale = norm_parts(beside(first_low, first_near), first_gain)
-    first_low = first_low * first_scale
-    first_near = first_near * first_scale
-    latent_w[0:256, :] = first_low
+    *near_columns, gain, first_bias = picked_lanes(first_end, 5)
+    square = first_low * first_low
+    square = square[:, :LANES] + square[:, LANES:] + first_near * first_near
+    root = lax.rsqrt(row_sums(square) + 1e-12)
+    scale = gain * root
+    roots[0:256, :] = root
+    scales[0:256, :] = scale
+    latent_w[0:256, :] = first_low * twice(scale)
     for i in range(3):
-        coord_w[:, i * LANES : (i + 1) * LANES] = jnp.broadcast_to(
-            0.5 * first_near[:, i : i + 1], (256, LANES)
-        )
+        coord_w[:, i * LANES : (i + 1) * LANES] = 0.5 * near_columns[i] * scale
 
     second_a = second_w[:, 0:256]
     second_b = second_w[:, 256:512]
-    second_gain = second_w[:, 512:513]
-    second_bias = second_w[:, 513:514]
-    head = jnp.broadcast_to(second_w[:, 514:515], (HID, LANES))
+    gain, second_bias, head = picked_lanes(second_w[:, 512:640], 3)
     head_w[:, :LANES] = 0.5 * head
     head_w[:, LANES:] = head
-    _, second_scale = norm_parts(second_w[:, 0:512], second_gain)
-    second_a = second_a * second_scale
-    second_b = second_b * second_scale
+    square = second_a * second_a + second_b * second_b
+    root = lax.rsqrt(row_sums(square[:, :LANES] + square[:, LANES:]) + 1e-12)
+    scale = gain * root
+    roots[256:768, :] = root
+    scales[256:768, :] = scale
+    second_a = second_a * twice(scale)
+    second_b = second_b * twice(scale)
     is_hidden = rows_of_lanes(1, (HID, 256)) < MIDDLE
     hidden_cols = jnp.where(is_hidden, second_a, second_b)
     latent_cols = pltpu.roll(jnp.where(is_hidden, second_b, second_a), 3, 1)
@@ -342,8 +364,8 @@
     by_code = mm_nt(
         beside(weight_hi, weight_hi, weight_lo), beside(code_hi, code_lo, code_hi)
     )
-    table[0:256, :] = 0.5 * (by_code[0:256, :] + first_bias)
-    table[256:768, :] = 0.5 * (by_code[256:768, :] + second_bias)
+    table[0:256, :] = 0.5 * (by_code[0:256, :] + twice(first_bias))
+    table[256:768, :] = 0.5 * (by_code[256:768, :] + twice(second_bias))
 
     for ref in (sum_two, sum_codes, sum_coord, sum_head):
         clear(ref, 64)
@@ -541,7 +563,7 @@
 def code_kernel(codes_ref, latent_w, sum_codes, sum_count, sum_loss, code_grad_ref, facts_ref):
     codes = codes_ref[...]
     count = jnp.sum(sum_count[...], axis=0, keepdims=True)
-    count = jnp.broadcast_to(count, (LANES, CODE_ROWS)).T[:, 0:1]
+    count = twice(jnp.broadcast_to(count, (LANES, CODE_ROWS)).T)
     turned_hi, turned_lo = halves(sum_codes[...].T)
     weight_hi, weight_lo = halves(latent_w[...])
     code_grad = mm(
@@ -555,16 +577,13 @@
     facts_ref[...] = jnp.where(left, total_of(code_grad * code_grad), loss)
 
 
-def norm_parts(direction, gain):
-    root = lax.rsqrt(jnp.sum(direction * direction, axis=1, keepdims=True) + 1e-12)
-    return root, gain * root
-
-
 def weight_kernel(
     core_ref,
     codes_ref,
     first_w,
     second_w,
+    roots,
+    scales,
     sum_two,
     sum_codes,
     sum_coord,
@@ -585,24 +604,25 @@
     by_hi, by_lo = halves(by_code)
     latent_grad = mm(beside(by_hi, by_hi, by_lo), stacked(code_hi, code_lo, code_hi))
 
-    bias_grad = jnp.sum(by_code, axis=1, keepdims=True)
+    bias_grad = row_sums(by_code[:, :LANES] + by_code[:, LANES:])
     lane = rows_of_lanes(1, (256, LANES))
     real = rows_of_lanes(0, (256, LANES)) < MIDDLE
     near_grad = 0.0
     for i in range(3):
-        column = jnp.sum(sum_coord[:, i * LANES : (i + 1) * LANES], axis=1, keepdims=True)
+        column = row_sums(sum_coord[:, i * LANES : (i + 1) * LANES])
         near_grad = jnp.where(lane == i, column, near_grad)
     low_grad = latent_grad[0:256, :]
     first_low = first_w[:, : 2 * LANES]
     first_near = jnp.where(lane < 3, first_w[:, 2 * LANES :], 0.0)
-    root, scale = norm_parts(beside(first_low, first_near), first_w[:, 2 * LANES + 3 : 2 * LANES + 4])
-    along = jnp.sum(first_low * low_grad, axis=1, keepdims=True)
-    along = along + jnp.sum(first_near * near_grad, axis=1, keepdims=True)
+    root, scale = roots[0:256, :], scales[0:256, :]
+    product = first_low * low_grad
+    product = product[:, :LANES] + product[:, LANES:] + first_near * near_grad
+    along = row_sums(product)
     inward = scale * root * root * along
     end = scale * near_grad - first_near * inward
     end = jnp.where(lane == 3, root * along, end)
     end = jnp.where(lane == 4, bias_grad[0:256, :], end)
-    low_grad = scale * low_grad - first_low * inward
+    low_grad = twice(scale) * low_grad - first_low * twice(inward)
     first_grad[:, : 2 * LANES] = jnp.where(beside(real, real), low_grad, 0.0)
     first_grad[:, 2 * LANES :] = jnp.where(real, end, 0.0)
 
@@ -613,12 +633,13 @@
     grad_b = jnp.where(is_hidden, moved, hidden_grad)
     second_a = second_w[:, 0:256]
     second_b = second_w[:, 256:512]
-    root, scale = norm_parts(second_w[:, 0:512], second_w[:, 512:513])
-    along = jnp.sum(second_a * grad_a + second_b * grad_b, axis=1, keepdims=True)
+    root, scale = roots[256:768, :], scales[256:768, :]
+    product = second_a * grad_a + second_b * grad_b
+    along = row_sums(product[:, :LANES] + product[:, LANES:])
     inward = scale * root * root * along
-    second_grad[:, 0:256] = scale * grad_a - second_a * inward
-    second_grad[:, 256:512] = scale * grad_b - second_b * inward
-    head_grad = jnp.sum(sum_head[...], axis=1, keepdims=True)
+    second_grad[:, 0:256] = twice(scale) * grad_a - second_a * twice(inward)
+    second_grad[:, 256:512] = twice(scale) * grad_b - second_b * twice(inward)
+    head_grad = row_sums(sum_head[...])
     lane = rows_of_lanes(1, (HID, LANES))
     end = jnp.where(lane == 0, root * along, 0.0)
     end = jnp.where(lane == 1, bias_grad[256:768, :], end)
@@ -682,11 +703,11 @@
 def main_kernel(
     core_ref, mine_ref, other_ref, codes_ref, keep_ref, give_ref, code_grad_ref, facts_ref, *scratch
 ):
-    first_w, second_w, latent_w, *sums = scratch[:9]
-    flat = scratch[9]
+    first_w, second_w, latent_w, roots, scales, *sums = scratch[:11]
+    flat = scratch[11]
     loop_kernel(core_ref, mine_ref, other_ref, codes_ref, *scratch[:-3])
     code_kernel(codes_ref, latent_w, sums[1], sums[4], sums[5], code_grad_ref, facts_ref)
-    weight_kernel(core_ref, codes_ref, first_w, second_w, *sums, keep_ref, give_ref, flat, *scratch[-3:])
+    weight_kernel(core_ref, codes_ref, first_w, second_w, roots, scales, *sums, keep_ref, give_ref, flat, *scratch[-3:])
 
 
 def main_call(core, mine, other, codes):
@@ -696,6 +717,8 @@
         ((256, 3 * LANES), F32),
         ((HID, 5 * LANES), F32),
         ((768, 256), F32),
+        ((768, LANES), F32),
+        ((768, LANES), F32),
         ((HID, 256), F32),
         ((768, 256), F32),
         ((256, 3 * LANES), F32),

time: 93.3 us -> 92.9 us (level)
  no operation moved by 1% of the time
where the time goes in v16:
time: 92.9 us; the launch traced here: 92.5 us
  blocking collectives  61.7 us (66%)
  Pallas kernels  24.2 us (26%)
  waiting for transfers between devices  5.4 us (6%)
    all_to_all x3, blocking collectives, exchange(): return lax.all_to_all(v, ('z', 'wide'), split_axis=0, concat_axis=0)  61.7 us
    pallas_call x1, Pallas kernels, main_call(): pl.pallas_call(main_kernel, out_shape=(boxes, boxes, f32(CODE_ROWS, LATEN...  20.2 us
    ppermute x3, waiting for transfers between devices, swap_cores(): return lax.ppermute(v, 'core', [(0, 1), (1, 0)])  5.4 us
    pallas_call x1, Pallas kernels, pack_boxes(): pl.pallas_call(pack_kernel, out_shape=f32(PEERS * BOX_ROWS, LANES), in_sp...  2.56 us
  transfers between devices with their start and end apart: 3, of which 3 were waited for; matrix products, arithmetic and copies ran while one was open for 0% of the time, Pallas kernels for 0%

profile of v16, /device:TPU:0, one launch (start us, length us, event | category | flops | bytes accessed | tf_op | source)
XLA Modules:
  0.0 92.5 jit_solution(17176683496638732844)
XLA Ops:
  0.6 2.6 %shard_map.168 = f32[1536,128]{1,0:T(8,128)} custom-call(f32[21,128]{1,0:T(8,128)} %bitcast.24, f32[3,1024]{1,0:T(4,128)} %coords_hbm.1, f32[1,1024]{1,0:T(1,128)} %bitcast.30, s32[1,1024]{1,0:T(1,128)} %bitcast.31), custom_call_target="tpu_custom_call" | custom-call | tf_op jit(solution)/shard_map/pallas_call | solution.py:686
  3.2 0.0 copy-start
  3.2 27.6 %all_to_all.15 = f32[64,24,128]{2,1,0:T(8,128)S(1)} all-to-all(f32[64,24,128]{2,1,0:T(8,128)} %bitcast.28), channel_id=1, replica_groups=mesh['z'=4,'core'=2,'wide'=16] {'z','wide'}, dimensions={0} | all-to-all | bytes 1572864 | tf_op jit(solution)/shard_map/all_to_all | solution.py:871
  30.9 0.0 collective-permute-start
  30.9 2.3 %collective-permute-done = f32[64,24,128]{2,1,0:T(8,128)S(1)} collective-permute-done((f32[64,24,128]{2,1,0:T(8,128)S(1)}, f32[64,24,128]{2,1,0:T(8,128)S(1)}, u32[]{:S(2)}, u32[]{:S(2)}) %collective-permute-start) | collective-permute-done | bytes 786464 | tf_op jit(solution)/shard_map/ppermute | solution.py:867
  33.1 0.0 copy-done
  33.1 20.2 %shard_map.169 = (f32[1344,128]{1,0:T(8,128)S(1)}, f32[1344,128]{1,0:T(8,128)S(1)}, f32[256,256]{1,0:T(8,128)S(1)}, f32[8,128]{1,0:T(8,128)S(1)}) custom-call(s32[1]{0:T(128)} %bitcast.core_ref, f32[1536,128]{1,0:T(8,128)S(1)} %bitcast.20, f32[1536,128]{1,0:T(8,128)S(1)} %bitcast.22, f32[256,256]{1,0:T(8,128)S(1)} %copy-done), custom_call_target="tpu_custom_call" | custom-call | tf_op jit(solution)/shard_map/pallas_call | solution.py:758
  53.3 0.3 collective-permute-start.1
  53.6 2.0 %collective-permute-done.1 = f32[1344,128]{1,0:T(8,128)S(1)} collective-permute-done((f32[1344,128]{1,0:T(8,128)S(1)}, f32[1344,128]{1,0:T(8,128)S(1)}, u32[]{:S(2)}, u32[]{:S(2)}) %collective-permute-start.1) | collective-permute-done | bytes 688160 | tf_op jit(solution)/shard_map/ppermute | solution.py:867
  55.6 0.1 add.6
  55.7 19.8 %all_to_all.16 = f32[64,1,2688]{2,1,0:T(1,128)S(1)} all-to-all(f32[64,1,2688]{2,1,0:T(1,128)S(1)} %bitcast.29), channel_id=1, replica_groups=mesh['z'=4,'core'=2,'wide'=16] {'z','wide'}, dimensions={0} | all-to-all | bytes 1376256 | tf_op jit(solution)/shard_map/all_to_all | solution.py:871
  75.5 0.0 copy-start.1
  75.5 0.0 copy-start.2
  75.5 0.2 shard_map.170
  75.7 0.0 collective-permute-start.2
  75.7 1.2 %collective-permute-done.2 = f32[8,128]{1,0:T(8,128)S(1)} collective-permute-done((f32[8,128]{1,0:T(8,128)S(1)}, f32[8,128]{1,0:T(8,128)S(1)}, u32[]{:S(2)}, u32[]{:S(2)}) %collective-permute-start.2) | collective-permute-done | bytes 4128 | tf_op jit(solution)/shard_map/ppermute | solution.py:867
  76.9 0.0 copy-start.3
  76.9 0.0 copy-start.4
  76.9 0.0 copy-start.5
  76.9 14.2 %all_to_all.17 = f32[64,1,128]{2,1,0:T(1,128)S(1)} all-to-all(f32[64,1,128]{2,1,0:T(1,128)S(1)} %reshape.87), channel_id=1, replica_groups=mesh['z'=4,'core'=2,'wide'=16] {'z','wide'}, dimensions={0} | all-to-all | bytes 65536 | tf_op jit(solution)/shard_map/all_to_all | solution.py:871
  91.1 0.0 copy-done.1
  91.2 0.0 copy-done.2
  91.2 0.0 copy-done.3
  91.2 0.0 copy-done.4
  91.2 0.0 copy-done.5
  91.2 1.3 %shard_map.171 = (f32[1,1]{1,0:T(1,128)}, f32[1,1]{1,0:T(1,128)}, f32[21,128]{1,0:T(8,128)}, f32[21,128]{1,0:T(8,128)}, f32[21,128]{1,0:T(8,128)}, /*index=5*/bf...) custom-call(f32[64,128]{1,0:T(8,128)S(1)} %bitcast.23, ...), custom_call_target="tpu_custom_call" | custom-call | tf_op jit(solution)/shard_map/pallas_call | solution.py:857
  (3 shorter events, 0.0 us)
Async XLA Ops:
  3.2 29.9 %copy-start = (f32[256,256]{1,0:T(8,128)S(1)}, f32[256,256]{1,0:T(8,128)}, u32[]{:S(2)}) copy-start(f32[256,256]{1,0:T(8,128)} %codes_ref.3) | copy-start | bytes 786436
  30.9 2.3 %collective-permute-start = (f32[64,24,128]{2,1,0:T(8,128)S(1)}, f32[64,24,128]{2,1,0:T(8,128)S(1)}, u32[]{:S(2)}, u32[]{:S(2)}) collective-permute-start(f32[64,24,128]{2,1,0:T(8,128)S(1)} %all_to_all.15), channel_id=1, source_target_pairs={{0,16},{16,0},{1,17},{17,1},{2,18},{18,2},{3,19},{19,3},{4,20},{20... | collective-permute-start | bytes 2359304 | tf_op jit(solution)/shard_map/ppermute | solution.py:867
  53.3 2.2 %collective-permute-start.1 = (f32[1344,128]{1,0:T(8,128)S(1)}, f32[1344,128]{1,0:T(8,128)S(1)}, u32[]{:S(2)}, u32[]{:S(2)}) collective-permute-start(f32[1344,128]{1,0:T(8,128)S(1)} %get-tuple-element.27), channel_id=1, source_target_pairs={{0,16},{16,0},{1,17},{17,1},{2,18},{18,2},{3,19},{19,3},{4,20},{20... | collective-permute-start | bytes 2064392 | tf_op jit(solution)/shard_map/ppermute | solution.py:867
  75.5 15.6 %copy-start.1 = (f32[256,256]{1,0:T(8,128)S(1)}, f32[256,256]{1,0:T(8,128)}, u32[]{:S(2)}) copy-start(f32[256,256]{1,0:T(8,128)} %code_first_ref.1) | copy-start | bytes 786436
  75.5 15.6 %copy-start.2 = (f32[256,256]{1,0:T(8,128)S(1)}, f32[256,256]{1,0:T(8,128)}, u32[]{:S(2)}) copy-start(f32[256,256]{1,0:T(8,128)} %code_second_ref.1) | copy-start | bytes 786436
  75.7 1.2 %collective-permute-start.2 = (f32[8,128]{1,0:T(8,128)S(1)}, f32[8,128]{1,0:T(8,128)S(1)}, u32[]{:S(2)}, u32[]{:S(2)}) collective-permute-start(f32[8,128]{1,0:T(8,128)S(1)} %get-tuple-element.29), channel_id=1, source_target_pairs={{0,16},{16,0},{1,17},{17,1},{2,18},{18,2},{3,19},{19,3},{4,20},{20... | collective-permute-start | bytes 12296 | tf_op jit(solution)/shard_map/ppermute | solution.py:867
  76.9 14.3 %copy-start.3 = (f32[2688]{0:T(1024)S(1)}, f32[2688]{0:T(1024)}, u32[]{:S(2)}) copy-start(f32[2688]{0:T(1024)} %param.9) | copy-start | bytes 32260
  76.9 14.3 %copy-start.4 = (f32[2688]{0:T(1024)S(1)}, f32[2688]{0:T(1024)}, u32[]{:S(2)}) copy-start(f32[2688]{0:T(1024)} %param.10) | copy-start | bytes 32260
  76.9 14.3 %copy-start.5 = (f32[2688]{0:T(1024)S(1)}, f32[2688]{0:T(1024)}, u32[]{:S(2)}) copy-start(f32[2688]{0:T(1024)} %param.11) | copy-start | bytes 32260

commit v17 on v16

--- a/solution.py
+++ b/solution.py
@@ -96,43 +96,16 @@
     return jnp.concatenate(parts, axis=0)
 
 
-def pack_kernel(
-    weights_hbm,
-    coords_hbm,
-    distances_hbm,
-    index_hbm,
-    out_hbm,
-    weights_ref,
-    coords_ref,
-    distances_ref,
-    index_ref,
-    staged,
-    sems,
-):
-    pairs = [
-        (index_hbm, index_ref),
-        (weights_hbm, weights_ref),
-        (coords_hbm, coords_ref),
-        (distances_hbm, distances_ref),
-    ]
-    copies = [
-        pltpu.make_async_copy(source, target, sems.at[i])
-        for i, (source, target) in enumerate(pairs)
-    ]
-    for copy in copies:
-        copy.start()
-    copies[1].wait()
+def pack_kernel(weights_ref, points_ref, index_ref, out_ref):
     shard = stacked(weights_ref[...], jnp.zeros((BOX_ROWS - SHARD_ROWS, LANES), F32))
 
     def fill(i, carry):
         for k in range(8):
             place = pl.ds(pl.multiple_of((i * 8 + k) * BOX_ROWS, 8), BOX_ROWS)
-            staged[place, :] = shard
+            out_ref[place, :] = shard
         return carry
 
     lax.fori_loop(0, PEERS // 8, fill, 0)
-    for i in (0, 2, 3):
-        copies[i].wait()
     index = index_ref[...]
     owner = lax.shift_right_logical(index, 8)
     row = lax.bitwise_and(index, CODE_ROWS - 1)
@@ -148,8 +121,8 @@
     ]
     placed = jnp.sum(sent * beside(*ranks), axis=0, keepdims=True).astype(jnp.int32)
     at_slot = rows_of_lanes(0, (SLOTS, POINTS_DEV)) == placed
-    values = [coords_ref[i : i + 1, :] for i in range(3)]
-    values += [distances_ref[...], (row + 1).astype(F32)]
+    values = [points_ref[i : i + 1, :] for i in range(4)]
+    values.append((row + 1).astype(F32))
     pieces = [[], [], []]
     for value in values:
         for k, third in enumerate(thirds(value)):
@@ -163,10 +136,7 @@
         for core in range(2):
             place = pl.ds(z * 16 * BOX_ROWS + SHARD_ROWS + core, 16, stride=BOX_ROWS)
             first = z * 32 + core * 16
-            staged[place, :] = boxes[first : first + 16, :]
-    out = pltpu.make_async_copy(staged, out_hbm, sems.at[4])
-    out.start()
-    out.wait()
+            out_ref[place, :] = boxes[first : first + 16, :]
 
 
 def unit_groups(count, stride_rows, extra, first_entry):
@@ -536,13 +506,19 @@
             low_lo[s, r : r + chunk, :] = low
         yield
 
-        sum_two[...] += mm_nt(
-            beside(bar_hi[s], bar_hi[s], bar_lo[s], gate_hi[s], gate_hi[s], gate_lo[s]),
-            beside(hid_hi[s], hid_lo[s], hid_hi[s], tang_hi[s], tang_lo[s], tang_hi[s]),
-        )
-        marks = stacked(hot[s], hot[s])
-        sum_codes[256:768, :] += mm(beside(bar_hi[s], bar_lo[s]), marks)
-        sum_codes[0:256, :] += mm(beside(low_hi[s], low_lo[s]), marks)
+        if s % 2 == 0:
+            return
+        both = (s - 1, s)
+        left, right = [], []
+        for k in both:
+            left += [bar_hi[k], bar_hi[k], bar_lo[k], gate_hi[k], gate_hi[k], gate_lo[k]]
+            right += [hid_hi[k], hid_lo[k], hid_hi[k], tang_hi[k], tang_lo[k], tang_hi[k]]
+        sum_two[...] += mm_nt(beside(*left), beside(*right))
+        marks = stacked(*[hot[k] for k in both for _ in range(2)])
+        bars = beside(*[ref[k] for k in both for ref in (bar_hi, bar_lo)])
+        sum_codes[256:768, :] += mm(bars, marks)
+        bars = beside(*[ref[k] for k in both for ref in (low_hi, low_lo)])
+        sum_codes[0:256, :] += mm(bars, marks)
 
     def step_body(step, carry):
         waiting = [block_stages(step, s) for s in range(SUBS)]
@@ -674,7 +650,6 @@
 PARAMS = pltpu.CompilerParams(vmem_limit_bytes=48 * 1024 * 1024)
 
 
-HBM = pl.BlockSpec(memory_space=pltpu.HBM)
 SMEM = pl.BlockSpec(memory_space=pltpu.SMEM)
 
 
@@ -682,22 +657,14 @@
     return jax.ShapeDtypeStruct(shape, F32)
 
 
-def pack_boxes(weights, coords, distances, index):
+def pack_boxes(weights, points, index):
     return pl.pallas_call(
         pack_kernel,
         out_shape=f32(PEERS * BOX_ROWS, LANES),
-        in_specs=[HBM] * 4,
-        out_specs=HBM,
-        scratch_shapes=[
-            pltpu.VMEM(weights.shape, F32),
-            pltpu.VMEM(coords.shape, F32),
-            pltpu.VMEM(distances.shape, F32),
-            pltpu.VMEM(index.shape, jnp.int32),
-            pltpu.VMEM((PEERS * BOX_ROWS, LANES), F32),
-            pltpu.SemaphoreType.DMA((5,)),
-        ],
-        compiler_params=pltpu.CompilerParams(vmem_limit_bytes=60 * 1024 * 1024),
-    )(weights, coords, distances, index)
+        in_specs=vmem(3),
+        out_specs=vmem(1)[0],
+        compiler_params=PARAMS,
+    )(weights, points, index)
 
 
 def main_kernel(
@@ -831,9 +798,8 @@
     moment_one_out[...] = first
     moment_two_out[...] = second
     weights_copy_out[...] = value.astype(BF16)
-
-    def step(i, carry):
-        rows = pl.ds(pl.multiple_of(i * 64, 8), 64)
+    for r in range(0, CODE_ROWS, 32):
+        rows = slice(r, r + 32)
         value, first, second = adam_update(
             codes_ref[rows, :],
             code_first_ref[rows, :],
@@ -845,9 +811,6 @@
         code_first_out[rows, :] = first
         code_second_out[rows, :] = second
         codes_copy_out[rows, :] = value.astype(BF16)
-        return carry
-
-    lax.fori_loop(0, CODE_ROWS // 64, step, 0)
 
 
 def update_all(*args):
@@ -884,8 +847,7 @@
 ):
     boxes = pack_boxes(
         weights_flat.reshape(SHARD_ROWS, LANES),
-        coords,
-        distances.reshape(1, POINTS_DEV),
+        jnp.concatenate([coords, distances[None]]),
         shape_index.reshape(1, POINTS_DEV),
     )
     mine = exchange(boxes.reshape(PEERS, BOX_ROWS, LANES))

time: 92.9 us -> 93.2 us (level)
    pallas_call x1, Pallas kernels: 2.56 us -> 0.91 us  [pack_boxes(): pl.pallas_call(pack_kernel, out_shape=f32(PEERS * BOX_ROWS, LANES), in_sp...]
    pallas_call x1, Pallas kernels: 20.2 us -> 21.7 us  [main_call(): pl.pallas_call(main_kernel, out_shape=(boxes, boxes, f32(CODE_ROWS, LATEN...]
where the time goes in v17:
time: 93.2 us; the launch traced here: 92.8 us
  blocking collectives  61.4 us (66%)
  Pallas kernels  23.9 us (26%)
  waiting for transfers between devices  5.41 us (6%)
    all_to_all x3, blocking collectives, exchange(): return lax.all_to_all(v, ('z', 'wide'), split_axis=0, concat_axis=0)  61.4 us
    pallas_call x1, Pallas kernels, main_call(): pl.pallas_call(main_kernel, out_shape=(boxes, boxes, f32(CODE_ROWS, LATEN...  21.7 us
    ppermute x3, waiting for transfers between devices, swap_cores(): return lax.ppermute(v, 'core', [(0, 1), (1, 0)])  5.41 us
  transfers between devices with their start and end apart: 3, of which 3 were waited for; matrix products, arithmetic and copies ran while one was open for 0% of the time, Pallas kernels for 0%

profile of v17, /device:TPU:0, one launch (start us, length us, event | category | flops | bytes accessed | tf_op | source)
XLA Modules:
  0.0 92.8 jit_solution(6605031767387103257)
XLA Ops:
  0.6 0.0 copy-start.3
  0.7 0.0 copy-start.6
  0.7 0.8 pad_maximum_fusion.points_ref
  1.4 0.0 copy-done.3
  1.4 0.0 copy-done.6
  1.4 0.9 shard_map.168
  2.4 0.0 copy-start
  2.4 27.4 %all_to_all.15 = f32[64,24,128]{2,1,0:T(8,128)S(1)} all-to-all(f32[64,24,128]{2,1,0:T(8,128)S(1)} %bitcast.21), channel_id=1, replica_groups=mesh['z'=4,'core'=2,'wide'=16] {'z','wide'}, dimensions={0} | all-to-all | bytes 1572864 | tf_op jit(solution)/shard_map/all_to_all | solution.py:834
  29.8 0.0 collective-permute-start
  29.8 2.3 %collective-permute-done = f32[64,24,128]{2,1,0:T(8,128)S(1)} collective-permute-done((f32[64,24,128]{2,1,0:T(8,128)S(1)}, f32[64,24,128]{2,1,0:T(8,128)S(1)}, u32[]{:S(2)}, u32[]{:S(2)}) %collective-permute-start) | collective-permute-done | bytes 786464 | tf_op jit(solution)/shard_map/ppermute | solution.py:830
  32.1 0.0 copy-done
  32.1 21.7 %shard_map.169 = (f32[1344,128]{1,0:T(8,128)S(1)}, f32[1344,128]{1,0:T(8,128)S(1)}, f32[256,256]{1,0:T(8,128)S(1)}, f32[8,128]{1,0:T(8,128)S(1)}) custom-call(s32[1]{0:T(128)} %bitcast.core_ref, f32[1536,128]{1,0:T(8,128)S(1)} %bitcast.20, f32[1536,128]{1,0:T(8,128)S(1)} %bitcast.23, f32[256,256]{1,0:T(8,128)S(1)} %copy-done), custom_call_target="tpu_custom_call" | custom-call | tf_op jit(solution)/shard_map/pallas_call | solution.py:725
  53.8 0.4 collective-permute-start.1
  54.2 2.0 %collective-permute-done.1 = f32[1344,128]{1,0:T(8,128)S(1)} collective-permute-done((f32[1344,128]{1,0:T(8,128)S(1)}, f32[1344,128]{1,0:T(8,128)S(1)}, u32[]{:S(2)}, u32[]{:S(2)}) %collective-permute-start.1) | collective-permute-done | bytes 688160 | tf_op jit(solution)/shard_map/ppermute | solution.py:830
  56.2 0.1 add.6
  56.3 19.8 %all_to_all.16 = f32[64,1,2688]{2,1,0:T(1,128)S(1)} all-to-all(f32[64,1,2688]{2,1,0:T(1,128)S(1)} %bitcast.30), channel_id=1, replica_groups=mesh['z'=4,'core'=2,'wide'=16] {'z','wide'}, dimensions={0} | all-to-all | bytes 1376256 | tf_op jit(solution)/shard_map/all_to_all | solution.py:834
  76.1 0.0 copy-start.1
  76.1 0.0 copy-start.2
  76.1 0.2 shard_map.170
  76.3 0.0 collective-permute-start.2
  76.3 1.2 %collective-permute-done.2 = f32[8,128]{1,0:T(8,128)S(1)} collective-permute-done((f32[8,128]{1,0:T(8,128)S(1)}, f32[8,128]{1,0:T(8,128)S(1)}, u32[]{:S(2)}, u32[]{:S(2)}) %collective-permute-start.2) | collective-permute-done | bytes 4128 | tf_op jit(solution)/shard_map/ppermute | solution.py:830
  77.5 0.0 copy-start.4
  77.5 0.0 copy-start.5
  77.5 14.1 %all_to_all.17 = f32[64,1,128]{2,1,0:T(1,128)S(1)} all-to-all(f32[64,1,128]{2,1,0:T(1,128)S(1)} %reshape.83), channel_id=1, replica_groups=mesh['z'=4,'core'=2,'wide'=16] {'z','wide'}, dimensions={0} | all-to-all | bytes 65536 | tf_op jit(solution)/shard_map/all_to_all | solution.py:834
  91.6 0.0 copy-done.1
  91.6 0.0 copy-done.2
  91.6 0.0 copy-done.4
  91.7 0.0 copy-done.5
  91.7 1.2 %shard_map.171 = (f32[1,1]{1,0:T(1,128)}, f32[1,1]{1,0:T(1,128)}, f32[21,128]{1,0:T(8,128)}, f32[21,128]{1,0:T(8,128)}, f32[21,128]{1,0:T(8,128)}, /*index=5*/bf...) custom-call(f32[64,128]{1,0:T(8,128)S(1)} %bitcast.24, ...), custom_call_target="tpu_custom_call" | custom-call | tf_op jit(solution)/shard_map/pallas_call | solution.py:820
  (3 shorter events, 0.0 us)
Async XLA Ops:
  0.6 0.8 copy-start.3
  0.7 0.8 copy-start.6
  2.4 29.7 %copy-start = (f32[256,256]{1,0:T(8,128)S(1)}, f32[256,256]{1,0:T(8,128)}, u32[]{:S(2)}) copy-start(f32[256,256]{1,0:T(8,128)} %codes_ref.3) | copy-start | bytes 786436
  29.8 2.3 %collective-permute-start = (f32[64,24,128]{2,1,0:T(8,128)S(1)}, f32[64,24,128]{2,1,0:T(8,128)S(1)}, u32[]{:S(2)}, u32[]{:S(2)}) collective-permute-start(f32[64,24,128]{2,1,0:T(8,128)S(1)} %all_to_all.15), channel_id=1, source_target_pairs={{0,16},{16,0},{1,17},{17,1},{2,18},{18,2},{3,19},{19,3},{4,20},{20... | collective-permute-start | bytes 2359304 | tf_op jit(solution)/shard_map/ppermute | solution.py:830
  53.8 2.4 %collective-permute-start.1 = (f32[1344,128]{1,0:T(8,128)S(1)}, f32[1344,128]{1,0:T(8,128)S(1)}, u32[]{:S(2)}, u32[]{:S(2)}) collective-permute-start(f32[1344,128]{1,0:T(8,128)S(1)} %get-tuple-element.27), channel_id=1, source_target_pairs={{0,16},{16,0},{1,17},{17,1},{2,18},{18,2},{3,19},{19,3},{4,20},{20... | collective-permute-start | bytes 2064392 | tf_op jit(solution)/shard_map/ppermute | solution.py:830
  76.1 15.5 %copy-start.1 = (f32[256,256]{1,0:T(8,128)S(1)}, f32[256,256]{1,0:T(8,128)}, u32[]{:S(2)}) copy-start(f32[256,256]{1,0:T(8,128)} %code_first_ref.1) | copy-start | bytes 786436
  76.1 15.5 %copy-start.2 = (f32[256,256]{1,0:T(8,128)S(1)}, f32[256,256]{1,0:T(8,128)}, u32[]{:S(2)}) copy-start(f32[256,256]{1,0:T(8,128)} %code_second_ref.1) | copy-start | bytes 786436
  76.3 1.2 %collective-permute-start.2 = (f32[8,128]{1,0:T(8,128)S(1)}, f32[8,128]{1,0:T(8,128)S(1)}, u32[]{:S(2)}, u32[]{:S(2)}) collective-permute-start(f32[8,128]{1,0:T(8,128)S(1)} %get-tuple-element.29), channel_id=1, source_target_pairs={{0,16},{16,0},{1,17},{17,1},{2,18},{18,2},{3,19},{19,3},{4,20},{20... | collective-permute-start | bytes 12296 | tf_op jit(solution)/shard_map/ppermute | solution.py:830
  77.5 14.1 %copy-start.4 = (f32[2688]{0:T(1024)S(1)}, f32[2688]{0:T(1024)}, u32[]{:S(2)}) copy-start(f32[2688]{0:T(1024)} %param.10) | copy-start | bytes 32260
  77.5 14.1 %copy-start.5 = (f32[2688]{0:T(1024)S(1)}, f32[2688]{0:T(1024)}, u32[]{:S(2)}) copy-start(f32[2688]{0:T(1024)} %param.11) | copy-start | bytes 32260

commit v18 on v17

--- a/solution.py
+++ b/solution.py
@@ -468,6 +468,9 @@
             )
         yield
         act_tang[s] = mm(lhs_two[...], stacked(tang_hi[s], tang_lo[s], tang_hi[s]))
+        sum_two[...] += mm_nt(
+            beside(gate_hi[s], gate_hi[s], gate_lo[s]), beside(tang_hi[s], tang_lo[s], tang_hi[s])
+        )
 
         for c in range(0, CODE_ROWS, LANES):
             code = (rows_of_lanes(1, (LANES, LANES)) + c).astype(F32)
@@ -493,6 +496,11 @@
         yield
 
         back_one[s] = mm(lhs_back[...], stacked(bar_hi[s], bar_lo[s], bar_hi[s]))
+        sum_two[...] += mm_nt(
+            beside(bar_hi[s], bar_hi[s], bar_lo[s]), beside(hid_hi[s], hid_lo[s], hid_hi[s])
+        )
+        marks = stacked(hot[s], hot[s])
+        sum_codes[256:768, :] += mm(beside(bar_hi[s], bar_lo[s]), marks)
         yield
         for r in low_chunks:
             bar = (
@@ -506,19 +514,7 @@
             low_lo[s, r : r + chunk, :] = low
         yield
 
-        if s % 2 == 0:
-            return
-        both = (s - 1, s)
-        left, right = [], []
-        for k in both:
-            left += [bar_hi[k], bar_hi[k], bar_lo[k], gate_hi[k], gate_hi[k], gate_lo[k]]
-            right += [hid_hi[k], hid_lo[k], hid_hi[k], tang_hi[k], tang_lo[k], tang_hi[k]]
-        sum_two[...] += mm_nt(beside(*left), beside(*right))
-        marks = stacked(*[hot[k] for k in both for _ in range(2)])
-        bars = beside(*[ref[k] for k in both for ref in (bar_hi, bar_lo)])
-        sum_codes[256:768, :] += mm(bars, marks)
-        bars = beside(*[ref[k] for k in both for ref in (low_hi, low_lo)])
-        sum_codes[0:256, :] += mm(bars, marks)
+        sum_codes[0:256, :] += mm(beside(low_hi[s], low_lo[s]), marks)
 
     def step_body(step, carry):
         waiting = [block_stages(step, s) for s in range(SUBS)]

time: 93.2 us -> 91.6 us (0.983)
  Pallas kernels: 23.9 us -> 22.4 us
    pallas_call x1, Pallas kernels: 21.7 us -> 20.2 us  [main_call(): pl.pallas_call(main_kernel, out_shape=(boxes, boxes, f32(CODE_ROWS, LATEN...]
where the time goes in v18:
time: 91.6 us; the launch traced here: 91.3 us
  blocking collectives  61.6 us (67%)
  Pallas kernels  22.4 us (24%)
  waiting for transfers between devices  5.4 us (6%)
    all_to_all x3, blocking collectives, exchange(): return lax.all_to_all(v, ('z', 'wide'), split_axis=0, concat_axis=0)  61.6 us
    pallas_call x1, Pallas kernels, main_call(): pl.pallas_call(main_kernel, out_shape=(boxes, boxes, f32(CODE_ROWS, LATEN...  20.2 us
    ppermute x3, waiting for transfers between devices, swap_cores(): return lax.ppermute(v, 'core', [(0, 1), (1, 0)])  5.4 us
  transfers between devices with their start and end apart: 3, of which 3 were waited for; matrix products, arithmetic and copies ran while one was open for 0% of the time, Pallas kernels for 0%

profile of v18, /device:TPU:0, one launch (start us, length us, event | category | flops | bytes accessed | tf_op | source)
XLA Modules:
  0.0 91.3 jit_solution(9994283893586618785)
XLA Ops:
  0.6 0.0 copy-start.3
  0.7 0.0 copy-start.6
  0.7 0.8 pad_maximum_fusion.points_ref
  1.4 0.0 copy-done.3
  1.4 0.0 copy-done.6
  1.4 0.9 shard_map.168
  2.4 0.0 copy-start
  2.4 27.4 %all_to_all.15 = f32[64,24,128]{2,1,0:T(8,128)S(1)} all-to-all(f32[64,24,128]{2,1,0:T(8,128)S(1)} %bitcast.21), channel_id=1, replica_groups=mesh['z'=4,'core'=2,'wide'=16] {'z','wide'}, dimensions={0} | all-to-all | bytes 1572864 | tf_op jit(solution)/shard_map/all_to_all | solution.py:830
  29.8 0.0 collective-permute-start
  29.8 2.3 %collective-permute-done = f32[64,24,128]{2,1,0:T(8,128)S(1)} collective-permute-done((f32[64,24,128]{2,1,0:T(8,128)S(1)}, f32[64,24,128]{2,1,0:T(8,128)S(1)}, u32[]{:S(2)}, u32[]{:S(2)}) %collective-permute-start) | collective-permute-done | bytes 786464 | tf_op jit(solution)/shard_map/ppermute | solution.py:826
  32.1 0.0 copy-done
  32.1 20.2 %shard_map.169 = (f32[1344,128]{1,0:T(8,128)S(1)}, f32[1344,128]{1,0:T(8,128)S(1)}, f32[256,256]{1,0:T(8,128)S(1)}, f32[8,128]{1,0:T(8,128)S(1)}) custom-call(s32[1]{0:T(128)} %bitcast.core_ref, f32[1536,128]{1,0:T(8,128)S(1)} %bitcast.20, f32[1536,128]{1,0:T(8,128)S(1)} %bitcast.23, f32[256,256]{1,0:T(8,128)S(1)} %copy-done), custom_call_target="tpu_custom_call" | custom-call | tf_op jit(solution)/shard_map/pallas_call | solution.py:721
  52.3 0.3 collective-permute-start.1
  52.5 2.0 %collective-permute-done.1 = f32[1344,128]{1,0:T(8,128)S(1)} collective-permute-done((f32[1344,128]{1,0:T(8,128)S(1)}, f32[1344,128]{1,0:T(8,128)S(1)}, u32[]{:S(2)}, u32[]{:S(2)}) %collective-permute-start.1) | collective-permute-done | bytes 688160 | tf_op jit(solution)/shard_map/ppermute | solution.py:826
  54.5 0.1 add.6
  54.6 20.0 %all_to_all.16 = f32[64,1,2688]{2,1,0:T(1,128)S(1)} all-to-all(f32[64,1,2688]{2,1,0:T(1,128)S(1)} %bitcast.30), channel_id=1, replica_groups=mesh['z'=4,'core'=2,'wide'=16] {'z','wide'}, dimensions={0} | all-to-all | bytes 1376256 | tf_op jit(solution)/shard_map/all_to_all | solution.py:830
  74.6 0.0 copy-start.1
  74.6 0.0 copy-start.2
  74.6 0.2 shard_map.170
  74.8 0.0 collective-permute-start.2
  74.8 1.2 %collective-permute-done.2 = f32[8,128]{1,0:T(8,128)S(1)} collective-permute-done((f32[8,128]{1,0:T(8,128)S(1)}, f32[8,128]{1,0:T(8,128)S(1)}, u32[]{:S(2)}, u32[]{:S(2)}) %collective-permute-start.2) | collective-permute-done | bytes 4128 | tf_op jit(solution)/shard_map/ppermute | solution.py:826
  76.0 0.0 copy-start.4
  76.0 0.0 copy-start.5
  76.0 14.1 %all_to_all.17 = f32[64,1,128]{2,1,0:T(1,128)S(1)} all-to-all(f32[64,1,128]{2,1,0:T(1,128)S(1)} %reshape.83), channel_id=1, replica_groups=mesh['z'=4,'core'=2,'wide'=16] {'z','wide'}, dimensions={0} | all-to-all | bytes 65536 | tf_op jit(solution)/shard_map/all_to_all | solution.py:830
  90.1 0.0 copy-done.1
  90.1 0.0 copy-done.2
  90.1 0.0 copy-done.4
  90.1 0.0 copy-done.5
  90.2 1.2 %shard_map.171 = (f32[1,1]{1,0:T(1,128)}, f32[1,1]{1,0:T(1,128)}, f32[21,128]{1,0:T(8,128)}, f32[21,128]{1,0:T(8,128)}, f32[21,128]{1,0:T(8,128)}, /*index=5*/bf...) custom-call(f32[64,128]{1,0:T(8,128)S(1)} %bitcast.24, ...), custom_call_target="tpu_custom_call" | custom-call | tf_op jit(solution)/shard_map/pallas_call | solution.py:816
  (3 shorter events, 0.0 us)
Async XLA Ops:
  0.6 0.8 copy-start.3
  0.7 0.8 copy-start.6
  2.4 29.7 %copy-start = (f32[256,256]{1,0:T(8,128)S(1)}, f32[256,256]{1,0:T(8,128)}, u32[]{:S(2)}) copy-start(f32[256,256]{1,0:T(8,128)} %codes_ref.3) | copy-start | bytes 786436
  29.8 2.3 %collective-permute-start = (f32[64,24,128]{2,1,0:T(8,128)S(1)}, f32[64,24,128]{2,1,0:T(8,128)S(1)}, u32[]{:S(2)}, u32[]{:S(2)}) collective-permute-start(f32[64,24,128]{2,1,0:T(8,128)S(1)} %all_to_all.15), channel_id=1, source_target_pairs={{0,16},{16,0},{1,17},{17,1},{2,18},{18,2},{3,19},{19,3},{4,20},{20... | collective-permute-start | bytes 2359304 | tf_op jit(solution)/shard_map/ppermute | solution.py:826
  52.3 2.2 %collective-permute-start.1 = (f32[1344,128]{1,0:T(8,128)S(1)}, f32[1344,128]{1,0:T(8,128)S(1)}, u32[]{:S(2)}, u32[]{:S(2)}) collective-permute-start(f32[1344,128]{1,0:T(8,128)S(1)} %get-tuple-element.27), channel_id=1, source_target_pairs={{0,16},{16,0},{1,17},{17,1},{2,18},{18,2},{3,19},{19,3},{4,20},{20... | collective-permute-start | bytes 2064392 | tf_op jit(solution)/shard_map/ppermute | solution.py:826
  74.6 15.5 %copy-start.1 = (f32[256,256]{1,0:T(8,128)S(1)}, f32[256,256]{1,0:T(8,128)}, u32[]{:S(2)}) copy-start(f32[256,256]{1,0:T(8,128)} %code_first_ref.1) | copy-start | bytes 786436
  74.6 15.5 %copy-start.2 = (f32[256,256]{1,0:T(8,128)S(1)}, f32[256,256]{1,0:T(8,128)}, u32[]{:S(2)}) copy-start(f32[256,256]{1,0:T(8,128)} %code_second_ref.1) | copy-start | bytes 786436
  74.8 1.2 %collective-permute-start.2 = (f32[8,128]{1,0:T(8,128)S(1)}, f32[8,128]{1,0:T(8,128)S(1)}, u32[]{:S(2)}, u32[]{:S(2)}) collective-permute-start(f32[8,128]{1,0:T(8,128)S(1)} %get-tuple-element.29), channel_id=1, source_target_pairs={{0,16},{16,0},{1,17},{17,1},{2,18},{18,2},{3,19},{19,3},{4,20},{20... | collective-permute-start | bytes 12296 | tf_op jit(solution)/shard_map/ppermute | solution.py:826
  76.0 14.1 %copy-start.4 = (f32[2688]{0:T(1024)S(1)}, f32[2688]{0:T(1024)}, u32[]{:S(2)}) copy-start(f32[2688]{0:T(1024)} %param.10) | copy-start | bytes 32260
  76.0 14.1 %copy-start.5 = (f32[2688]{0:T(1024)S(1)}, f32[2688]{0:T(1024)}, u32[]{:S(2)}) copy-start(f32[2688]{0:T(1024)} %param.11) | copy-start | bytes 32260

commit v19 on v18

--- a/solution.py
+++ b/solution.py
@@ -247,6 +247,7 @@
     slope_one,
     curve_one,
     back_one,
+    back_two,
     hid_hi,
     hid_lo,
     hot,
@@ -412,6 +413,16 @@
         summed = jnp.sum(total, axis=0, keepdims=True)
         yield
 
+        predicted = jnp.tanh(2.0 * summed + head_bias)
+        flank = 1.0 - predicted * predicted
+        capped = jnp.tanh(predicted / DELTA)
+        misfit = DELTA * capped - DELTA * jnp.tanh(target / DELTA)
+        square = misfit * misfit + SMOOTH * SMOOTH
+        inverse = lax.rsqrt(square)
+        fitting = square * inverse
+        by_fit = misfit * inverse * (1.0 - capped * capped)
+        share_flank = valid * (1.0 / ALL_POINTS) * flank
+
         back_one[s] = mm(lhs_back[...], stacked(gate_hi[s], gate_lo[s], gate_hi[s]))
         yield
         totals = [jnp.zeros((8, BLOCK), F32) for _ in range(3)]
@@ -427,22 +438,15 @@
             for i in range(3)
         ]
 
-        predicted = jnp.tanh(2.0 * summed + head_bias)
-        flank = 1.0 - predicted * predicted
         slope = [flank * q for q in lead]
         excess = slope[0] * slope[0] + slope[1] * slope[1] + slope[2] * slope[2] - 1.0
-        capped = jnp.tanh(predicted / DELTA)
-        misfit = DELTA * capped - DELTA * jnp.tanh(target / DELTA)
-        fitting = jnp.sqrt(misfit * misfit + SMOOTH * SMOOTH)
         sum_loss[0:1, :] += valid * (fitting + EIK_WEIGHT * excess * excess)
-        share = valid * (1.0 / ALL_POINTS)
         pull = [(4.0 * EIK_WEIGHT) * excess * v for v in slope]
         by_flank = sum(p * q for p, q in zip(pull, lead))
-        by_predicted = misfit / fitting * (1.0 - capped * capped) - 2.0 * predicted * by_flank
-        bar_out = share * by_predicted * flank
+        bar_out = share_flank * (by_fit - 2.0 * predicted * by_flank)
         sum_loss[1:2, :] += bar_out
         half_bar = 0.5 * bar_out
-        pull = [share * flank * p for p in pull]
+        pull = [share_flank * p for p in pull]
 
         last = stacked(blank5, *pull)
         twice = [2.0 * p for p in pull]
@@ -452,9 +456,6 @@
                 grad = grad + across(coord_w[r : r + chunk, i * LANES : (i + 1) * LANES]) * twice[i]
             slope = slope_one[s, r : r + chunk, :]
             back = back_one[s, r : r + chunk, :]
-            near = back * slope
-            for i in range(3):
-                sum_coord[r : r + chunk, i * LANES : (i + 1) * LANES] += folded(near * pull[i])
             through = grad * slope
             if r + chunk == 256:
                 inside = rows_of_lanes(0, (8, BLOCK)) < MIDDLE - 248
@@ -495,7 +496,7 @@
             bar_lo[s, r : r + chunk, :] = low
         yield
 
-        back_one[s] = mm(lhs_back[...], stacked(bar_hi[s], bar_lo[s], bar_hi[s]))
+        back_two[s] = mm(lhs_back[...], stacked(bar_hi[s], bar_lo[s], bar_hi[s]))
         sum_two[...] += mm_nt(
             beside(bar_hi[s], bar_hi[s], bar_lo[s]), beside(hid_hi[s], hid_lo[s], hid_hi[s])
         )
@@ -503,12 +504,13 @@
         sum_codes[256:768, :] += mm(beside(bar_hi[s], bar_lo[s]), marks)
         yield
         for r in low_chunks:
-            bar = (
-                back_one[s, r : r + chunk, :] * slope_one[s, r : r + chunk, :]
-                + curve_one[s, r : r + chunk, :]
-            )
+            slope = slope_one[s, r : r + chunk, :]
+            bar = back_two[s, r : r + chunk, :] * slope + curve_one[s, r : r + chunk, :]
+            near = back_one[s, r : r + chunk, :] * slope
             for i in range(3):
-                sum_coord[r : r + chunk, i * LANES : (i + 1) * LANES] += folded(bar * place[i])
+                sum_coord[r : r + chunk, i * LANES : (i + 1) * LANES] += folded(
+                    bar * place[i] + near * pull[i]
+                )
             high, low = halves(bar)
             low_hi[s, r : r + chunk, :] = high
             low_lo[s, r : r + chunk, :] = low
@@ -695,6 +697,7 @@
         ((256, 3 * LANES), F32),
         ((HID, 2 * LANES), F32),
         ((LANES, LANES), F32),
+        (pair, F32),
         (pair, F32),
         (pair, F32),
         (pair, F32),

time: 91.6 us -> 91.8 us (level)
  no operation moved by 1% of the time
where the time goes in v19:
time: 91.8 us; the launch traced here: 91.5 us
  blocking collectives  61.6 us (67%)
  Pallas kernels  22.6 us (25%)
  waiting for transfers between devices  5.4 us (6%)
    all_to_all x3, blocking collectives, exchange(): return lax.all_to_all(v, ('z', 'wide'), split_axis=0, concat_axis=0)  61.6 us
    pallas_call x1, Pallas kernels, main_call(): pl.pallas_call(main_kernel, out_shape=(boxes, boxes, f32(CODE_ROWS, LATEN...  20.3 us
    ppermute x3, waiting for transfers between devices, swap_cores(): return lax.ppermute(v, 'core', [(0, 1), (1, 0)])  5.4 us
  transfers between devices with their start and end apart: 3, of which 3 were waited for; matrix products, arithmetic and copies ran while one was open for 0% of the time, Pallas kernels for 0%

profile of v19, /device:TPU:0, one launch (start us, length us, event | category | flops | bytes accessed | tf_op | source)
XLA Modules:
  0.0 91.5 jit_solution(5504283250798731369)
XLA Ops:
  0.6 0.0 copy-start.3
  0.7 0.0 copy-start.6
  0.7 0.8 pad_maximum_fusion.points_ref
  1.4 0.0 copy-done.3
  1.4 0.0 copy-done.6
  1.4 0.9 shard_map.168
  2.4 0.0 copy-start
  2.4 27.4 %all_to_all.15 = f32[64,24,128]{2,1,0:T(8,128)S(1)} all-to-all(f32[64,24,128]{2,1,0:T(8,128)S(1)} %bitcast.21), channel_id=1, replica_groups=mesh['z'=4,'core'=2,'wide'=16] {'z','wide'}, dimensions={0} | all-to-all | bytes 1572864 | tf_op jit(solution)/shard_map/all_to_all | solution.py:833
  29.8 0.0 collective-permute-start
  29.8 2.3 %collective-permute-done = f32[64,24,128]{2,1,0:T(8,128)S(1)} collective-permute-done((f32[64,24,128]{2,1,0:T(8,128)S(1)}, f32[64,24,128]{2,1,0:T(8,128)S(1)}, u32[]{:S(2)}, u32[]{:S(2)}) %collective-permute-start) | collective-permute-done | bytes 786464 | tf_op jit(solution)/shard_map/ppermute | solution.py:829
  32.1 0.0 copy-done
  32.1 20.3 %shard_map.169 = (f32[1344,128]{1,0:T(8,128)S(1)}, f32[1344,128]{1,0:T(8,128)S(1)}, f32[256,256]{1,0:T(8,128)S(1)}, f32[8,128]{1,0:T(8,128)S(1)}) custom-call(s32[1]{0:T(128)} %bitcast.core_ref, f32[1536,128]{1,0:T(8,128)S(1)} %bitcast.20, f32[1536,128]{1,0:T(8,128)S(1)} %bitcast.23, f32[256,256]{1,0:T(8,128)S(1)} %copy-done), custom_call_target="tpu_custom_call" | custom-call | tf_op jit(solution)/shard_map/pallas_call | solution.py:724
  52.4 0.3 collective-permute-start.1
  52.7 2.0 %collective-permute-done.1 = f32[1344,128]{1,0:T(8,128)S(1)} collective-permute-done((f32[1344,128]{1,0:T(8,128)S(1)}, f32[1344,128]{1,0:T(8,128)S(1)}, u32[]{:S(2)}, u32[]{:S(2)}) %collective-permute-start.1) | collective-permute-done | bytes 688160 | tf_op jit(solution)/shard_map/ppermute | solution.py:829
  54.6 0.1 add.6
  54.7 20.0 %all_to_all.16 = f32[64,1,2688]{2,1,0:T(1,128)S(1)} all-to-all(f32[64,1,2688]{2,1,0:T(1,128)S(1)} %bitcast.30), channel_id=1, replica_groups=mesh['z'=4,'core'=2,'wide'=16] {'z','wide'}, dimensions={0} | all-to-all | bytes 1376256 | tf_op jit(solution)/shard_map/all_to_all | solution.py:833
  74.8 0.0 copy-start.1
  74.8 0.0 copy-start.2
  74.8 0.2 shard_map.170
  74.9 0.0 collective-permute-start.2
  74.9 1.2 %collective-permute-done.2 = f32[8,128]{1,0:T(8,128)S(1)} collective-permute-done((f32[8,128]{1,0:T(8,128)S(1)}, f32[8,128]{1,0:T(8,128)S(1)}, u32[]{:S(2)}, u32[]{:S(2)}) %collective-permute-start.2) | collective-permute-done | bytes 4128 | tf_op jit(solution)/shard_map/ppermute | solution.py:829
  76.1 0.0 copy-start.4
  76.1 0.0 copy-start.5
  76.2 14.1 %all_to_all.17 = f32[64,1,128]{2,1,0:T(1,128)S(1)} all-to-all(f32[64,1,128]{2,1,0:T(1,128)S(1)} %reshape.83), channel_id=1, replica_groups=mesh['z'=4,'core'=2,'wide'=16] {'z','wide'}, dimensions={0} | all-to-all | bytes 65536 | tf_op jit(solution)/shard_map/all_to_all | solution.py:833
  90.3 0.0 copy-done.1
  90.3 0.0 copy-done.2
  90.3 0.0 copy-done.4
  90.3 0.0 copy-done.5
  90.3 1.2 %shard_map.171 = (f32[1,1]{1,0:T(1,128)}, f32[1,1]{1,0:T(1,128)}, f32[21,128]{1,0:T(8,128)}, f32[21,128]{1,0:T(8,128)}, f32[21,128]{1,0:T(8,128)}, /*index=5*/bf...) custom-call(f32[64,128]{1,0:T(8,128)S(1)} %bitcast.24, ...), custom_call_target="tpu_custom_call" | custom-call | tf_op jit(solution)/shard_map/pallas_call | solution.py:819
  (3 shorter events, 0.0 us)
Async XLA Ops:
  0.6 0.8 copy-start.3
  0.7 0.8 copy-start.6
  2.4 29.7 %copy-start = (f32[256,256]{1,0:T(8,128)S(1)}, f32[256,256]{1,0:T(8,128)}, u32[]{:S(2)}) copy-start(f32[256,256]{1,0:T(8,128)} %codes_ref.3) | copy-start | bytes 786436
  29.8 2.3 %collective-permute-start = (f32[64,24,128]{2,1,0:T(8,128)S(1)}, f32[64,24,128]{2,1,0:T(8,128)S(1)}, u32[]{:S(2)}, u32[]{:S(2)}) collective-permute-start(f32[64,24,128]{2,1,0:T(8,128)S(1)} %all_to_all.15), channel_id=1, source_target_pairs={{0,16},{16,0},{1,17},{17,1},{2,18},{18,2},{3,19},{19,3},{4,20},{20... | collective-permute-start | bytes 2359304 | tf_op jit(solution)/shard_map/ppermute | solution.py:829
  52.4 2.2 %collective-permute-start.1 = (f32[1344,128]{1,0:T(8,128)S(1)}, f32[1344,128]{1,0:T(8,128)S(1)}, u32[]{:S(2)}, u32[]{:S(2)}) collective-permute-start(f32[1344,128]{1,0:T(8,128)S(1)} %get-tuple-element.27), channel_id=1, source_target_pairs={{0,16},{16,0},{1,17},{17,1},{2,18},{18,2},{3,19},{19,3},{4,20},{20... | collective-permute-start | bytes 2064392 | tf_op jit(solution)/shard_map/ppermute | solution.py:829
  74.8 15.5 %copy-start.1 = (f32[256,256]{1,0:T(8,128)S(1)}, f32[256,256]{1,0:T(8,128)}, u32[]{:S(2)}) copy-start(f32[256,256]{1,0:T(8,128)} %code_first_ref.1) | copy-start | bytes 786436
  74.8 15.5 %copy-start.2 = (f32[256,256]{1,0:T(8,128)S(1)}, f32[256,256]{1,0:T(8,128)}, u32[]{:S(2)}) copy-start(f32[256,256]{1,0:T(8,128)} %code_second_ref.1) | copy-start | bytes 786436
  74.9 1.2 %collective-permute-start.2 = (f32[8,128]{1,0:T(8,128)S(1)}, f32[8,128]{1,0:T(8,128)S(1)}, u32[]{:S(2)}, u32[]{:S(2)}) collective-permute-start(f32[8,128]{1,0:T(8,128)S(1)} %get-tuple-element.29), channel_id=1, source_target_pairs={{0,16},{16,0},{1,17},{17,1},{2,18},{18,2},{3,19},{19,3},{4,20},{20... | collective-permute-start | bytes 12296 | tf_op jit(solution)/shard_map/ppermute | solution.py:829
  76.1 14.1 %copy-start.4 = (f32[2688]{0:T(1024)S(1)}, f32[2688]{0:T(1024)}, u32[]{:S(2)}) copy-start(f32[2688]{0:T(1024)} %param.10) | copy-start | bytes 32260
  76.1 14.1 %copy-start.5 = (f32[2688]{0:T(1024)S(1)}, f32[2688]{0:T(1024)}, u32[]{:S(2)}) copy-start(f32[2688]{0:T(1024)} %param.11) | copy-start | bytes 32260

commit v20 on v19

--- a/solution.py
+++ b/solution.py
@@ -348,7 +348,7 @@
         return beside(*[spots[pl.ds(first + i, 1), :] for i in range(TILES)])
 
     blank5 = jnp.zeros((5, BLOCK), F32)
-    chunk = 8192 // BLOCK
+    chunk = 4096 // BLOCK
     low_chunks = range(0, 256, chunk)
     high_chunks = range(0, HID, chunk)
 

time: 91.8 us -> 91.8 us (level)
  no operation moved by 1% of the time
where the time goes in v20:
time: 91.8 us; the launch traced here: 91.5 us
  blocking collectives  61.6 us (67%)
  Pallas kernels  22.6 us (25%)
  waiting for transfers between devices  5.41 us (6%)
    all_to_all x3, blocking collectives, exchange(): return lax.all_to_all(v, ('z', 'wide'), split_axis=0, concat_axis=0)  61.6 us
    pallas_call x1, Pallas kernels, main_call(): pl.pallas_call(main_kernel, out_shape=(boxes, boxes, f32(CODE_ROWS, LATEN...  20.3 us
    ppermute x3, waiting for transfers between devices, swap_cores(): return lax.ppermute(v, 'core', [(0, 1), (1, 0)])  5.41 us
  transfers between devices with their start and end apart: 3, of which 3 were waited for; matrix products, arithmetic and copies ran while one was open for 0% of the time, Pallas kernels for 0%

profile of v20, /device:TPU:0, one launch (start us, length us, event | category | flops | bytes accessed | tf_op | source)
XLA Modules:
  0.0 91.5 jit_solution(10615874009274029926)
XLA Ops:
  0.6 0.0 copy-start.3
  0.7 0.0 copy-start.6
  0.7 0.8 pad_maximum_fusion.points_ref
  1.4 0.0 copy-done.3
  1.4 0.0 copy-done.6
  1.4 0.9 shard_map.168
  2.4 0.0 copy-start
  2.4 27.4 %all_to_all.15 = f32[64,24,128]{2,1,0:T(8,128)S(1)} all-to-all(f32[64,24,128]{2,1,0:T(8,128)S(1)} %bitcast.21), channel_id=1, replica_groups=mesh['z'=4,'core'=2,'wide'=16] {'z','wide'}, dimensions={0} | all-to-all | bytes 1572864 | tf_op jit(solution)/shard_map/all_to_all | solution.py:833
  29.8 0.0 collective-permute-start
  29.8 2.3 %collective-permute-done = f32[64,24,128]{2,1,0:T(8,128)S(1)} collective-permute-done((f32[64,24,128]{2,1,0:T(8,128)S(1)}, f32[64,24,128]{2,1,0:T(8,128)S(1)}, u32[]{:S(2)}, u32[]{:S(2)}) %collective-permute-start) | collective-permute-done | bytes 786464 | tf_op jit(solution)/shard_map/ppermute | solution.py:829
  32.1 0.0 copy-done
  32.1 20.3 %shard_map.169 = (f32[1344,128]{1,0:T(8,128)S(1)}, f32[1344,128]{1,0:T(8,128)S(1)}, f32[256,256]{1,0:T(8,128)S(1)}, f32[8,128]{1,0:T(8,128)S(1)}) custom-call(s32[1]{0:T(128)} %bitcast.core_ref, f32[1536,128]{1,0:T(8,128)S(1)} %bitcast.20, f32[1536,128]{1,0:T(8,128)S(1)} %bitcast.23, f32[256,256]{1,0:T(8,128)S(1)} %copy-done), custom_call_target="tpu_custom_call" | custom-call | tf_op jit(solution)/shard_map/pallas_call | solution.py:724
  52.4 0.3 collective-permute-start.1
  52.7 2.0 %collective-permute-done.1 = f32[1344,128]{1,0:T(8,128)S(1)} collective-permute-done((f32[1344,128]{1,0:T(8,128)S(1)}, f32[1344,128]{1,0:T(8,128)S(1)}, u32[]{:S(2)}, u32[]{:S(2)}) %collective-permute-start.1) | collective-permute-done | bytes 688160 | tf_op jit(solution)/shard_map/ppermute | solution.py:829
  54.6 0.1 add.6
  54.7 20.0 %all_to_all.16 = f32[64,1,2688]{2,1,0:T(1,128)S(1)} all-to-all(f32[64,1,2688]{2,1,0:T(1,128)S(1)} %bitcast.30), channel_id=1, replica_groups=mesh['z'=4,'core'=2,'wide'=16] {'z','wide'}, dimensions={0} | all-to-all | bytes 1376256 | tf_op jit(solution)/shard_map/all_to_all | solution.py:833
  74.8 0.0 copy-start.1
  74.8 0.0 copy-start.2
  74.8 0.2 shard_map.170
  74.9 0.0 collective-permute-start.2
  75.0 1.2 %collective-permute-done.2 = f32[8,128]{1,0:T(8,128)S(1)} collective-permute-done((f32[8,128]{1,0:T(8,128)S(1)}, f32[8,128]{1,0:T(8,128)S(1)}, u32[]{:S(2)}, u32[]{:S(2)}) %collective-permute-start.2) | collective-permute-done | bytes 4128 | tf_op jit(solution)/shard_map/ppermute | solution.py:829
  76.1 0.0 copy-start.4
  76.2 0.0 copy-start.5
  76.2 14.1 %all_to_all.17 = f32[64,1,128]{2,1,0:T(1,128)S(1)} all-to-all(f32[64,1,128]{2,1,0:T(1,128)S(1)} %reshape.83), channel_id=1, replica_groups=mesh['z'=4,'core'=2,'wide'=16] {'z','wide'}, dimensions={0} | all-to-all | bytes 65536 | tf_op jit(solution)/shard_map/all_to_all | solution.py:833
  90.3 0.0 copy-done.1
  90.3 0.0 copy-done.2
  90.3 0.0 copy-done.4
  90.3 0.0 copy-done.5
  90.3 1.2 %shard_map.171 = (f32[1,1]{1,0:T(1,128)}, f32[1,1]{1,0:T(1,128)}, f32[21,128]{1,0:T(8,128)}, f32[21,128]{1,0:T(8,128)}, f32[21,128]{1,0:T(8,128)}, /*index=5*/bf...) custom-call(f32[64,128]{1,0:T(8,128)S(1)} %bitcast.24, ...), custom_call_target="tpu_custom_call" | custom-call | tf_op jit(solution)/shard_map/pallas_call | solution.py:819
  (3 shorter events, 0.0 us)
Async XLA Ops:
  0.6 0.8 copy-start.3
  0.7 0.8 copy-start.6
  2.4 29.7 %copy-start = (f32[256,256]{1,0:T(8,128)S(1)}, f32[256,256]{1,0:T(8,128)}, u32[]{:S(2)}) copy-start(f32[256,256]{1,0:T(8,128)} %codes_ref.3) | copy-start | bytes 786436
  29.8 2.3 %collective-permute-start = (f32[64,24,128]{2,1,0:T(8,128)S(1)}, f32[64,24,128]{2,1,0:T(8,128)S(1)}, u32[]{:S(2)}, u32[]{:S(2)}) collective-permute-start(f32[64,24,128]{2,1,0:T(8,128)S(1)} %all_to_all.15), channel_id=1, source_target_pairs={{0,16},{16,0},{1,17},{17,1},{2,18},{18,2},{3,19},{19,3},{4,20},{20... | collective-permute-start | bytes 2359304 | tf_op jit(solution)/shard_map/ppermute | solution.py:829
  52.4 2.2 %collective-permute-start.1 = (f32[1344,128]{1,0:T(8,128)S(1)}, f32[1344,128]{1,0:T(8,128)S(1)}, u32[]{:S(2)}, u32[]{:S(2)}) collective-permute-start(f32[1344,128]{1,0:T(8,128)S(1)} %get-tuple-element.27), channel_id=1, source_target_pairs={{0,16},{16,0},{1,17},{17,1},{2,18},{18,2},{3,19},{19,3},{4,20},{20... | collective-permute-start | bytes 2064392 | tf_op jit(solution)/shard_map/ppermute | solution.py:829
  74.8 15.5 %copy-start.1 = (f32[256,256]{1,0:T(8,128)S(1)}, f32[256,256]{1,0:T(8,128)}, u32[]{:S(2)}) copy-start(f32[256,256]{1,0:T(8,128)} %code_first_ref.1) | copy-start | bytes 786436
  74.8 15.5 %copy-start.2 = (f32[256,256]{1,0:T(8,128)S(1)}, f32[256,256]{1,0:T(8,128)}, u32[]{:S(2)}) copy-start(f32[256,256]{1,0:T(8,128)} %code_second_ref.1) | copy-start | bytes 786436
  74.9 1.2 %collective-permute-start.2 = (f32[8,128]{1,0:T(8,128)S(1)}, f32[8,128]{1,0:T(8,128)S(1)}, u32[]{:S(2)}, u32[]{:S(2)}) collective-permute-start(f32[8,128]{1,0:T(8,128)S(1)} %get-tuple-element.29), channel_id=1, source_target_pairs={{0,16},{16,0},{1,17},{17,1},{2,18},{18,2},{3,19},{19,3},{4,20},{20... | collective-permute-start | bytes 12296 | tf_op jit(solution)/shard_map/ppermute | solution.py:829
  76.1 14.1 %copy-start.4 = (f32[2688]{0:T(1024)S(1)}, f32[2688]{0:T(1024)}, u32[]{:S(2)}) copy-start(f32[2688]{0:T(1024)} %param.10) | copy-start | bytes 32260
  76.2 14.1 %copy-start.5 = (f32[2688]{0:T(1024)S(1)}, f32[2688]{0:T(1024)}, u32[]{:S(2)}) copy-start(f32[2688]{0:T(1024)} %param.11) | copy-start | bytes 32260

commit v21 on v18

--- a/solution.py
+++ b/solution.py
@@ -27,7 +27,7 @@
 DEVICES = 128
 PEERS = 64
 SHARD_ROWS = 21
-BOX_ROWS = 24
+BOX_ROWS = 23
 SLOTS = 16
 POINTS_DEV = 1024
 CODE_ROWS = 256
@@ -101,7 +101,7 @@
 
     def fill(i, carry):
         for k in range(8):
-            place = pl.ds(pl.multiple_of((i * 8 + k) * BOX_ROWS, 8), BOX_ROWS)
+            place = pl.ds(pl.multiple_of(i * 8 * BOX_ROWS, 8) + k * BOX_ROWS, BOX_ROWS)
             out_ref[place, :] = shard
         return carry
 
@@ -846,7 +846,7 @@
         jnp.concatenate([coords, distances[None]]),
         shape_index.reshape(1, POINTS_DEV),
     )
-    mine = exchange(boxes.reshape(PEERS, BOX_ROWS, LANES))
+    mine = exchange(boxes.reshape(PEERS, 1, BOX_ROWS * LANES))
     other = swap_cores(mine)
     core = lax.axis_index("core").astype(jnp.int32).reshape(1)
     keep, give, code_grad, facts = main_call(

time: 91.6 us -> 91.3 us (level)
  no operation moved by 1% of the time
where the time goes in v21:
time: 91.3 us; the launch traced here: 91 us
  blocking collectives  61.2 us (67%)
  Pallas kernels  22.4 us (25%)
  waiting for transfers between devices  5.36 us (6%)
    all_to_all x3, blocking collectives, exchange(): return lax.all_to_all(v, ('z', 'wide'), split_axis=0, concat_axis=0)  61.2 us
    pallas_call x1, Pallas kernels, main_call(): pl.pallas_call(main_kernel, out_shape=(boxes, boxes, f32(CODE_ROWS, LATEN...  20.2 us
    ppermute x3, waiting for transfers between devices, swap_cores(): return lax.ppermute(v, 'core', [(0, 1), (1, 0)])  5.36 us
  transfers between devices with their start and end apart: 3, of which 3 were waited for; matrix products, arithmetic and copies ran while one was open for 0% of the time, Pallas kernels for 0%

profile of v21, /device:TPU:0, one launch (start us, length us, event | category | flops | bytes accessed | tf_op | source)
XLA Modules:
  0.0 91.0 jit_solution(334347738410185518)
XLA Ops:
  0.6 0.0 copy-start.3
  0.7 0.0 copy-start.6
  0.7 0.8 pad_maximum_fusion.points_ref
  1.4 0.0 copy-done.3
  1.4 0.0 copy-done.6
  1.4 0.9 shard_map.168
  2.4 0.0 copy-start
  2.4 27.1 %all_to_all.15 = f32[64,1,2944]{2,1,0:T(1,128)S(1)} all-to-all(f32[64,1,2944]{2,1,0:T(1,128)S(1)} %bitcast.20), channel_id=1, replica_groups=mesh['z'=4,'core'=2,'wide'=16] {'z','wide'}, dimensions={0} | all-to-all | bytes 1507328 | tf_op jit(solution)/shard_map/all_to_all | solution.py:830
  29.4 0.0 collective-permute-start
  29.5 2.2 %collective-permute-done = f32[64,1,2944]{2,1,0:T(1,128)S(1)} collective-permute-done((f32[64,1,2944]{2,1,0:T(1,128)S(1)}, f32[64,1,2944]{2,1,0:T(1,128)S(1)}, u32[]{:S(2)}, u32[]{:S(2)}) %collective-permute-start) | collective-permute-done | bytes 753696 | tf_op jit(solution)/shard_map/ppermute | solution.py:826
  31.7 0.0 copy-done
  31.7 20.2 %shard_map.169 = (f32[1344,128]{1,0:T(8,128)S(1)}, f32[1344,128]{1,0:T(8,128)S(1)}, f32[256,256]{1,0:T(8,128)S(1)}, f32[8,128]{1,0:T(8,128)S(1)}) custom-call(s32[1]{0:T(128)} %bitcast.core_ref, f32[1472,128]{1,0:T(8,128)S(1)} %bitcast.21, f32[1472,128]{1,0:T(8,128)S(1)} %bitcast.23, f32[256,256]{1,0:T(8,128)S(1)} %copy-done), custom_call_target="tpu_custom_call" | custom-call | tf_op jit(solution)/shard_map/pallas_call | solution.py:721
  51.9 0.3 collective-permute-start.1
  52.1 2.0 %collective-permute-done.1 = f32[1344,128]{1,0:T(8,128)S(1)} collective-permute-done((f32[1344,128]{1,0:T(8,128)S(1)}, f32[1344,128]{1,0:T(8,128)S(1)}, u32[]{:S(2)}, u32[]{:S(2)}) %collective-permute-start.1) | collective-permute-done | bytes 688160 | tf_op jit(solution)/shard_map/ppermute | solution.py:826
  54.1 0.1 add.6
  54.2 20.0 %all_to_all.16 = f32[64,1,2688]{2,1,0:T(1,128)S(1)} all-to-all(f32[64,1,2688]{2,1,0:T(1,128)S(1)} %bitcast.30), channel_id=1, replica_groups=mesh['z'=4,'core'=2,'wide'=16] {'z','wide'}, dimensions={0} | all-to-all | bytes 1376256 | tf_op jit(solution)/shard_map/all_to_all | solution.py:830
  74.3 0.0 copy-start.1
  74.3 0.0 copy-start.2
  74.3 0.2 shard_map.170
  74.4 0.0 collective-permute-start.2
  74.4 1.2 %collective-permute-done.2 = f32[8,128]{1,0:T(8,128)S(1)} collective-permute-done((f32[8,128]{1,0:T(8,128)S(1)}, f32[8,128]{1,0:T(8,128)S(1)}, u32[]{:S(2)}, u32[]{:S(2)}) %collective-permute-start.2) | collective-permute-done | bytes 4128 | tf_op jit(solution)/shard_map/ppermute | solution.py:826
  75.6 0.0 copy-start.4
  75.6 0.0 copy-start.5
  75.6 14.1 %all_to_all.17 = f32[64,1,128]{2,1,0:T(1,128)S(1)} all-to-all(f32[64,1,128]{2,1,0:T(1,128)S(1)} %reshape.83), channel_id=1, replica_groups=mesh['z'=4,'core'=2,'wide'=16] {'z','wide'}, dimensions={0} | all-to-all | bytes 65536 | tf_op jit(solution)/shard_map/all_to_all | solution.py:830
  89.8 0.0 copy-done.1
  89.8 0.0 copy-done.2
  89.8 0.0 copy-done.4
  89.8 0.0 copy-done.5
  89.8 1.2 %shard_map.171 = (f32[1,1]{1,0:T(1,128)}, f32[1,1]{1,0:T(1,128)}, f32[21,128]{1,0:T(8,128)}, f32[21,128]{1,0:T(8,128)}, f32[21,128]{1,0:T(8,128)}, /*index=5*/bf...) custom-call(f32[64,128]{1,0:T(8,128)S(1)} %bitcast.24, ...), custom_call_target="tpu_custom_call" | custom-call | tf_op jit(solution)/shard_map/pallas_call | solution.py:816
  (3 shorter events, 0.0 us)
Async XLA Ops:
  0.6 0.8 copy-start.3
  0.7 0.8 copy-start.6
  2.4 29.3 %copy-start = (f32[256,256]{1,0:T(8,128)S(1)}, f32[256,256]{1,0:T(8,128)}, u32[]{:S(2)}) copy-start(f32[256,256]{1,0:T(8,128)} %codes_ref.3) | copy-start | bytes 786436
  29.4 2.2 %collective-permute-start = (f32[64,1,2944]{2,1,0:T(1,128)S(1)}, f32[64,1,2944]{2,1,0:T(1,128)S(1)}, u32[]{:S(2)}, u32[]{:S(2)}) collective-permute-start(f32[64,1,2944]{2,1,0:T(1,128)S(1)} %all_to_all.15), channel_id=1, source_target_pairs={{0,16},{16,0},{1,17},{17,1},{2,18},{18,2},{3,19},{19,3},{4,20},{20... | collective-permute-start | bytes 2261000 | tf_op jit(solution)/shard_map/ppermute | solution.py:826
  51.9 2.2 %collective-permute-start.1 = (f32[1344,128]{1,0:T(8,128)S(1)}, f32[1344,128]{1,0:T(8,128)S(1)}, u32[]{:S(2)}, u32[]{:S(2)}) collective-permute-start(f32[1344,128]{1,0:T(8,128)S(1)} %get-tuple-element.27), channel_id=1, source_target_pairs={{0,16},{16,0},{1,17},{17,1},{2,18},{18,2},{3,19},{19,3},{4,20},{20... | collective-permute-start | bytes 2064392 | tf_op jit(solution)/shard_map/ppermute | solution.py:826
  74.3 15.5 %copy-start.1 = (f32[256,256]{1,0:T(8,128)S(1)}, f32[256,256]{1,0:T(8,128)}, u32[]{:S(2)}) copy-start(f32[256,256]{1,0:T(8,128)} %code_first_ref.1) | copy-start | bytes 786436
  74.3 15.5 %copy-start.2 = (f32[256,256]{1,0:T(8,128)S(1)}, f32[256,256]{1,0:T(8,128)}, u32[]{:S(2)}) copy-start(f32[256,256]{1,0:T(8,128)} %code_second_ref.1) | copy-start | bytes 786436
  74.4 1.2 %collective-permute-start.2 = (f32[8,128]{1,0:T(8,128)S(1)}, f32[8,128]{1,0:T(8,128)S(1)}, u32[]{:S(2)}, u32[]{:S(2)}) collective-permute-start(f32[8,128]{1,0:T(8,128)S(1)} %get-tuple-element.29), channel_id=1, source_target_pairs={{0,16},{16,0},{1,17},{17,1},{2,18},{18,2},{3,19},{19,3},{4,20},{20... | collective-permute-start | bytes 12296 | tf_op jit(solution)/shard_map/ppermute | solution.py:826
  75.6 14.1 %copy-start.4 = (f32[2688]{0:T(1024)S(1)}, f32[2688]{0:T(1024)}, u32[]{:S(2)}) copy-start(f32[2688]{0:T(1024)} %param.10) | copy-start | bytes 32260
  75.6 14.1 %copy-start.5 = (f32[2688]{0:T(1024)S(1)}, f32[2688]{0:T(1024)}, u32[]{:S(2)}) copy-start(f32[2688]{0:T(1024)} %param.11) | copy-start | bytes 32260
